TPU v7x, 32 devices: a whole 2x2x4 slice. The times are simulated.
32 devices in a mesh: rows: 4 (over z), seq: 8 (over y, x, core).
Axes of the slice: x: 2, y: 2, z: 4, core: 2. Of those that a mesh axis runs over, the one named last changes fastest.
Arguments:
- hidden_in: bfloat16 [8, 512, 2048], P('rows', 'seq'), may hold values from -6 to 6
- attn_gain: bfloat16 [2048], P(('rows', 'seq')), may hold values from 0.5 to 1.5
- query_weight: bfloat16 [2048, 2048], P(('rows', 'seq')), may hold values from -0.125 to 0.125
- key_weight: bfloat16 [2048, 2048], P(('rows', 'seq')), may hold values from -0.125 to 0.125
- value_weight: bfloat16 [2048, 2048], P(('rows', 'seq')), may hold values from -0.125 to 0.125
- rate_weight: bfloat16 [2048, 32], P(('rows', 'seq')), may hold values from -0.125 to 0.125
- gate_weight: bfloat16 [2048, 2048], P(('rows', 'seq')), may hold values from -0.125 to 0.125
- init_weight: bfloat16 [2048, 64], P(('rows', 'seq')), may hold values from -0.75 to 0.75
- init_bias: bfloat16 [2048], P(('rows', 'seq')), may hold values from -2 to 2
- inner_gain: bfloat16 [2048], P(('rows', 'seq')), may hold values from 0.5 to 1.5
- inner_shift: bfloat16 [2048], P(('rows', 'seq')), may hold values from -2 to 2
- post_gain: bfloat16 [2048], P(('rows', 'seq')), may hold values from 0.5 to 1.5
- post_shift: bfloat16 [2048], P(('rows', 'seq')), may hold values from -2 to 2
- out_weight: bfloat16 [2048, 2048], P(('rows', 'seq')), may hold values from -0.25 to 0.25
- ffn_gain: bfloat16 [2048], P(('rows', 'seq')), may hold values from 0.5 to 1.5
- ffn_gate_weight: bfloat16 [2048, 5504], P(('rows', 'seq')), may hold values from -0.125 to 0.125
- ffn_up_weight: bfloat16 [2048, 5504], P(('rows', 'seq')), may hold values from -0.125 to 0.125
- ffn_down_weight: bfloat16 [5504, 2048], P(('rows', 'seq')), may hold values from -0.15625 to 0.15625
- doc_starts: int32 [8, 6], P('rows'), may hold values from 0 to 496, as said below
- out_grad: bfloat16 [8, 512, 2048], P('rows', 'seq'), may hold values from -6 to 6
Outputs:
- block_out: bfloat16 [8, 512, 2048], P('rows', 'seq')
- hidden_grad: float32 [8, 512, 2048], P('rows', 'seq')
- attn_gain_grad: float32 [2048], P(('rows', 'seq'))
- query_weight_grad: float32 [2048, 2048], P(('rows', 'seq'))
- key_weight_grad: float32 [2048, 2048], P(('rows', 'seq'))
- value_weight_grad: float32 [2048, 2048], P(('rows', 'seq'))
- rate_weight_grad: float32 [2048, 32], P(('rows', 'seq'))
- gate_weight_grad: float32 [2048, 2048], P(('rows', 'seq'))
- init_weight_grad: float32 [2048, 64], P(('rows', 'seq'))
- init_bias_grad: float32 [2048], P(('rows', 'seq'))
- inner_gain_grad: float32 [2048], P(('rows', 'seq'))
- inner_shift_grad: float32 [2048], P(('rows', 'seq'))
- post_gain_grad: float32 [2048], P(('rows', 'seq'))
- post_shift_grad: float32 [2048], P(('rows', 'seq'))
- out_weight_grad: float32 [2048, 2048], P(('rows', 'seq'))
- ffn_gain_grad: float32 [2048], P(('rows', 'seq'))
- ffn_gate_weight_grad: float32 [2048, 5504], P(('rows', 'seq'))
- ffn_up_weight_grad: float32 [2048, 5504], P(('rows', 'seq'))
- ffn_down_weight_grad: float32 [5504, 2048], P(('rows', 'seq'))
Inputs may be any that keep to these rules, and one draw needn't show every extreme that they name: `doc_starts`: every entry is a multiple of 16; entries of a row come in no particular order and may repeat. Position 0 of every row restarts as well. In each aligned block of 2 rows one row, drawn from the seed, has all its entries below 64 or above 448, with 0 and 496 among them.
All inputs are finite; a program needn't handle non-finite values.
Results may differ from a plain program's by a relative error of at most 0.0094.
Values may be sent and summed in bfloat16 or wider, within the bound.
No kernel may reach another device: no remote copies, remote signals or barrier semaphores. Data moves between devices by JAX's collectives and lax.ppermute only.
A program may use at most 448 MiB of HBM per device.

v0:
```python
import jax
import jax.numpy as jnp
from jax import lax
from jax.sharding import PartitionSpec as P

MINI = 16


EPSILON = 1e-06
BASE_RATE = 1.0
HIGHEST = lax.Precision.HIGHEST


def passed_along(value, axis, steps):
    count = lax.axis_size(axis)
    first, last = (max(0, -steps), min(count, count - steps))
    return lax.ppermute(value, axis, [(source, source + steps) for source in range(first, last)])


def standardize(values):
    center = values - jnp.mean(values, axis=-1, keepdims=True)
    spread = jnp.sqrt(jnp.mean(center * center, axis=-1, keepdims=True) + EPSILON)
    return (center / spread, spread)


def inner_step(carried, inputs, init_weight, init_offset, inner_gain, inner_shift):
    queries, keys_in, values_in, logits, restart = inputs
    start_state = jnp.concatenate([init_weight, init_offset[:, None, :]], axis=1)
    carried = jnp.where(restart[:, None, None, None], start_state[None], carried)
    weight = carried[:, :, :-1, :]
    offset = carried[:, :, -1, :]
    first_pass = jnp.einsum("rthd,rhde->rthe", keys_in, weight, precision=HIGHEST) + offset[:, None]
    normed, spread = standardize(first_pass)
    residue = (normed * inner_gain + inner_shift - (values_in - keys_in)) * inner_gain
    inner_grad = (
        residue
        - jnp.mean(residue, axis=-1, keepdims=True)
        - normed * jnp.mean(residue * normed, axis=-1, keepdims=True)
    ) / spread
    batch_len = queries.shape[1]
    head_dim = queries.shape[-1]
    position = jnp.arange(batch_len)
    causal = (position[:, None] >= position[None, :]).astype(jnp.float32)
    token_scale = 1.0 / (position + 1).astype(jnp.float32)
    rate_values = jax.nn.sigmoid(logits) * (BASE_RATE / head_dim)
    step_sizes = (token_scale[:, None] * causal)[None, None] * jnp.transpose(
        rate_values, (0, 2, 1)
    )[:, :, None, :]
    affinity = jnp.einsum("rthd,rshd->rhts", queries, keys_in, precision=HIGHEST)
    combined = (
        jnp.einsum("rthd,rhde->rthe", queries, weight, precision=HIGHEST)
        + offset[:, None]
        - jnp.einsum(
            "rhts,rshe->rthe", step_sizes * (affinity + 1.0), inner_grad, precision=HIGHEST
        )
    )
    rebuilt, _ = standardize(combined)
    result = queries + rebuilt * inner_gain + inner_shift
    per_source = jnp.transpose(step_sizes[:, :, -1, :], (0, 2, 1))
    weighted = per_source[..., None] * keys_in
    new_weight = weight - jnp.einsum("rshd,rshe->rhde", weighted, inner_grad, precision=HIGHEST)
    new_offset = offset - jnp.sum(per_source[..., None] * inner_grad, axis=1)
    return (jnp.concatenate([new_weight, new_offset[:, :, None, :]], axis=2), result)


def run_blocks(
    state,
    queries,
    keys_in,
    values_in,
    logits,
    restarts,
    init_weight,
    init_offset,
    inner_gain,
    inner_shift,
):

    def advance(carried, inputs):
        return jax.checkpoint(inner_step)(
            carried, inputs, init_weight, init_offset, inner_gain, inner_shift
        )

    return lax.scan(advance, state, (queries, keys_in, values_in, logits, restarts))


def gelu_tanh(values):
    return jax.nn.gelu(values, approximate=True)


def unpack_mixer(gathered, head_count, head_dim):
    return (
        gathered[0].astype(jnp.float32),
        gathered[1],
        gathered[2],
        gathered[3],
        gathered[4],
        gathered[5],
        gathered[6].astype(jnp.float32).reshape(head_count, head_dim, head_dim),
        gathered[7].astype(jnp.float32).reshape(head_count, head_dim),
        gathered[8].astype(jnp.float32).reshape(head_count, head_dim),
        gathered[9].astype(jnp.float32).reshape(head_count, head_dim),
        gathered[10].astype(jnp.float32),
        gathered[11].astype(jnp.float32),
        gathered[12],
        gathered[13].astype(jnp.float32),
    )


def shards(
    hidden_in,
    attn_gain,
    query_weight,
    key_weight,
    value_weight,
    rate_weight,
    gate_weight,
    init_weight,
    init_bias,
    inner_gain,
    inner_shift,
    post_gain,
    post_shift,
    out_weight,
    ffn_gain,
    ffn_gate_weight,
    ffn_up_weight,
    ffn_down_weight,
    doc_starts,
    out_grad,
):
    rows_here, stretch_len, model_width = hidden_in.shape
    head_count = rate_weight.shape[1]
    head_dim = init_weight.shape[1]
    blocks = stretch_len // MINI
    chain_len = lax.axis_size("seq")
    mixer_full = (
        lax.all_gather(attn_gain, ("rows", "seq"), axis=0, tiled=True),
        lax.all_gather(query_weight, ("rows", "seq"), axis=0, tiled=True),
        lax.all_gather(key_weight, ("rows", "seq"), axis=0, tiled=True),
        lax.all_gather(value_weight, ("rows", "seq"), axis=0, tiled=True),
        lax.all_gather(rate_weight, ("rows", "seq"), axis=0, tiled=True),
        lax.all_gather(gate_weight, ("rows", "seq"), axis=0, tiled=True),
        lax.all_gather(init_weight, ("rows", "seq"), axis=0, tiled=True),
        lax.all_gather(init_bias, ("rows", "seq"), axis=0, tiled=True),
        lax.all_gather(inner_gain, ("rows", "seq"), axis=0, tiled=True),
        lax.all_gather(inner_shift, ("rows", "seq"), axis=0, tiled=True),
        lax.all_gather(post_gain, ("rows", "seq"), axis=0, tiled=True),
        lax.all_gather(post_shift, ("rows", "seq"), axis=0, tiled=True),
        lax.all_gather(out_weight, ("rows", "seq"), axis=0, tiled=True),
        lax.all_gather(ffn_gain, ("rows", "seq"), axis=0, tiled=True),
    )
    (
        gain_attn,
        query_full,
        key_full,
        value_full,
        rate_full,
        gate_full,
        init_heads,
        bias_heads,
        inner_scale,
        inner_offset,
        post_scale,
        post_offset,
        output_full,
        gain_ffn,
    ) = unpack_mixer(mixer_full, head_count, head_dim)
    tokens = hidden_in.astype(jnp.float32).reshape(-1, model_width)
    inverse_one = lax.rsqrt(jnp.mean(tokens * tokens, axis=-1, keepdims=True) + EPSILON)
    normed = (tokens * inverse_one * gain_attn).astype(jnp.bfloat16)

    def project(matrix):
        return jnp.dot(normed, matrix, preferred_element_type=jnp.float32)

    queries = project(query_full)
    keys_out = project(key_full)
    values_out = project(value_full)
    gate_pre = project(gate_full)
    logits = project(rate_full)

    def arrange(values):
        return values.reshape(rows_here, blocks, MINI, head_count, -1).transpose(1, 0, 2, 3, 4)

    position = lax.axis_index("seq") * stretch_len + jnp.arange(blocks, dtype=jnp.int32) * MINI
    restarts = jnp.logical_or(
        position[None, :] == 0, jnp.any(doc_starts[:, :, None] == position[None, None, :], axis=1)
    ).T

    def stretch_pass(
        state,
        block_queries,
        block_keys,
        block_values,
        block_logits,
        start_weight,
        start_offset,
        gain_heads,
        shift_heads,
    ):
        return run_blocks(
            state,
            block_queries,
            block_keys,
            block_values,
            block_logits,
            restarts,
            start_weight,
            start_offset,
            gain_heads,
            shift_heads,
        )

    local_inputs = (
        arrange(queries),
        arrange(keys_out),
        arrange(values_out),
        arrange(logits)[..., 0],
        init_heads,
        bias_heads,
        inner_scale,
        inner_offset,
    )
    empty_state = jnp.zeros((rows_here, head_count, head_dim + 1, head_dim), jnp.float32)

    def forward_turn(turn_index, state):
        advanced, _ = stretch_pass(state, *local_inputs)
        return passed_along(advanced, "seq", 1)

    state_in = lax.fori_loop(0, chain_len - 1, forward_turn, empty_state)
    (state_out, results), pull_chain = jax.vjp(stretch_pass, state_in, *local_inputs)
    inner_out = results.transpose(1, 0, 2, 3, 4).reshape(-1, model_width)
    post_norm, post_spread = standardize(inner_out)
    post_out = post_norm * post_scale + post_offset
    gelu_value, gelu_pull = jax.vjp(gelu_tanh, gate_pre)
    gated = (gelu_value * post_out).astype(jnp.bfloat16)
    residual = tokens + jnp.dot(gated, output_full, preferred_element_type=jnp.float32)
    inverse_two = lax.rsqrt(jnp.mean(residual * residual, axis=-1, keepdims=True) + EPSILON)
    ffn_in = (residual * inverse_two * gain_ffn).astype(jnp.bfloat16)
    cotangent = out_grad.reshape(-1, model_width)
    ffn_full = (
        lax.all_gather(ffn_gate_weight, ("rows", "seq"), axis=0, tiled=True),
        lax.all_gather(ffn_up_weight, ("rows", "seq"), axis=0, tiled=True),
        lax.all_gather(ffn_down_weight, ("rows", "seq"), axis=0, tiled=True),
    )
    gate_value = jnp.dot(ffn_in, ffn_full[0], preferred_element_type=jnp.float32)
    up_value = jnp.dot(ffn_in, ffn_full[1], preferred_element_type=jnp.float32)
    sigmoid_gate = jax.nn.sigmoid(gate_value)
    active = (gate_value * sigmoid_gate * up_value).astype(jnp.bfloat16)
    summed = residual + jnp.dot(active, ffn_full[2], preferred_element_type=jnp.float32)
    block_out = summed.astype(jnp.bfloat16).reshape(rows_here, stretch_len, model_width)
    ffn_again = (
        lax.all_gather(ffn_gate_weight, ("rows", "seq"), axis=0, tiled=True),
        lax.all_gather(ffn_up_weight, ("rows", "seq"), axis=0, tiled=True),
        lax.all_gather(ffn_down_weight, ("rows", "seq"), axis=0, tiled=True),
    )
    gate_wide, up_wide, down_wide = (ffn_again[0], ffn_again[1], ffn_again[2])
    delta_active = jnp.einsum("td,fd->tf", cotangent, down_wide, preferred_element_type=jnp.float32)
    grad_down = jnp.einsum("tf,td->fd", active, cotangent, preferred_element_type=jnp.float32)
    delta_up = (delta_active * gate_value * sigmoid_gate).astype(jnp.bfloat16)
    delta_gate = (
        delta_active * up_value * sigmoid_gate * (1.0 + gate_value * (1.0 - sigmoid_gate))
    ).astype(jnp.bfloat16)
    grad_gate = jnp.einsum("td,tf->df", ffn_in, delta_gate, preferred_element_type=jnp.float32)
    grad_up = jnp.einsum("td,tf->df", ffn_in, delta_up, preferred_element_type=jnp.float32)
    delta_ffn = jnp.einsum(
        "tf,df->td", delta_up, up_wide, preferred_element_type=jnp.float32
    ) + jnp.einsum("tf,df->td", delta_gate, gate_wide, preferred_element_type=jnp.float32)
    ffn_grads = (
        lax.psum_scatter(grad_gate, ("rows", "seq"), scatter_dimension=0, tiled=True),
        lax.psum_scatter(grad_up, ("rows", "seq"), scatter_dimension=0, tiled=True),
        lax.psum_scatter(grad_down, ("rows", "seq"), scatter_dimension=0, tiled=True),
    )
    grad_gain_ffn = jnp.sum(delta_ffn * residual * inverse_two, axis=0)
    scaled_two = delta_ffn * gain_ffn
    delta_after = (
        cotangent.astype(jnp.float32)
        + inverse_two * scaled_two
        - residual * inverse_two**3 * jnp.mean(scaled_two * residual, axis=-1, keepdims=True)
    )
    delta_branch = delta_after.astype(jnp.bfloat16)
    grad_output = jnp.einsum("td,te->de", gated, delta_branch, preferred_element_type=jnp.float32)
    delta_gated = jnp.einsum(
        "te,de->td", delta_branch, output_full, preferred_element_type=jnp.float32
    )
    delta_pre = gelu_pull(delta_gated * post_out)[0].astype(jnp.bfloat16)
    delta_post = delta_gated * gelu_value
    grad_post_scale = jnp.sum(delta_post * post_norm, axis=0)
    grad_post_shift = jnp.sum(delta_post, axis=0)
    delta_norm = delta_post * post_scale
    delta_inner = (
        delta_norm
        - jnp.mean(delta_norm, axis=-1, keepdims=True)
        - post_norm * jnp.mean(delta_norm * post_norm, axis=-1, keepdims=True)
    ) / post_spread
    delta_results = delta_inner.reshape(rows_here, blocks, MINI, head_count, head_dim).transpose(
        1, 0, 2, 3, 4
    )

    def backward_turn(turn_index, state_grad):
        pulled_turn = pull_chain((state_grad, delta_results))
        return passed_along(pulled_turn[0], "seq", -1)

    incoming = lax.fori_loop(0, chain_len - 1, backward_turn, jnp.zeros_like(state_out))
    pulled = pull_chain((incoming, delta_results))

    def flatten_heads(values):
        return values.transpose(1, 0, 2, 3, 4).reshape(-1, model_width).astype(jnp.bfloat16)

    delta_queries = flatten_heads(pulled[1])
    delta_keys = flatten_heads(pulled[2])
    delta_values = flatten_heads(pulled[3])
    delta_rates = pulled[4].transpose(1, 0, 2, 3).reshape(-1, head_count).astype(jnp.bfloat16)

    def weight_grad(delta):
        return jnp.einsum("td,te->de", normed, delta, preferred_element_type=jnp.float32)

    def back_project(delta, matrix):
        return jnp.einsum("te,de->td", delta, matrix, preferred_element_type=jnp.float32)

    delta_normed = (
        back_project(delta_queries, query_full)
        + back_project(delta_keys, key_full)
        + back_project(delta_values, value_full)
        + back_project(delta_pre, gate_full)
        + back_project(delta_rates, rate_full)
    )
    grad_gain_attn = jnp.sum(delta_normed * tokens * inverse_one, axis=0)
    scaled_one = delta_normed * gain_attn
    hidden_grad = (
        delta_after
        + inverse_one * scaled_one
        - tokens * inverse_one**3 * jnp.mean(scaled_one * tokens, axis=-1, keepdims=True)
    )
    mixer_grads = (
        lax.psum_scatter(grad_gain_attn, ("rows", "seq"), scatter_dimension=0, tiled=True),
        lax.psum_scatter(
            weight_grad(delta_queries), ("rows", "seq"), scatter_dimension=0, tiled=True
        ),
        lax.psum_scatter(weight_grad(delta_keys), ("rows", "seq"), scatter_dimension=0, tiled=True),
        lax.psum_scatter(
            weight_grad(delta_values), ("rows", "seq"), scatter_dimension=0, tiled=True
        ),
        lax.psum_scatter(
            weight_grad(delta_rates), ("rows", "seq"), scatter_dimension=0, tiled=True
        ),
        lax.psum_scatter(weight_grad(delta_pre), ("rows", "seq"), scatter_dimension=0, tiled=True),
        lax.psum_scatter(
            pulled[5].reshape(-1, head_dim), ("rows", "seq"), scatter_dimension=0, tiled=True
        ),
        lax.psum_scatter(pulled[6].reshape(-1), ("rows", "seq"), scatter_dimension=0, tiled=True),
        lax.psum_scatter(pulled[7].reshape(-1), ("rows", "seq"), scatter_dimension=0, tiled=True),
        lax.psum_scatter(pulled[8].reshape(-1), ("rows", "seq"), scatter_dimension=0, tiled=True),
        lax.psum_scatter(grad_post_scale, ("rows", "seq"), scatter_dimension=0, tiled=True),
        lax.psum_scatter(grad_post_shift, ("rows", "seq"), scatter_dimension=0, tiled=True),
        lax.psum_scatter(grad_output, ("rows", "seq"), scatter_dimension=0, tiled=True),
        lax.psum_scatter(grad_gain_ffn, ("rows", "seq"), scatter_dimension=0, tiled=True),
    )
    return (
        block_out,
        hidden_grad.reshape(rows_here, stretch_len, model_width),
        mixer_grads[0],
        mixer_grads[1],
        mixer_grads[2],
        mixer_grads[3],
        mixer_grads[4],
        mixer_grads[5],
        mixer_grads[6],
        mixer_grads[7],
        mixer_grads[8],
        mixer_grads[9],
        mixer_grads[10],
        mixer_grads[11],
        mixer_grads[12],
        mixer_grads[13],
        ffn_grads[0],
        ffn_grads[1],
        ffn_grads[2],
    )


def solution(mesh):
    return jax.shard_map(
        shards,
        mesh=mesh,
        in_specs=(
            P("rows", "seq", None),
            P(("rows", "seq")),
            P(("rows", "seq"), None),
            P(("rows", "seq"), None),
            P(("rows", "seq"), None),
            P(("rows", "seq"), None),
            P(("rows", "seq"), None),
            P(("rows", "seq"), None),
            P(("rows", "seq")),
            P(("rows", "seq")),
            P(("rows", "seq")),
            P(("rows", "seq")),
            P(("rows", "seq")),
            P(("rows", "seq"), None),
            P(("rows", "seq")),
            P(("rows", "seq"), None),
            P(("rows", "seq"), None),
            P(("rows", "seq"), None),
            P("rows", None),
            P("rows", "seq", None),
        ),
        out_specs=(
            P("rows", "seq", None),
            P("rows", "seq", None),
            P(("rows", "seq")),
            P(("rows", "seq"), None),
            P(("rows", "seq"), None),
            P(("rows", "seq"), None),
            P(("rows", "seq"), None),
            P(("rows", "seq"), None),
            P(("rows", "seq"), None),
            P(("rows", "seq")),
            P(("rows", "seq")),
            P(("rows", "seq")),
            P(("rows", "seq")),
            P(("rows", "seq")),
            P(("rows", "seq"), None),
            P(("rows", "seq")),
            P(("rows", "seq"), None),
            P(("rows", "seq"), None),
            P(("rows", "seq"), None),
        ),
        check_vma=False,
    )
```

profile of v0, /device:TPU:0, one launch (start us, length us, event | category | flops | bytes accessed | tf_op | source)
XLA Modules:
  0.0 5122.9 jit_solution(68795810483459148)
XLA Ops:
  14.6 42.7 all-reduce.22
  68.1 43.3 all_gather.56
  111.5 38.0 all-gather
  151.7 12.3 copy.221
  173.4 12.3 copy.222
  194.0 814.8 %while.124 = (s32[]{:T(128)}, f32[2,32,65,64]{2,3,1,0:T(8,128)S(1)}, pred[4,2]{1,0:T(4,128)(4,1)}, f32[32,65,64]{2,1,0:T(8,128)S(1)}, f32[4,2,16,32]{2,3,1,0:T(8...) while((s32[]{:T(128)}, f32[2,32,65,64]{2,3,1,0:T(8,128)S(1)}, ...), condition=%wide.region_10.11_spmd.clone, body=%wide.region_2.10_spmd.sunk.clone | while | flops 103430704 | bytes 25831204 | solution.py:230
  196.6 75.1 %while.123 = (s32[]{:T(128)}, f32[2,32,65,64]{3,2,1,0:T(8,128)}, pred[4,2]{1,0:T(4,128)(4,1)}, f32[32,65,64]{2,1,0:T(8,128)S(1)}, f32[4,2,16,32]{2,3,1,0:T(8,128...) while((s32[]{:T(128)}, f32[2,32,65,64]{3,2,1,0:T(8,128)}, ...), condition=%wide.region_9.9_spmd, body=%wide.region_3.8_spmd.sunk | while | flops 103430704 | bytes 17311288 | solution.py:84
  282.9 75.1 %while.123 = (s32[]{:T(128)}, f32[2,32,65,64]{3,2,1,0:T(8,128)}, pred[4,2]{1,0:T(4,128)(4,1)}, f32[32,65,64]{2,1,0:T(8,128)S(1)}, f32[4,2,16,32]{2,3,1,0:T(8,128...) while((s32[]{:T(128)}, f32[2,32,65,64]{3,2,1,0:T(8,128)}, ...), condition=%wide.region_9.9_spmd, body=%wide.region_3.8_spmd.sunk | while | flops 103430704 | bytes 17311288 | solution.py:84
  361.1 36.6 collective-permute-start
  403.8 75.2 %while.123 = (s32[]{:T(128)}, f32[2,32,65,64]{3,2,1,0:T(8,128)}, pred[4,2]{1,0:T(4,128)(4,1)}, f32[32,65,64]{2,1,0:T(8,128)S(1)}, f32[4,2,16,32]{2,3,1,0:T(8,128...) while((s32[]{:T(128)}, f32[2,32,65,64]{3,2,1,0:T(8,128)}, ...), condition=%wide.region_9.9_spmd, body=%wide.region_3.8_spmd.sunk | while | flops 103430704 | bytes 17311288 | solution.py:84
  482.1 24.9 collective-permute-start
  512.9 75.3 %while.123 = (s32[]{:T(128)}, f32[2,32,65,64]{3,2,1,0:T(8,128)}, pred[4,2]{1,0:T(4,128)(4,1)}, f32[32,65,64]{2,1,0:T(8,128)S(1)}, f32[4,2,16,32]{2,3,1,0:T(8,128...) while((s32[]{:T(128)}, f32[2,32,65,64]{3,2,1,0:T(8,128)}, ...), condition=%wide.region_9.9_spmd, body=%wide.region_3.8_spmd.sunk | while | flops 103430704 | bytes 17311288 | solution.py:84
  591.4 51.2 collective-permute-start
  648.5 74.9 %while.123 = (s32[]{:T(128)}, f32[2,32,65,64]{3,2,1,0:T(8,128)}, pred[4,2]{1,0:T(4,128)(4,1)}, f32[32,65,64]{2,1,0:T(8,128)S(1)}, f32[4,2,16,32]{2,3,1,0:T(8,128...) while((s32[]{:T(128)}, f32[2,32,65,64]{3,2,1,0:T(8,128)}, ...), condition=%wide.region_9.9_spmd, body=%wide.region_3.8_spmd.sunk | while | flops 103430704 | bytes 17311288 | solution.py:84
  726.5 50.8 collective-permute-start
  783.2 75.3 %while.123 = (s32[]{:T(128)}, f32[2,32,65,64]{3,2,1,0:T(8,128)}, pred[4,2]{1,0:T(4,128)(4,1)}, f32[32,65,64]{2,1,0:T(8,128)S(1)}, f32[4,2,16,32]{2,3,1,0:T(8,128...) while((s32[]{:T(128)}, f32[2,32,65,64]{3,2,1,0:T(8,128)}, ...), condition=%wide.region_9.9_spmd, body=%wide.region_3.8_spmd.sunk | while | flops 103430704 | bytes 17311288 | solution.py:84
  861.6 35.9 collective-permute-start
  903.5 74.8 %while.123 = (s32[]{:T(128)}, f32[2,32,65,64]{3,2,1,0:T(8,128)}, pred[4,2]{1,0:T(4,128)(4,1)}, f32[32,65,64]{2,1,0:T(8,128)S(1)}, f32[4,2,16,32]{2,3,1,0:T(8,128...) while((s32[]{:T(128)}, f32[2,32,65,64]{3,2,1,0:T(8,128)}, ...), condition=%wide.region_9.9_spmd, body=%wide.region_3.8_spmd.sunk | while | flops 103430704 | bytes 17311288 | solution.py:84
  981.4 23.7 collective-permute-start
  1012.4 12.3 copy.227
  1024.7 6.7 convolution_bitcast_fusion.4
  1033.0 93.0 %while.127 = (s32[]{:T(128)}, f32[2,32,65,64]{3,2,1,0:T(8,128)S(1)}, f32[4,2,16,32,64]{4,2,3,1,0:T(8,128)}, f32[4,2,32,65,64]{4,3,2,1,0:T(8,128)}, pred[4,2]{1,0...) while((s32[]{:T(128)}, f32[2,32,65,64]{3,2,1,0:T(8,128)S(1)}, ...), condition=%wide.region_19.20_spmd.clone.clone, body=%wide.region_11.19_spmd.clone.sunk.clone | while | flops 179321344 | bytes 22950436 | solution.py:84
  1144.7 22.5 reshape.850
  1167.2 13.5 fusion.257
  1180.7 12.2 fusion.256
  1192.9 14.6 multiply_convert_fusion
  1207.5 14.0 fusion.258
  1221.5 13.7 multiply_reduce_fusion.30
  1236.4 8.5 multiply_reduce_fusion.31
  1252.4 1060.1 %while.126 = (s32[]{:T(128)}, f32[2,32,65,64]{2,3,1,0:T(8,128)}, f32[4,2,32,65,64]{4,3,2,1,0:T(8,128)}, f32[4,2,16,32,64]{4,2,3,1,0:T(8,128)}, f32[4,2,16,32,64]...) while((s32[]{:T(128)}, f32[2,32,65,64]{2,3,1,0:T(8,128)}, ...), condition=%wide.region_44.45_spmd.clone, body=%wide.region_26.44_spmd.sunk.clone | while | flops 296856128 | bytes 46816968 | solution.py:304
  1254.8 118.3 %while.125 = (s32[]{:T(128)}, f32[2,32,65,64]{3,2,1,0:T(8,128)S(1)}, f32[4,2,32,65,64]{4,3,2,1,0:T(8,128)}, f32[4,2,16,32,64]{4,2,3,1,0:T(8,128)}, f32[4,2,16,32...) while((s32[]{:T(128)}, f32[2,32,65,64]{3,2,1,0:T(8,128)S(1)}, ...), condition=%wide.region_43.43_spmd, body=%wide.region_27.42_spmd.sunk | while | flops 296856128 | bytes 34037080 | solution.py:84
  1376.4 26.1 collective-permute-done.1
  1406.0 118.3 %while.125 = (s32[]{:T(128)}, f32[2,32,65,64]{3,2,1,0:T(8,128)S(1)}, f32[4,2,32,65,64]{4,3,2,1,0:T(8,128)}, f32[4,2,16,32,64]{4,2,3,1,0:T(8,128)}, f32[4,2,16,32...) while((s32[]{:T(128)}, f32[2,32,65,64]{3,2,1,0:T(8,128)S(1)}, ...), condition=%wide.region_43.43_spmd, body=%wide.region_27.42_spmd.sunk | while | flops 296856128 | bytes 34037080 | solution.py:84
  1527.6 26.9 collective-permute-done.1
  1558.0 118.3 %while.125 = (s32[]{:T(128)}, f32[2,32,65,64]{3,2,1,0:T(8,128)S(1)}, f32[4,2,32,65,64]{4,3,2,1,0:T(8,128)}, f32[4,2,16,32,64]{4,2,3,1,0:T(8,128)}, f32[4,2,16,32...) while((s32[]{:T(128)}, f32[2,32,65,64]{3,2,1,0:T(8,128)S(1)}, ...), condition=%wide.region_43.43_spmd, body=%wide.region_27.42_spmd.sunk | while | flops 296856128 | bytes 34037080 | solution.py:84
  1679.6 26.3 collective-permute-done.1
  1709.4 118.3 %while.125 = (s32[]{:T(128)}, f32[2,32,65,64]{3,2,1,0:T(8,128)S(1)}, f32[4,2,32,65,64]{4,3,2,1,0:T(8,128)}, f32[4,2,16,32,64]{4,2,3,1,0:T(8,128)}, f32[4,2,16,32...) while((s32[]{:T(128)}, f32[2,32,65,64]{3,2,1,0:T(8,128)S(1)}, ...), condition=%wide.region_43.43_spmd, body=%wide.region_27.42_spmd.sunk | while | flops 296856128 | bytes 34037080 | solution.py:84
  1831.0 26.3 collective-permute-done.1
  1860.7 118.3 %while.125 = (s32[]{:T(128)}, f32[2,32,65,64]{3,2,1,0:T(8,128)S(1)}, f32[4,2,32,65,64]{4,3,2,1,0:T(8,128)}, f32[4,2,16,32,64]{4,2,3,1,0:T(8,128)}, f32[4,2,16,32...) while((s32[]{:T(128)}, f32[2,32,65,64]{3,2,1,0:T(8,128)S(1)}, ...), condition=%wide.region_43.43_spmd, body=%wide.region_27.42_spmd.sunk | while | flops 296856128 | bytes 34037080 | solution.py:84
  1982.3 26.3 collective-permute-done.1
  2012.0 118.3 %while.125 = (s32[]{:T(128)}, f32[2,32,65,64]{3,2,1,0:T(8,128)S(1)}, f32[4,2,32,65,64]{4,3,2,1,0:T(8,128)}, f32[4,2,16,32,64]{4,2,3,1,0:T(8,128)}, f32[4,2,16,32...) while((s32[]{:T(128)}, f32[2,32,65,64]{3,2,1,0:T(8,128)S(1)}, ...), condition=%wide.region_43.43_spmd, body=%wide.region_27.42_spmd.sunk | while | flops 296856128 | bytes 34037080 | solution.py:84
  2133.6 26.3 collective-permute-done.1
  2163.4 118.3 %while.125 = (s32[]{:T(128)}, f32[2,32,65,64]{3,2,1,0:T(8,128)S(1)}, f32[4,2,32,65,64]{4,3,2,1,0:T(8,128)}, f32[4,2,16,32,64]{4,2,3,1,0:T(8,128)}, f32[4,2,16,32...) while((s32[]{:T(128)}, f32[2,32,65,64]{3,2,1,0:T(8,128)S(1)}, ...), condition=%wide.region_43.43_spmd, body=%wide.region_27.42_spmd.sunk | while | flops 296856128 | bytes 34037080 | solution.py:84
  2285.0 26.3 collective-permute-done.1
  2316.4 265.8 %while.128 = (s32[]{:T(128)}, f32[32,64,64]{2,1,0:T(8,128)}, f32[32,64]{1,0:T(8,128)}, f32[32,64]{1,0:T(8,128)}, f32[32,64]{1,0:T(8,128)}, /*index=5*/f32[2,32,6...) while((s32[]{:T(128)}, f32[32,64,64]{2,1,0:T(8,128)}, ...), condition=%wide.region_70.71_spmd.clone.clone, body=%wide.region_45.70_spmd.clone.sunk.clone | while | flops 488797760 | bytes 84381272 | solution.py:84
  2587.4 8.1 fusion.260
  2597.8 8.1 fusion.261
  2608.2 8.2 fusion.262
  2618.1 9.9 fusion.234
  2628.1 9.7 fusion.227
  2639.3 17.5 fusion.264
  2658.1 17.4 fusion.265
  2678.2 17.6 fusion.266
  2695.8 779.1 %fusion.4 = f32[176,2048]{1,0:T(8,128)S(1)} fusion(f32[5504,2048]{1,0:T(8,128)} %fusion.266), kind=kCustom, calls=%all-reduce-scatter | all-reduce-scatter fusion | flops 11534337 | bytes 46530560
  3476.0 18.6 collective-permute-start.2
  3507.8 7.5 convolution_add_fusion.7
  3515.3 8.3 convolution_add_fusion.6
  3532.7 83.6 %all-reduce.21 = (f32[2048]{0:T(1024)S(1)}, f32[2048]{0:T(1024)S(1)}, f32[2048]{0:T(1024)S(1)}, f32[2048]{0:T(1024)S(1)}, f32[2048]{0:T(1024)S(1)}, /*index=5*/f32[2048]{0:T(1024)S(1)}, f32[2048]{0:T(1024)S(1)}) all-reduce(f32[2048]{0:T(1024)S(1)} %get-tuple-element.1884, ...), channel_id=2, replica_groups=mesh['rows'=4,'seq'=8] {'rows','seq'}, use_global_device_ids=true, to_apply=%region_73.74.clone | all-reduce | flops 14336 | bytes 114688
  3624.4 7.9 concatenate.37
  3635.0 143.0 %reduce-scatter.18.cloned.1.call-done = f32[64,2048]{1,0:T(8,128)} async-done(((f32[2048,2048]{1,0:T(8,128)}), f32[64,2048]{1,0:T(8,128)}) %reduce-scatter.18.cloned.1.call-update) | async-done | bytes 524304 | tf_op jit(solution)/shard_map/reduce_scatter | solution.py:341
  3778.0 187.3 %reduce-scatter.20.cloned.1.call-done = f32[64,2048]{1,0:T(8,128)} async-done(((f32[2048,2048]{1,0:T(8,128)}), f32[64,2048]{1,0:T(8,128)}) %reduce-scatter.20.cloned.1.call-update) | async-done | bytes 524304 | tf_op jit(solution)/shard_map/reduce_scatter | solution.py:347
  3965.3 187.2 %reduce-scatter.24.cloned.1.call-done = f32[64,2048]{1,0:T(8,128)} async-done(((f32[2048,2048]{1,0:T(8,128)}), f32[64,2048]{1,0:T(8,128)}) %reduce-scatter.24.cloned.1.call-update) | async-done | bytes 524304 | tf_op jit(solution)/shard_map/reduce_scatter | solution.py:356
  4152.5 478.7 %reduce-scatter.26.cloned.1.call-done = f32[64,5504]{1,0:T(8,128)} async-done(((f32[2048,5504]{1,0:T(8,128)}), f32[64,5504]{1,0:T(8,128)}) %reduce-scatter.26.cloned.1.call-update) | async-done | bytes 1409040 | tf_op jit(solution)/shard_map/reduce_scatter | solution.py:270
  4631.2 485.0 %reduce-scatter.28.cloned.1.call-done = f32[64,5504]{1,0:T(8,128)} async-done(((f32[2048,5504]{1,0:T(8,128)}), f32[64,5504]{1,0:T(8,128)}) %reduce-scatter.28.cloned.1.call-update) | async-done | bytes 1409040 | tf_op jit(solution)/shard_map/reduce_scatter | solution.py:271
  (3169 shorter events, 1904.3 us)
Async XLA Ops:
  7.3 144.4 %all-gather.13.cloned.1.call-start = ((), (), s32[]{:S(2)}) async-start(), calls=%async_computation.10 | async-start | bytes 8650752 | tf_op jit(solution)/shard_map/all_gather | solution.py:140
  8.0 165.4 %all-gather.15.cloned.1.call-start = ((), (), s32[]{:S(2)}) async-start(), calls=%async_computation.11 | async-start | bytes 8650752 | tf_op jit(solution)/shard_map/all_gather | solution.py:141
  8.7 1003.7 %all-gather.17.cloned.1.call-start = ((), (), s32[]{:S(2)}) async-start(), calls=%async_computation.12 | async-start | bytes 8650752 | tf_op jit(solution)/shard_map/all_gather | solution.py:139
  9.5 1123.5 %all-gather.11.cloned.1.call-start = ((), (), s32[]{:S(2)}) async-start(), calls=%async_computation.9 | async-start | bytes 8650752 | tf_op jit(solution)/shard_map/all_gather | solution.py:143
  10.1 1128.9 %all-gather.19.cloned.1.call-start = ((), (), s32[]{:S(2)}) async-start(), calls=%async_computation.13 | async-start | bytes 8650752 | tf_op jit(solution)/shard_map/all_gather | solution.py:150
  10.6 1134.1 %all-gather.25.cloned.1.call-start = ((), (), s32[]{:S(2)}) async-start(), calls=%async_computation.24 | async-start | bytes 23789568 | tf_op jit(solution)/shard_map/all_gather | solution.py:244
  11.2 1169.5 %all-gather.23.cloned.1.call-start = ((), (), s32[]{:S(2)}) async-start(), calls=%async_computation.15 | async-start | bytes 23248896 | tf_op jit(solution)/shard_map/all_gather | solution.py:243
  12.0 1180.9 %all-gather.21.cloned.1.call-start = ((), (), s32[]{:S(2)}) async-start(), calls=%async_computation.14 | async-start | bytes 23248896 | tf_op jit(solution)/shard_map/all_gather | solution.py:242
  12.7 3610.2 %reduce-scatter.30.cloned.1.call-start = ((), (), s32[]{:S(2)}) async-start(), calls=%async_computation.25 | async-start | bytes 1081344
  65.8 45.7 copy-start.101
  65.8 45.7 copy-start.113
  66.1 83.5 %copy-start.116 = (f32[128]{0:T(128)}, f32[128]{0:T(128)S(1)}, u32[]{:S(2)}) copy-start(f32[128]{0:T(128)S(1)} %rsqrt.53) | copy-start | bytes 1540
  66.3 119.4 %copy-start.27 = (bf16[2,64,2048]{2,1,0:T(8,128)(2,1)}, bf16[2,64,2048]{2,1,0:T(8,128)(2,1)S(1)}, u32[]{:S(2)}) copy-start(bf16[2,64,2048]{2,1,0:T(8,128)(2,1)S(1)} %fusion.218) | copy-start | bytes 1572868
  111.5 52.4 %copy-start.2 = (f32[32,64,64]{2,1,0:T(8,128)}, f32[32,64,64]{2,1,0:T(8,128)S(1)}, u32[]{:S(2)}) copy-start(f32[32,64,64]{2,1,0:T(8,128)S(1)} %convert.1) | copy-start | bytes 1572868
  274.8 6.1 collective-permute-start
  361.1 40.6 collective-permute-start
  482.1 28.7 collective-permute-start
  591.4 55.0 %collective-permute-start = (f32[2,32,65,64]{2,3,1,0:T(8,128)}, f32[2,32,65,64]{2,3,1,0:T(8,128)S(1)}, u32[]{:S(2)}, u32[]{:S(2)}) collective-permute-start(f32[2,32,65,64]{2,3,1,0:T(8,128)} %copy.287), channel_id=1, source_target_pairs={{0,1},{1,2},{2,3},{3,4},{4,5},{5,6},{6,7},{8,9},{9,10},{10,11},{11... | collective-permute-start | bytes 3194888 | tf_op jit(solution)/shard_map/while/body/eval_jaxpr/ppermute | solution.py:17
  726.5 54.7 %collective-permute-start = (f32[2,32,65,64]{2,3,1,0:T(8,128)}, f32[2,32,65,64]{2,3,1,0:T(8,128)S(1)}, u32[]{:S(2)}, u32[]{:S(2)}) collective-permute-start(f32[2,32,65,64]{2,3,1,0:T(8,128)} %copy.287), channel_id=1, source_target_pairs={{0,1},{1,2},{2,3},{3,4},{4,5},{5,6},{6,7},{8,9},{9,10},{10,11},{11... | collective-permute-start | bytes 3194888 | tf_op jit(solution)/shard_map/while/body/eval_jaxpr/ppermute | solution.py:17
  861.6 39.8 collective-permute-start
  981.4 27.5 collective-permute-start
  1128.2 116.7 %copy-start.109 = (f32[128]{0:T(128)}, f32[128]{0:T(128)S(1)}, u32[]{:S(2)}) copy-start(f32[128]{0:T(128)S(1)} %div.522) | copy-start | bytes 1540
  1128.8 116.2 %copy-start.111 = (f32[128]{0:T(128)}, f32[128]{0:T(128)S(1)}, u32[]{:S(2)}) copy-start(f32[128]{0:T(128)S(1)} %sqrt.132) | copy-start | bytes 1540
  1132.9 112.0 %copy-start.29 = (f32[128,2048]{1,0:T(8,128)}, f32[128,2048]{1,0:T(8,128)S(1)}, u32[]{:S(2)}) copy-start(f32[128,2048]{1,0:T(8,128)S(1)} %reshape.815) | copy-start | bytes 3145732
  1144.5 90.7 %copy-start.32 = (f32[128,2048]{1,0:T(8,128)}, f32[128,2048]{1,0:T(8,128)S(1)}, u32[]{:S(2)}) copy-start(f32[128,2048]{1,0:T(8,128)S(1)} %get-tuple-element.2132) | copy-start | bytes 3145732
  1144.7 48.2 copy-start.51
  1144.7 22.5 copy-start.64
  1375.1 27.4 collective-permute-start.1
  1526.3 28.2 collective-permute-start.1
  1678.3 27.6 collective-permute-start.1
  1829.7 27.6 collective-permute-start.1
  1981.0 27.6 collective-permute-start.1
  2132.3 27.6 collective-permute-start.1
  2283.7 27.6 collective-permute-start.1
  2341.3 31.2 copy-start.4
  2355.0 21.6 copy-start.6
  2355.0 21.5 copy-start.25
  2399.7 31.2 copy-start.4
  2413.3 21.6 copy-start.6
  2413.4 21.5 copy-start.25
  2459.1 31.2 copy-start.4
  2472.7 21.6 copy-start.6
  2472.8 21.5 copy-start.25
  2518.5 31.2 copy-start.4
  2532.1 21.6 copy-start.6
  2532.2 21.5 copy-start.25
  2585.6 1049.3 %reduce-scatter.22.cloned.1.call-start = ((), (), s32[]{:S(2)}) async-start(), calls=%async_computation.20 | async-start | bytes 1081344 | tf_op jit(solution)/shard_map/reduce_scatter | solution.py:348
  2586.2 1048.7 %reduce-scatter.14.cloned.1.call-start = ((), (), s32[]{:S(2)}) async-start(), calls=%async_computation.16 | async-start | bytes 17301504 | tf_op jit(solution)/shard_map/reduce_scatter | solution.py:337
  2595.5 1039.4 %reduce-scatter.16.cloned.1.call-start = ((), (), s32[]{:S(2)}) async-start(), calls=%async_computation.17 | async-start | bytes 17301504 | tf_op jit(solution)/shard_map/reduce_scatter | solution.py:340
  2605.9 1172.0 %reduce-scatter.18.cloned.1.call-start = ((), (), s32[]{:S(2)}) async-start(), calls=%async_computation.18 | async-start | bytes 17301504 | tf_op jit(solution)/shard_map/reduce_scatter | solution.py:341
  2616.5 1348.7 %reduce-scatter.20.cloned.1.call-start = ((), (), s32[]{:S(2)}) async-start(), calls=%async_computation.19 | async-start | bytes 17301504 | tf_op jit(solution)/shard_map/reduce_scatter | solution.py:347
  2628.0 1524.5 %reduce-scatter.24.cloned.1.call-start = ((), (), s32[]{:S(2)}) async-start(), calls=%async_computation.21 | async-start | bytes 17301504 | tf_op jit(solution)/shard_map/reduce_scatter | solution.py:356
  2637.8 1993.4 %reduce-scatter.26.cloned.1.call-start = ((), (), s32[]{:S(2)}) async-start(), calls=%async_computation.22 | async-start | bytes 46497792 | tf_op jit(solution)/shard_map/reduce_scatter | solution.py:270
  2656.8 2459.4 %reduce-scatter.28.cloned.1.call-start = ((), (), s32[]{:S(2)}) async-start(), calls=%async_computation.23 | async-start | bytes 46497792 | tf_op jit(solution)/shard_map/reduce_scatter | solution.py:271
  3474.9 26.2 copy-start.47
  3474.9 19.7 copy-start.69
  3476.0 25.1 copy-start.71
  3476.0 148.4 %collective-permute-start.2 = (f32[124,2048]{1,0:T(8,128)}, f32[124,2048]{1,0:T(8,128)}, u32[]{:S(2)}, u32[]{:S(2)}) collective-permute-start(f32[124,2048]{1,0:T(8,128)} %slice.96), channel_id=1, source_target_pairs={{0,1},{1,2},{2,3},{3,4},{4,5},{5,6},{6,7},{7,8},{8,9},{9,10},{10,1... | collective-permute-start | bytes 3047432
  3494.6 29.0 slice-start
  3494.6 29.0 slice-start.1
  3501.2 22.4 slice-start.2
  3529.8 90.5 %copy-start.56 = (f32[128,2048]{1,0:T(8,128)S(1)}, f32[128,2048]{1,0:T(8,128)}, u32[]{:S(2)}) copy-start(f32[128,2048]{1,0:T(8,128)} %copy-done.55) | copy-start | bytes 3145732
  3529.8 90.5 %copy-start.119 = (f32[128]{0:T(128)S(1)}, f32[128]{0:T(128)}, u32[]{:S(2)}) copy-start(f32[128]{0:T(128)} %multiply_multiply_fusion.13) | copy-start | bytes 1540
  3532.7 91.7 %copy-start.48 = (f32[176,2048]{1,0:T(8,128)S(1)}, f32[176,2048]{1,0:T(8,128)}, u32[]{:S(2)}) copy-start(f32[176,2048]{1,0:T(8,128)} %copy-done.47) | copy-start | bytes 4325380
  (374 other events, 1531.2 us)
Sparse Core Ops, SparseCore 0:
  11.0 82.7 all-gather.12
  96.7 76.6 all-gather.14
  176.2 76.1 all-gather.16
  255.1 83.4 all-gather.10
  341.3 75.9 all-gather.18
  420.0 160.0 all-gather.24
  583.0 155.2 all-gather.22
  741.1 145.5 all-gather.20
  2585.8 184.7 reduce-scatter.29
  2773.3 142.3 reduce-scatter.21
  2918.6 350.1 reduce-scatter.13
  3271.5 318.0 reduce-scatter.15
  3592.5 185.4 reduce-scatter.17
  3780.7 184.5 reduce-scatter.19
  3968.0 184.4 reduce-scatter.23
  4155.2 475.9 reduce-scatter.25
  4633.9 482.1 reduce-scatter.27
where the time goes:
time: 5150 us; the launch traced here: 5120 us
  waiting for transfers between devices  1700 us (33%)
  matrix products  1150 us (22%)
  blocking collectives  987 us (19%)
  other arithmetic  545 us (11%)
  local copies, waits for them, and re-layouts  425 us (8%)
  starting transfers between devices  254 us (5%)
    unnamed x3, blocking collectives  905 us
    reduce_scatter x1, waiting for transfers between devices, shards(): lax.psum_scatter(grad_up, ('rows', 'seq'), scatter_dimension=0, tiled=True)  485 us
    reduce_scatter x1, waiting for transfers between devices, shards(): lax.psum_scatter(grad_gate, ('rows', 'seq'), scatter_dimension=0, tiled=T...  479 us
    dot_general x100, matrix products, inner_step(): jnp.einsum('rthd,rhde->rthe', keys_in, weight, precision=HIGHEST)  293 us
    dot_general x68, matrix products, inner_step(): jnp.einsum('rshd,rshe->rhde', weighted, inner_grad, precision=HIGHEST)  266 us
    ppermute x14, starting transfers between devices, passed_along(): lax.ppermute(value, axis, [(source, source + steps) for source in range(f...  234 us
    ppermute x14, waiting for transfers between devices, passed_along(): lax.ppermute(value, axis, [(source, source + steps) for source in range(f...  211 us
    dot_general x72, matrix products, inner_step(): jnp.einsum('rthd,rhde->rthe', queries, weight, precision=HIGHEST)  203 us
  transfers between devices with their start and end apart: 32, of which 20 were waited for; matrix products, arithmetic and copies ran while one was open for 34% of the time, Pallas kernels for 0%

commit v1 on v0

v1 whole, which is shorter than its diff:
```python
import functools
import jax
import jax.numpy as jnp
from jax import lax
from jax.experimental import pallas as pl
from jax.experimental.pallas import tpu as pltpu
from jax.sharding import PartitionSpec as P

MINI = 16
EPSILON = 1e-06
BASE_RATE = 1.0
F32 = jnp.float32
BF16 = jnp.bfloat16
NN = (((1,), (0,)), ((), ()))
NT = (((1,), (1,)), ((), ()))
TN = (((0,), (0,)), ((), ()))


def mm(left, right, dims):
    return lax.dot_general(left, right, dims, preferred_element_type=F32)


def packed(block, heads, head_dim, parts):
    turned = block.T
    width = block.shape[0] // parts
    return [
        jnp.concatenate(
            [
                turned[h * head_dim : (h + 1) * head_dim, j * width : (j + 1) * width]
                for h in range(heads)
            ],
            axis=1,
        )
        for j in range(parts)
    ]


def unpacked(pieces, heads):
    width = pieces[0].shape[1] // heads
    turned = jnp.concatenate(
        [
            jnp.concatenate([piece[:, h * width : (h + 1) * width] for piece in pieces], axis=1)
            for h in range(heads)
        ],
        axis=0,
    )
    return turned.T


def mean0(values):
    return jnp.mean(values, axis=0, keepdims=True)


def masks(chains, head_dim, dtype):
    lanes = chains * MINI
    rows = lax.broadcasted_iota(jnp.int32, (chains * head_dim, lanes), 0) // head_dim
    cols = lax.broadcasted_iota(jnp.int32, (chains * head_dim, lanes), 1) // MINI
    spread = rows == cols
    source = lax.broadcasted_iota(jnp.int32, (lanes, lanes), 0)
    target = lax.broadcasted_iota(jnp.int32, (lanes, lanes), 1)
    together = (source // MINI) == (target // MINI)
    earlier = jnp.logical_and(together, source <= target)
    scale = jnp.where(earlier, 1.0 / ((target % MINI) + 1).astype(F32), 0.0)
    return spread, together, scale


def spread_out(values, spread, chains):
    return jnp.where(spread, jnp.concatenate([values] * chains, axis=0), jnp.zeros((), values.dtype))


def forward_kernel(
    heads, head_dim, parts,
    slot_ref, queries_ref, keys_ref, values_ref, rate_ref, again_ref, again_wide_ref,
    start_ref, start_bias_ref, gain_ref, shift_ref,
    out_ref, normed_ref, spread_ref, grad_ref, rebuilt_ref, respread_ref, mix_ref, weight_ref,
    state, bias,
):
    chains = rate_ref.shape[-1] // MINI
    spread, together, scale = masks(chains, head_dim, BF16)
    ones = jnp.where(together, 1.0 / MINI, 0.0).astype(BF16)
    gain, shift = gain_ref[...], shift_ref[...]

    @pl.when(pl.program_id(0) == 0)
    def _():
        state[...] = jnp.zeros_like(state)
        bias[...] = jnp.zeros_like(bias)

    all_queries = packed(queries_ref[...], heads, head_dim, parts)
    all_keys = packed(keys_ref[...], heads, head_dim, parts)
    all_values = packed(values_ref[...], heads, head_dim, parts)
    weight = state[...]
    offset = bias[...]
    results = []
    for j in range(parts):
        query, key, value = all_queries[j], all_keys[j], all_values[j]
        rate = rate_ref[0, j : j + 1, :]
        low_key, low_query = key.astype(BF16), query.astype(BF16)
        wide_key = spread_out(low_key, spread, chains)
        wide_query = spread_out(low_query, spread, chains)
        mix = ((mm(low_key, low_query, TN) + 1.0) * scale).astype(BF16)
        weight = jnp.where(again_wide_ref[0, j : j + 1, :] > 0.0, start_ref[...], weight)
        offset = jnp.where(again_ref[0, j : j + 1, :] > 0.0, start_bias_ref[...], offset)
        low_weight = weight.astype(BF16)
        first = mm(low_weight, wide_key, NN) + offset
        center = first - mean0(first)
        inverse = lax.rsqrt(mean0(center * center) + EPSILON)
        normed = center * inverse
        residue = (normed * gain + shift - (value - key)) * gain
        inner = (residue - mean0(residue) - normed * mean0(residue * normed)) * inverse
        rated = (inner * rate).astype(BF16)
        combined = mm(low_weight, wide_query, NN) + offset - mm(rated, mix, NN)
        centered = combined - mean0(combined)
        inverse_out = lax.rsqrt(mean0(centered * centered) + EPSILON)
        rebuilt = centered * inverse_out
        results.append(query + rebuilt * gain + shift)
        weight = weight - mm(rated, wide_key, NT) * (1.0 / MINI)
        offset = offset - mm(rated, ones, NN)
        normed_ref[0, j] = normed
        grad_ref[0, j] = inner
        rebuilt_ref[0, j] = rebuilt
        spread_ref[0, j : j + 1, :] = inverse
        respread_ref[0, j : j + 1, :] = inverse_out
        mix_ref[0, j] = mix
        weight_ref[0, j] = low_weight
    out_ref[...] = unpacked(results, heads)
    state[...] = weight
    bias[...] = offset


def gathered_back(wide, lane_chain, head_dim, chains):
    total = wide[:head_dim]
    for c in range(1, chains):
        total = jnp.where(lane_chain == c, wide[c * head_dim : (c + 1) * head_dim], total)
    return total


def backward_kernel(
    heads, head_dim, parts,
    slot_ref, queries_ref, keys_ref, values_ref, delta_ref, rate_ref, again_ref, again_wide_ref,
    gain_ref, shift_ref,
    normed_ref, spread_ref, grad_ref, rebuilt_ref, respread_ref, mix_ref, weight_ref,
    dquery_ref, dkey_ref, dvalue_ref, drate_ref, dstart_ref, dstart_bias_ref, dgain_ref, dshift_ref,
    state, bias,
):
    chains = rate_ref.shape[-1] // MINI
    lanes = chains * MINI
    spread, together, scale = masks(chains, head_dim, BF16)
    ones = jnp.where(together, 1.0, 0.0).astype(BF16)
    lane_chain = lax.broadcasted_iota(jnp.int32, (head_dim, lanes), 1) // MINI
    gain, shift = gain_ref[...], shift_ref[...]

    @pl.when(pl.program_id(0) == 0)
    def _():
        state[...] = jnp.zeros_like(state)
        bias[...] = jnp.zeros_like(bias)
        dstart_ref[...] = jnp.zeros_like(dstart_ref)
        dstart_bias_ref[...] = jnp.zeros_like(dstart_bias_ref)
        dgain_ref[...] = jnp.zeros_like(dgain_ref)
        dshift_ref[...] = jnp.zeros_like(dshift_ref)

    all_queries = packed(queries_ref[...], heads, head_dim, parts)
    all_keys = packed(keys_ref[...], heads, head_dim, parts)
    all_values = packed(values_ref[...], heads, head_dim, parts)
    all_deltas = packed(delta_ref[...], heads, head_dim, parts)
    dweight = state[...]
    doffset = bias[...]
    dstart, dstart_bias = dstart_ref[...], dstart_bias_ref[...]
    dgain, dshift = dgain_ref[...], dshift_ref[...]
    dqueries, dkeys, dvalues = [None] * parts, [None] * parts, [None] * parts
    for j in reversed(range(parts)):
        query, key, value, delta = all_queries[j], all_keys[j], all_values[j], all_deltas[j]
        rate = rate_ref[0, j : j + 1, :]
        normed, inner, rebuilt = normed_ref[0, j], grad_ref[0, j], rebuilt_ref[0, j]
        inverse, inverse_out = spread_ref[0, j : j + 1, :], respread_ref[0, j : j + 1, :]
        mix, weight = mix_ref[0, j], weight_ref[0, j]
        low_key, low_query = key.astype(BF16), query.astype(BF16)
        wide_key = spread_out(low_key, spread, chains)
        wide_query = spread_out(low_query, spread, chains)
        rated = (inner * rate).astype(BF16)
        dnorm = delta * gain
        dcombined = (dnorm - mean0(dnorm) - rebuilt * mean0(dnorm * rebuilt)) * inverse_out
        low_dcombined = dcombined.astype(BF16)
        drated = -mm(low_dcombined, mix, NT)
        dscore = (-mm(rated, low_dcombined, TN) * scale).astype(BF16)
        low_dweight = dweight.astype(BF16)
        drated = drated - (mm(low_dweight, wide_key, NN) + doffset) * (1.0 / MINI)
        dinner = drated * rate
        drate_ref[0, j : j + 1, :] = jnp.sum(drated * inner, axis=0, keepdims=True)
        scaled = dinner * inverse
        offset_residue = normed * gain + shift - (value - key)
        residue = offset_residue * gain
        along = mean0(scaled * normed)
        dresidue = scaled - mean0(scaled) - normed * along
        gained = dresidue * gain
        dnormed = gained * gain - scaled * mean0(residue * normed) - residue * along
        dfirst = (
            dnormed - mean0(dnormed) - normed * (mean0(dnormed * normed) + mean0(dinner * inner))
        ) * inverse
        low_dfirst = dfirst.astype(BF16)
        dvalues[j] = -gained
        back_key = gathered_back(mm(weight, low_dfirst, TN), lane_chain, head_dim, chains)
        back_query = gathered_back(mm(weight, low_dcombined, TN), lane_chain, head_dim, chains)
        back_state = gathered_back(mm(low_dweight, rated, TN), lane_chain, head_dim, chains)
        dkeys[j] = gained + back_key - back_state * (1.0 / MINI) + mm(low_query, dscore, NT)
        dqueries[j] = delta + back_query + mm(low_key, dscore, NN)
        dgain = dgain + delta * rebuilt + dresidue * offset_residue + gained * normed
        dshift = dshift + delta + gained
        dweight = dweight + mm(low_dfirst, wide_key, NT) + mm(low_dcombined, wide_query, NT)
        both = (dfirst + dcombined).astype(BF16)
        doffset = doffset + mm(both, ones, NN)
        again_wide = again_wide_ref[0, j : j + 1, :] > 0.0
        again = again_ref[0, j : j + 1, :] > 0.0
        dstart = dstart + jnp.where(again_wide, dweight, 0.0)
        dstart_bias = dstart_bias + jnp.where(again, doffset, 0.0)
        dweight = jnp.where(again_wide, 0.0, dweight)
        doffset = jnp.where(again, 0.0, doffset)
    dquery_ref[...] = unpacked(dqueries, heads).astype(dquery_ref.dtype)
    dkey_ref[...] = unpacked(dkeys, heads).astype(dkey_ref.dtype)
    dvalue_ref[...] = unpacked(dvalues, heads).astype(dvalue_ref.dtype)
    state[...] = dweight
    bias[...] = doffset
    dstart_ref[...] = dstart
    dstart_bias_ref[...] = dstart_bias
    dgain_ref[...] = dgain
    dshift_ref[...] = dshift


def whole(shape):
    return pl.BlockSpec(shape, lambda *_: (0,) * len(shape))


def inner_forward(slot, queries, keys, values, rates, again, again_wide, start, start_bias, gain, shift, heads, head_dim, parts):
    steps, _, lanes = rates.shape
    tokens = queries.shape[0] // steps
    wide = start.shape[1]
    at_slot = pl.BlockSpec((tokens, heads * head_dim), lambda i, s: (jnp.bitwise_xor(i, s[0]), 0))

    def stepped(*shape):
        return pl.BlockSpec((1,) + shape, lambda i, s: (i,) + (0,) * len(shape))

    saved = [
        ((parts, head_dim, lanes), F32), ((parts, lanes), F32), ((parts, head_dim, lanes), F32),
        ((parts, head_dim, lanes), F32), ((parts, lanes), F32),
        ((parts, lanes, lanes), BF16), ((parts, head_dim, wide), BF16),
    ]
    return pl.pallas_call(
        functools.partial(forward_kernel, heads, head_dim, parts),
        out_shape=[jax.ShapeDtypeStruct(queries.shape, F32)]
        + [jax.ShapeDtypeStruct((steps,) + shape, kind) for shape, kind in saved],
        grid_spec=pltpu.PrefetchScalarGridSpec(
            num_scalar_prefetch=1,
            grid=(steps,),
            in_specs=[at_slot] * 3
            + [stepped(parts, lanes), stepped(parts, lanes), stepped(parts, wide)]
            + [whole(start.shape), whole(start_bias.shape), whole(gain.shape), whole(shift.shape)],
            out_specs=[at_slot] + [stepped(*shape) for shape, _ in saved],
            scratch_shapes=[pltpu.VMEM(start.shape, F32), pltpu.VMEM(start_bias.shape, F32)],
        ),
        compiler_params=pltpu.CompilerParams(
            dimension_semantics=("arbitrary",), vmem_limit_bytes=40 * 1024 * 1024
        ),
        name="inner_forward",
    )(slot, queries, keys, values, rates, again, again_wide, start, start_bias, gain, shift)


def inner_backward(slot, queries, keys, values, deltas, rates, again, again_wide, gain, shift, saved, heads, head_dim, parts):
    steps, _, lanes = rates.shape
    tokens = queries.shape[0] // steps
    wide = again_wide.shape[-1]
    at_slot = pl.BlockSpec(
        (tokens, heads * head_dim), lambda i, s: (jnp.bitwise_xor(steps - 1 - i, s[0]), 0)
    )

    def stepped(*shape):
        return pl.BlockSpec((1,) + shape, lambda i, s: (steps - 1 - i,) + (0,) * len(shape))

    return pl.pallas_call(
        functools.partial(backward_kernel, heads, head_dim, parts),
        out_shape=[jax.ShapeDtypeStruct(queries.shape, BF16)] * 3
        + [
            jax.ShapeDtypeStruct(rates.shape, F32),
            jax.ShapeDtypeStruct((head_dim, wide), F32),
            jax.ShapeDtypeStruct((head_dim, lanes), F32),
            jax.ShapeDtypeStruct((head_dim, lanes), F32),
            jax.ShapeDtypeStruct((head_dim, lanes), F32),
        ],
        grid_spec=pltpu.PrefetchScalarGridSpec(
            num_scalar_prefetch=1,
            grid=(steps,),
            in_specs=[at_slot] * 4
            + [stepped(parts, lanes), stepped(parts, lanes), stepped(parts, wide)]
            + [whole(gain.shape), whole(shift.shape)]
            + [stepped(*array.shape[1:]) for array in saved],
            out_specs=[at_slot] * 3
            + [stepped(parts, lanes), whole((head_dim, wide))]
            + [whole((head_dim, lanes))] * 3,
            scratch_shapes=[pltpu.VMEM((head_dim, wide), F32), pltpu.VMEM((head_dim, lanes), F32)],
        ),
        compiler_params=pltpu.CompilerParams(
            dimension_semantics=("arbitrary",), vmem_limit_bytes=40 * 1024 * 1024
        ),
        name="inner_backward",
    )(slot, queries, keys, values, deltas, rates, again, again_wide, gain, shift, *saved)


def bit_exchange(value, axis, bit):
    count = lax.axis_size(axis)
    return lax.ppermute(value, axis, [(i, i ^ bit) for i in range(count)])


def seq_bits():
    count = lax.axis_size("seq")
    bits = [1 << p for p in range(count.bit_length() - 1)]
    return bits


def gather_blocks(block):
    bits = seq_bits()
    near, far = bits[0], bits[1:]
    ways = max(1, len(far))
    width = block.shape[-1]
    pieces = []
    for way in range(ways):
        low, high = way * width // ways, (way + 1) * width // ways
        held = {0: block[:, low:high]}
        for step in range(len(far)):
            bit = far[(way + step) % len(far)]
            keys = sorted(held)
            moved = bit_exchange(jnp.stack([held[k] for k in keys]), "seq", bit)
            for n, k in enumerate(keys):
                held[k | bit] = moved[n]
        pieces.append(jnp.stack([held[k] for k in sorted(held)]))
    half = jnp.concatenate(pieces, axis=-1)
    other = bit_exchange(half, "seq", near)
    return jnp.stack([half, other], axis=1).reshape((-1,) + block.shape)


def reduce_blocks(blocks):
    bits = seq_bits()
    near, far = bits[0], bits[1:]
    ways = max(1, len(far))
    width = blocks.shape[-1]
    blocks = blocks.reshape((-1, 2) + blocks.shape[1:])
    half = blocks[:, 0] + bit_exchange(blocks[:, 1].astype(BF16), "seq", near).astype(F32)
    pieces = []
    for way in range(ways):
        low, high = way * width // ways, (way + 1) * width // ways
        held = {2 * k: half[k, :, low:high] for k in range(half.shape[0])}
        for step in range(len(far)):
            bit = far[(way + step) % len(far)]
            away = sorted(k for k in held if k & bit)
            moved = bit_exchange(jnp.stack([held[k].astype(BF16) for k in away]), "seq", bit)
            for n, k in enumerate(away):
                held[k ^ bit] = held[k ^ bit] + moved[n].astype(F32)
                del held[k]
        pieces.append(held[0])
    return jnp.concatenate(pieces, axis=-1)


def gelu_tanh(values):
    return jax.nn.gelu(values, approximate=True)


def shards(
    hidden_in,
    attn_gain,
    query_weight,
    key_weight,
    value_weight,
    rate_weight,
    gate_weight,
    init_weight,
    init_bias,
    inner_gain,
    inner_shift,
    post_gain,
    post_shift,
    out_weight,
    ffn_gain,
    ffn_gate_weight,
    ffn_up_weight,
    ffn_down_weight,
    doc_starts,
    out_grad,
):
    rows_here, stretch, model = hidden_in.shape
    head_count = rate_weight.shape[1]
    head_dim = init_weight.shape[1]
    parts = stretch // MINI
    seq_count = lax.axis_size("seq")
    rows_count = lax.axis_size("rows")
    share = model // (seq_count * rows_count)
    hidden_share = ffn_down_weight.shape[0]
    heads = head_count // seq_count
    width = heads * head_dim
    aligned = share % head_dim == 0
    groups, span = (rows_count, share) if aligned else (1, width)
    me = lax.axis_index("seq")
    slots = jnp.bitwise_xor(jnp.arange(seq_count, dtype=jnp.int32), me)
    everywhere = ("rows", "seq")

    def by_owner(values, group, size):
        split = values.reshape(values.shape[0], group, seq_count, size)
        return split.transpose(2, 0, 1, 3).reshape(seq_count, values.shape[0], group * size)

    def columns_in(values):
        mine = lax.all_to_all(values, "seq", 0, 0, tiled=True)
        return lax.all_gather(mine.reshape(-1, values.shape[-1]), "rows", axis=0, tiled=True)

    def columns_out(values):
        summed = lax.psum_scatter(values.astype(BF16), "rows", scatter_dimension=0, tiled=True)
        return lax.all_to_all(summed.reshape(seq_count, share, -1), "seq", 0, 0, tiled=True)

    def from_owner(values, group, size):
        split = values.reshape(seq_count, share, group, size)
        return split.transpose(1, 2, 0, 3).reshape(share, -1).astype(F32)

    def own_part(values):
        split = values.reshape(groups, seq_count, span, -1)
        return lax.dynamic_index_in_dim(split, me, 1, keepdims=False).reshape(width, -1)

    def placed(values):
        split = values.reshape(groups, 1, span, -1)
        here = (jnp.arange(seq_count) == me).reshape(1, -1, 1, 1)
        return jnp.where(here, split, 0.0).reshape(model, -1)

    def reordered(values):
        return values.reshape(rows_here, parts, MINI, -1).transpose(1, 0, 2, 3).reshape(-1, model)

    def restored(values):
        return values.reshape(parts, rows_here, MINI, -1).transpose(1, 0, 2, 3).reshape(rows_here, stretch, -1)

    vectors = jnp.stack(
        [attn_gain, ffn_gain, init_bias, inner_gain, inner_shift, post_gain, post_shift], axis=1
    )
    count = vectors.shape[1]
    small = lax.all_gather(
        jnp.concatenate([init_weight, rate_weight, vectors], axis=1), everywhere, axis=0, tiled=True
    )
    qkv_weight = columns_in(
        jnp.concatenate([by_owner(w, groups, span) for w in (query_weight, key_weight, value_weight)], axis=2)
    )
    gate_own = columns_in(by_owner(gate_weight, groups, span))
    if aligned:
        out_own = lax.all_gather(out_weight, "rows", axis=0, tiled=True)
    else:
        out_own = own_part(lax.all_gather(out_weight, everywhere, axis=0, tiled=True))
    ffn_wide = columns_in(
        jnp.concatenate(
            [by_owner(w, rows_count, hidden_share) for w in (ffn_gate_weight, ffn_up_weight)], axis=2
        )
    )
    hidden_units = rows_count * hidden_share
    gate_wide, up_wide = ffn_wide[:, :hidden_units], ffn_wide[:, hidden_units:]
    down_wide = lax.all_gather(ffn_down_weight, "rows", axis=0, tiled=True)

    gain_attn = small[:, head_dim + head_count].astype(F32)
    gain_ffn = small[:, head_dim + head_count + 1].astype(F32)
    own_small = own_part(small)
    own_vectors = own_small[:, head_dim + head_count :].astype(F32)
    rate_all = small[:, head_dim : head_dim + head_count].reshape(model, groups, seq_count, -1)
    rate_own = lax.dynamic_index_in_dim(rate_all, me, 2, keepdims=False).reshape(model, heads)
    lanes = heads * rows_here * MINI

    def by_lane(values, repeat):
        turned = values.reshape(heads, head_dim).T
        return jnp.broadcast_to(turned[:, :, None], (head_dim, heads, repeat)).reshape(head_dim, -1)

    bias_lanes = by_lane(own_vectors[:, 2], rows_here * MINI)
    gain_lanes = by_lane(own_vectors[:, 3], rows_here * MINI)
    shift_lanes = by_lane(own_vectors[:, 4], rows_here * MINI)
    post_scale, post_offset = own_vectors[:, 5], own_vectors[:, 6]
    start = own_small[:, :head_dim].astype(F32).reshape(heads, head_dim, head_dim).transpose(2, 0, 1)
    start = jnp.broadcast_to(start[:, :, None], (head_dim, heads, rows_here, head_dim)).reshape(head_dim, -1)

    steps = seq_count
    position = jnp.arange(steps * parts, dtype=jnp.int32) * MINI
    restarts = jnp.logical_or(
        position[:, None] == 0, jnp.any(doc_starts[None] == position[:, None, None], axis=2)
    ).astype(F32)

    def by_chain(repeat):
        wide = jnp.broadcast_to(
            restarts[:, None, :, None], (steps * parts, heads, rows_here, repeat)
        )
        return wide.reshape(steps, parts, -1)

    again, again_wide = by_chain(MINI), by_chain(head_dim)

    hidden = reordered(hidden_in)
    cotangent = reordered(out_grad)
    tokens = hidden.astype(F32)
    tokens_all = gather_blocks(hidden).reshape(-1, model).astype(F32)
    inverse_all = lax.rsqrt(jnp.mean(tokens_all * tokens_all, axis=-1, keepdims=True) + EPSILON)
    plain_all = tokens_all * inverse_all
    normed = (plain_all * gain_attn).astype(BF16)

    def project(matrix):
        return jnp.dot(normed, matrix, preferred_element_type=F32)

    qkv = project(qkv_weight)
    queries, keys, values = (qkv[:, n * width : (n + 1) * width] for n in range(3))
    gate_pre = project(gate_own)
    logits = project(rate_own)
    slope = jax.nn.sigmoid(logits)

    def to_lanes(per_token):
        ordered = jnp.take(per_token.reshape(steps, -1, heads), slots, axis=0)
        ordered = ordered.reshape(steps, parts, rows_here * MINI, heads)
        return ordered.transpose(0, 1, 3, 2).reshape(steps, parts, lanes)

    def from_lanes(per_lane):
        ordered = per_lane.reshape(steps, parts, heads, rows_here * MINI).transpose(0, 1, 3, 2)
        return jnp.take(ordered.reshape(steps, -1, heads), slots, axis=0).reshape(-1, heads)

    rates = to_lanes(slope * (BASE_RATE / head_dim))
    slot = me.astype(jnp.int32).reshape(1)
    inner_out, *saved = inner_forward(
        slot, queries, keys, values, rates, again, again_wide, start, bias_lanes, gain_lanes,
        shift_lanes, heads, head_dim, parts,
    )
    def feature_mean(*values):
        sums = jnp.stack([jnp.sum(v, axis=1) for v in values]).reshape(len(values), steps, -1)
        total = lax.psum(jnp.take(sums, slots, axis=1), "seq") / model
        return jnp.take(total, slots, axis=1).reshape(len(values), -1, 1)

    moments = feature_mean(inner_out, inner_out * inner_out)
    post_mean = moments[0]
    post_inverse = lax.rsqrt(moments[1] - post_mean * post_mean + EPSILON)
    post_norm = (inner_out - post_mean) * post_inverse
    post_out = post_norm * post_scale + post_offset
    gelu_value, gelu_pull = jax.vjp(gelu_tanh, gate_pre)
    gated = (gelu_value * post_out).astype(BF16)
    branch = jnp.dot(gated, out_own, preferred_element_type=F32)
    residual = tokens + reduce_blocks(branch.reshape(steps, -1, model))

    inverse_two = lax.rsqrt(jnp.mean(residual * residual, axis=-1, keepdims=True) + EPSILON)
    ffn_in = gather_blocks((residual * inverse_two * gain_ffn).astype(BF16)).reshape(-1, model)
    cot_all = gather_blocks(cotangent).reshape(-1, model)
    gate_value = jnp.dot(ffn_in, gate_wide, preferred_element_type=F32)
    up_value = jnp.dot(ffn_in, up_wide, preferred_element_type=F32)
    sigmoid_gate = jax.nn.sigmoid(gate_value)
    active = (gate_value * sigmoid_gate * up_value).astype(BF16)
    down = jnp.dot(active, down_wide, preferred_element_type=F32)
    delta_active = jnp.einsum("td,fd->tf", cot_all, down_wide, preferred_element_type=F32)
    delta_up = (delta_active * gate_value * sigmoid_gate).astype(BF16)
    delta_gate = (
        delta_active * up_value * sigmoid_gate * (1.0 + gate_value * (1.0 - sigmoid_gate))
    ).astype(BF16)
    delta_ffn = jnp.einsum("tf,df->td", delta_up, up_wide, preferred_element_type=F32) + jnp.einsum(
        "tf,df->td", delta_gate, gate_wide, preferred_element_type=F32
    )
    delta_ffn = reduce_blocks(delta_ffn.reshape(steps, -1, model))
    block_out = residual + reduce_blocks(down.reshape(steps, -1, model))

    def token_grad(left, right):
        return jnp.einsum("td,te->de", left, right, preferred_element_type=F32)

    grad_down = lax.psum_scatter(
        token_grad(active, cot_all).astype(BF16), "rows", scatter_dimension=0, tiled=True
    ).astype(F32)
    grad_gate = from_owner(columns_out(token_grad(ffn_in, delta_gate)), rows_count, hidden_share)
    grad_up = from_owner(columns_out(token_grad(ffn_in, delta_up)), rows_count, hidden_share)

    grad_gain_ffn = jnp.sum(delta_ffn * residual * inverse_two, axis=0)
    scaled_two = delta_ffn * gain_ffn
    delta_after = (
        cotangent.astype(F32)
        + inverse_two * scaled_two
        - residual * inverse_two**3 * jnp.mean(scaled_two * residual, axis=-1, keepdims=True)
    )
    delta_branch = gather_blocks(delta_after.astype(BF16)).reshape(-1, model)

    grad_out = token_grad(gated, delta_branch)
    if aligned:
        grad_out = lax.psum_scatter(grad_out.astype(BF16), "rows", scatter_dimension=0, tiled=True)
    else:
        grad_out = lax.psum_scatter(
            placed(grad_out).astype(BF16), everywhere, scatter_dimension=0, tiled=True
        )
    delta_gated = jnp.einsum("te,de->td", delta_branch, out_own, preferred_element_type=F32)
    delta_pre = gelu_pull(delta_gated * post_out)[0].astype(BF16)
    delta_post = delta_gated * gelu_value
    grad_post_scale = jnp.sum(delta_post * post_norm, axis=0)
    grad_post_shift = jnp.sum(delta_post, axis=0)
    delta_norm = delta_post * post_scale
    means = feature_mean(delta_norm, delta_norm * post_norm)
    delta_inner = (delta_norm - means[0] - post_norm * means[1]) * post_inverse
    (
        delta_queries, delta_keys, delta_values, delta_rates,
        grad_start, grad_bias, grad_inner_gain, grad_inner_shift,
    ) = inner_backward(
        slot, queries, keys, values, delta_inner, rates, again, again_wide, gain_lanes, shift_lanes,
        saved, heads, head_dim, parts,
    )
    delta_logits = (
        from_lanes(delta_rates) * slope * (1.0 - slope) * (BASE_RATE / head_dim)
    ).astype(BF16)
    delta_qkv = jnp.concatenate([delta_queries, delta_keys, delta_values], axis=1)

    def back_project(delta, matrix):
        return jnp.einsum("te,de->td", delta, matrix, preferred_element_type=F32)

    delta_normed = (
        back_project(delta_qkv, qkv_weight)
        + back_project(delta_pre, gate_own)
        + back_project(delta_logits, rate_own)
    )
    grad_gain_attn = jnp.sum(delta_normed * plain_all, axis=0)
    delta_normed = reduce_blocks(delta_normed.reshape(steps, -1, model))
    inverse_one = lax.rsqrt(jnp.mean(tokens * tokens, axis=-1, keepdims=True) + EPSILON)
    scaled_one = delta_normed * gain_attn
    hidden_grad = (
        delta_after
        + inverse_one * scaled_one
        - tokens * inverse_one**3 * jnp.mean(scaled_one * tokens, axis=-1, keepdims=True)
    )
    qkv_grads = columns_out(token_grad(normed, delta_qkv))
    grad_query, grad_key, grad_value = (
        from_owner(qkv_grads[:, :, n * width : (n + 1) * width], groups, span) for n in range(3)
    )
    grad_gate_weight = from_owner(columns_out(token_grad(normed, delta_pre)), groups, span)

    def lane_sum(per_lane, repeat):
        return per_lane.reshape(head_dim, heads, repeat).sum(axis=2).T.reshape(width, 1)

    grad_start = grad_start.reshape(head_dim, heads, rows_here, head_dim).sum(axis=2)
    grad_start = grad_start.transpose(1, 2, 0).reshape(width, head_dim)
    grad_bias = grad_bias.reshape(head_dim, heads, rows_here, MINI)[..., 0]
    grad_rate = token_grad(normed, delta_logits).reshape(model, groups, 1, -1)
    here = (jnp.arange(seq_count) == me).reshape(1, 1, -1, 1)
    grad_rate = jnp.where(here, grad_rate, 0.0).reshape(model, head_count)
    own_grads = jnp.concatenate(
        [
            grad_start,
            lane_sum(grad_bias, rows_here),
            lane_sum(grad_inner_gain, rows_here * MINI),
            lane_sum(grad_inner_shift, rows_here * MINI),
            grad_post_scale[:, None],
            grad_post_shift[:, None],
        ],
        axis=1,
    )
    small_grads = lax.psum_scatter(
        jnp.concatenate(
            [placed(own_grads), grad_rate, grad_gain_attn[:, None], grad_gain_ffn[:, None]], axis=1
        ),
        everywhere, scatter_dimension=0, tiled=True,
    )
    after = head_dim + 5
    return (
        restored(block_out).astype(BF16),
        restored(hidden_grad),
        small_grads[:, after + head_count],
        grad_query,
        grad_key,
        grad_value,
        small_grads[:, after : after + head_count],
        grad_gate_weight,
        small_grads[:, :head_dim],
        small_grads[:, head_dim],
        small_grads[:, head_dim + 1],
        small_grads[:, head_dim + 2],
        small_grads[:, head_dim + 3],
        small_grads[:, head_dim + 4],
        grad_out.astype(F32),
        small_grads[:, after + head_count + 1],
        grad_gate,
        grad_up,
        grad_down,
    )


def solution(mesh):
    split = P(("rows", "seq"))
    matrix = P(("rows", "seq"), None)
    tokens = P("rows", "seq", None)
    return jax.shard_map(
        shards,
        mesh=mesh,
        in_specs=(
            tokens, split, matrix, matrix, matrix, matrix, matrix, matrix, split, split, split, split,
            split, matrix, split, matrix, matrix, matrix, P("rows", None), tokens,
        ),
        out_specs=(
            tokens, tokens, split, matrix, matrix, matrix, matrix, matrix, matrix, split, split, split,
            split, split, matrix, split, matrix, matrix, matrix,
        ),
        check_vma=False,
    )
```

time: 5150 us -> 812 us (0.16)
  waiting for transfers between devices: 1700 us -> 191 us
  matrix products: 1150 us -> 111 us
  blocking collectives: 987 us -> 180 us
  other arithmetic: 545 us -> 88.9 us
  local copies, waits for them, and re-layouts: 425 us -> 131 us
  starting transfers between devices: 254 us -> 50.7 us
    reduce_scatter x8 -> x6, waiting for transfers between devices: 1480 us -> 76.9 us  [the longest x4 51.9 us: columns_out(): lax.psum_scatter(values.astype(BF16), 'rows', scatter_dimension=0, tiled=...]
    dot_general x382 -> x21, matrix products: 1150 us -> 111 us  [the longest x7 32.2 us: token_grad(): return jnp.einsum('td,te->de', left, right, preferred_element_type=F32)]
    unnamed x3 -> x1, blocking collectives: 905 us -> 57.6 us
    reduce_sum x395 -> x9, other arithmetic: 285 us -> 5.98 us  [the longest x1 2.95 us: shards(): jnp.mean(tokens_all * tokens_all, axis=-1, keepdims=True) + EPSILON]
    ppermute x14 -> x40, starting transfers between devices: 234 us -> 32.1 us  [bit_exchange(): return lax.ppermute(value, axis, [(i, i ^ bit) for i in range(count)])]
    squeeze x160 -> x0, local copies, waits for them, and re-layouts: 164 us -> none  [run_blocks(): lax.scan(advance, state, (queries, keys_in, values_in, logits, restarts))]
    ppermute x14 -> x40, waiting for transfers between devices: 211 us -> 102 us  [bit_exchange(): return lax.ppermute(value, axis, [(i, i ^ bit) for i in range(count)])]
    while x678 -> x0, local copies, waits for them, and re-layouts: 89.1 us -> none  [the longest x28 65.4 us: run_blocks(): lax.scan(advance, state, (queries, keys_in, values_in, logits, restarts))]
  transfers between devices with their start and end apart: 32 -> 56, of which waited for: 20 -> 23; matrix products, arithmetic and copies ran while one was open for 34% -> 40% of each run, Pallas kernels for 0% -> 4%
where the time goes in v1:
time: 812 us; the launch traced here: 805 us
  waiting for transfers between devices  191 us (24%)
  blocking collectives  180 us (22%)
  local copies, waits for them, and re-layouts  131 us (16%)
  matrix products  111 us (14%)
  other arithmetic  88.9 us (11%)
  starting transfers between devices  50.7 us (6%)
  Pallas kernels  36.1 us (4%)
  between operations  17.1 us (2%)
    ppermute x40, waiting for transfers between devices, bit_exchange(): return lax.ppermute(value, axis, [(i, i ^ bit) for i in range(count)])  102 us
    unnamed x1, blocking collectives  57.6 us
    reduce_scatter x4, waiting for transfers between devices, columns_out(): lax.psum_scatter(values.astype(BF16), 'rows', scatter_dimension=0, tiled=...  51.9 us
    all_to_all x3, blocking collectives, columns_in(): mine = lax.all_to_all(values, 'seq', 0, 0, tiled=True)  50.4 us
    all_gather x1, blocking collectives, shards(): lax.all_gather(jnp.concatenate([init_weight, rate_weight, vectors], axis=...  45.7 us
    unnamed x274, local copies, waits for them, and re-layouts  37.2 us
    dot_general x7, matrix products, token_grad(): return jnp.einsum('td,te->de', left, right, preferred_element_type=F32)  32.2 us
    ppermute x40, starting transfers between devices, bit_exchange(): return lax.ppermute(value, axis, [(i, i ^ bit) for i in range(count)])  32.1 us
  transfers between devices with their start and end apart: 56, of which 23 were waited for; matrix products, arithmetic and copies ran while one was open for 40% of the time, Pallas kernels for 4%

profile of v1, /device:TPU:0, one launch (start us, length us, event | category | flops | bytes accessed | tf_op | source)
XLA Modules:
  0.0 805.0 jit_solution(15771266072255233194)
XLA Ops:
  12.5 17.6 %all_to_all.35 = bf16[8,64,768]{2,1,0:T(8,128)(2,1)} all-to-all(bf16[8,64,768]{2,1,0:T(8,128)(2,1)S(1)} %pad_maximum_fusion.7), channel_id=1, replica_groups=mesh['rows'=4,'seq'=8] {'seq'}, dimensions={0} | all-to-all | bytes 1572864 | tf_op jit(solution)/shard_map/all_to_all | solution.py:407
  31.3 10.0 %all_to_all.36 = bf16[8,64,256]{2,1,0:T(8,128)(2,1)} all-to-all(bf16[8,64,256]{2,1,0:T(8,128)(2,1)S(1)} %reshape.641), channel_id=1, replica_groups=mesh['rows'=4,'seq'=8] {'seq'}, dimensions={0} | all-to-all | bytes 524288 | tf_op jit(solution)/shard_map/all_to_all | solution.py:407
  44.2 6.3 collective-permute-done.2
  55.1 45.7 %all_gather.18 = bf16[2048,103]{1,0:T(8,128)(2,1)S(1)} all-gather(bf16[64,103]{1,0:T(8,128)(2,1)S(1)} %concatenate.73), channel_id=1, replica_groups=mesh['rows'=4,'seq'=8] {'rows','seq'}, dimensions={0}, use_global_device_ids=true | all-gather | bytes 435072 | tf_op jit(solution)/shard_map/all_gather | solution.py:437
  110.4 3.0 multiply_reduce_fusion.1
  119.3 3.9 multiply_convert_fusion.1
  123.2 6.1 fusion.85
  129.6 15.3 %inner_forward.1 = (f32[1024,256]{1,0:T(8,128)S(1)}, f32[8,4,64,128]{3,2,1,0:T(8,128)S(1)}, f32[8,4,128]{2,1,0:T(4,128)S(1)}, f32[8,4,64,128]{3,2,1,0:T(8,128)S(...) custom-call(s32[1]{0:T(128)} %bitcast.20.slot_ref, ...), custom_call_target="tpu_custom_call" | custom-call | tf_op jit(solution)/shard_map/inner_forward/pallas_call | solution.py:246
  152.0 12.4 %psum.14 = f32[2,8,128]{2,0,1:T(2,128)S(1)} all-reduce(f32[2,8,128]{2,0,1:T(2,128)S(1)} %select_bitcast_fusion.3), channel_id=1, replica_groups=mesh['rows'=4,'seq'=8] {'seq'}, use_global_device_ids=true, to_apply=%region_4.7 | all-reduce | flops 2048 | bytes 16384 | tf_op jit(solution)/shard_map/psum | solution.py:524
  165.9 5.5 multiply_convert_fusion.6
  174.0 3.3 copy-done.22
  179.0 4.9 reshape.665
  186.6 3.0 reshape.666
  189.6 4.9 reshape.667
  197.1 3.0 reshape.668
  202.0 22.7 %all_to_all.37 = bf16[8,64,1376]{2,1,0:T(8,128)(2,1)} all-to-all(bf16[8,64,1376]{2,1,0:T(8,128)(2,1)S(1)} %pad_maximum_fusion.4), channel_id=1, replica_groups=mesh['rows'=4,'seq'=8] {'seq'}, dimensions={0} | all-to-all | bytes 2818048 | tf_op jit(solution)/shard_map/all_to_all | solution.py:407
  226.3 4.5 fusion.69
  233.3 16.6 %collective-permute-done.22 = bf16[1,128,1024]{2,1,0:T(8,128)(2,1)S(1)} collective-permute-done((bf16[1,128,1024]{2,1,0:T(8,128)(2,1)S(1)}, bf16[1,128,1024]{2,1,0:T(8,128)(2,1)S(1)}, u32[]{:S(2)}, u32[]{:S(2)}) %collective-permute-start.22) | collective-permute-done | bytes 262176 | tf_op jit(solution)/shard_map/ppermute | solution.py:308
  254.3 16.3 %collective-permute-done.20 = bf16[1,128,1024]{2,1,0:T(8,128)(2,1)S(1)} collective-permute-done((bf16[1,128,1024]{2,1,0:T(8,128)(2,1)S(1)}, bf16[1,128,1024]{2,1,0:T(8,128)(2,1)S(1)}, u32[]{:S(2)}, u32[]{:S(2)}) %collective-permute-start.20) | collective-permute-done | bytes 262176 | tf_op jit(solution)/shard_map/ppermute | solution.py:308
  278.0 5.7 collective-permute-done.21
  288.2 6.6 collective-permute-done.10
  295.7 9.9 %collective-permute-done.13 = bf16[2,128,1024]{2,1,0:T(8,128)(2,1)S(1)} collective-permute-done((bf16[2,128,1024]{2,1,0:T(8,128)(2,1)S(1)}, bf16[2,128,1024]{2,1,0:T(8,128)(2,1)S(1)}, u32[]{:S(2)}, u32[]{:S(2)}) %collective-permute-start.13) | collective-permute-done | bytes 524320 | tf_op jit(solution)/shard_map/ppermute | solution.py:308
  313.6 3.2 reshape.755
  316.9 7.9 fusion.88
  329.3 8.6 %fusion.7 = f32[1024,688]{0,1:T(8,128)} fusion(bf16[1024,2048]{1,0:T(8,128)(2,1)} %bitcast.351, bf16[2048,1376]{1,0:T(8,128)(2,1)} %all-gather.13.cloned.1.call-done), kind=kOutput, calls=%fused_computation.39 | convolution fusion | flops 2885681152 | bytes 10158080 | tf_op jit(solution)/shard_map/dot_general | solution.py:541
  338.0 7.4 multiply_convert_fusion.2
  345.4 3.5 fusion.87
  350.3 7.2 fusion.5
  357.4 7.0 convolution_add_fusion
  365.3 4.5 fusion.67
  370.6 4.5 fusion.65
  381.7 4.4 convolution_convert_fusion.2
  386.4 5.5 collective-permute-done.16
  396.3 6.9 collective-permute-done.26
  407.7 2.7 collective-permute-done.17
  412.0 2.8 collective-permute-done.27
  421.9 6.0 collective-permute-done.32
  430.1 9.9 %collective-permute-done.33 = bf16[2,128,1024]{2,1,0:T(8,128)(2,1)S(1)} collective-permute-done((bf16[2,128,1024]{2,1,0:T(8,128)(2,1)S(1)}, bf16[2,128,1024]{2,1,0:T(8,128)(2,1)S(1)}, u32[]{:S(2)}, u32[]{:S(2)}) %collective-permute-start.33) | collective-permute-done | bytes 524320 | tf_op jit(solution)/shard_map/ppermute | solution.py:308
  442.0 4.5 convolution_convert_fusion.1
  456.0 4.3 multiply_reduce_fusion.3
  461.7 13.8 %psum.15 = f32[2,8,128]{2,0,1:T(2,128)S(1)} all-reduce(f32[2,8,128]{2,0,1:T(2,128)S(1)} %select_bitcast_fusion.1), channel_id=1, replica_groups=mesh['rows'=4,'seq'=8] {'seq'}, use_global_device_ids=true, to_apply=%region_10.13 | all-reduce | flops 2048 | bytes 16384 | tf_op jit(solution)/shard_map/psum | solution.py:524
  484.9 20.8 %inner_backward.1 = (bf16[1024,256]{1,0:T(8,128)(2,1)S(1)}, bf16[1024,256]{1,0:T(8,128)(2,1)S(1)}, bf16[1024,256]{1,0:T(8,128)(2,1)S(1)}, f32[8,4,128]{2,1,0:T(4...) custom-call(s32[1]{0:T(128)} %bitcast.20.slot_ref, ...), custom_call_target="tpu_custom_call" | custom-call | tf_op jit(solution)/shard_map/inner_backward/pallas_call | solution.py:277
  515.7 2.9 fusion.82
  521.6 4.6 fusion.90
  527.6 6.4 fusion.89
  534.1 6.1 multiply_reduce_fusion
  541.9 3.1 pad_maximum_fusion.6
  545.1 4.5 convolution_convert_fusion.4
  549.8 2.7 fusion.13
  553.2 6.3 convolution_convert_fusion
  559.5 7.4 convolution_convert_fusion.3
  569.2 3.5 all-to-all-start.5
  575.0 6.0 fusion.62
  586.3 3.7 all-to-all-start.6
  589.9 57.6 %fusion = bf16[176,2048]{1,0:T(8,128)(2,1)S(1)} fusion(bf16[688,2048]{1,0:T(8,128)(2,1)} %convolution_convert_fusion.3), kind=kCustom, calls=%all-reduce-scatter | all-reduce-scatter fusion | flops 1441793 | bytes 3539456
  651.1 5.0 concatenate.94
  661.7 3.3 collective-permute-start.39
  665.0 3.6 all-to-all-start.4
  672.8 3.2 reshape.691
  680.2 3.2 reshape.692
  689.3 22.5 %reduce-scatter.15.cloned.1.call-done = bf16[64,2048]{1,0:T(8,128)(2,1)} async-done(((bf16[256,2048]{1,0:T(8,128)(2,1)}), bf16[64,2048]{1,0:T(8,128)(2,1)}) %reduce-scatter.15.cloned.1.call-update) | async-done | bytes 262160 | tf_op jit(solution)/shard_map/reduce_scatter | solution.py:576
  721.3 51.9 %reduce-scatter.11.cloned.1.call-done = bf16[512,768]{1,0:T(8,128)(2,1)} async-done(((bf16[2048,768]{1,0:T(8,128)(2,1)}), bf16[512,768]{1,0:T(8,128)(2,1)}) %reduce-scatter.11.cloned.1.call-update) | async-done | bytes 786448 | tf_op jit(solution)/shard_map/reduce_scatter | solution.py:411
  773.2 4.5 all-to-all-start.3
  780.7 9.5 %all-to-all-done.3 = bf16[8,64,768]{2,1,0:T(8,128)(2,1)} async-done(((bf16[8,64,768]{2,1,0:T(8,128)(2,1)}), bf16[8,64,768]{2,1,0:T(8,128)(2,1)}, u32[]{:S(2)}, u32[]{:S(2)}) %all-to-all-start.3) | async-done | bytes 786464 | tf_op jit(solution)/shard_map/all_to_all | solution.py:412
  (581 shorter events, 204.1 us)
Async XLA Ops:
  7.2 116.0 %all-gather.9.cloned.1.call-start = ((), (), s32[]{:S(2)}) async-start(), calls=%async_computation.14 | async-start | bytes 3932160 | tf_op jit(solution)/shard_map/all_gather | solution.py:408
  30.2 135.7 %all-gather.7.cloned.1.call-start = ((), (), s32[]{:S(2)}) async-start(), calls=%async_computation.13 | async-start | bytes 1310720 | tf_op jit(solution)/shard_map/all_gather | solution.py:408
  41.4 130.0 %all-gather.11.cloned.1.call-start = ((), (), s32[]{:S(2)}) async-start(), calls=%async_computation.15 | async-start | bytes 1310720 | tf_op jit(solution)/shard_map/all_gather | solution.py:445
  42.1 271.5 %all-gather.15.cloned.1.call-start = ((), (), s32[]{:S(2)}) async-start(), calls=%async_computation.23 | async-start | bytes 3604480 | tf_op jit(solution)/shard_map/all_gather | solution.py:455
  43.1 7.5 collective-permute-start.2
  43.7 10.1 %collective-permute-start = (bf16[1,128,1024]{2,1,0:T(8,128)(2,1)S(1)}, bf16[1,128,1024]{2,1,0:T(8,128)(2,1)S(1)}, u32[]{:S(2)}, u32[]{:S(2)}) collective-permute-start(bf16[1,128,1024]{2,1,0:T(8,128)(2,1)S(1)} %get-tuple-element.227), channel_id=1, source_target_pairs={{0,2},{1,3},{2,0},{3,1},{4,6},{5,7},{6,4},{7,5},{8,10},{9,11},{10,... | collective-permute-start | bytes 786440 | tf_op jit(solution)/shard_map/ppermute | solution.py:308
  51.4 50.4 %collective-permute-start.3 = (bf16[2,128,1024]{2,1,0:T(8,128)(2,1)}, bf16[2,128,1024]{2,1,0:T(8,128)(2,1)S(1)}, u32[]{:S(2)}, u32[]{:S(2)}) collective-permute-start(bf16[2,128,1024]{2,1,0:T(8,128)(2,1)} %pad_maximum_fusion.9), channel_id=1, source_target_pairs={{0,2},{1,3},{2,0},{3,1},{4,6},{5,7},{6,4},{7,5},{8,10},{9,11},{10,... | collective-permute-start | bytes 1572872 | tf_op jit(solution)/shard_map/ppermute | solution.py:308
  52.7 276.6 %all-gather.13.cloned.1.call-start = ((), (), s32[]{:S(2)}) async-start(), calls=%async_computation.16 | async-start | bytes 7208960 | tf_op jit(solution)/shard_map/all_gather | solution.py:408
  54.7 47.2 %collective-permute-start.1 = (bf16[2,128,1024]{2,1,0:T(8,128)(2,1)}, bf16[2,128,1024]{2,1,0:T(8,128)(2,1)S(1)}, u32[]{:S(2)}, u32[]{:S(2)}) collective-permute-start(bf16[2,128,1024]{2,1,0:T(8,128)(2,1)} %pad_maximum_fusion.8), channel_id=1, source_target_pairs={{0,4},{1,5},{2,6},{3,7},{4,0},{5,1},{6,2},{7,3},{8,12},{9,13},{10,... | collective-permute-start | bytes 1572872 | tf_op jit(solution)/shard_map/ppermute | solution.py:308
  103.4 6.9 collective-permute-start.4
  108.0 310.3 %copy-start.92 = (f32[2048]{0:T(1024)}, f32[2048]{0:T(1024)S(1)}, u32[]{:S(2)}) copy-start(f32[2048]{0:T(1024)S(1)} %get-tuple-element.157) | copy-start | bytes 24580
  179.0 47.3 %collective-permute-start.5 = (bf16[4,128,2048]{2,1,0:T(8,128)(2,1)}, bf16[4,128,2048]{2,1,0:T(8,128)(2,1)}, u32[]{:S(2)}, u32[]{:S(2)}) collective-permute-start(bf16[4,128,2048]{2,1,0:T(8,128)(2,1)} %fusion.14), channel_id=1, source_target_pairs={{0,1},{1,0},{2,3},{3,2},{4,5},{5,4},{6,7},{7,6},{8,9},{9,8},{10,11... | collective-permute-start | bytes 6291464 | tf_op jit(solution)/shard_map/ppermute | solution.py:308
  224.7 342.2 %reduce-scatter.17.cloned.1.call-start = ((), (), s32[]{:S(2)}) async-start(), calls=%async_computation.21 | async-start | bytes 3522560 | tf_op jit(solution)/shard_map/reduce_scatter | solution.py:411
  231.0 21.3 %collective-permute-start.6 = (bf16[2,128,1024]{2,1,0:T(8,128)(2,1)S(1)}, bf16[2,128,1024]{2,1,0:T(8,128)(2,1)S(1)}, u32[]{:S(2)}, u32[]{:S(2)}) collective-permute-start(bf16[2,128,1024]{2,1,0:T(8,128)(2,1)S(1)} %pad_maximum_fusion.10), channel_id=1, source_target_pairs={{0,2},{1,3},{2,0},{3,1},{4,6},{5,7},{6,4},{7,5},{8,10},{9,11},{10,... | collective-permute-start | bytes 1572872 | tf_op jit(solution)/shard_map/ppermute | solution.py:308
  231.1 21.2 %collective-permute-start.8 = (bf16[2,128,1024]{2,1,0:T(8,128)(2,1)S(1)}, bf16[2,128,1024]{2,1,0:T(8,128)(2,1)S(1)}, u32[]{:S(2)}, u32[]{:S(2)}) collective-permute-start(bf16[2,128,1024]{2,1,0:T(8,128)(2,1)S(1)} %slice.495), channel_id=1, source_target_pairs={{0,4},{1,5},{2,6},{3,7},{4,0},{5,1},{6,2},{7,3},{8,12},{9,13},{10,... | collective-permute-start | bytes 1572872 | tf_op jit(solution)/shard_map/ppermute | solution.py:308
  231.6 18.4 %collective-permute-start.22 = (bf16[1,128,1024]{2,1,0:T(8,128)(2,1)S(1)}, bf16[1,128,1024]{2,1,0:T(8,128)(2,1)S(1)}, u32[]{:S(2)}, u32[]{:S(2)}) collective-permute-start(bf16[1,128,1024]{2,1,0:T(8,128)(2,1)S(1)} %get-tuple-element.220), channel_id=1, source_target_pairs={{0,4},{1,5},{2,6},{3,7},{4,0},{5,1},{6,2},{7,3},{8,12},{9,13},{10,... | collective-permute-start | bytes 786440 | tf_op jit(solution)/shard_map/ppermute | solution.py:308
  250.0 22.0 %collective-permute-start.23 = (bf16[2,128,1024]{2,1,0:T(8,128)(2,1)S(1)}, bf16[2,128,1024]{2,1,0:T(8,128)(2,1)S(1)}, u32[]{:S(2)}, u32[]{:S(2)}) collective-permute-start(bf16[2,128,1024]{2,1,0:T(8,128)(2,1)S(1)} %pad_maximum_fusion.15), channel_id=1, source_target_pairs={{0,2},{1,3},{2,0},{3,1},{4,6},{5,7},{6,4},{7,5},{8,10},{9,11},{10,... | collective-permute-start | bytes 1572872 | tf_op jit(solution)/shard_map/ppermute | solution.py:308
  251.8 18.8 %collective-permute-start.20 = (bf16[1,128,1024]{2,1,0:T(8,128)(2,1)S(1)}, bf16[1,128,1024]{2,1,0:T(8,128)(2,1)S(1)}, u32[]{:S(2)}, u32[]{:S(2)}) collective-permute-start(bf16[1,128,1024]{2,1,0:T(8,128)(2,1)S(1)} %get-tuple-element.219), channel_id=1, source_target_pairs={{0,2},{1,3},{2,0},{3,1},{4,6},{5,7},{6,4},{7,5},{8,10},{9,11},{10,... | collective-permute-start | bytes 786440 | tf_op jit(solution)/shard_map/ppermute | solution.py:308
  252.5 20.3 %collective-permute-start.7 = (bf16[1,128,1024]{2,1,0:T(8,128)(2,1)S(1)}, bf16[1,128,1024]{2,1,0:T(8,128)(2,1)S(1)}, u32[]{:S(2)}, u32[]{:S(2)}) collective-permute-start(bf16[1,128,1024]{2,1,0:T(8,128)(2,1)S(1)} %get-tuple-element.197), channel_id=1, source_target_pairs={{0,4},{1,5},{2,6},{3,7},{4,0},{5,1},{6,2},{7,3},{8,12},{9,13},{10,... | collective-permute-start | bytes 786440 | tf_op jit(solution)/shard_map/ppermute | solution.py:308
  252.9 20.8 %collective-permute-start.9 = (bf16[1,128,1024]{2,1,0:T(8,128)(2,1)S(1)}, bf16[1,128,1024]{2,1,0:T(8,128)(2,1)S(1)}, u32[]{:S(2)}, u32[]{:S(2)}) collective-permute-start(bf16[1,128,1024]{2,1,0:T(8,128)(2,1)S(1)} %get-tuple-element.198), channel_id=1, source_target_pairs={{0,2},{1,3},{2,0},{3,1},{4,6},{5,7},{6,4},{7,5},{8,10},{9,11},{10,... | collective-permute-start | bytes 786440 | tf_op jit(solution)/shard_map/ppermute | solution.py:308
  271.4 12.3 %collective-permute-start.21 = (bf16[2,128,1024]{2,1,0:T(8,128)(2,1)}, bf16[2,128,1024]{2,1,0:T(8,128)(2,1)}, u32[]{:S(2)}, u32[]{:S(2)}) collective-permute-start(bf16[2,128,1024]{2,1,0:T(8,128)(2,1)} %pad_maximum_fusion.14), channel_id=1, source_target_pairs={{0,4},{1,5},{2,6},{3,7},{4,0},{5,1},{6,2},{7,3},{8,12},{9,13},{10,... | collective-permute-start | bytes 1572872 | tf_op jit(solution)/shard_map/ppermute | solution.py:308
  275.6 140.8 %copy-start.98 = (f32[4,2,16]{2,1,0:T(2,128)}, f32[4,2,16]{2,1,0:T(2,128)S(1)}, u32[]{:S(2)}) copy-start(f32[4,2,16]{2,1,0:T(2,128)S(1)} %get-tuple-element.236) | copy-start | bytes 1540
  277.3 10.1 %collective-permute-start.12 = (bf16[1,128,1024]{2,1,0:T(8,128)(2,1)S(1)}, bf16[1,128,1024]{2,1,0:T(8,128)(2,1)S(1)}, u32[]{:S(2)}, u32[]{:S(2)}) collective-permute-start(bf16[1,128,1024]{2,1,0:T(8,128)(2,1)S(1)} %get-tuple-element.224), channel_id=1, source_target_pairs={{0,4},{1,5},{2,6},{3,7},{4,0},{5,1},{6,2},{7,3},{8,12},{9,13},{10,... | collective-permute-start | bytes 786440 | tf_op jit(solution)/shard_map/ppermute | solution.py:308
  285.6 25.4 %collective-permute-start.24 = (bf16[4,128,2048]{2,1,0:T(8,128)(2,1)S(1)}, bf16[4,128,2048]{2,1,0:T(8,128)(2,1)S(1)}, u32[]{:S(2)}, u32[]{:S(2)}) collective-permute-start(bf16[4,128,2048]{2,1,0:T(8,128)(2,1)S(1)} %maximum_maximum_fusion.2), channel_id=1, source_target_pairs={{0,1},{1,0},{2,3},{3,2},{4,5},{5,4},{6,7},{7,6},{8,9},{9,8},{10,11... | collective-permute-start | bytes 6291464 | tf_op jit(solution)/shard_map/ppermute | solution.py:308
  285.6 9.2 %collective-permute-start.10 = (bf16[1,128,1024]{2,1,0:T(8,128)(2,1)S(1)}, bf16[1,128,1024]{2,1,0:T(8,128)(2,1)S(1)}, u32[]{:S(2)}, u32[]{:S(2)}) collective-permute-start(bf16[1,128,1024]{2,1,0:T(8,128)(2,1)S(1)} %get-tuple-element.223), channel_id=1, source_target_pairs={{0,2},{1,3},{2,0},{3,1},{4,6},{5,7},{6,4},{7,5},{8,10},{9,11},{10,... | collective-permute-start | bytes 786440 | tf_op jit(solution)/shard_map/ppermute | solution.py:308
  287.4 18.2 %collective-permute-start.13 = (bf16[2,128,1024]{2,1,0:T(8,128)(2,1)S(1)}, bf16[2,128,1024]{2,1,0:T(8,128)(2,1)S(1)}, u32[]{:S(2)}, u32[]{:S(2)}) collective-permute-start(bf16[2,128,1024]{2,1,0:T(8,128)(2,1)S(1)} %pad_maximum_fusion.12), channel_id=1, source_target_pairs={{0,2},{1,3},{2,0},{3,1},{4,6},{5,7},{6,4},{7,5},{8,10},{9,11},{10,... | collective-permute-start | bytes 1572872 | tf_op jit(solution)/shard_map/ppermute | solution.py:308
  294.9 13.2 %collective-permute-start.11 = (bf16[2,128,1024]{2,1,0:T(8,128)(2,1)S(1)}, bf16[2,128,1024]{2,1,0:T(8,128)(2,1)S(1)}, u32[]{:S(2)}, u32[]{:S(2)}) collective-permute-start(bf16[2,128,1024]{2,1,0:T(8,128)(2,1)S(1)} %pad_maximum_fusion.11), channel_id=1, source_target_pairs={{0,4},{1,5},{2,6},{3,7},{4,0},{5,1},{6,2},{7,3},{8,12},{9,13},{10,... | collective-permute-start | bytes 1572872 | tf_op jit(solution)/shard_map/ppermute | solution.py:308
  309.6 15.4 %collective-permute-start.14 = (bf16[4,128,2048]{2,1,0:T(8,128)(2,1)}, bf16[4,128,2048]{2,1,0:T(8,128)(2,1)}, u32[]{:S(2)}, u32[]{:S(2)}) collective-permute-start(bf16[4,128,2048]{2,1,0:T(8,128)(2,1)} %maximum_maximum_fusion.1), channel_id=1, source_target_pairs={{0,1},{1,0},{2,3},{3,2},{4,5},{5,4},{6,7},{7,6},{8,9},{9,8},{10,11... | collective-permute-start | bytes 6291464 | tf_op jit(solution)/shard_map/ppermute | solution.py:308
  349.2 16.0 %collective-permute-start.15 = (bf16[4,128,2048]{2,1,0:T(8,128)(2,1)S(1)}, bf16[4,128,2048]{2,1,0:T(8,128)(2,1)}, u32[]{:S(2)}, u32[]{:S(2)}) collective-permute-start(bf16[4,128,2048]{2,1,0:T(8,128)(2,1)S(1)} %fusion.12), channel_id=1, source_target_pairs={{0,1},{1,0},{2,3},{3,2},{4,5},{5,4},{6,7},{7,6},{8,9},{9,8},{10,11... | collective-permute-start | bytes 6291464 | tf_op jit(solution)/shard_map/ppermute | solution.py:308
  364.7 5.9 collective-permute-start.25
  376.8 15.1 %collective-permute-start.16 = (bf16[2,128,1024]{2,1,0:T(8,128)(2,1)}, bf16[2,128,1024]{2,1,0:T(8,128)(2,1)}, u32[]{:S(2)}, u32[]{:S(2)}) collective-permute-start(bf16[2,128,1024]{2,1,0:T(8,128)(2,1)} %pad_maximum_fusion.13), channel_id=1, source_target_pairs={{0,2},{1,3},{2,0},{3,1},{4,6},{5,7},{6,4},{7,5},{8,10},{9,11},{10,... | collective-permute-start | bytes 1572872 | tf_op jit(solution)/shard_map/ppermute | solution.py:308
  378.5 15.1 %collective-permute-start.18 = (bf16[2,128,1024]{2,1,0:T(8,128)(2,1)}, bf16[2,128,1024]{2,1,0:T(8,128)(2,1)}, u32[]{:S(2)}, u32[]{:S(2)}) collective-permute-start(bf16[2,128,1024]{2,1,0:T(8,128)(2,1)} %slice.515), channel_id=1, source_target_pairs={{0,4},{1,5},{2,6},{3,7},{4,0},{5,1},{6,2},{7,3},{8,12},{9,13},{10,... | collective-permute-start | bytes 1572872 | tf_op jit(solution)/shard_map/ppermute | solution.py:308
  379.6 23.5 %collective-permute-start.26 = (bf16[2,128,1024]{2,1,0:T(8,128)(2,1)}, bf16[2,128,1024]{2,1,0:T(8,128)(2,1)}, u32[]{:S(2)}, u32[]{:S(2)}) collective-permute-start(bf16[2,128,1024]{2,1,0:T(8,128)(2,1)} %pad_maximum_fusion.16), channel_id=1, source_target_pairs={{0,2},{1,3},{2,0},{3,1},{4,6},{5,7},{6,4},{7,5},{8,10},{9,11},{10,... | collective-permute-start | bytes 1572872 | tf_op jit(solution)/shard_map/ppermute | solution.py:308
  380.5 24.4 %collective-permute-start.28 = (bf16[2,128,1024]{2,1,0:T(8,128)(2,1)}, bf16[2,128,1024]{2,1,0:T(8,128)(2,1)}, u32[]{:S(2)}, u32[]{:S(2)}) collective-permute-start(bf16[2,128,1024]{2,1,0:T(8,128)(2,1)} %slice.532), channel_id=1, source_target_pairs={{0,4},{1,5},{2,6},{3,7},{4,0},{5,1},{6,2},{7,3},{8,12},{9,13},{10,... | collective-permute-start | bytes 1572872 | tf_op jit(solution)/shard_map/ppermute | solution.py:308
  386.2 186.6 %reduce-scatter.19.cloned.1.call-start = ((), (), s32[]{:S(2)}) async-start(), calls=%async_computation.22 | async-start | bytes 3522560 | tf_op jit(solution)/shard_map/reduce_scatter | solution.py:411
  395.2 15.3 %collective-permute-start.17 = (bf16[1,128,1024]{2,1,0:T(8,128)(2,1)S(1)}, bf16[1,128,1024]{2,1,0:T(8,128)(2,1)S(1)}, u32[]{:S(2)}, u32[]{:S(2)}) collective-permute-start(bf16[1,128,1024]{2,1,0:T(8,128)(2,1)S(1)} %get-tuple-element.193), channel_id=1, source_target_pairs={{0,4},{1,5},{2,6},{3,7},{4,0},{5,1},{6,2},{7,3},{8,12},{9,13},{10,... | collective-permute-start | bytes 786440 | tf_op jit(solution)/shard_map/ppermute | solution.py:308
  395.5 14.9 %collective-permute-start.19 = (bf16[1,128,1024]{2,1,0:T(8,128)(2,1)S(1)}, bf16[1,128,1024]{2,1,0:T(8,128)(2,1)S(1)}, u32[]{:S(2)}, u32[]{:S(2)}) collective-permute-start(bf16[1,128,1024]{2,1,0:T(8,128)(2,1)S(1)} %get-tuple-element.194), channel_id=1, source_target_pairs={{0,2},{1,3},{2,0},{3,1},{4,6},{5,7},{6,4},{7,5},{8,10},{9,11},{10,... | collective-permute-start | bytes 786440 | tf_op jit(solution)/shard_map/ppermute | solution.py:308
  406.5 8.3 %collective-permute-start.27 = (bf16[1,128,1024]{2,1,0:T(8,128)(2,1)S(1)}, bf16[1,128,1024]{2,1,0:T(8,128)(2,1)S(1)}, u32[]{:S(2)}, u32[]{:S(2)}) collective-permute-start(bf16[1,128,1024]{2,1,0:T(8,128)(2,1)S(1)} %get-tuple-element.189), channel_id=1, source_target_pairs={{0,4},{1,5},{2,6},{3,7},{4,0},{5,1},{6,2},{7,3},{8,12},{9,13},{10,... | collective-permute-start | bytes 786440 | tf_op jit(solution)/shard_map/ppermute | solution.py:308
  406.9 7.9 collective-permute-start.29
  420.6 7.3 collective-permute-start.32
  421.0 7.4 collective-permute-start.30
  427.9 12.1 %collective-permute-start.33 = (bf16[2,128,1024]{2,1,0:T(8,128)(2,1)S(1)}, bf16[2,128,1024]{2,1,0:T(8,128)(2,1)S(1)}, u32[]{:S(2)}, u32[]{:S(2)}) collective-permute-start(bf16[2,128,1024]{2,1,0:T(8,128)(2,1)S(1)} %pad_maximum_fusion.18), channel_id=1, source_target_pairs={{0,2},{1,3},{2,0},{3,1},{4,6},{5,7},{6,4},{7,5},{8,10},{9,11},{10,... | collective-permute-start | bytes 1572872 | tf_op jit(solution)/shard_map/ppermute | solution.py:308
  428.5 11.8 %collective-permute-start.31 = (bf16[2,128,1024]{2,1,0:T(8,128)(2,1)S(1)}, bf16[2,128,1024]{2,1,0:T(8,128)(2,1)S(1)}, u32[]{:S(2)}, u32[]{:S(2)}) collective-permute-start(bf16[2,128,1024]{2,1,0:T(8,128)(2,1)S(1)} %pad_maximum_fusion.17), channel_id=1, source_target_pairs={{0,4},{1,5},{2,6},{3,7},{4,0},{5,1},{6,2},{7,3},{8,12},{9,13},{10,... | collective-permute-start | bytes 1572872 | tf_op jit(solution)/shard_map/ppermute | solution.py:308
  441.9 9.4 %collective-permute-start.34 = (bf16[4,128,2048]{2,1,0:T(8,128)(2,1)}, bf16[4,128,2048]{2,1,0:T(8,128)(2,1)}, u32[]{:S(2)}, u32[]{:S(2)}) collective-permute-start(bf16[4,128,2048]{2,1,0:T(8,128)(2,1)} %maximum_maximum_fusion.3), channel_id=1, source_target_pairs={{0,1},{1,0},{2,3},{3,2},{4,5},{5,4},{6,7},{7,6},{8,9},{9,8},{10,11... | collective-permute-start | bytes 6291464 | tf_op jit(solution)/shard_map/ppermute | solution.py:308
  446.5 218.5 %reduce-scatter.13.cloned.1.call-start = ((), (), s32[]{:S(2)}) async-start(), calls=%async_computation.19 | async-start | bytes 1310720 | tf_op jit(solution)/shard_map/reduce_scatter | solution.py:411
  521.1 164.8 %reduce-scatter.9.cloned.1.call-start = ((), (), s32[]{:S(2)}) async-start(), calls=%async_computation.17 | async-start | bytes 1081344 | tf_op jit(solution)/shard_map/reduce_scatter | solution.py:644
  545.0 166.8 %reduce-scatter.15.cloned.1.call-start = ((), (), s32[]{:S(2)}) async-start(), calls=%async_computation.20 | async-start | bytes 1310720 | tf_op jit(solution)/shard_map/reduce_scatter | solution.py:576
  549.5 223.6 %reduce-scatter.11.cloned.1.call-start = ((), (), s32[]{:S(2)}) async-start(), calls=%async_computation.18 | async-start | bytes 3932160 | tf_op jit(solution)/shard_map/reduce_scatter | solution.py:411
  552.4 22.6 %collective-permute-start.35 = (bf16[4,128,2048]{2,1,0:T(8,128)(2,1)S(1)}, bf16[4,128,2048]{2,1,0:T(8,128)(2,1)}, u32[]{:S(2)}, u32[]{:S(2)}) collective-permute-start(bf16[4,128,2048]{2,1,0:T(8,128)(2,1)S(1)} %fusion.13), channel_id=1, source_target_pairs={{0,1},{1,0},{2,3},{3,2},{4,5},{5,4},{6,7},{7,6},{8,9},{9,8},{10,11... | collective-permute-start | bytes 6291464 | tf_op jit(solution)/shard_map/ppermute | solution.py:308
  569.2 17.1 %all-to-all-start.5 = ((bf16[8,64,688]{2,1,0:T(8,128)(2,1)}), bf16[8,64,688]{2,1,0:T(8,128)(2,1)S(1)}, u32[]{:S(2)}, u32[]{:S(2)}) async-start(bf16[8,64,688]{2,1,0:T(8,128)(2,1)} %bitcast.126), calls=%async_computation.10 | async-start | bytes 1572864 | tf_op jit(solution)/shard_map/all_to_all | solution.py:412
  581.0 68.2 %copy-start.118 = (u32[32]{0:T(128)S(1)}, u32[32]{0:T(128)}, u32[]{:S(2)}) copy-start(u32[32]{0:T(128)} %constant.77) | copy-start | bytes 388
  582.0 77.3 %collective-permute-start.36 = (bf16[2,128,1024]{2,1,0:T(8,128)(2,1)}, bf16[2,128,1024]{2,1,0:T(8,128)(2,1)}, u32[]{:S(2)}, u32[]{:S(2)}) collective-permute-start(bf16[2,128,1024]{2,1,0:T(8,128)(2,1)} %pad_maximum_fusion.19), channel_id=1, source_target_pairs={{0,2},{1,3},{2,0},{3,1},{4,6},{5,7},{6,4},{7,5},{8,10},{9,11},{10,... | collective-permute-start | bytes 1572872 | tf_op jit(solution)/shard_map/ppermute | solution.py:308
  583.8 75.5 %collective-permute-start.38 = (bf16[2,128,1024]{2,1,0:T(8,128)(2,1)S(1)}, bf16[2,128,1024]{2,1,0:T(8,128)(2,1)}, u32[]{:S(2)}, u32[]{:S(2)}) collective-permute-start(bf16[2,128,1024]{2,1,0:T(8,128)(2,1)S(1)} %slice.551), channel_id=1, source_target_pairs={{0,4},{1,5},{2,6},{3,7},{4,0},{5,1},{6,2},{7,3},{8,12},{9,13},{10,... | collective-permute-start | bytes 1572872 | tf_op jit(solution)/shard_map/ppermute | solution.py:308
  586.2 72.2 %copy-start.79 = (bf16[2,4,16,2048]{3,2,0,1:T(8,128)(2,1)S(1)}, bf16[2,4,16,2048]{3,2,0,1:T(8,128)(2,1)}, u32[]{:S(2)}) copy-start(bf16[2,4,16,2048]{3,2,0,1:T(8,128)(2,1)} %get-tuple-element.211) | copy-start | bytes 1572868
  586.3 78.7 %all-to-all-start.6 = ((bf16[8,64,688]{2,1,0:T(8,128)(2,1)}), bf16[8,64,688]{2,1,0:T(8,128)(2,1)S(1)}, u32[]{:S(2)}, u32[]{:S(2)}) async-start(bf16[8,64,688]{2,1,0:T(8,128)(2,1)} %bitcast.128), calls=%async_computation.12 | async-start | bytes 1572864 | tf_op jit(solution)/shard_map/all_to_all | solution.py:412
  647.6 3.5 collective-permute-start.40
  661.6 56.6 %collective-permute-start.37 = (bf16[1,128,1024]{2,1,0:T(8,128)(2,1)}, bf16[1,128,1024]{2,1,0:T(8,128)(2,1)S(1)}, u32[]{:S(2)}, u32[]{:S(2)}) collective-permute-start(bf16[1,128,1024]{2,1,0:T(8,128)(2,1)} %get-tuple-element.185), channel_id=1, source_target_pairs={{0,4},{1,5},{2,6},{3,7},{4,0},{5,1},{6,2},{7,3},{8,12},{9,13},{10,... | collective-permute-start | bytes 786440 | tf_op jit(solution)/shard_map/ppermute | solution.py:308
  661.7 56.5 %collective-permute-start.39 = (bf16[1,128,1024]{2,1,0:T(8,128)(2,1)}, bf16[1,128,1024]{2,1,0:T(8,128)(2,1)}, u32[]{:S(2)}, u32[]{:S(2)}) collective-permute-start(bf16[1,128,1024]{2,1,0:T(8,128)(2,1)} %get-tuple-element.186), channel_id=1, source_target_pairs={{0,2},{1,3},{2,0},{3,1},{4,6},{5,7},{6,4},{7,5},{8,10},{9,11},{10,... | collective-permute-start | bytes 786440 | tf_op jit(solution)/shard_map/ppermute | solution.py:308
  665.0 48.6 %all-to-all-start.4 = ((bf16[8,64,256]{2,1,0:T(8,128)(2,1)}), bf16[8,64,256]{2,1,0:T(8,128)(2,1)S(1)}, u32[]{:S(2)}, u32[]{:S(2)}) async-start(bf16[8,64,256]{2,1,0:T(8,128)(2,1)} %bitcast.382), calls=%async_computation.7 | async-start | bytes 524288 | tf_op jit(solution)/shard_map/all_to_all | solution.py:412
  715.6 62.1 %copy-start.93 = (f32[2048]{0:T(1024)S(1)}, f32[2048]{0:T(1024)}, u32[]{:S(2)}) copy-start(f32[2048]{0:T(1024)} %copy-done.92) | copy-start | bytes 24580
  715.6 62.1 %copy-start.99 = (f32[4,2,16]{2,1,0:T(2,128)S(1)}, f32[4,2,16]{2,1,0:T(2,128)}, u32[]{:S(2)}) copy-start(f32[4,2,16]{2,1,0:T(2,128)} %copy-done.98) | copy-start | bytes 1540
  715.6 62.1 %copy-start.103 = (f32[4,2,16]{2,1,0:T(2,128)S(1)}, f32[4,2,16]{2,1,0:T(2,128)}, u32[]{:S(2)}) copy-start(f32[4,2,16]{2,1,0:T(2,128)} %copy-done.102) | copy-start | bytes 1540
  715.7 62.1 %copy-start.104 = (f32[4,2,16]{2,1,0:T(2,128)S(1)}, f32[4,2,16]{2,1,0:T(2,128)}, u32[]{:S(2)}) copy-start(f32[4,2,16]{2,1,0:T(2,128)} %get-tuple-element.235) | copy-start | bytes 1540
  773.2 17.1 %all-to-all-start.3 = ((bf16[8,64,768]{2,1,0:T(8,128)(2,1)}), bf16[8,64,768]{2,1,0:T(8,128)(2,1)}, u32[]{:S(2)}, u32[]{:S(2)}) async-start(bf16[8,64,768]{2,1,0:T(8,128)(2,1)} %bitcast.374), calls=%async_computation.5 | async-start | bytes 1572864 | tf_op jit(solution)/shard_map/all_to_all | solution.py:412
  (122 other events, 1457.9 us)
Sparse Core Ops, SparseCore 0:
  30.3 64.9 all-gather.8
  96.9 26.9 all-gather.6
  125.5 27.4 all-gather.10
  154.4 58.6 all-gather.14
  224.8 103.0 all-gather.12
  386.3 52.5 reduce-scatter.16
  446.6 52.9 reduce-scatter.18
  521.2 24.5 reduce-scatter.12
  548.8 137.1 reduce-scatter.8
  688.6 23.0 reduce-scatter.14
  714.2 58.9 reduce-scatter.10

commit v2 on v1

--- a/solution.py
+++ b/solution.py
@@ -229,11 +229,16 @@
     return pl.BlockSpec(shape, lambda *_: (0,) * len(shape))
 
 
+def place(step, own, count):
+    apart = jnp.bitwise_xor(step, own)
+    return jnp.bitwise_and(apart, 1) * (count // 2) + lax.shift_right_logical(apart, 1)
+
+
 def inner_forward(slot, queries, keys, values, rates, again, again_wide, start, start_bias, gain, shift, heads, head_dim, parts):
     steps, _, lanes = rates.shape
     tokens = queries.shape[0] // steps
     wide = start.shape[1]
-    at_slot = pl.BlockSpec((tokens, heads * head_dim), lambda i, s: (jnp.bitwise_xor(i, s[0]), 0))
+    at_slot = pl.BlockSpec((tokens, heads * head_dim), lambda i, s: (place(i, s[0], steps), 0))
 
     def stepped(*shape):
         return pl.BlockSpec((1,) + shape, lambda i, s: (i,) + (0,) * len(shape))
@@ -268,7 +273,7 @@
     tokens = queries.shape[0] // steps
     wide = again_wide.shape[-1]
     at_slot = pl.BlockSpec(
-        (tokens, heads * head_dim), lambda i, s: (jnp.bitwise_xor(steps - 1 - i, s[0]), 0)
+        (tokens, heads * head_dim), lambda i, s: (place(steps - 1 - i, s[0], steps), 0)
     )
 
     def stepped(*shape):
@@ -303,58 +308,118 @@
     )(slot, queries, keys, values, deltas, rates, again, again_wide, gain, shift, *saved)
 
 
-def bit_exchange(value, axis, bit):
+def cut_heads_kernel(groups, seq_count, span, *refs):
+    out_ref = refs[-1]
+    for s in range(seq_count):
+        pieces = [
+            ref[:, at : at + span].astype(F32)
+            for ref in refs[:-1]
+            for at in ((g * seq_count + s) * span for g in range(groups))
+        ]
+        out_ref[s] = jnp.concatenate(pieces, axis=1).astype(out_ref.dtype)
+
+
+def cut_heads(weights, groups, seq_count, span):
+    rows = weights[0].shape[0]
+    return pl.pallas_call(
+        functools.partial(cut_heads_kernel, groups, seq_count, span),
+        out_shape=jax.ShapeDtypeStruct((seq_count, rows, len(weights) * groups * span), BF16),
+        compiler_params=pltpu.CompilerParams(vmem_limit_bytes=40 * 1024 * 1024),
+        name="cut_heads",
+    )(*weights)
+
+
+def join_heads_kernel(groups, seq_count, span, parts_ref, *refs):
+    for n, ref in enumerate(refs):
+        pieces = []
+        for g in range(groups):
+            for s in range(seq_count):
+                at = (n * groups + g) * span
+                pieces.append(parts_ref[s, :, at : at + span].astype(F32))
+        ref[...] = jnp.concatenate(pieces, axis=1)
+
+
+def join_heads(parts, count, groups, seq_count, span):
+    whole_row = jax.ShapeDtypeStruct((parts.shape[1], groups * seq_count * span), F32)
+    return pl.pallas_call(
+        functools.partial(join_heads_kernel, groups, seq_count, span),
+        out_shape=[whole_row] * count,
+        compiler_params=pltpu.CompilerParams(vmem_limit_bytes=40 * 1024 * 1024),
+        name="join_heads",
+    )(parts)
+
+
+def exchange(value, axis, bit):
     count = lax.axis_size(axis)
     return lax.ppermute(value, axis, [(i, i ^ bit) for i in range(count)])
 
 
-def seq_bits():
-    count = lax.axis_size("seq")
-    bits = [1 << p for p in range(count.bit_length() - 1)]
-    return bits
-
-
-def gather_blocks(block):
-    bits = seq_bits()
+def bits_of(axis):
+    return [(axis, 1 << p) for p in range(lax.axis_size(axis).bit_length() - 1)]
+
+
+def cuts_of(width, ways):
+    unit = 128 if width >= 128 * ways else 1
+    return [unit * (n * (width // unit) // ways) for n in range(ways)] + [width]
+
+
+def gather_blocks(block, bits, tied=None):
     near, far = bits[0], bits[1:]
     ways = max(1, len(far))
-    width = block.shape[-1]
-    pieces = []
-    for way in range(ways):
-        low, high = way * width // ways, (way + 1) * width // ways
-        held = {0: block[:, low:high]}
-        for step in range(len(far)):
-            bit = far[(way + step) % len(far)]
-            keys = sorted(held)
-            moved = bit_exchange(jnp.stack([held[k] for k in keys]), "seq", bit)
+    cuts = cuts_of(block.shape[-1], ways)
+    held = [{0: block[:, cuts[way] : cuts[way + 1]]} for way in range(ways)]
+    for step in range(len(far)):
+        for way in range(ways):
+            bit = (way + step) % len(far)
+            keys = sorted(held[way])
+            moved = exchange(jnp.stack([held[way][k] for k in keys]), *far[bit])
             for n, k in enumerate(keys):
-                held[k | bit] = moved[n]
-        pieces.append(jnp.stack([held[k] for k in sorted(held)]))
-    half = jnp.concatenate(pieces, axis=-1)
-    other = bit_exchange(half, "seq", near)
-    return jnp.stack([half, other], axis=1).reshape((-1,) + block.shape)
-
-
-def reduce_blocks(blocks):
-    bits = seq_bits()
+                held[way][k | 1 << bit] = moved[n]
+    half = jnp.concatenate([jnp.stack([h[k] for k in sorted(h)]) for h in held], axis=-1)
+    if tied is not None:
+        half, tied = lax.optimization_barrier((half, tied))
+    whole = jnp.concatenate([half, exchange(half, *near)], axis=0)
+    return whole if tied is None else (whole, tied)
+
+
+def reduce_blocks(own, away, bits, kind=BF16):
     near, far = bits[0], bits[1:]
     ways = max(1, len(far))
-    width = blocks.shape[-1]
-    blocks = blocks.reshape((-1, 2) + blocks.shape[1:])
-    half = blocks[:, 0] + bit_exchange(blocks[:, 1].astype(BF16), "seq", near).astype(F32)
-    pieces = []
-    for way in range(ways):
-        low, high = way * width // ways, (way + 1) * width // ways
-        held = {2 * k: half[k, :, low:high] for k in range(half.shape[0])}
-        for step in range(len(far)):
-            bit = far[(way + step) % len(far)]
-            away = sorted(k for k in held if k & bit)
-            moved = bit_exchange(jnp.stack([held[k].astype(BF16) for k in away]), "seq", bit)
-            for n, k in enumerate(away):
-                held[k ^ bit] = held[k ^ bit] + moved[n].astype(F32)
-                del held[k]
-        pieces.append(held[0])
-    return jnp.concatenate(pieces, axis=-1)
+    cuts = cuts_of(own.shape[-1], ways)
+    half = own.astype(F32) + exchange(away.astype(kind), *near).astype(F32)
+    held = [
+        {k: half[k, :, cuts[way] : cuts[way + 1]] for k in range(half.shape[0])} for way in range(ways)
+    ]
+    for step in range(len(far)):
+        for way in range(ways):
+            bit = (way + step) % len(far)
+            gone = sorted(k for k in held[way] if k >> bit & 1)
+            moved = exchange(jnp.stack([held[way][k].astype(kind) for k in gone]), *far[bit])
+            for n, k in enumerate(gone):
+                held[way][k ^ 1 << bit] = held[way][k ^ 1 << bit] + moved[n].astype(F32)
+                del held[way][k]
+    return jnp.concatenate([h[0] for h in held], axis=-1)
+
+
+def has_bit(axis, bit):
+    return jnp.bitwise_and(lax.axis_index(axis), bit) > 0
+
+
+def gather_natural(value, bits):
+    for axis, bit in bits:
+        other = exchange(value, axis, bit)
+        high = has_bit(axis, bit)
+        value = jnp.concatenate([jnp.where(high, other, value), jnp.where(high, value, other)], axis=0)
+    return value
+
+
+def halved(value, dim, axis, bit):
+    half = value.shape[dim] // 2
+    high = has_bit(axis, bit)
+    low_half = lax.slice_in_dim(value, 0, half, axis=dim)
+    high_half = lax.slice_in_dim(value, half, 2 * half, axis=dim)
+    other = exchange(jnp.where(high, low_half, high_half), axis, bit)
+    return jnp.where(high, high_half, low_half) + other
 
 
 def gelu_tanh(values):
@@ -387,33 +452,31 @@
     head_count = rate_weight.shape[1]
     head_dim = init_weight.shape[1]
     parts = stretch // MINI
+    local = rows_here * stretch
     seq_count = lax.axis_size("seq")
     rows_count = lax.axis_size("rows")
     share = model // (seq_count * rows_count)
-    hidden_share = ffn_down_weight.shape[0]
+    unit_share = ffn_down_weight.shape[0]
     heads = head_count // seq_count
     width = heads * head_dim
     aligned = share % head_dim == 0
     groups, span = (rows_count, share) if aligned else (1, width)
     me = lax.axis_index("seq")
-    slots = jnp.bitwise_xor(jnp.arange(seq_count, dtype=jnp.int32), me)
     everywhere = ("rows", "seq")
-
-    def by_owner(values, group, size):
-        split = values.reshape(values.shape[0], group, seq_count, size)
-        return split.transpose(2, 0, 1, 3).reshape(seq_count, values.shape[0], group * size)
-
-    def columns_in(values):
-        mine = lax.all_to_all(values, "seq", 0, 0, tiled=True)
-        return lax.all_gather(mine.reshape(-1, values.shape[-1]), "rows", axis=0, tiled=True)
+    seq_bits = bits_of("seq")
+    row_bits = bits_of("rows")
+    units = rows_count * unit_share
+    spare = -unit_share % 16
+
+    def shuffled(values):
+        return lax.all_to_all(values, "seq", 0, 0, tiled=True).reshape(-1, values.shape[-1])
+
+    def row_sums(values):
+        summed = lax.psum_scatter(values, "rows", scatter_dimension=0, tiled=True)
+        return summed.reshape(seq_count, share, -1)
 
     def columns_out(values):
-        summed = lax.psum_scatter(values.astype(BF16), "rows", scatter_dimension=0, tiled=True)
-        return lax.all_to_all(summed.reshape(seq_count, share, -1), "seq", 0, 0, tiled=True)
-
-    def from_owner(values, group, size):
-        split = values.reshape(seq_count, share, group, size)
-        return split.transpose(1, 2, 0, 3).reshape(share, -1).astype(F32)
+        return lax.all_to_all(values, "seq", 0, 0, tiled=True)
 
     def own_part(values):
         split = values.reshape(groups, seq_count, span, -1)
@@ -430,29 +493,43 @@
     def restored(values):
         return values.reshape(parts, rows_here, MINI, -1).transpose(1, 0, 2, 3).reshape(rows_here, stretch, -1)
 
+    real = jnp.min(doc_starts) >= 0
+
+    def apart(part, *operands):
+        shapes = jax.eval_shape(part, *operands)
+        blank = lambda *_: jax.tree.map(lambda s: jnp.zeros(s.shape, s.dtype), shapes)
+        return lax.cond(real, part, blank, *operands)
+
     vectors = jnp.stack(
         [attn_gain, ffn_gain, init_bias, inner_gain, inner_shift, post_gain, post_shift], axis=1
     )
-    count = vectors.shape[1]
-    small = lax.all_gather(
-        jnp.concatenate([init_weight, rate_weight, vectors], axis=1), everywhere, axis=0, tiled=True
-    )
-    qkv_weight = columns_in(
-        jnp.concatenate([by_owner(w, groups, span) for w in (query_weight, key_weight, value_weight)], axis=2)
-    )
-    gate_own = columns_in(by_owner(gate_weight, groups, span))
+    small = jnp.concatenate([init_weight, rate_weight, vectors], axis=1)
+    small = jnp.pad(small, ((0, 0), (0, -small.shape[1] % 128)))
+    hidden, cotangent = reordered(hidden_in), reordered(out_grad)
     if aligned:
         out_own = lax.all_gather(out_weight, "rows", axis=0, tiled=True)
     else:
         out_own = own_part(lax.all_gather(out_weight, everywhere, axis=0, tiled=True))
-    ffn_wide = columns_in(
-        jnp.concatenate(
-            [by_owner(w, rows_count, hidden_share) for w in (ffn_gate_weight, ffn_up_weight)], axis=2
-        )
-    )
-    hidden_units = rows_count * hidden_share
-    gate_wide, up_wide = ffn_wide[:, :hidden_units], ffn_wide[:, hidden_units:]
-    down_wide = lax.all_gather(ffn_down_weight, "rows", axis=0, tiled=True)
+    mixer_cut = shuffled(
+        cut_heads((query_weight, key_weight, value_weight, gate_weight), groups, seq_count, span)
+    )
+    mixer_cut, hidden, cotangent, small, ffn_gate_weight, ffn_up_weight = lax.optimization_barrier(
+        (mixer_cut, hidden, cotangent, small, ffn_gate_weight, ffn_up_weight)
+    )
+    mixer_weight = lax.all_gather(mixer_cut, "rows", axis=0, tiled=True)
+    ffn_cut = cut_heads((ffn_gate_weight, ffn_up_weight), rows_count, seq_count, unit_share)
+
+    def gather_inputs(hidden, cotangent, small, ffn_cut):
+        hidden_all = gather_blocks(hidden, seq_bits).reshape(-1, model)
+        cot_all = gather_blocks(cotangent, seq_bits).reshape(-1, model)
+        small = gather_natural(small, row_bits).reshape(rows_count, share, -1)
+        small = small.transpose(1, 0, 2).reshape(share, -1)
+        small = gather_natural(small, seq_bits).reshape(seq_count, share, rows_count, -1)
+        small = small.transpose(2, 0, 1, 3).reshape(model, -1)
+        return hidden_all, cot_all, small, shuffled(ffn_cut)
+
+    hidden_all, cot_all, small, ffn_cut = apart(gather_inputs, hidden, cotangent, small, ffn_cut)
+    ffn_wide = lax.all_gather(ffn_cut, "rows", axis=0, tiled=True)
 
     gain_attn = small[:, head_dim + head_count].astype(F32)
     gain_ffn = small[:, head_dim + head_count + 1].astype(F32)
@@ -487,20 +564,24 @@
 
     again, again_wide = by_chain(MINI), by_chain(head_dim)
 
-    hidden = reordered(hidden_in)
-    cotangent = reordered(out_grad)
-    tokens = hidden.astype(F32)
-    tokens_all = gather_blocks(hidden).reshape(-1, model).astype(F32)
+    order = jnp.arange(steps, dtype=jnp.int32)
+    slots = place(order, me, steps)
+    blocks = jnp.bitwise_xor(order % (steps // 2) * 2 + order // (steps // 2), me)
+
+    tokens_all = hidden_all.astype(F32)
     inverse_all = lax.rsqrt(jnp.mean(tokens_all * tokens_all, axis=-1, keepdims=True) + EPSILON)
     plain_all = tokens_all * inverse_all
     normed = (plain_all * gain_attn).astype(BF16)
 
+
     def project(matrix):
         return jnp.dot(normed, matrix, preferred_element_type=F32)
 
-    qkv = project(qkv_weight)
+    qkv = project(mixer_weight[:, : 3 * width])
+    qkv, ffn_down_weight = lax.optimization_barrier((qkv, ffn_down_weight))
+    down_wide = lax.all_gather(ffn_down_weight, "rows", axis=0, tiled=True)
     queries, keys, values = (qkv[:, n * width : (n + 1) * width] for n in range(3))
-    gate_pre = project(gate_own)
+    gate_pre = project(mixer_weight[:, 3 * width :])
     logits = project(rate_own)
     slope = jax.nn.sigmoid(logits)
 
@@ -511,18 +592,20 @@
 
     def from_lanes(per_lane):
         ordered = per_lane.reshape(steps, parts, heads, rows_here * MINI).transpose(0, 1, 3, 2)
-        return jnp.take(ordered.reshape(steps, -1, heads), slots, axis=0).reshape(-1, heads)
+        return jnp.take(ordered.reshape(steps, -1, heads), blocks, axis=0).reshape(-1, heads)
 
     rates = to_lanes(slope * (BASE_RATE / head_dim))
     slot = me.astype(jnp.int32).reshape(1)
+
     inner_out, *saved = inner_forward(
         slot, queries, keys, values, rates, again, again_wide, start, bias_lanes, gain_lanes,
         shift_lanes, heads, head_dim, parts,
     )
-    def feature_mean(*values):
-        sums = jnp.stack([jnp.sum(v, axis=1) for v in values]).reshape(len(values), steps, -1)
+
+    def feature_mean(*arrays):
+        sums = jnp.stack([jnp.sum(v, axis=1) for v in arrays]).reshape(len(arrays), steps, -1)
         total = lax.psum(jnp.take(sums, slots, axis=1), "seq") / model
-        return jnp.take(total, slots, axis=1).reshape(len(values), -1, 1)
+        return jnp.take(total, blocks, axis=1).reshape(len(arrays), -1, 1)
 
     moments = feature_mean(inner_out, inner_out * inner_out)
     post_mean = moments[0]
@@ -531,61 +614,81 @@
     post_out = post_norm * post_scale + post_offset
     gelu_value, gelu_pull = jax.vjp(gelu_tanh, gate_pre)
     gated = (gelu_value * post_out).astype(BF16)
-    branch = jnp.dot(gated, out_own, preferred_element_type=F32)
-    residual = tokens + reduce_blocks(branch.reshape(steps, -1, model))
-
-    inverse_two = lax.rsqrt(jnp.mean(residual * residual, axis=-1, keepdims=True) + EPSILON)
-    ffn_in = gather_blocks((residual * inverse_two * gain_ffn).astype(BF16)).reshape(-1, model)
-    cot_all = gather_blocks(cotangent).reshape(-1, model)
-    gate_value = jnp.dot(ffn_in, gate_wide, preferred_element_type=F32)
-    up_value = jnp.dot(ffn_in, up_wide, preferred_element_type=F32)
+
+    def reduced(left, matrix, dims, bits):
+        half = left.shape[0] // 2
+        away = lax.dot_general(left[half:], matrix, dims, preferred_element_type=F32).astype(BF16)
+        own = lax.dot_general(left[:half], matrix, dims, preferred_element_type=F32)
+        return reduce_blocks(
+            own.reshape(-1, local, model), away.reshape(-1, local, model), bits
+        )
+
+    def rms_inverse(values):
+        return lax.rsqrt(jnp.mean(values * values, axis=-1, keepdims=True) + EPSILON)
+
+    def into_ffn(gated, out_own, hidden, gain_ffn):
+        residual = hidden.astype(F32) + reduced(gated, out_own, NN, seq_bits)
+        scaled = (residual * rms_inverse(residual) * gain_ffn).astype(BF16)
+        return residual, gather_blocks(scaled, seq_bits).reshape(-1, model)
+
+    residual, ffn_in = apart(into_ffn, gated, out_own, hidden, gain_ffn)
+    gate_up = jnp.dot(ffn_in, ffn_wide, preferred_element_type=F32)
+    gate_value, up_value = gate_up[:, :units], gate_up[:, units:]
     sigmoid_gate = jax.nn.sigmoid(gate_value)
     active = (gate_value * sigmoid_gate * up_value).astype(BF16)
-    down = jnp.dot(active, down_wide, preferred_element_type=F32)
-    delta_active = jnp.einsum("td,fd->tf", cot_all, down_wide, preferred_element_type=F32)
+
+    def token_grad(left, right):
+        return lax.dot_general(left, right, TN, preferred_element_type=F32)
+
+    grad_down = token_grad(active, cot_all).astype(BF16).reshape(rows_count, unit_share, model)
+    grad_down = jnp.pad(grad_down, ((0, 0), (0, spare), (0, 0))).reshape(-1, model)
+    grad_down, down_wide = lax.optimization_barrier((grad_down, down_wide))
+    grad_down = lax.psum_scatter(grad_down, "rows", scatter_dimension=0, tiled=True)
+    grad_down = grad_down[:unit_share].astype(F32)
+    delta_active = lax.dot_general(cot_all, down_wide, NT, preferred_element_type=F32)
     delta_up = (delta_active * gate_value * sigmoid_gate).astype(BF16)
     delta_gate = (
         delta_active * up_value * sigmoid_gate * (1.0 + gate_value * (1.0 - sigmoid_gate))
     ).astype(BF16)
-    delta_ffn = jnp.einsum("tf,df->td", delta_up, up_wide, preferred_element_type=F32) + jnp.einsum(
-        "tf,df->td", delta_gate, gate_wide, preferred_element_type=F32
-    )
-    delta_ffn = reduce_blocks(delta_ffn.reshape(steps, -1, model))
-    block_out = residual + reduce_blocks(down.reshape(steps, -1, model))
-
-    def token_grad(left, right):
-        return jnp.einsum("td,te->de", left, right, preferred_element_type=F32)
-
-    grad_down = lax.psum_scatter(
-        token_grad(active, cot_all).astype(BF16), "rows", scatter_dimension=0, tiled=True
-    ).astype(F32)
-    grad_gate = from_owner(columns_out(token_grad(ffn_in, delta_gate)), rows_count, hidden_share)
-    grad_up = from_owner(columns_out(token_grad(ffn_in, delta_up)), rows_count, hidden_share)
-
-    grad_gain_ffn = jnp.sum(delta_ffn * residual * inverse_two, axis=0)
-    scaled_two = delta_ffn * gain_ffn
-    delta_after = (
-        cotangent.astype(F32)
-        + inverse_two * scaled_two
-        - residual * inverse_two**3 * jnp.mean(scaled_two * residual, axis=-1, keepdims=True)
-    )
-    delta_branch = gather_blocks(delta_after.astype(BF16)).reshape(-1, model)
-
-    grad_out = token_grad(gated, delta_branch)
-    if aligned:
-        grad_out = lax.psum_scatter(grad_out.astype(BF16), "rows", scatter_dimension=0, tiled=True)
-    else:
-        grad_out = lax.psum_scatter(
-            placed(grad_out).astype(BF16), everywhere, scatter_dimension=0, tiled=True
+    delta_both = jnp.concatenate([delta_gate, delta_up], axis=1)
+
+    def out_of_ffn(delta_both, ffn_wide, active, down_wide, residual, gain_ffn, cotangent):
+        delta_ffn = reduced(delta_both, ffn_wide, NT, seq_bits)
+        inverse_two = rms_inverse(residual)
+        grad_gain_ffn = jnp.sum(delta_ffn * residual * inverse_two, axis=0)
+        scaled_two = delta_ffn * gain_ffn
+        delta_after = (
+            cotangent.astype(F32)
+            + inverse_two * scaled_two
+            - residual * inverse_two**3 * jnp.mean(scaled_two * residual, axis=-1, keepdims=True)
         )
-    delta_gated = jnp.einsum("te,de->td", delta_branch, out_own, preferred_element_type=F32)
+        delta_branch = gather_blocks(delta_after.astype(BF16), seq_bits).reshape(-1, model)
+        block_out = residual + reduced(active, down_wide, NN, seq_bits)
+        return grad_gain_ffn, delta_after, delta_branch, block_out
+
+    grad_ffn = token_grad(ffn_in, delta_both).astype(BF16)
+    delta_both, grad_ffn = lax.optimization_barrier((delta_both, grad_ffn))
+    ffn_sums = row_sums(grad_ffn)
+    grad_gain_ffn, delta_after, delta_branch, block_out = apart(
+        out_of_ffn, delta_both, ffn_wide, active, down_wide, residual, gain_ffn, cotangent
+    )
+
+    grad_out = token_grad(gated, delta_branch).astype(BF16)
+    delta_gated = lax.dot_general(delta_branch, out_own, NT, preferred_element_type=F32)
     delta_pre = gelu_pull(delta_gated * post_out)[0].astype(BF16)
+    grad_gate_weight = token_grad(normed, delta_pre).astype(BF16)
+    delta_gated, grad_out, grad_gate_weight = lax.optimization_barrier(
+        (delta_gated, grad_out, grad_gate_weight)
+    )
+    gate_sums = row_sums(grad_gate_weight)
     delta_post = delta_gated * gelu_value
     grad_post_scale = jnp.sum(delta_post * post_norm, axis=0)
     grad_post_shift = jnp.sum(delta_post, axis=0)
     delta_norm = delta_post * post_scale
     means = feature_mean(delta_norm, delta_norm * post_norm)
     delta_inner = (delta_norm - means[0] - post_norm * means[1]) * post_inverse
+
+    delta_inner, ffn_sums, grad_down = lax.optimization_barrier((delta_inner, ffn_sums, grad_down))
     (
         delta_queries, delta_keys, delta_values, delta_rates,
         grad_start, grad_bias, grad_inner_gain, grad_inner_shift,
@@ -597,29 +700,19 @@
         from_lanes(delta_rates) * slope * (1.0 - slope) * (BASE_RATE / head_dim)
     ).astype(BF16)
     delta_qkv = jnp.concatenate([delta_queries, delta_keys, delta_values], axis=1)
+    delta_qkv, gate_sums = lax.optimization_barrier((delta_qkv, gate_sums))
+    grad_qkv = token_grad(normed, delta_qkv).astype(BF16)
+    delta_qkv, delta_logits, grad_qkv = lax.optimization_barrier((delta_qkv, delta_logits, grad_qkv))
+    qkv_sums = row_sums(grad_qkv)
+    grad_rate = token_grad(normed, delta_logits)
+    grad_rate, grad_out = lax.optimization_barrier((grad_rate, grad_out))
+    if aligned:
+        grad_out = lax.psum_scatter(grad_out, "rows", scatter_dimension=0, tiled=True)
+    else:
+        grad_out = lax.psum_scatter(placed(grad_out), everywhere, scatter_dimension=0, tiled=True)
 
     def back_project(delta, matrix):
-        return jnp.einsum("te,de->td", delta, matrix, preferred_element_type=F32)
-
-    delta_normed = (
-        back_project(delta_qkv, qkv_weight)
-        + back_project(delta_pre, gate_own)
-        + back_project(delta_logits, rate_own)
-    )
-    grad_gain_attn = jnp.sum(delta_normed * plain_all, axis=0)
-    delta_normed = reduce_blocks(delta_normed.reshape(steps, -1, model))
-    inverse_one = lax.rsqrt(jnp.mean(tokens * tokens, axis=-1, keepdims=True) + EPSILON)
-    scaled_one = delta_normed * gain_attn
-    hidden_grad = (
-        delta_after
-        + inverse_one * scaled_one
-        - tokens * inverse_one**3 * jnp.mean(scaled_one * tokens, axis=-1, keepdims=True)
-    )
-    qkv_grads = columns_out(token_grad(normed, delta_qkv))
-    grad_query, grad_key, grad_value = (
-        from_owner(qkv_grads[:, :, n * width : (n + 1) * width], groups, span) for n in range(3)
-    )
-    grad_gate_weight = from_owner(columns_out(token_grad(normed, delta_pre)), groups, span)
+        return lax.dot_general(delta, matrix, NT, preferred_element_type=F32)
 
     def lane_sum(per_lane, repeat):
         return per_lane.reshape(head_dim, heads, repeat).sum(axis=2).T.reshape(width, 1)
@@ -627,7 +720,7 @@
     grad_start = grad_start.reshape(head_dim, heads, rows_here, head_dim).sum(axis=2)
     grad_start = grad_start.transpose(1, 2, 0).reshape(width, head_dim)
     grad_bias = grad_bias.reshape(head_dim, heads, rows_here, MINI)[..., 0]
-    grad_rate = token_grad(normed, delta_logits).reshape(model, groups, 1, -1)
+    grad_rate = grad_rate.reshape(model, groups, 1, -1)
     here = (jnp.arange(seq_count) == me).reshape(1, 1, -1, 1)
     grad_rate = jnp.where(here, grad_rate, 0.0).reshape(model, head_count)
     own_grads = jnp.concatenate(
@@ -641,17 +734,50 @@
         ],
         axis=1,
     )
-    small_grads = lax.psum_scatter(
-        jnp.concatenate(
-            [placed(own_grads), grad_rate, grad_gain_attn[:, None], grad_gain_ffn[:, None]], axis=1
-        ),
-        everywhere, scatter_dimension=0, tiled=True,
+    small_grads = jnp.concatenate([placed(own_grads), grad_rate, grad_gain_ffn[:, None]], axis=1)
+
+    def out_of_mixer(
+        delta_mixer, mixer_weight, delta_logits, rate_own, plain_all, hidden, delta_after, gain_attn,
+        small_grads, ffn_sums, gate_sums,
+    ):
+        delta_normed = back_project(delta_mixer, mixer_weight) + back_project(delta_logits, rate_own)
+        grad_gain_attn = jnp.sum(delta_normed * plain_all, axis=0)
+        small_grads = jnp.concatenate([small_grads, grad_gain_attn[:, None]], axis=1)
+        small_grads = jnp.pad(small_grads, ((0, 0), (0, -small_grads.shape[1] % 128)))
+        small_grads = small_grads.reshape(rows_count, seq_count, share, -1)
+        for axis, bit in reversed(seq_bits):
+            small_grads = halved(small_grads, 1, axis, bit)
+        for axis, bit in reversed(row_bits):
+            small_grads = halved(small_grads, 0, axis, bit)
+        small_grads = small_grads.reshape(share, -1)
+        grad_gate, grad_up = join_heads(
+            columns_out(ffn_sums), 2, rows_count, seq_count, unit_share
+        )
+        grad_gate_weight, = join_heads(columns_out(gate_sums), 1, groups, seq_count, span)
+        delta_normed = delta_normed.reshape(2, -1, local, model)
+        delta_normed = reduce_blocks(delta_normed[0], delta_normed[1], seq_bits)
+        tokens = hidden.astype(F32)
+        inverse_one = rms_inverse(tokens)
+        scaled_one = delta_normed * gain_attn
+        hidden_grad = (
+            delta_after
+            + inverse_one * scaled_one
+            - tokens * inverse_one**3 * jnp.mean(scaled_one * tokens, axis=-1, keepdims=True)
+        )
+        return hidden_grad, small_grads, grad_gate, grad_up, grad_gate_weight
+
+    hidden_grad, small_grads, grad_gate, grad_up, grad_gate_weight = apart(
+        out_of_mixer, jnp.concatenate([delta_qkv, delta_pre], axis=1), mixer_weight, delta_logits,
+        rate_own, plain_all, hidden, delta_after, gain_attn, small_grads, ffn_sums, gate_sums,
+    )
+    grad_query, grad_key, grad_value = join_heads(
+        columns_out(qkv_sums), 3, groups, seq_count, span
     )
     after = head_dim + 5
     return (
         restored(block_out).astype(BF16),
         restored(hidden_grad),
-        small_grads[:, after + head_count],
+        small_grads[:, after + head_count + 1],
         grad_query,
         grad_key,
         grad_value,
@@ -664,7 +790,7 @@
         small_grads[:, head_dim + 3],
         small_grads[:, head_dim + 4],
         grad_out.astype(F32),
-        small_grads[:, after + head_count + 1],
+        small_grads[:, after + head_count],
         grad_gate,
         grad_up,
         grad_down,

time: 812 us -> 661 us (0.81)
  blocking collectives: 180 us -> 40.5 us
  local copies, waits for them, and re-layouts: 131 us -> 90.7 us
  starting transfers between devices: 50.7 us -> 71.7 us
  waiting for transfers between devices: 191 us -> 208 us
  other arithmetic: 88.9 us -> 80.7 us
    reduce_scatter x6 -> x5, waiting for transfers between devices: 76.9 us -> 0.03 us  [the longest x3 0.02 us: row_sums(): summed = lax.psum_scatter(values, 'rows', scatter_dimension=0, tiled=True)]
    unnamed x1 -> x0, blocking collectives: 57.6 us -> none
    all_to_all x3 -> x0, blocking collectives: 50.4 us -> none  [columns_in(): mine = lax.all_to_all(values, 'seq', 0, 0, tiled=True)]
    all_gather x1 -> x0, blocking collectives: 45.7 us -> none  [shards(): lax.all_gather(jnp.concatenate([init_weight, rate_weight, vectors], axis=...]
    ppermute x40 -> x50, waiting for transfers between devices: 102 us -> 137 us  [exchange(): return lax.ppermute(value, axis, [(i, i ^ bit) for i in range(count)])]
    all_gather x1, waiting for transfers between devices: 0.01 us -> 30.9 us  [shards(): down_wide = lax.all_gather(ffn_down_weight, 'rows', axis=0, tiled=True)]
    convert_element_type x22 -> x0, local copies, waits for them, and re-layouts: 30.8 us -> none  [the longest x18 25.9 us: from_owner(): return split.transpose(1, 2, 0, 3).reshape(share, -1).astype(F32)]
    another operation x25 -> x18, other arithmetic: 34.1 us -> 11.6 us
  transfers between devices with their start and end apart: 56 -> 64, of which waited for: 23 -> 40; matrix products, arithmetic and copies ran while one was open for 40% -> 36% of each run, Pallas kernels for 4% -> 6%
where the time goes in v2:
time: 661 us; the launch traced here: 660 us
  waiting for transfers between devices  208 us (31%)
  matrix products  107 us (16%)
  local copies, waits for them, and re-layouts  90.7 us (14%)
  other arithmetic  80.7 us (12%)
  starting transfers between devices  71.7 us (11%)
  Pallas kernels  43.7 us (7%)
  blocking collectives  40.5 us (6%)
  between operations  15.5 us (2%)
    ppermute x50, waiting for transfers between devices, exchange(): return lax.ppermute(value, axis, [(i, i ^ bit) for i in range(count)])  137 us
    ppermute x50, starting transfers between devices, exchange(): return lax.ppermute(value, axis, [(i, i ^ bit) for i in range(count)])  49.6 us
    psum x2, blocking collectives, feature_mean(): total = lax.psum(jnp.take(sums, slots, axis=1), 'seq') / model  40.5 us
    dot_general x6, matrix products, token_grad(): return lax.dot_general(left, right, TN, preferred_element_type=F32)  37.2 us
    all_gather x1, waiting for transfers between devices, shards(): down_wide = lax.all_gather(ffn_down_weight, 'rows', axis=0, tiled=True)  30.9 us
    unnamed x111, local copies, waits for them, and re-layouts  29.2 us
    pallas_call x1, Pallas kernels, inner_backward(): pl.pallas_call(functools.partial(backward_kernel, heads, head_dim, parts)...  20.8 us
    all_gather x1, waiting for transfers between devices, shards(): ffn_wide = lax.all_gather(ffn_cut, 'rows', axis=0, tiled=True)  18.9 us
  transfers between devices with their start and end apart: 64, of which 40 were waited for; matrix products, arithmetic and copies ran while one was open for 36% of the time, Pallas kernels for 6%

profile of v2, /device:TPU:0, one launch (start us, length us, event | category | flops | bytes accessed | tf_op | source)
XLA Modules:
  0.0 659.6 jit_solution(8426716277358364814)
XLA Ops:
  12.6 5.2 all-to-all-start.3
  25.5 7.7 %all-to-all-done.3 = bf16[8,64,1024]{2,1,0:T(8,128)(2,1)S(1)} async-done(((bf16[8,64,1024]{2,1,0:T(8,128)(2,1)}), bf16[8,64,1024]{2,1,0:T(8,128)(2,1)S(1)}, u32[]{:S(2)}, u32[]{:S(2)}) %all-to-all-start.3) | async-done | bytes 1048608 | tf_op jit(solution)/shard_map/all_to_all | solution.py:472
  38.7 70.0 %conditional.4 = (bf16[1024,2048]{1,0:T(8,128)(2,1)}, bf16[2048,128]{1,0:T(8,128)(2,1)S(1)}, bf16[512,1376]{1,0:T(8,128)(2,1)}, f32[1024,2048]{1,0:T(8,128)}, f32[1024,1]{0,1:T(1,128)S(1)}) conditional(s32[]{:T(128)} %convert_element_type.311, () %tuple.60, (bf16[128,2048]{1,0:T(8,128)(2,1)S(1)}, bf16[64,128]{1,0:T(8,128)(2,1)S(1)}, ...), branch_computations={%region_1.2_spmd, %region_2.4_spmd} | conditional | flops 105102336 | bytes 90346512 | solution.py:501
  57.5 9.1 %collective-permute-done.3 = bf16[2,128,1024]{2,1,0:T(8,128)(2,1)S(1)} collective-permute-done((bf16[2,128,1024]{2,1,0:T(8,128)(2,1)S(1)}, bf16[2,128,1024]{2,1,0:T(8,128)(2,1)S(1)}, u32[]{:S(2)}, u32[]{:S(2)}) %collective-permute-start.3) | collective-permute-done | bytes 524320 | tf_op jit(solution)/shard_map/cond/branch_1_fun/ppermute | solution.py:354
  69.3 6.1 collective-permute-done.13
  79.4 5.0 collective-permute-done.8
  84.9 4.3 all-to-all-start
  89.2 3.6 collective-permute-done.9
  95.0 3.5 pad_maximum_fusion
  98.6 6.2 multiply_reduce_fusion
  104.8 4.0 all-to-all-done
  112.5 7.7 %multiply_convert_fusion.1 = (bf16[1024,2048]{1,0:T(8,128)(2,1)S(1)}, f32[1024,2048]{1,0:T(8,128)}) fusion(f32[2048]{0:T(1024)S(1)} %bitcast.261, f32[1024,2048]{1,0:T(8,128)} %get-tuple-element.234, f32[1024]{0:T(1024)S(1)} %bitcast.271), kind=kLoop, calls=%fused_computation.152 | loop fusion | flops 6291456 | bytes 20983808 | tf_op jit(solution)/shard_map/convert_element_type | solution.py:574
  125.4 6.1 fusion.37
  131.8 15.3 %inner_forward.1 = (f32[1024,256]{1,0:T(8,128)S(1)}, f32[8,4,64,128]{3,2,1,0:T(8,128)S(1)}, f32[8,4,128]{2,1,0:T(4,128)S(1)}, f32[8,4,64,128]{3,2,1,0:T(8,128)S(...) custom-call(s32[1]{0:T(128)} %bitcast.60.slot_ref, ...), custom_call_target="tpu_custom_call" | custom-call | tf_op jit(solution)/shard_map/inner_forward/pallas_call | solution.py:251
  155.0 12.6 %psum.14 = f32[2,8,128]{2,0,1:T(2,128)S(1)} all-reduce(f32[2,8,128]{2,0,1:T(2,128)S(1)} %select_bitcast_fusion.3), channel_id=1, replica_groups=mesh['rows'=4,'seq'=8] {'seq'}, use_global_device_ids=true, to_apply=%region_7.10 | all-reduce | flops 2048 | bytes 16384 | tf_op jit(solution)/shard_map/psum | solution.py:607
  168.3 5.2 multiply_convert_fusion.5
  173.5 59.2 %conditional.5 = (f32[128,2048]{1,0:T(8,128)}, bf16[1024,2048]{1,0:T(8,128)(2,1)}) conditional(s32[]{:T(128)} %convert_element_type.311, () %tuple.59, (bf16[128,2048]{1,0:T(8,128)(2,1)}, bf16[1024,256]{1,0:T(8,128)(2,1)}, bf16[256,2048]{1,0:T(8,128)(2,1)}, f32[2048]{0:T(1024)S(1)}) %tuple.194), branch_computations={%region_8.11_spmd, %region_9.13_spmd} | conditional | flops 1130889344 | bytes 82323904 | solution.py:501
  182.9 12.4 %collective-permute-done.16 = bf16[2,128,1024]{2,1,0:T(8,128)(2,1)S(1)} collective-permute-done((bf16[2,128,1024]{2,1,0:T(8,128)(2,1)S(1)}, bf16[2,128,1024]{2,1,0:T(8,128)(2,1)S(1)}, u32[]{:S(2)}, u32[]{:S(2)}) %collective-permute-start.16) | collective-permute-done | bytes 524320 | tf_op jit(solution)/shard_map/cond/branch_1_fun/ppermute | solution.py:354
  198.8 4.4 collective-permute-done.17
  209.2 4.7 collective-permute-done.22
  216.9 8.6 %collective-permute-done.23 = bf16[2,128,1024]{2,1,0:T(8,128)(2,1)S(1)} collective-permute-done((bf16[2,128,1024]{2,1,0:T(8,128)(2,1)S(1)}, bf16[2,128,1024]{2,1,0:T(8,128)(2,1)S(1)}, u32[]{:S(2)}, u32[]{:S(2)}) %collective-permute-start.23) | collective-permute-done | bytes 524320 | tf_op jit(solution)/shard_map/cond/branch_1_fun/ppermute | solution.py:354
  226.4 4.1 collective-permute-done.24
  232.7 18.9 %all-gather.10.cloned.1.call-done = bf16[2048,1376]{1,0:T(8,128)(2,1)} async-done(((bf16[512,1376]{1,0:T(8,128)(2,1)}), bf16[2048,1376]{1,0:T(8,128)(2,1)}) %all-gather.10.cloned.1.call-update) | async-done | bytes 5636112 | tf_op jit(solution)/shard_map/all_gather | solution.py:532
  251.6 10.0 %fusion.85 = f32[1024,1376]{0,1:T(8,128)S(1)} fusion(bf16[1024,2048]{1,0:T(8,128)(2,1)} %get-tuple-element.242, bf16[2048,1376]{1,0:T(8,128)(2,1)} %all-gather.10.cloned.1.call-done), kind=kOutput, calls=%fused_computation.277 | convolution fusion | flops 5771362304 | bytes 15466496 | tf_op jit(solution)/shard_map/dot_general | solution.py:635
  266.1 6.6 convolution_convert_fusion.5
  272.7 3.2 reshape.447
  275.9 3.8 pad.13
  279.7 30.9 %all-gather.12.cloned.1.call-done = bf16[4,172,2048]{2,1,0:T(8,128)(2,1)} async-done(((bf16[1,172,2048]{2,1,0:T(8,128)(2,1)}), bf16[4,172,2048]{2,1,0:T(8,128)(2,1)}) %all-gather.12.cloned.1.call-update) | async-done | bytes 2818064 | tf_op jit(solution)/shard_map/all_gather | solution.py:582
  310.6 3.2 reshape.521
  314.3 8.8 %multiply_convert_fusion.3 = (bf16[1024,688]{0,1:T(8,128)(2,1)S(1)}, bf16[1024,688]{0,1:T(8,128)(2,1)S(1)}) fusion(f32[1024,1376]{0,1:T(8,128)} %copy-done.27, bf16[1024,2048]{1,0:T(8,128)(2,1)} %get-tuple-element.241, bf16[688,2048]{1,0:T(8,128)(2,1)} %reshape.521), kind=kOutput, calls=%fused_computation.161 | convolution fusion | flops 2894839808 | bytes 15466496 | tf_op jit(solution)/shard_map/dot_general | solution.py:648
  324.8 11.2 %convolution_convert_fusion.3 = bf16[2048,1376]{0,1:T(8,128)(2,1)} fusion(bf16[1024,2048]{1,0:T(8,128)(2,1)} %get-tuple-element.242, bf16[1024,688]{0,1:T(8,128)(2,1)S(1)} %get-tuple-element.624, bf16[1024,688]{0,1:T(8,128)(2,1)S(1)} %get-tuple-element.623), kind=kOutput, calls=%fused_computation.153 | convolution fusion | flops 5779816448 | bytes 12648448 | tf_op jit(solution)/shard_map/dot_general | solution.py:641
  336.2 96.4 %conditional.6 = (f32[128,2048]{1,0:T(8,128)}, bf16[1024,2048]{1,0:T(8,128)(2,1)S(1)}, f32[128,2048]{1,0:T(8,128)}, f32[2048,1]{0,1:T(1,128)S(1)}) conditional(s32[]{:T(128)} %convert_element_type.311, () %tuple.57, (bf16[128,2048]{1,0:T(8,128)(2,1)}, f32[128,2048]{1,0:T(8,128)}, bf16[1024,1376]{0,1:T(8,128)(2,1)}, bf16[2048,1376]{1,0:T(8,128)(2,1)}, ...), branch_computations={%region_11.14_spmd, %region_12.18_spmd} | conditional | flops 8723625984 | bytes 185039008 | solution.py:501
  336.3 4.6 copy.243
  341.0 7.9 %convolution_convert_fusion.2 = bf16[512,2048]{1,0:T(8,128)(2,1)} fusion(bf16[2048,1376]{1,0:T(8,128)(2,1)} %get-tuple-element.120, bf16[1024,1376]{1,0:T(8,128)(2,1)} %copy.243), kind=kOutput, calls=%fused_computation.65 | convolution fusion | flops 2886729728 | bytes 9306112 | tf_op jit(solution)/shard_map/cond/branch_1_fun/dot_general | solution.py:620
  351.4 4.0 convolution_convert_fusion.1
  357.8 5.7 fusion.10
  373.3 8.0 %collective-permute-done.26 = bf16[2,128,1024]{2,1,0:T(8,128)(2,1)S(1)} collective-permute-done((bf16[2,128,1024]{2,1,0:T(8,128)(2,1)S(1)}, bf16[2,128,1024]{2,1,0:T(8,128)(2,1)S(1)}, u32[]{:S(2)}, u32[]{:S(2)}) %collective-permute-start.26) | collective-permute-done | bytes 524320 | tf_op jit(solution)/shard_map/cond/branch_1_fun/ppermute | solution.py:354
  384.7 7.8 %collective-permute-done.36 = bf16[2,128,1024]{2,1,0:T(8,128)(2,1)S(1)} collective-permute-done((bf16[2,128,1024]{2,1,0:T(8,128)(2,1)S(1)}, bf16[2,128,1024]{2,1,0:T(8,128)(2,1)S(1)}, u32[]{:S(2)}, u32[]{:S(2)}) %collective-permute-start.36) | collective-permute-done | bytes 524320 | tf_op jit(solution)/shard_map/cond/branch_1_fun/ppermute | solution.py:354
  396.0 3.4 collective-permute-done.27
  409.2 5.2 collective-permute-done.32
  416.7 10.1 %collective-permute-done.33 = bf16[2,128,1024]{2,1,0:T(8,128)(2,1)S(1)} collective-permute-done((bf16[2,128,1024]{2,1,0:T(8,128)(2,1)S(1)}, bf16[2,128,1024]{2,1,0:T(8,128)(2,1)S(1)}, u32[]{:S(2)}, u32[]{:S(2)}) %collective-permute-start.33) | collective-permute-done | bytes 524320 | tf_op jit(solution)/shard_map/cond/branch_1_fun/ppermute | solution.py:354
  427.7 4.1 collective-permute-done.34
  434.5 3.5 fusion.86
  440.6 3.2 fusion.48
  443.8 4.6 convolution_convert_fusion.7
  448.4 4.6 convolution_convert_fusion.6
  455.6 3.7 multiply_reduce_fusion.6
  460.1 27.9 %psum.15 = f32[2,8,128]{2,0,1:T(2,128)S(1)} all-reduce(f32[2,8,128]{2,0,1:T(2,128)S(1)} %select_bitcast_fusion.1), channel_id=1, replica_groups=mesh['rows'=4,'seq'=8] {'seq'}, use_global_device_ids=true, to_apply=%region_18.21 | all-reduce | flops 2048 | bytes 16384 | tf_op jit(solution)/shard_map/psum | solution.py:607
  504.9 20.8 %inner_backward.1 = (bf16[1024,256]{1,0:T(8,128)(2,1)S(1)}, bf16[1024,256]{1,0:T(8,128)(2,1)S(1)}, bf16[1024,256]{1,0:T(8,128)(2,1)S(1)}, f32[8,4,128]{2,1,0:T(4...) custom-call(s32[1]{0:T(128)} %bitcast.60.slot_ref, ...), custom_call_target="tpu_custom_call" | custom-call | tf_op jit(solution)/shard_map/inner_backward/pallas_call | solution.py:282
  528.2 7.4 %convolution_convert_fusion.4 = bf16[2048,768]{1,0:T(8,128)(2,1)} fusion(bf16[1024,2048]{1,0:T(8,128)(2,1)} %copy-done.22, bf16[1024,768]{1,0:T(8,128)(2,1)S(1)} %pad_maximum_fusion.23), kind=kOutput, calls=%fused_computation.155 | convolution fusion | flops 3222798336 | bytes 8912896 | tf_op jit(solution)/shard_map/dot_general | solution.py:641
  541.5 93.9 %conditional.7 = (f32[128,2048]{1,0:T(8,128)}, f32[64,128]{1,0:T(8,128)}, f32[64,5504]{1,0:T(8,128)}, f32[64,5504]{1,0:T(8,128)}, f32[64,2048]{1,0:T(8,128)}, /*...) conditional(s32[]{:T(128)} %convert_element_type.311, () %tuple.67, ...), branch_computations={%region_28.31_spmd, %region_29.35_spmd} | conditional | flops 4330277888 | bytes 138425792 | solution.py:501
  543.7 7.1 %fusion.84 = f32[1024,2048]{1,0:T(8,128)S(1)} fusion(bf16[1024,1024]{1,0:T(8,128)(2,1)} %get-tuple-element.126, bf16[2048,1024]{1,0:T(8,128)(2,1)} %get-tuple-element.127), kind=kOutput, calls=%fused_computation.276 | convolution fusion | flops 4294967296 | bytes 14680064 | tf_op jit(solution)/shard_map/cond/branch_1_fun/dot_general | solution.py:715
  550.9 4.6 multiply_reduce_fusion.5
  560.3 3.9 slice.681
  564.2 7.7 %collective-permute-done.45 = f32[4,4,64,128]{3,2,1,0:T(8,128)S(1)} collective-permute-done((f32[4,4,64,128]{3,2,1,0:T(8,128)S(1)}, f32[4,4,64,128]{3,2,1,0:T(8,128)S(1)}, u32[]{:S(2)}, u32[]{:S(2)}) %collective-permute-start.45) | collective-permute-done | bytes 524320 | tf_op jit(solution)/shard_map/cond/branch_1_fun/ppermute | solution.py:354
  572.7 5.8 collective-permute-done.46
  578.7 4.5 all-to-all-start.2
  583.2 4.8 slice.489
  588.0 6.1 fusion.70
  597.9 3.6 all-to-all-start.1
  604.2 4.9 collective-permute-done.41
  614.2 4.4 collective-permute-start.44
  635.4 3.5 all-to-all-start.4
  645.2 6.3 all-to-all-done.4.parts_ref
  (465 shorter events, 206.4 us)
Async XLA Ops:
  12.6 20.6 %all-to-all-start.3 = ((bf16[8,64,1024]{2,1,0:T(8,128)(2,1)}), bf16[8,64,1024]{2,1,0:T(8,128)(2,1)S(1)}, u32[]{:S(2)}, u32[]{:S(2)}) async-start(bf16[8,64,1024]{2,1,0:T(8,128)(2,1)} %cut_heads.2), calls=%async_computation.3 | async-start | bytes 2097152 | tf_op jit(solution)/shard_map/all_to_all | solution.py:472
  17.8 107.6 %all-gather.6.cloned.1.call-start = ((), (), s32[]{:S(2)}) async-start(), calls=%async_computation.10 | async-start | bytes 5242880 | tf_op jit(solution)/shard_map/all_gather | solution.py:519
  34.2 139.4 %all-gather.8.cloned.1.call-start = ((), (), s32[]{:S(2)}) async-start(), calls=%async_computation.11 | async-start | bytes 1310720 | tf_op jit(solution)/shard_map/all_gather | solution.py:510
  34.9 216.7 %all-gather.10.cloned.1.call-start = ((), (), s32[]{:S(2)}) async-start(), calls=%async_computation.12 | async-start | bytes 7208960 | tf_op jit(solution)/shard_map/all_gather | solution.py:532
  38.7 5.9 collective-permute-start.5
  40.4 11.5 %collective-permute-start = (bf16[1,128,1024]{2,1,0:T(8,128)(2,1)S(1)}, bf16[1,128,1024]{2,1,0:T(8,128)(2,1)S(1)}, u32[]{:S(2)}, u32[]{:S(2)}) collective-permute-start(bf16[1,128,1024]{2,1,0:T(8,128)(2,1)S(1)} %get-tuple-element.560), channel_id=1, source_target_pairs={{0,2},{1,3},{2,0},{3,1},{4,6},{5,7},{6,4},{7,5},{8,10},{9,11},{10,... | collective-permute-start | bytes 786440 | tf_op jit(solution)/shard_map/cond/branch_1_fun/ppermute | solution.py:354
  41.0 9.2 %collective-permute-start.2 = (bf16[1,128,1024]{2,1,0:T(8,128)(2,1)S(1)}, bf16[1,128,1024]{2,1,0:T(8,128)(2,1)S(1)}, u32[]{:S(2)}, u32[]{:S(2)}) collective-permute-start(bf16[1,128,1024]{2,1,0:T(8,128)(2,1)S(1)} %get-tuple-element.561), channel_id=1, source_target_pairs={{0,4},{1,5},{2,6},{3,7},{4,0},{5,1},{6,2},{7,3},{8,12},{9,13},{10,... | collective-permute-start | bytes 786440 | tf_op jit(solution)/shard_map/cond/branch_1_fun/ppermute | solution.py:354
  41.7 13.7 %collective-permute-start.10 = (bf16[1,128,1024]{2,1,0:T(8,128)(2,1)S(1)}, bf16[1,128,1024]{2,1,0:T(8,128)(2,1)S(1)}, u32[]{:S(2)}, u32[]{:S(2)}) collective-permute-start(bf16[1,128,1024]{2,1,0:T(8,128)(2,1)S(1)} %get-tuple-element.554), channel_id=1, source_target_pairs={{0,2},{1,3},{2,0},{3,1},{4,6},{5,7},{6,4},{7,5},{8,10},{9,11},{10,... | collective-permute-start | bytes 786440 | tf_op jit(solution)/shard_map/cond/branch_1_fun/ppermute | solution.py:354
  43.2 12.8 %collective-permute-start.12 = (bf16[1,128,1024]{2,1,0:T(8,128)(2,1)S(1)}, bf16[1,128,1024]{2,1,0:T(8,128)(2,1)S(1)}, u32[]{:S(2)}, u32[]{:S(2)}) collective-permute-start(bf16[1,128,1024]{2,1,0:T(8,128)(2,1)S(1)} %get-tuple-element.555), channel_id=1, source_target_pairs={{0,4},{1,5},{2,6},{3,7},{4,0},{5,1},{6,2},{7,3},{8,12},{9,13},{10,... | collective-permute-start | bytes 786440 | tf_op jit(solution)/shard_map/cond/branch_1_fun/ppermute | solution.py:354
  44.7 7.8 %collective-permute-start.6 = (bf16[128,128]{1,0:T(8,128)(2,1)S(1)}, bf16[128,128]{1,0:T(8,128)(2,1)S(1)}, u32[]{:S(2)}, u32[]{:S(2)}) collective-permute-start(bf16[128,128]{1,0:T(8,128)(2,1)S(1)} %pad_maximum_fusion.9), channel_id=1, source_target_pairs={{0,16},{8,24},{16,0},{24,8},{1,17},{9,25},{17,1},{25,9},{2,18},{10... | collective-permute-start | bytes 98312 | tf_op jit(solution)/shard_map/cond/branch_1_fun/ppermute | solution.py:354
  50.3 16.3 %collective-permute-start.3 = (bf16[2,128,1024]{2,1,0:T(8,128)(2,1)S(1)}, bf16[2,128,1024]{2,1,0:T(8,128)(2,1)S(1)}, u32[]{:S(2)}, u32[]{:S(2)}) collective-permute-start(bf16[2,128,1024]{2,1,0:T(8,128)(2,1)S(1)} %pad_maximum_fusion.2), channel_id=1, source_target_pairs={{0,2},{1,3},{2,0},{3,1},{4,6},{5,7},{6,4},{7,5},{8,10},{9,11},{10,... | collective-permute-start | bytes 1572872 | tf_op jit(solution)/shard_map/cond/branch_1_fun/ppermute | solution.py:354
  51.9 15.2 %collective-permute-start.1 = (bf16[2,128,1024]{2,1,0:T(8,128)(2,1)S(1)}, bf16[2,128,1024]{2,1,0:T(8,128)(2,1)S(1)}, u32[]{:S(2)}, u32[]{:S(2)}) collective-permute-start(bf16[2,128,1024]{2,1,0:T(8,128)(2,1)S(1)} %pad_maximum_fusion.1), channel_id=1, source_target_pairs={{0,4},{1,5},{2,6},{3,7},{4,0},{5,1},{6,2},{7,3},{8,12},{9,13},{10,... | collective-permute-start | bytes 1572872 | tf_op jit(solution)/shard_map/cond/branch_1_fun/ppermute | solution.py:354
  55.4 21.4 %collective-permute-start.11 = (bf16[2,128,1024]{2,1,0:T(8,128)(2,1)S(1)}, bf16[2,128,1024]{2,1,0:T(8,128)(2,1)S(1)}, u32[]{:S(2)}, u32[]{:S(2)}) collective-permute-start(bf16[2,128,1024]{2,1,0:T(8,128)(2,1)S(1)} %pad_maximum_fusion.4), channel_id=1, source_target_pairs={{0,4},{1,5},{2,6},{3,7},{4,0},{5,1},{6,2},{7,3},{8,12},{9,13},{10,... | collective-permute-start | bytes 1572872 | tf_op jit(solution)/shard_map/cond/branch_1_fun/ppermute | solution.py:354
  56.1 19.3 %collective-permute-start.13 = (bf16[2,128,1024]{2,1,0:T(8,128)(2,1)S(1)}, bf16[2,128,1024]{2,1,0:T(8,128)(2,1)S(1)}, u32[]{:S(2)}, u32[]{:S(2)}) collective-permute-start(bf16[2,128,1024]{2,1,0:T(8,128)(2,1)S(1)} %pad_maximum_fusion.5), channel_id=1, source_target_pairs={{0,2},{1,3},{2,0},{3,1},{4,6},{5,7},{6,4},{7,5},{8,10},{9,11},{10,... | collective-permute-start | bytes 1572872 | tf_op jit(solution)/shard_map/cond/branch_1_fun/ppermute | solution.py:354
  68.6 26.4 %collective-permute-start.4 = (bf16[4,128,2048]{2,1,0:T(8,128)(2,1)}, bf16[4,128,2048]{2,1,0:T(8,128)(2,1)}, u32[]{:S(2)}, u32[]{:S(2)}) collective-permute-start(bf16[4,128,2048]{2,1,0:T(8,128)(2,1)} %maximum_maximum_fusion), channel_id=1, source_target_pairs={{0,1},{1,0},{2,3},{3,2},{4,5},{5,4},{6,7},{7,6},{8,9},{9,8},{10,11... | collective-permute-start | bytes 6291464 | tf_op jit(solution)/shard_map/cond/branch_1_fun/ppermute | solution.py:354
  68.7 9.6 %collective-permute-start.7 = (bf16[64,512]{1,0:T(8,128)(2,1)S(1)}, bf16[64,512]{1,0:T(8,128)(2,1)S(1)}, u32[]{:S(2)}, u32[]{:S(2)}) collective-permute-start(bf16[64,512]{1,0:T(8,128)(2,1)S(1)} %bitcast.259), channel_id=1, source_target_pairs={{0,1},{1,0},{2,3},{3,2},{4,5},{5,4},{6,7},{7,6},{8,9},{9,8},{10,11... | collective-permute-start | bytes 196616 | tf_op jit(solution)/shard_map/cond/branch_1_fun/ppermute | solution.py:354
  78.3 20.2 %collective-permute-start.14 = (bf16[4,128,2048]{2,1,0:T(8,128)(2,1)}, bf16[4,128,2048]{2,1,0:T(8,128)(2,1)}, u32[]{:S(2)}, u32[]{:S(2)}) collective-permute-start(bf16[4,128,2048]{2,1,0:T(8,128)(2,1)} %maximum_maximum_fusion.1), channel_id=1, source_target_pairs={{0,1},{1,0},{2,3},{3,2},{4,5},{5,4},{6,7},{7,6},{8,9},{9,8},{10,11... | collective-permute-start | bytes 6291464 | tf_op jit(solution)/shard_map/cond/branch_1_fun/ppermute | solution.py:354
  78.4 6.0 collective-permute-start.8
  84.4 8.3 %collective-permute-start.9 = (bf16[256,512]{1,0:T(8,128)(2,1)S(1)}, bf16[256,512]{1,0:T(8,128)(2,1)S(1)}, u32[]{:S(2)}, u32[]{:S(2)}) collective-permute-start(bf16[256,512]{1,0:T(8,128)(2,1)S(1)} %pad_maximum_fusion.6), channel_id=1, source_target_pairs={{0,4},{1,5},{2,6},{3,7},{4,0},{5,1},{6,2},{7,3},{8,12},{9,13},{10,... | collective-permute-start | bytes 786440 | tf_op jit(solution)/shard_map/cond/branch_1_fun/ppermute | solution.py:354
  84.9 23.9 %all-to-all-start = ((bf16[8,64,1376]{2,1,0:T(8,128)(2,1)}), bf16[8,64,1376]{2,1,0:T(8,128)(2,1)}, u32[]{:S(2)}, u32[]{:S(2)}) async-start(bf16[8,64,1376]{2,1,0:T(8,128)(2,1)} %get-tuple-element.111), calls=%async_computation | async-start | bytes 2883584 | tf_op jit(solution)/shard_map/cond/branch_1_fun/all_to_all | solution.py:472
  108.8 201.8 %all-gather.12.cloned.1.call-start = ((), (), s32[]{:S(2)}) async-start(), calls=%async_computation.18 | async-start | bytes 3604480 | tf_op jit(solution)/shard_map/all_gather | solution.py:582
  167.6 323.8 %reduce-scatter.8.cloned.1.call-start = ((), (), s32[]{:S(2)}) async-start(), calls=%async_computation.14 | async-start | bytes 3604480 | tf_op jit(solution)/shard_map/reduce_scatter | solution.py:646
  175.8 4.2 collective-permute-start.15
  181.3 14.0 %collective-permute-start.16 = (bf16[2,128,1024]{2,1,0:T(8,128)(2,1)S(1)}, bf16[2,128,1024]{2,1,0:T(8,128)(2,1)S(1)}, u32[]{:S(2)}, u32[]{:S(2)}) collective-permute-start(bf16[2,128,1024]{2,1,0:T(8,128)(2,1)S(1)} %pad_maximum_fusion.11), channel_id=1, source_target_pairs={{0,2},{1,3},{2,0},{3,1},{4,6},{5,7},{6,4},{7,5},{8,10},{9,11},{10,... | collective-permute-start | bytes 1572872 | tf_op jit(solution)/shard_map/cond/branch_1_fun/ppermute | solution.py:354
  181.4 14.0 %collective-permute-start.18 = (bf16[2,128,1024]{2,1,0:T(8,128)(2,1)S(1)}, bf16[2,128,1024]{2,1,0:T(8,128)(2,1)S(1)}, u32[]{:S(2)}, u32[]{:S(2)}) collective-permute-start(bf16[2,128,1024]{2,1,0:T(8,128)(2,1)S(1)} %slice.451), channel_id=1, source_target_pairs={{0,4},{1,5},{2,6},{3,7},{4,0},{5,1},{6,2},{7,3},{8,12},{9,13},{10,... | collective-permute-start | bytes 1572872 | tf_op jit(solution)/shard_map/cond/branch_1_fun/ppermute | solution.py:354
  195.6 7.7 %collective-permute-start.17 = (bf16[1,128,1024]{2,1,0:T(8,128)(2,1)S(1)}, bf16[1,128,1024]{2,1,0:T(8,128)(2,1)S(1)}, u32[]{:S(2)}, u32[]{:S(2)}) collective-permute-start(bf16[1,128,1024]{2,1,0:T(8,128)(2,1)S(1)} %get-tuple-element.574), channel_id=1, source_target_pairs={{0,4},{1,5},{2,6},{3,7},{4,0},{5,1},{6,2},{7,3},{8,12},{9,13},{10,... | collective-permute-start | bytes 786440 | tf_op jit(solution)/shard_map/cond/branch_1_fun/ppermute | solution.py:354
  197.1 7.3 %collective-permute-start.19 = (bf16[1,128,1024]{2,1,0:T(8,128)(2,1)S(1)}, bf16[1,128,1024]{2,1,0:T(8,128)(2,1)S(1)}, u32[]{:S(2)}, u32[]{:S(2)}) collective-permute-start(bf16[1,128,1024]{2,1,0:T(8,128)(2,1)S(1)} %get-tuple-element.575), channel_id=1, source_target_pairs={{0,2},{1,3},{2,0},{3,1},{4,6},{5,7},{6,4},{7,5},{8,10},{9,11},{10,... | collective-permute-start | bytes 786440 | tf_op jit(solution)/shard_map/cond/branch_1_fun/ppermute | solution.py:354
  207.3 6.6 collective-permute-start.22
  207.9 7.3 %collective-permute-start.20 = (bf16[1,128,1024]{2,1,0:T(8,128)(2,1)S(1)}, bf16[1,128,1024]{2,1,0:T(8,128)(2,1)S(1)}, u32[]{:S(2)}, u32[]{:S(2)}) collective-permute-start(bf16[1,128,1024]{2,1,0:T(8,128)(2,1)S(1)} %get-tuple-element.578), channel_id=1, source_target_pairs={{0,2},{1,3},{2,0},{3,1},{4,6},{5,7},{6,4},{7,5},{8,10},{9,11},{10,... | collective-permute-start | bytes 786440 | tf_op jit(solution)/shard_map/cond/branch_1_fun/ppermute | solution.py:354
  214.0 11.5 %collective-permute-start.23 = (bf16[2,128,1024]{2,1,0:T(8,128)(2,1)S(1)}, bf16[2,128,1024]{2,1,0:T(8,128)(2,1)S(1)}, u32[]{:S(2)}, u32[]{:S(2)}) collective-permute-start(bf16[2,128,1024]{2,1,0:T(8,128)(2,1)S(1)} %pad_maximum_fusion.13), channel_id=1, source_target_pairs={{0,2},{1,3},{2,0},{3,1},{4,6},{5,7},{6,4},{7,5},{8,10},{9,11},{10,... | collective-permute-start | bytes 1572872 | tf_op jit(solution)/shard_map/cond/branch_1_fun/ppermute | solution.py:354
  215.3 10.8 %collective-permute-start.21 = (bf16[2,128,1024]{2,1,0:T(8,128)(2,1)S(1)}, bf16[2,128,1024]{2,1,0:T(8,128)(2,1)S(1)}, u32[]{:S(2)}, u32[]{:S(2)}) collective-permute-start(bf16[2,128,1024]{2,1,0:T(8,128)(2,1)S(1)} %pad_maximum_fusion.12), channel_id=1, source_target_pairs={{0,4},{1,5},{2,6},{3,7},{4,0},{5,1},{6,2},{7,3},{8,12},{9,13},{10,... | collective-permute-start | bytes 1572872 | tf_op jit(solution)/shard_map/cond/branch_1_fun/ppermute | solution.py:354
  226.3 4.2 collective-permute-start.24
  313.8 180.1 %reduce-scatter.6.cloned.1.call-start = ((), (), s32[]{:S(2)}) async-start(), calls=%async_computation.13 | async-start | bytes 7045120 | tf_op jit(solution)/shard_map/reduce_scatter | solution.py:475
  336.1 190.3 %reduce-scatter.10.cloned.1.call-start = ((), (), s32[]{:S(2)}) async-start(), calls=%async_computation.15 | async-start | bytes 1310720 | tf_op jit(solution)/shard_map/reduce_scatter | solution.py:475
  348.9 14.7 %collective-permute-start.25 = (bf16[4,128,2048]{2,1,0:T(8,128)(2,1)}, bf16[4,128,2048]{2,1,0:T(8,128)(2,1)}, u32[]{:S(2)}, u32[]{:S(2)}) collective-permute-start(bf16[4,128,2048]{2,1,0:T(8,128)(2,1)} %bitcast.20), channel_id=1, source_target_pairs={{0,1},{1,0},{2,3},{3,2},{4,5},{5,4},{6,7},{7,6},{8,9},{9,8},{10,11... | collective-permute-start | bytes 6291464 | tf_op jit(solution)/shard_map/cond/branch_1_fun/ppermute | solution.py:354
  355.4 13.7 %collective-permute-start.35 = (bf16[4,128,2048]{2,1,0:T(8,128)(2,1)S(1)}, bf16[4,128,2048]{2,1,0:T(8,128)(2,1)S(1)}, u32[]{:S(2)}, u32[]{:S(2)}) collective-permute-start(bf16[4,128,2048]{2,1,0:T(8,128)(2,1)S(1)} %bitcast.282), channel_id=1, source_target_pairs={{0,1},{1,0},{2,3},{3,2},{4,5},{5,4},{6,7},{7,6},{8,9},{9,8},{10,11... | collective-permute-start | bytes 6291464 | tf_op jit(solution)/shard_map/cond/branch_1_fun/ppermute | solution.py:354
  366.4 14.8 %collective-permute-start.26 = (bf16[2,128,1024]{2,1,0:T(8,128)(2,1)S(1)}, bf16[2,128,1024]{2,1,0:T(8,128)(2,1)S(1)}, u32[]{:S(2)}, u32[]{:S(2)}) collective-permute-start(bf16[2,128,1024]{2,1,0:T(8,128)(2,1)S(1)} %pad_maximum_fusion.16), channel_id=1, source_target_pairs={{0,2},{1,3},{2,0},{3,1},{4,6},{5,7},{6,4},{7,5},{8,10},{9,11},{10,... | collective-permute-start | bytes 1572872 | tf_op jit(solution)/shard_map/cond/branch_1_fun/ppermute | solution.py:354
  367.7 14.8 %collective-permute-start.28 = (bf16[2,128,1024]{2,1,0:T(8,128)(2,1)S(1)}, bf16[2,128,1024]{2,1,0:T(8,128)(2,1)S(1)}, u32[]{:S(2)}, u32[]{:S(2)}) collective-permute-start(bf16[2,128,1024]{2,1,0:T(8,128)(2,1)S(1)} %slice.468), channel_id=1, source_target_pairs={{0,4},{1,5},{2,6},{3,7},{4,0},{5,1},{6,2},{7,3},{8,12},{9,13},{10,... | collective-permute-start | bytes 1572872 | tf_op jit(solution)/shard_map/cond/branch_1_fun/ppermute | solution.py:354
  370.4 22.1 %collective-permute-start.36 = (bf16[2,128,1024]{2,1,0:T(8,128)(2,1)S(1)}, bf16[2,128,1024]{2,1,0:T(8,128)(2,1)S(1)}, u32[]{:S(2)}, u32[]{:S(2)}) collective-permute-start(bf16[2,128,1024]{2,1,0:T(8,128)(2,1)S(1)} %pad_maximum_fusion.19), channel_id=1, source_target_pairs={{0,2},{1,3},{2,0},{3,1},{4,6},{5,7},{6,4},{7,5},{8,10},{9,11},{10,... | collective-permute-start | bytes 1572872 | tf_op jit(solution)/shard_map/cond/branch_1_fun/ppermute | solution.py:354
  371.0 22.7 %collective-permute-start.38 = (bf16[2,128,1024]{2,1,0:T(8,128)(2,1)S(1)}, bf16[2,128,1024]{2,1,0:T(8,128)(2,1)S(1)}, u32[]{:S(2)}, u32[]{:S(2)}) collective-permute-start(bf16[2,128,1024]{2,1,0:T(8,128)(2,1)S(1)} %slice.485), channel_id=1, source_target_pairs={{0,4},{1,5},{2,6},{3,7},{4,0},{5,1},{6,2},{7,3},{8,12},{9,13},{10,... | collective-permute-start | bytes 1572872 | tf_op jit(solution)/shard_map/cond/branch_1_fun/ppermute | solution.py:354
  382.6 16.7 %collective-permute-start.27 = (bf16[1,128,1024]{2,1,0:T(8,128)(2,1)S(1)}, bf16[1,128,1024]{2,1,0:T(8,128)(2,1)S(1)}, u32[]{:S(2)}, u32[]{:S(2)}) collective-permute-start(bf16[1,128,1024]{2,1,0:T(8,128)(2,1)S(1)} %get-tuple-element.588), channel_id=1, source_target_pairs={{0,4},{1,5},{2,6},{3,7},{4,0},{5,1},{6,2},{7,3},{8,12},{9,13},{10,... | collective-permute-start | bytes 786440 | tf_op jit(solution)/shard_map/cond/branch_1_fun/ppermute | solution.py:354
  384.2 15.2 %collective-permute-start.29 = (bf16[1,128,1024]{2,1,0:T(8,128)(2,1)S(1)}, bf16[1,128,1024]{2,1,0:T(8,128)(2,1)S(1)}, u32[]{:S(2)}, u32[]{:S(2)}) collective-permute-start(bf16[1,128,1024]{2,1,0:T(8,128)(2,1)S(1)} %get-tuple-element.589), channel_id=1, source_target_pairs={{0,2},{1,3},{2,0},{3,1},{4,6},{5,7},{6,4},{7,5},{8,10},{9,11},{10,... | collective-permute-start | bytes 786440 | tf_op jit(solution)/shard_map/cond/branch_1_fun/ppermute | solution.py:354
  393.9 9.9 %collective-permute-start.37 = (bf16[1,128,1024]{2,1,0:T(8,128)(2,1)S(1)}, bf16[1,128,1024]{2,1,0:T(8,128)(2,1)S(1)}, u32[]{:S(2)}, u32[]{:S(2)}) collective-permute-start(bf16[1,128,1024]{2,1,0:T(8,128)(2,1)S(1)} %get-tuple-element.584), channel_id=1, source_target_pairs={{0,4},{1,5},{2,6},{3,7},{4,0},{5,1},{6,2},{7,3},{8,12},{9,13},{10,... | collective-permute-start | bytes 786440 | tf_op jit(solution)/shard_map/cond/branch_1_fun/ppermute | solution.py:354
  395.4 8.3 %collective-permute-start.39 = (bf16[1,128,1024]{2,1,0:T(8,128)(2,1)S(1)}, bf16[1,128,1024]{2,1,0:T(8,128)(2,1)S(1)}, u32[]{:S(2)}, u32[]{:S(2)}) collective-permute-start(bf16[1,128,1024]{2,1,0:T(8,128)(2,1)S(1)} %get-tuple-element.585), channel_id=1, source_target_pairs={{0,2},{1,3},{2,0},{3,1},{4,6},{5,7},{6,4},{7,5},{8,10},{9,11},{10,... | collective-permute-start | bytes 786440 | tf_op jit(solution)/shard_map/cond/branch_1_fun/ppermute | solution.py:354
  407.1 7.3 %collective-permute-start.32 = (bf16[1,128,1024]{2,1,0:T(8,128)(2,1)S(1)}, bf16[1,128,1024]{2,1,0:T(8,128)(2,1)S(1)}, u32[]{:S(2)}, u32[]{:S(2)}) collective-permute-start(bf16[1,128,1024]{2,1,0:T(8,128)(2,1)S(1)} %get-tuple-element.596), channel_id=1, source_target_pairs={{0,4},{1,5},{2,6},{3,7},{4,0},{5,1},{6,2},{7,3},{8,12},{9,13},{10,... | collective-permute-start | bytes 786440 | tf_op jit(solution)/shard_map/cond/branch_1_fun/ppermute | solution.py:354
  408.6 7.2 %collective-permute-start.30 = (bf16[1,128,1024]{2,1,0:T(8,128)(2,1)S(1)}, bf16[1,128,1024]{2,1,0:T(8,128)(2,1)S(1)}, u32[]{:S(2)}, u32[]{:S(2)}) collective-permute-start(bf16[1,128,1024]{2,1,0:T(8,128)(2,1)S(1)} %get-tuple-element.595), channel_id=1, source_target_pairs={{0,2},{1,3},{2,0},{3,1},{4,6},{5,7},{6,4},{7,5},{8,10},{9,11},{10,... | collective-permute-start | bytes 786440 | tf_op jit(solution)/shard_map/cond/branch_1_fun/ppermute | solution.py:354
  414.4 12.4 %collective-permute-start.33 = (bf16[2,128,1024]{2,1,0:T(8,128)(2,1)S(1)}, bf16[2,128,1024]{2,1,0:T(8,128)(2,1)S(1)}, u32[]{:S(2)}, u32[]{:S(2)}) collective-permute-start(bf16[2,128,1024]{2,1,0:T(8,128)(2,1)S(1)} %pad_maximum_fusion.18), channel_id=1, source_target_pairs={{0,2},{1,3},{2,0},{3,1},{4,6},{5,7},{6,4},{7,5},{8,10},{9,11},{10,... | collective-permute-start | bytes 1572872 | tf_op jit(solution)/shard_map/cond/branch_1_fun/ppermute | solution.py:354
  415.8 11.6 %collective-permute-start.31 = (bf16[2,128,1024]{2,1,0:T(8,128)(2,1)S(1)}, bf16[2,128,1024]{2,1,0:T(8,128)(2,1)S(1)}, u32[]{:S(2)}, u32[]{:S(2)}) collective-permute-start(bf16[2,128,1024]{2,1,0:T(8,128)(2,1)S(1)} %pad_maximum_fusion.17), channel_id=1, source_target_pairs={{0,4},{1,5},{2,6},{3,7},{4,0},{5,1},{6,2},{7,3},{8,12},{9,13},{10,... | collective-permute-start | bytes 1572872 | tf_op jit(solution)/shard_map/cond/branch_1_fun/ppermute | solution.py:354
  427.6 4.2 collective-permute-start.34
  455.6 179.8 %reduce-scatter.12.cloned.1.call-start = ((), (), s32[]{:S(2)}) async-start(), calls=%async_computation.16 | async-start | bytes 3932160 | tf_op jit(solution)/shard_map/reduce_scatter | solution.py:475
  535.6 107.8 %reduce-scatter.14.cloned.1.call-start = ((), (), s32[]{:S(2)}) async-start(), calls=%async_computation.17 | async-start | bytes 1310720 | tf_op jit(solution)/shard_map/reduce_scatter | solution.py:710
  559.7 12.1 %collective-permute-start.45 = (f32[4,4,64,128]{3,2,1,0:T(8,128)S(1)}, f32[4,4,64,128]{3,2,1,0:T(8,128)S(1)}, u32[]{:S(2)}, u32[]{:S(2)}) collective-permute-start(f32[4,4,64,128]{3,2,1,0:T(8,128)S(1)} %slice_select_fusion), channel_id=1, source_target_pairs={{0,4},{1,5},{2,6},{3,7},{4,0},{5,1},{6,2},{7,3},{8,12},{9,13},{10,... | collective-permute-start | bytes 1572872 | tf_op jit(solution)/shard_map/cond/branch_1_fun/ppermute | solution.py:354
  564.2 23.8 %collective-permute-start.40 = (bf16[4,128,2048]{2,1,0:T(8,128)(2,1)}, bf16[4,128,2048]{2,1,0:T(8,128)(2,1)}, u32[]{:S(2)}, u32[]{:S(2)}) collective-permute-start(bf16[4,128,2048]{2,1,0:T(8,128)(2,1)} %bitcast.32), channel_id=1, source_target_pairs={{0,1},{1,0},{2,3},{3,2},{4,5},{5,4},{6,7},{7,6},{8,9},{9,8},{10,11... | collective-permute-start | bytes 6291464 | tf_op jit(solution)/shard_map/cond/branch_1_fun/ppermute | solution.py:354
  572.0 6.6 collective-permute-start.46
  578.6 9.3 %collective-permute-start.47 = (f32[4,1,64,128]{3,2,1,0:T(8,128)S(1)}, f32[4,1,64,128]{3,2,1,0:T(8,128)S(1)}, u32[]{:S(2)}, u32[]{:S(2)}) collective-permute-start(f32[4,1,64,128]{3,2,1,0:T(8,128)S(1)} %slice_select_fusion.2), channel_id=1, source_target_pairs={{0,1},{1,0},{2,3},{3,2},{4,5},{5,4},{6,7},{7,6},{8,9},{9,8},{10,11... | collective-permute-start | bytes 393224 | tf_op jit(solution)/shard_map/cond/branch_1_fun/ppermute | solution.py:354
  578.7 19.2 %all-to-all-start.2 = ((bf16[8,64,256]{2,1,0:T(8,128)(2,1)}), bf16[8,64,256]{2,1,0:T(8,128)(2,1)S(1)}, u32[]{:S(2)}, u32[]{:S(2)}) async-start(bf16[8,64,256]{2,1,0:T(8,128)(2,1)} %get-tuple-element.141), calls=%async_computation.2 | async-start | bytes 524288 | tf_op jit(solution)/shard_map/cond/branch_1_fun/all_to_all | solution.py:479
  594.2 14.9 %collective-permute-start.41 = (bf16[2,128,1024]{2,1,0:T(8,128)(2,1)S(1)}, bf16[2,128,1024]{2,1,0:T(8,128)(2,1)}, u32[]{:S(2)}, u32[]{:S(2)}) collective-permute-start(bf16[2,128,1024]{2,1,0:T(8,128)(2,1)S(1)} %pad_maximum_fusion.20), channel_id=1, source_target_pairs={{0,2},{1,3},{2,0},{3,1},{4,6},{5,7},{6,4},{7,5},{8,10},{9,11},{10,... | collective-permute-start | bytes 1572872 | tf_op jit(solution)/shard_map/cond/branch_1_fun/ppermute | solution.py:354
  596.2 14.9 %collective-permute-start.43 = (bf16[2,128,1024]{2,1,0:T(8,128)(2,1)S(1)}, bf16[2,128,1024]{2,1,0:T(8,128)(2,1)}, u32[]{:S(2)}, u32[]{:S(2)}) collective-permute-start(bf16[2,128,1024]{2,1,0:T(8,128)(2,1)S(1)} %slice.498), channel_id=1, source_target_pairs={{0,4},{1,5},{2,6},{3,7},{4,0},{5,1},{6,2},{7,3},{8,12},{9,13},{10,... | collective-permute-start | bytes 1572872 | tf_op jit(solution)/shard_map/cond/branch_1_fun/ppermute | solution.py:354
  597.7 5.2 collective-permute-start.48
  597.9 28.6 %all-to-all-start.1 = ((bf16[8,64,1376]{2,1,0:T(8,128)(2,1)}), bf16[8,64,1376]{2,1,0:T(8,128)(2,1)S(1)}, u32[]{:S(2)}, u32[]{:S(2)}) async-start(bf16[8,64,1376]{2,1,0:T(8,128)(2,1)} %get-tuple-element.138), calls=%async_computation.1 | async-start | bytes 2883584 | tf_op jit(solution)/shard_map/cond/branch_1_fun/all_to_all | solution.py:479
  603.0 15.6 %collective-permute-start.49 = (f32[1,1,64,128]{3,2,1,0:T(8,128)S(1)}, f32[1,1,64,128]{3,2,1,0:T(8,128)S(1)}, u32[]{:S(2)}, u32[]{:S(2)}) collective-permute-start(f32[1,1,64,128]{3,2,1,0:T(8,128)S(1)} %slice_select_fusion.4), channel_id=1, source_target_pairs={{0,8},{8,0},{16,24},{24,16},{1,9},{9,1},{17,25},{25,17},{2,10},{10... | collective-permute-start | bytes 98312 | tf_op jit(solution)/shard_map/cond/branch_1_fun/ppermute | solution.py:354
  612.7 18.3 %collective-permute-start.42 = (bf16[1,128,1024]{2,1,0:T(8,128)(2,1)S(1)}, bf16[1,128,1024]{2,1,0:T(8,128)(2,1)S(1)}, u32[]{:S(2)}, u32[]{:S(2)}) collective-permute-start(bf16[1,128,1024]{2,1,0:T(8,128)(2,1)S(1)} %get-tuple-element.603), channel_id=1, source_target_pairs={{0,4},{1,5},{2,6},{3,7},{4,0},{5,1},{6,2},{7,3},{8,12},{9,13},{10,... | collective-permute-start | bytes 786440 | tf_op jit(solution)/shard_map/cond/branch_1_fun/ppermute | solution.py:354
  614.2 16.8 %collective-permute-start.44 = (bf16[1,128,1024]{2,1,0:T(8,128)(2,1)S(1)}, bf16[1,128,1024]{2,1,0:T(8,128)(2,1)S(1)}, u32[]{:S(2)}, u32[]{:S(2)}) collective-permute-start(bf16[1,128,1024]{2,1,0:T(8,128)(2,1)S(1)} %get-tuple-element.604), channel_id=1, source_target_pairs={{0,2},{1,3},{2,0},{3,1},{4,6},{5,7},{6,4},{7,5},{8,10},{9,11},{10,... | collective-permute-start | bytes 786440 | tf_op jit(solution)/shard_map/cond/branch_1_fun/ppermute | solution.py:354
  635.4 16.1 %all-to-all-start.4 = ((bf16[8,64,768]{2,1,0:T(8,128)(2,1)}), bf16[8,64,768]{2,1,0:T(8,128)(2,1)S(1)}, u32[]{:S(2)}, u32[]{:S(2)}) async-start(bf16[8,64,768]{2,1,0:T(8,128)(2,1)} %bitcast.233), calls=%async_computation.8 | async-start | bytes 1572864 | tf_op jit(solution)/shard_map/all_to_all | solution.py:479
  (67 other events, 1157.6 us)
Sparse Core Ops, SparseCore 0:
  34.3 80.9 all-gather.5
  116.8 26.9 all-gather.7
  145.4 106.2 all-gather.9
  253.1 57.4 all-gather.11
  313.9 54.8 reduce-scatter.7
  371.0 99.9 reduce-scatter.5
  473.3 27.6 reduce-scatter.9
  535.7 56.9 reduce-scatter.11
  595.1 27.8 reduce-scatter.13

commit v3 on v2

--- a/solution.py
+++ b/solution.py
@@ -9,6 +9,8 @@
 MINI = 16
 EPSILON = 1e-06
 BASE_RATE = 1.0
+GELU_SCALE = (2.0 / 3.141592653589793) ** 0.5
+GELU_CUBE = 0.044715
 F32 = jnp.float32
 BF16 = jnp.bfloat16
 NN = (((1,), (0,)), ((), ()))
@@ -72,7 +74,7 @@
     heads, head_dim, parts,
     slot_ref, queries_ref, keys_ref, values_ref, rate_ref, again_ref, again_wide_ref,
     start_ref, start_bias_ref, gain_ref, shift_ref,
-    out_ref, normed_ref, spread_ref, grad_ref, rebuilt_ref, respread_ref, mix_ref, weight_ref,
+    out_ref, sums_ref, normed_ref, spread_ref, grad_ref, rebuilt_ref, respread_ref, mix_ref, weight_ref,
     state, bias,
 ):
     chains = rate_ref.shape[-1] // MINI
@@ -122,7 +124,10 @@
         respread_ref[0, j : j + 1, :] = inverse_out
         mix_ref[0, j] = mix
         weight_ref[0, j] = low_weight
-    out_ref[...] = unpacked(results, heads)
+    out = unpacked(results, heads)
+    out_ref[...] = out
+    sums_ref[:, 0:1] = jnp.sum(out, axis=1, keepdims=True)
+    sums_ref[:, 1:2] = jnp.sum(out * out, axis=1, keepdims=True)
     state[...] = weight
     bias[...] = offset
 
@@ -136,10 +141,10 @@
 
 def backward_kernel(
     heads, head_dim, parts,
-    slot_ref, queries_ref, keys_ref, values_ref, delta_ref, rate_ref, again_ref, again_wide_ref,
-    gain_ref, shift_ref,
+    slot_ref, queries_ref, keys_ref, values_ref, pre_ref, post_ref, out_ref, token_ref,
+    rate_ref, again_ref, again_wide_ref, gain_ref, shift_ref,
     normed_ref, spread_ref, grad_ref, rebuilt_ref, respread_ref, mix_ref, weight_ref,
-    dquery_ref, dkey_ref, dvalue_ref, drate_ref, dstart_ref, dstart_bias_ref, dgain_ref, dshift_ref,
+    inputs_ref, all_ref, dstart_ref, dstart_bias_ref, dgain_ref, dshift_ref,
     state, bias,
 ):
     chains = rate_ref.shape[-1] // MINI
@@ -161,12 +166,15 @@
     all_queries = packed(queries_ref[...], heads, head_dim, parts)
     all_keys = packed(keys_ref[...], heads, head_dim, parts)
     all_values = packed(values_ref[...], heads, head_dim, parts)
-    all_deltas = packed(delta_ref[...], heads, head_dim, parts)
+    center, inverse_all = token_ref[:, 0:1], token_ref[:, 1:2]
+    along_post = (out_ref[...] - center) * inverse_all
+    delta_post = (post_ref[...] - token_ref[:, 2:3] - along_post * token_ref[:, 3:4]) * inverse_all
+    all_deltas = packed(delta_post, heads, head_dim, parts)
     dweight = state[...]
     doffset = bias[...]
     dstart, dstart_bias = dstart_ref[...], dstart_bias_ref[...]
     dgain, dshift = dgain_ref[...], dshift_ref[...]
-    dqueries, dkeys, dvalues = [None] * parts, [None] * parts, [None] * parts
+    dqueries, dkeys, dvalues, dlogits = ([None] * parts for _ in range(4))
     for j in reversed(range(parts)):
         query, key, value, delta = all_queries[j], all_keys[j], all_values[j], all_deltas[j]
         rate = rate_ref[0, j : j + 1, :]
@@ -185,7 +193,8 @@
         low_dweight = dweight.astype(BF16)
         drated = drated - (mm(low_dweight, wide_key, NN) + doffset) * (1.0 / MINI)
         dinner = drated * rate
-        drate_ref[0, j : j + 1, :] = jnp.sum(drated * inner, axis=0, keepdims=True)
+        bent = rate * (1.0 - rate * (head_dim / BASE_RATE))
+        dlogits[j] = jnp.sum(drated * inner, axis=0, keepdims=True) * bent
         scaled = dinner * inverse
         offset_residue = normed * gain + shift - (value - key)
         residue = offset_residue * gain
@@ -214,9 +223,18 @@
         dstart_bias = dstart_bias + jnp.where(again, doffset, 0.0)
         dweight = jnp.where(again_wide, 0.0, dweight)
         doffset = jnp.where(again, 0.0, doffset)
-    dquery_ref[...] = unpacked(dqueries, heads).astype(dquery_ref.dtype)
-    dkey_ref[...] = unpacked(dkeys, heads).astype(dkey_ref.dtype)
-    dvalue_ref[...] = unpacked(dvalues, heads).astype(dvalue_ref.dtype)
+    width = heads * head_dim
+    for n, pieces in enumerate((dqueries, dkeys, dvalues)):
+        natural = unpacked(pieces, heads).astype(inputs_ref.dtype)
+        inputs_ref[:, n * width : (n + 1) * width] = natural
+        all_ref[:, n * width : (n + 1) * width] = natural
+    all_ref[:, 3 * width : 4 * width] = pre_ref[...]
+    natural = unpacked(dlogits, heads)
+    spare = inputs_ref.shape[1] - 3 * width - heads
+    if spare:
+        natural = jnp.concatenate([natural, jnp.zeros((natural.shape[0], spare), F32)], axis=1)
+    inputs_ref[:, 3 * width :] = natural.astype(inputs_ref.dtype)
+    all_ref[:, 4 * width :] = natural.astype(all_ref.dtype)
     state[...] = dweight
     bias[...] = doffset
     dstart_ref[...] = dstart
@@ -250,7 +268,7 @@
     ]
     return pl.pallas_call(
         functools.partial(forward_kernel, heads, head_dim, parts),
-        out_shape=[jax.ShapeDtypeStruct(queries.shape, F32)]
+        out_shape=[jax.ShapeDtypeStruct(queries.shape, F32), jax.ShapeDtypeStruct((steps * tokens, 2), F32)]
         + [jax.ShapeDtypeStruct((steps,) + shape, kind) for shape, kind in saved],
         grid_spec=pltpu.PrefetchScalarGridSpec(
             num_scalar_prefetch=1,
@@ -258,20 +276,22 @@
             in_specs=[at_slot] * 3
             + [stepped(parts, lanes), stepped(parts, lanes), stepped(parts, wide)]
             + [whole(start.shape), whole(start_bias.shape), whole(gain.shape), whole(shift.shape)],
-            out_specs=[at_slot] + [stepped(*shape) for shape, _ in saved],
+            out_specs=[at_slot, pl.BlockSpec((tokens, 2), at_slot.index_map)]
+            + [stepped(*shape) for shape, _ in saved],
             scratch_shapes=[pltpu.VMEM(start.shape, F32), pltpu.VMEM(start_bias.shape, F32)],
         ),
         compiler_params=pltpu.CompilerParams(
-            dimension_semantics=("arbitrary",), vmem_limit_bytes=40 * 1024 * 1024
+            dimension_semantics=("arbitrary",), vmem_limit_bytes=63 * 1024 * 1024
         ),
         name="inner_forward",
     )(slot, queries, keys, values, rates, again, again_wide, start, start_bias, gain, shift)
 
 
-def inner_backward(slot, queries, keys, values, deltas, rates, again, again_wide, gain, shift, saved, heads, head_dim, parts):
+def inner_backward(slot, queries, keys, values, pre, deltas, outs, per_token, rates, again, again_wide, gain, shift, saved, heads, head_dim, parts):
     steps, _, lanes = rates.shape
     tokens = queries.shape[0] // steps
     wide = again_wide.shape[-1]
+    inputs = 3 * heads * head_dim + heads + -heads % 16
     at_slot = pl.BlockSpec(
         (tokens, heads * head_dim), lambda i, s: (place(steps - 1 - i, s[0], steps), 0)
     )
@@ -281,9 +301,9 @@
 
     return pl.pallas_call(
         functools.partial(backward_kernel, heads, head_dim, parts),
-        out_shape=[jax.ShapeDtypeStruct(queries.shape, BF16)] * 3
-        + [
-            jax.ShapeDtypeStruct(rates.shape, F32),
+        out_shape=[
+            jax.ShapeDtypeStruct((steps * tokens, inputs), BF16),
+            jax.ShapeDtypeStruct((steps * tokens, inputs + heads * head_dim), BF16),
             jax.ShapeDtypeStruct((head_dim, wide), F32),
             jax.ShapeDtypeStruct((head_dim, lanes), F32),
             jax.ShapeDtypeStruct((head_dim, lanes), F32),
@@ -292,61 +312,153 @@
         grid_spec=pltpu.PrefetchScalarGridSpec(
             num_scalar_prefetch=1,
             grid=(steps,),
-            in_specs=[at_slot] * 4
+            in_specs=[at_slot] * 6
+            + [pl.BlockSpec((tokens, per_token.shape[1]), at_slot.index_map)]
             + [stepped(parts, lanes), stepped(parts, lanes), stepped(parts, wide)]
             + [whole(gain.shape), whole(shift.shape)]
             + [stepped(*array.shape[1:]) for array in saved],
-            out_specs=[at_slot] * 3
-            + [stepped(parts, lanes), whole((head_dim, wide))]
+            out_specs=[
+                pl.BlockSpec((tokens, inputs), at_slot.index_map),
+                pl.BlockSpec((tokens, inputs + heads * head_dim), at_slot.index_map),
+                whole((head_dim, wide)),
+            ]
             + [whole((head_dim, lanes))] * 3,
             scratch_shapes=[pltpu.VMEM((head_dim, wide), F32), pltpu.VMEM((head_dim, lanes), F32)],
         ),
         compiler_params=pltpu.CompilerParams(
+            dimension_semantics=("arbitrary",), vmem_limit_bytes=63 * 1024 * 1024
+        ),
+        name="inner_backward",
+    )(slot, queries, keys, values, pre, deltas, outs, per_token, rates, again, again_wide, gain, shift, *saved)
+
+
+def cut_kernel(seq_count, kinds, *refs):
+    out_ref = refs[-1]
+    for s in range(seq_count):
+        pieces = []
+        for ref, (groups, span, gap, rest) in zip(refs, kinds):
+            rows = ref.shape[0]
+            for g in range(groups):
+                at = (g * seq_count + s) * span
+                pieces.append(ref[:, at : at + span].astype(F32))
+                if gap:
+                    pieces.append(jnp.zeros((rows, gap), F32))
+            if rest:
+                pieces.append(jnp.zeros((rows, rest), F32))
+        out_ref[s] = jnp.concatenate(pieces, axis=1).astype(out_ref.dtype)
+
+
+def cut_columns(weights, kinds, seq_count):
+    rows = weights[0].shape[0]
+    columns = sum(groups * (span + gap) + rest for groups, span, gap, rest in kinds)
+    return pl.pallas_call(
+        functools.partial(cut_kernel, seq_count, kinds),
+        out_shape=jax.ShapeDtypeStruct((seq_count, rows, columns), BF16),
+        compiler_params=pltpu.CompilerParams(vmem_limit_bytes=40 * 1024 * 1024),
+        name="cut_columns",
+    )(*weights)
+
+
+def join_kernel(seq_count, kinds, *refs):
+    count = len(kinds)
+    parts_ref, weights, grads, sums_ref = refs[0], refs[1 : 1 + count], refs[1 + count : -1], refs[-1]
+    total = 0.0
+    base = 0
+    for weight, ref, (groups, span, gap, rest) in zip(weights, grads, kinds):
+        pieces = []
+        for g in range(groups):
+            at = base + g * (span + gap)
+            pieces += [parts_ref[s, :, at : at + span].astype(F32) for s in range(seq_count)]
+        whole_row = jnp.concatenate(pieces, axis=1)
+        ref[...] = whole_row
+        total = total + jnp.sum(whole_row * weight[...].astype(F32), axis=1, keepdims=True)
+        base += groups * (span + gap) + rest
+    sums_ref[...] = total
+
+
+def join_columns(parts, weights, kinds):
+    return pl.pallas_call(
+        functools.partial(join_kernel, parts.shape[0], kinds),
+        out_shape=[jax.ShapeDtypeStruct(w.shape, F32) for w in weights]
+        + [jax.ShapeDtypeStruct((parts.shape[1], 1), F32)],
+        compiler_params=pltpu.CompilerParams(vmem_limit_bytes=40 * 1024 * 1024),
+        name="join_columns",
+    )(parts, *weights)
+
+
+def branch_kernel(
+    delta_ref, matrix_ref, pre_ref, out_ref, token_ref, scale_ref, offset_ref,
+    dpre_ref, dnorm_ref, sums_ref, dscale_ref, doffset_ref,
+):
+    @pl.when(pl.program_id(0) == 0)
+    def _():
+        dscale_ref[...] = jnp.zeros_like(dscale_ref)
+        doffset_ref[...] = jnp.zeros_like(doffset_ref)
+
+    delta_gated = mm(delta_ref[...], matrix_ref[...], NT)
+    scale = scale_ref[...]
+    norm = (out_ref[...] - token_ref[:, 0:1]) * token_ref[:, 1:2]
+    pre = pre_ref[...]
+    square = pre * pre
+    bend = jnp.tanh(GELU_SCALE * pre * (1.0 + GELU_CUBE * square))
+    half = 0.5 * (1.0 + bend)
+    slope = half + 0.5 * pre * (1.0 - bend * bend) * (GELU_SCALE * (1.0 + 3.0 * GELU_CUBE * square))
+    dpre_ref[...] = (delta_gated * (norm * scale + offset_ref[...]) * slope).astype(dpre_ref.dtype)
+    delta_post = delta_gated * (pre * half)
+    dscale_ref[...] += jnp.sum(delta_post * norm, axis=0, keepdims=True)
+    doffset_ref[...] += jnp.sum(delta_post, axis=0, keepdims=True)
+    dnorm = delta_post * scale
+    dnorm_ref[...] = dnorm
+    sums_ref[:, 0:1] = jnp.sum(dnorm, axis=1, keepdims=True)
+    sums_ref[:, 1:2] = jnp.sum(dnorm * norm, axis=1, keepdims=True)
+
+
+def branch_backward(delta, matrix, pre, out, per_token, scale, offset, block):
+    tokens, width = pre.shape
+
+    def by_block(array):
+        return pl.BlockSpec((block, array.shape[1]), lambda i: (i, 0))
+
+    row = jax.ShapeDtypeStruct((1, width), F32)
+    sums = jax.ShapeDtypeStruct((tokens, 2), F32)
+    return pl.pallas_call(
+        branch_kernel,
+        grid=(tokens // block,),
+        in_specs=[by_block(delta), whole(matrix.shape), by_block(pre), by_block(out), by_block(per_token)]
+        + [whole((1, width))] * 2,
+        out_shape=[jax.ShapeDtypeStruct(pre.shape, BF16), jax.ShapeDtypeStruct(pre.shape, F32), sums, row, row],
+        out_specs=[by_block(pre), by_block(pre), by_block(sums), whole((1, width)), whole((1, width))],
+        compiler_params=pltpu.CompilerParams(
+            dimension_semantics=("arbitrary",), vmem_limit_bytes=63 * 1024 * 1024
+        ),
+        name="branch_backward",
+    )(delta, matrix, pre, out, per_token, scale, offset)
+
+
+def spread_kernel(delta_ref, weight_ref, rate_ref, out_ref):
+    width = weight_ref.shape[1]
+    total = mm(delta_ref[:, :width], weight_ref[...], NT)
+    total = total + mm(delta_ref[:, width:], rate_ref[...], NT)
+    out_ref[...] = total.astype(out_ref.dtype)
+
+
+def spread_back(delta, first, tokens, weight, rate, kind, block):
+    model = weight.shape[0]
+    return pl.pallas_call(
+        spread_kernel,
+        grid=(model // block,),
+        in_specs=[
+            pl.BlockSpec((tokens, delta.shape[1]), lambda i: (first // tokens, 0)),
+            pl.BlockSpec((block, weight.shape[1]), lambda i: (i, 0)),
+            pl.BlockSpec((block, rate.shape[1]), lambda i: (i, 0)),
+        ],
+        out_specs=pl.BlockSpec((tokens, block), lambda i: (0, i)),
+        out_shape=jax.ShapeDtypeStruct((tokens, model), kind),
+        compiler_params=pltpu.CompilerParams(
             dimension_semantics=("arbitrary",), vmem_limit_bytes=40 * 1024 * 1024
         ),
-        name="inner_backward",
-    )(slot, queries, keys, values, deltas, rates, again, again_wide, gain, shift, *saved)
-
-
-def cut_heads_kernel(groups, seq_count, span, *refs):
-    out_ref = refs[-1]
-    for s in range(seq_count):
-        pieces = [
-            ref[:, at : at + span].astype(F32)
-            for ref in refs[:-1]
-            for at in ((g * seq_count + s) * span for g in range(groups))
-        ]
-        out_ref[s] = jnp.concatenate(pieces, axis=1).astype(out_ref.dtype)
-
-
-def cut_heads(weights, groups, seq_count, span):
-    rows = weights[0].shape[0]
-    return pl.pallas_call(
-        functools.partial(cut_heads_kernel, groups, seq_count, span),
-        out_shape=jax.ShapeDtypeStruct((seq_count, rows, len(weights) * groups * span), BF16),
-        compiler_params=pltpu.CompilerParams(vmem_limit_bytes=40 * 1024 * 1024),
-        name="cut_heads",
-    )(*weights)
-
-
-def join_heads_kernel(groups, seq_count, span, parts_ref, *refs):
-    for n, ref in enumerate(refs):
-        pieces = []
-        for g in range(groups):
-            for s in range(seq_count):
-                at = (n * groups + g) * span
-                pieces.append(parts_ref[s, :, at : at + span].astype(F32))
-        ref[...] = jnp.concatenate(pieces, axis=1)
-
-
-def join_heads(parts, count, groups, seq_count, span):
-    whole_row = jax.ShapeDtypeStruct((parts.shape[1], groups * seq_count * span), F32)
-    return pl.pallas_call(
-        functools.partial(join_heads_kernel, groups, seq_count, span),
-        out_shape=[whole_row] * count,
-        compiler_params=pltpu.CompilerParams(vmem_limit_bytes=40 * 1024 * 1024),
-        name="join_heads",
-    )(parts)
+        name="spread_back",
+    )(delta, weight, rate)
 
 
 def exchange(value, axis, bit):
@@ -465,8 +577,11 @@
     everywhere = ("rows", "seq")
     seq_bits = bits_of("seq")
     row_bits = bits_of("rows")
-    units = rows_count * unit_share
     spare = -unit_share % 16
+    head_kind = (groups, span, 0, 0)
+    rate_kind = (groups, heads // groups, 0, -heads % 16)
+    unit_kind = (rows_count, unit_share, spare, 0)
+    units = rows_count * (unit_share + spare)
 
     def shuffled(values):
         return lax.all_to_all(values, "seq", 0, 0, tiled=True).reshape(-1, values.shape[-1])
@@ -511,13 +626,14 @@
     else:
         out_own = own_part(lax.all_gather(out_weight, everywhere, axis=0, tiled=True))
     mixer_cut = shuffled(
-        cut_heads((query_weight, key_weight, value_weight, gate_weight), groups, seq_count, span)
+        cut_columns((query_weight, key_weight, value_weight, gate_weight), (head_kind,) * 4, seq_count)
     )
     mixer_cut, hidden, cotangent, small, ffn_gate_weight, ffn_up_weight = lax.optimization_barrier(
         (mixer_cut, hidden, cotangent, small, ffn_gate_weight, ffn_up_weight)
     )
-    mixer_weight = lax.all_gather(mixer_cut, "rows", axis=0, tiled=True)
-    ffn_cut = cut_heads((ffn_gate_weight, ffn_up_weight), rows_count, seq_count, unit_share)
+    late_cut, out_own = lax.optimization_barrier((mixer_cut, out_own))
+    mixer_weight = lax.all_gather(late_cut, "rows", axis=0, tiled=True)
+    ffn_cut = cut_columns((ffn_gate_weight, ffn_up_weight), (unit_kind,) * 2, seq_count)
 
     def gather_inputs(hidden, cotangent, small, ffn_cut):
         hidden_all = gather_blocks(hidden, seq_bits).reshape(-1, model)
@@ -574,64 +690,55 @@
     normed = (plain_all * gain_attn).astype(BF16)
 
 
-    def project(matrix):
-        return jnp.dot(normed, matrix, preferred_element_type=F32)
-
-    qkv = project(mixer_weight[:, : 3 * width])
-    qkv, ffn_down_weight = lax.optimization_barrier((qkv, ffn_down_weight))
-    down_wide = lax.all_gather(ffn_down_weight, "rows", axis=0, tiled=True)
-    queries, keys, values = (qkv[:, n * width : (n + 1) * width] for n in range(3))
-    gate_pre = project(mixer_weight[:, 3 * width :])
-    logits = project(rate_own)
-    slope = jax.nn.sigmoid(logits)
+    projected = jnp.dot(normed, mixer_weight, preferred_element_type=F32)
+    projected, ffn_down_weight = lax.optimization_barrier((projected, ffn_down_weight))
+    down_wide = lax.all_gather(
+        jnp.pad(ffn_down_weight, ((0, spare), (0, 0))), "rows", axis=0, tiled=True
+    )
+    queries, keys, values, gate_pre = (projected[:, n * width : (n + 1) * width] for n in range(4))
+    logits = jnp.dot(normed, rate_own, preferred_element_type=F32)
 
     def to_lanes(per_token):
         ordered = jnp.take(per_token.reshape(steps, -1, heads), slots, axis=0)
         ordered = ordered.reshape(steps, parts, rows_here * MINI, heads)
         return ordered.transpose(0, 1, 3, 2).reshape(steps, parts, lanes)
 
-    def from_lanes(per_lane):
-        ordered = per_lane.reshape(steps, parts, heads, rows_here * MINI).transpose(0, 1, 3, 2)
-        return jnp.take(ordered.reshape(steps, -1, heads), blocks, axis=0).reshape(-1, heads)
-
-    rates = to_lanes(slope * (BASE_RATE / head_dim))
+    rates = to_lanes(jax.nn.sigmoid(logits) * (BASE_RATE / head_dim))
     slot = me.astype(jnp.int32).reshape(1)
 
-    inner_out, *saved = inner_forward(
+    inner_out, inner_sums, *saved = inner_forward(
         slot, queries, keys, values, rates, again, again_wide, start, bias_lanes, gain_lanes,
         shift_lanes, heads, head_dim, parts,
     )
 
-    def feature_mean(*arrays):
-        sums = jnp.stack([jnp.sum(v, axis=1) for v in arrays]).reshape(len(arrays), steps, -1)
-        total = lax.psum(jnp.take(sums, slots, axis=1), "seq") / model
-        return jnp.take(total, blocks, axis=1).reshape(len(arrays), -1, 1)
-
-    moments = feature_mean(inner_out, inner_out * inner_out)
+    def feature_mean(sums):
+        count = sums.shape[1]
+        ordered = jnp.take(sums.T.reshape(count, steps, -1), slots, axis=1)
+        total = lax.psum(ordered, "seq") / model
+        return jnp.take(total, blocks, axis=1).reshape(count, -1, 1)
+
+    moments = feature_mean(inner_sums)
     post_mean = moments[0]
     post_inverse = lax.rsqrt(moments[1] - post_mean * post_mean + EPSILON)
     post_norm = (inner_out - post_mean) * post_inverse
     post_out = post_norm * post_scale + post_offset
-    gelu_value, gelu_pull = jax.vjp(gelu_tanh, gate_pre)
-    gated = (gelu_value * post_out).astype(BF16)
-
-    def reduced(left, matrix, dims, bits):
+    gated = (gelu_tanh(gate_pre) * post_out).astype(BF16)
+
+    def halves(left, matrix, dims):
         half = left.shape[0] // 2
         away = lax.dot_general(left[half:], matrix, dims, preferred_element_type=F32).astype(BF16)
         own = lax.dot_general(left[:half], matrix, dims, preferred_element_type=F32)
-        return reduce_blocks(
-            own.reshape(-1, local, model), away.reshape(-1, local, model), bits
-        )
+        return own.reshape(-1, local, model), away.reshape(-1, local, model)
 
     def rms_inverse(values):
         return lax.rsqrt(jnp.mean(values * values, axis=-1, keepdims=True) + EPSILON)
 
-    def into_ffn(gated, out_own, hidden, gain_ffn):
-        residual = hidden.astype(F32) + reduced(gated, out_own, NN, seq_bits)
+    def into_ffn(own, away, hidden, gain_ffn):
+        residual = hidden.astype(F32) + reduce_blocks(own, away, seq_bits)
         scaled = (residual * rms_inverse(residual) * gain_ffn).astype(BF16)
         return residual, gather_blocks(scaled, seq_bits).reshape(-1, model)
 
-    residual, ffn_in = apart(into_ffn, gated, out_own, hidden, gain_ffn)
+    residual, ffn_in = apart(into_ffn, *halves(gated, out_own, NN), hidden, gain_ffn)
     gate_up = jnp.dot(ffn_in, ffn_wide, preferred_element_type=F32)
     gate_value, up_value = gate_up[:, :units], gate_up[:, units:]
     sigmoid_gate = jax.nn.sigmoid(gate_value)
@@ -640,8 +747,7 @@
     def token_grad(left, right):
         return lax.dot_general(left, right, TN, preferred_element_type=F32)
 
-    grad_down = token_grad(active, cot_all).astype(BF16).reshape(rows_count, unit_share, model)
-    grad_down = jnp.pad(grad_down, ((0, 0), (0, spare), (0, 0))).reshape(-1, model)
+    grad_down = token_grad(active, cot_all).astype(BF16)
     grad_down, down_wide = lax.optimization_barrier((grad_down, down_wide))
     grad_down = lax.psum_scatter(grad_down, "rows", scatter_dimension=0, tiled=True)
     grad_down = grad_down[:unit_share].astype(F32)
@@ -652,10 +758,9 @@
     ).astype(BF16)
     delta_both = jnp.concatenate([delta_gate, delta_up], axis=1)
 
-    def out_of_ffn(delta_both, ffn_wide, active, down_wide, residual, gain_ffn, cotangent):
-        delta_ffn = reduced(delta_both, ffn_wide, NT, seq_bits)
+    def out_of_ffn(own, away, own_down, away_down, residual, gain_ffn, cotangent):
+        delta_ffn = reduce_blocks(own, away, seq_bits)
         inverse_two = rms_inverse(residual)
-        grad_gain_ffn = jnp.sum(delta_ffn * residual * inverse_two, axis=0)
         scaled_two = delta_ffn * gain_ffn
         delta_after = (
             cotangent.astype(F32)
@@ -663,56 +768,51 @@
             - residual * inverse_two**3 * jnp.mean(scaled_two * residual, axis=-1, keepdims=True)
         )
         delta_branch = gather_blocks(delta_after.astype(BF16), seq_bits).reshape(-1, model)
-        block_out = residual + reduced(active, down_wide, NN, seq_bits)
-        return grad_gain_ffn, delta_after, delta_branch, block_out
+        block_out = restored(residual + reduce_blocks(own_down, away_down, seq_bits)).astype(BF16)
+        return delta_after, delta_branch, block_out
 
     grad_ffn = token_grad(ffn_in, delta_both).astype(BF16)
     delta_both, grad_ffn = lax.optimization_barrier((delta_both, grad_ffn))
     ffn_sums = row_sums(grad_ffn)
-    grad_gain_ffn, delta_after, delta_branch, block_out = apart(
-        out_of_ffn, delta_both, ffn_wide, active, down_wide, residual, gain_ffn, cotangent
-    )
-
+    delta_after, delta_branch, block_out = apart(
+        out_of_ffn, *halves(delta_both, ffn_wide, NT), *halves(active, down_wide, NN), residual, gain_ffn,
+        cotangent,
+    )
+
+    delta_pre, delta_norm, norm_sums, grad_post_scale, grad_post_shift = branch_backward(
+        delta_branch, out_own, gate_pre, inner_out, jnp.concatenate([post_mean, post_inverse], axis=1),
+        post_scale[None], post_offset[None], local,
+    )
+    grad_gate_weight = token_grad(normed, delta_pre).astype(BF16)
+    norm_sums, grad_gate_weight = lax.optimization_barrier((norm_sums, grad_gate_weight))
+    means = feature_mean(norm_sums)
     grad_out = token_grad(gated, delta_branch).astype(BF16)
-    delta_gated = lax.dot_general(delta_branch, out_own, NT, preferred_element_type=F32)
-    delta_pre = gelu_pull(delta_gated * post_out)[0].astype(BF16)
-    grad_gate_weight = token_grad(normed, delta_pre).astype(BF16)
-    delta_gated, grad_out, grad_gate_weight = lax.optimization_barrier(
-        (delta_gated, grad_out, grad_gate_weight)
+    per_token = jnp.concatenate([post_mean, post_inverse, means[0], means[1]], axis=1)
+
+    per_token, grad_out, grad_gate_weight, ffn_sums, grad_down = lax.optimization_barrier(
+        (per_token, grad_out, grad_gate_weight, ffn_sums, grad_down)
     )
     gate_sums = row_sums(grad_gate_weight)
-    delta_post = delta_gated * gelu_value
-    grad_post_scale = jnp.sum(delta_post * post_norm, axis=0)
-    grad_post_shift = jnp.sum(delta_post, axis=0)
-    delta_norm = delta_post * post_scale
-    means = feature_mean(delta_norm, delta_norm * post_norm)
-    delta_inner = (delta_norm - means[0] - post_norm * means[1]) * post_inverse
-
-    delta_inner, ffn_sums, grad_down = lax.optimization_barrier((delta_inner, ffn_sums, grad_down))
     (
-        delta_queries, delta_keys, delta_values, delta_rates,
+        delta_inputs, delta_all,
         grad_start, grad_bias, grad_inner_gain, grad_inner_shift,
     ) = inner_backward(
-        slot, queries, keys, values, delta_inner, rates, again, again_wide, gain_lanes, shift_lanes,
-        saved, heads, head_dim, parts,
-    )
-    delta_logits = (
-        from_lanes(delta_rates) * slope * (1.0 - slope) * (BASE_RATE / head_dim)
-    ).astype(BF16)
-    delta_qkv = jnp.concatenate([delta_queries, delta_keys, delta_values], axis=1)
-    delta_qkv, gate_sums = lax.optimization_barrier((delta_qkv, gate_sums))
-    grad_qkv = token_grad(normed, delta_qkv).astype(BF16)
-    delta_qkv, delta_logits, grad_qkv = lax.optimization_barrier((delta_qkv, delta_logits, grad_qkv))
-    qkv_sums = row_sums(grad_qkv)
-    grad_rate = token_grad(normed, delta_logits)
-    grad_rate, grad_out = lax.optimization_barrier((grad_rate, grad_out))
+        slot, queries, keys, values, delta_pre, delta_norm, inner_out, per_token, rates, again, again_wide,
+        gain_lanes, shift_lanes, saved, heads, head_dim, parts,
+    )
+    ffn_parts = columns_out(ffn_sums)
+    delta_inputs, delta_all, ffn_parts = lax.optimization_barrier((delta_inputs, delta_all, ffn_parts))
+    grad_inputs = token_grad(normed, delta_inputs).astype(BF16)
+    delta_all, grad_inputs, grad_out = lax.optimization_barrier((delta_all, grad_inputs, grad_out))
+    input_sums = row_sums(grad_inputs)
     if aligned:
-        grad_out = lax.psum_scatter(grad_out, "rows", scatter_dimension=0, tiled=True)
-    else:
-        grad_out = lax.psum_scatter(placed(grad_out), everywhere, scatter_dimension=0, tiled=True)
-
-    def back_project(delta, matrix):
-        return lax.dot_general(delta, matrix, NT, preferred_element_type=F32)
+        grad_out = lax.psum_scatter(grad_out, "rows", scatter_dimension=0, tiled=True).astype(F32)
+
+    half = delta_all.shape[0] // 2
+    rate_wide = jnp.pad(rate_own, ((0, 0), (0, -heads % 16)))
+    away = spread_back(delta_all, half, half, mixer_weight, rate_wide, BF16, model // 4)
+    own = spread_back(delta_all, 0, half, mixer_weight, rate_wide, F32, model // 4)
+    away, own = away.reshape(-1, local, model), own.reshape(-1, local, model)
 
     def lane_sum(per_lane, repeat):
         return per_lane.reshape(head_dim, heads, repeat).sum(axis=2).T.reshape(width, 1)
@@ -720,42 +820,36 @@
     grad_start = grad_start.reshape(head_dim, heads, rows_here, head_dim).sum(axis=2)
     grad_start = grad_start.transpose(1, 2, 0).reshape(width, head_dim)
     grad_bias = grad_bias.reshape(head_dim, heads, rows_here, MINI)[..., 0]
-    grad_rate = grad_rate.reshape(model, groups, 1, -1)
-    here = (jnp.arange(seq_count) == me).reshape(1, 1, -1, 1)
-    grad_rate = jnp.where(here, grad_rate, 0.0).reshape(model, head_count)
     own_grads = jnp.concatenate(
         [
             grad_start,
             lane_sum(grad_bias, rows_here),
             lane_sum(grad_inner_gain, rows_here * MINI),
             lane_sum(grad_inner_shift, rows_here * MINI),
-            grad_post_scale[:, None],
-            grad_post_shift[:, None],
+            grad_post_scale.T,
+            grad_post_shift.T,
         ],
         axis=1,
     )
-    small_grads = jnp.concatenate([placed(own_grads), grad_rate, grad_gain_ffn[:, None]], axis=1)
-
-    def out_of_mixer(
-        delta_mixer, mixer_weight, delta_logits, rate_own, plain_all, hidden, delta_after, gain_attn,
-        small_grads, ffn_sums, gate_sums,
-    ):
-        delta_normed = back_project(delta_mixer, mixer_weight) + back_project(delta_logits, rate_own)
-        grad_gain_attn = jnp.sum(delta_normed * plain_all, axis=0)
-        small_grads = jnp.concatenate([small_grads, grad_gain_attn[:, None]], axis=1)
-        small_grads = jnp.pad(small_grads, ((0, 0), (0, -small_grads.shape[1] % 128)))
-        small_grads = small_grads.reshape(rows_count, seq_count, share, -1)
-        for axis, bit in reversed(seq_bits):
-            small_grads = halved(small_grads, 1, axis, bit)
-        for axis, bit in reversed(row_bits):
-            small_grads = halved(small_grads, 0, axis, bit)
-        small_grads = small_grads.reshape(share, -1)
-        grad_gate, grad_up = join_heads(
-            columns_out(ffn_sums), 2, rows_count, seq_count, unit_share
+    if aligned:
+        own_grads = jnp.pad(own_grads, ((0, 0), (0, -own_grads.shape[1] % 128)))
+    else:
+        own_grads = lax.psum_scatter(
+            placed(jnp.concatenate([own_grads.astype(BF16), grad_out], axis=1)),
+            everywhere, scatter_dimension=0, tiled=True,
+        ).astype(F32)
+
+    def out_of_mixer(own, away, hidden, delta_after, gain_attn, ffn_parts, gate_sums, own_grads):
+        grad_gate, grad_up, ffn_products = join_columns(
+            ffn_parts, (ffn_gate_weight, ffn_up_weight), (unit_kind,) * 2
         )
-        grad_gate_weight, = join_heads(columns_out(gate_sums), 1, groups, seq_count, span)
-        delta_normed = delta_normed.reshape(2, -1, local, model)
-        delta_normed = reduce_blocks(delta_normed[0], delta_normed[1], seq_bits)
+        grad_gate_weight, gate_products = join_columns(
+            columns_out(gate_sums), (gate_weight,), (head_kind,)
+        )
+        delta_normed = reduce_blocks(own, away, seq_bits)
+        if aligned:
+            for axis, bit in reversed(row_bits):
+                own_grads = halved(own_grads, 0, axis, bit)
         tokens = hidden.astype(F32)
         inverse_one = rms_inverse(tokens)
         scaled_one = delta_normed * gain_attn
@@ -764,33 +858,38 @@
             + inverse_one * scaled_one
             - tokens * inverse_one**3 * jnp.mean(scaled_one * tokens, axis=-1, keepdims=True)
         )
-        return hidden_grad, small_grads, grad_gate, grad_up, grad_gate_weight
-
-    hidden_grad, small_grads, grad_gate, grad_up, grad_gate_weight = apart(
-        out_of_mixer, jnp.concatenate([delta_qkv, delta_pre], axis=1), mixer_weight, delta_logits,
-        rate_own, plain_all, hidden, delta_after, gain_attn, small_grads, ffn_sums, gate_sums,
-    )
-    grad_query, grad_key, grad_value = join_heads(
-        columns_out(qkv_sums), 3, groups, seq_count, span
-    )
-    after = head_dim + 5
+        return (
+            restored(hidden_grad), grad_gate, grad_up, ffn_products, grad_gate_weight, gate_products,
+            own_grads,
+        )
+
+    (
+        hidden_grad, grad_gate, grad_up, ffn_products, grad_gate_weight, gate_products, own_grads
+    ) = apart(
+        out_of_mixer, own, away, hidden, delta_after, gain_attn, ffn_parts, gate_sums, own_grads
+    )
+    grad_query, grad_key, grad_value, grad_rate, input_products = join_columns(
+        columns_out(input_sums), (query_weight, key_weight, value_weight, rate_weight),
+        (head_kind,) * 3 + (rate_kind,),
+    )
+    grad_gain_attn = (input_products[:, 0] + gate_products[:, 0]) / attn_gain.astype(F32)
+    grad_gain_ffn = ffn_products[:, 0] / ffn_gain.astype(F32)
+    if not aligned:
+        grad_out = own_grads[:, head_dim + 5 :]
+    own_vectors_grads = list(own_grads[:, head_dim : head_dim + 5].T)
     return (
-        restored(block_out).astype(BF16),
-        restored(hidden_grad),
-        small_grads[:, after + head_count + 1],
+        block_out,
+        hidden_grad,
+        grad_gain_attn,
         grad_query,
         grad_key,
         grad_value,
-        small_grads[:, after : after + head_count],
+        grad_rate,
         grad_gate_weight,
-        small_grads[:, :head_dim],
-        small_grads[:, head_dim],
-        small_grads[:, head_dim + 1],
-        small_grads[:, head_dim + 2],
-        small_grads[:, head_dim + 3],
-        small_grads[:, head_dim + 4],
-        grad_out.astype(F32),
-        small_grads[:, after + head_count],
+        own_grads[:, :head_dim],
+        *own_vectors_grads,
+        grad_out,
+        grad_gain_ffn,
         grad_gate,
         grad_up,
         grad_down,

time: 661 us -> 602 us (0.911)
  local copies, waits for them, and re-layouts: 90.7 us -> 51.3 us
  Pallas kernels: 43.7 us -> 73.9 us
  matrix products: 107 us -> 83.4 us
  other arithmetic: 80.7 us -> 57.2 us
  blocking collectives: 40.5 us -> 27.3 us
  waiting for transfers between devices: 208 us -> 216 us
    dot_general x12 -> x8, matrix products: 51.2 us -> 28.8 us  [the longest x3 11.2 us: halves(): lax.dot_general(left[half:], matrix, dims, preferred_element_type=F32)]
    pallas_call x5 -> x8, Pallas kernels: 7.62 us -> 29.7 us  [the longest x2 8.94 us: spread_back(): pl.pallas_call(spread_kernel, grid=(model // block,), in_specs=[pl.BlockS...]
    all_gather x1, waiting for transfers between devices: 18.9 us -> 0.01 us  [shards(): ffn_wide = lax.all_gather(ffn_cut, 'rows', axis=0, tiled=True)]
    unnamed x111 -> x100, local copies, waits for them, and re-layouts: 29.2 us -> 12.2 us
    reduce_scatter x1, waiting for transfers between devices: 0.01 us -> 13.3 us  [shards(): lax.psum_scatter(grad_out, 'rows', scatter_dimension=0, tiled=True)]
    psum x2, blocking collectives: 40.5 us -> 27.3 us  [feature_mean(): total = lax.psum(ordered, 'seq') / model]
    reduce_scatter x3, waiting for transfers between devices: 0.02 us -> 13 us  [row_sums(): summed = lax.psum_scatter(values, 'rows', scatter_dimension=0, tiled=True)]
    another operation x4 -> x1, local copies, waits for them, and re-layouts: 8.65 us -> 0.79 us  [shards(): own_vectors_grads = list(own_grads[:, head_dim:head_dim + 5].T)]
  transfers between devices with their start and end apart: 64 -> 61, of which waited for: 40 -> 40; matrix products, arithmetic and copies ran while one was open for 36% -> 30% of each run, Pallas kernels for 6% -> 12%
where the time goes in v3:
time: 602 us; the launch traced here: 596 us
  waiting for transfers between devices  216 us (36%)
  matrix products  83.4 us (14%)
  Pallas kernels  73.9 us (12%)
  starting transfers between devices  69.9 us (12%)
  other arithmetic  57.2 us (10%)
  local copies, waits for them, and re-layouts  51.3 us (9%)
  blocking collectives  27.3 us (5%)
  between operations  15.9 us (3%)
    ppermute x47, waiting for transfers between devices, exchange(): return lax.ppermute(value, axis, [(i, i ^ bit) for i in range(count)])  136 us
    ppermute x47, starting transfers between devices, exchange(): return lax.ppermute(value, axis, [(i, i ^ bit) for i in range(count)])  47.9 us
    dot_general x5, matrix products, token_grad(): return lax.dot_general(left, right, TN, preferred_element_type=F32)  35.1 us
    psum x2, blocking collectives, feature_mean(): total = lax.psum(ordered, 'seq') / model  27.3 us
    all_gather x1, waiting for transfers between devices, shards(): lax.all_gather(jnp.pad(ffn_down_weight, ((0, spare), (0, 0))), 'rows', ax...  26.1 us
    pallas_call x1, Pallas kernels, inner_backward(): pl.pallas_call(functools.partial(backward_kernel, heads, head_dim, parts)...  25.6 us
    pallas_call x1, Pallas kernels, inner_forward(): pl.pallas_call(functools.partial(forward_kernel, heads, head_dim, parts),...  18.7 us
    all_to_all x2, waiting for transfers between devices, shuffled(): lax.all_to_all(values, 'seq', 0, 0, tiled=True)  17.2 us
  transfers between devices with their start and end apart: 61, of which 40 were waited for; matrix products, arithmetic and copies ran while one was open for 30% of the time, Pallas kernels for 12%

profile of v3, /device:TPU:0, one launch (start us, length us, event | category | flops | bytes accessed | tf_op | source)
XLA Modules:
  0.0 595.5 jit_solution(16868540970852059265)
XLA Ops:
  13.3 5.2 all-to-all-start.2
  20.8 13.1 %all-to-all-done.2 = bf16[8,64,1024]{2,1,0:T(8,128)(2,1)S(1)} async-done(((bf16[8,64,1024]{2,1,0:T(8,128)(2,1)}), bf16[8,64,1024]{2,1,0:T(8,128)(2,1)S(1)}, u32[]{:S(2)}, u32[]{:S(2)}) %all-to-all-start.2) | async-done | bytes 1048608 | tf_op jit(solution)/shard_map/all_to_all | solution.py:587
  33.9 6.5 %all-gather.5.cloned.1.call-done.matrix_ref = bf16[256,2048]{1,0:T(8,128)(2,1)} async-done(((bf16[64,2048]{1,0:T(8,128)(2,1)}), bf16[256,2048]{1,0:T(8,128)(2,1)}) %all-gather.5.cloned.1.call-update) | async-done | bytes 1048592 | tf_op jit(solution)/shard_map/all_gather | solution.py:625
  41.7 2.9 cut_columns.3
  44.7 71.4 %conditional.4 = (bf16[1024,2048]{1,0:T(8,128)(2,1)}, bf16[2048,128]{1,0:T(8,128)(2,1)S(1)}, bf16[512,1408]{1,0:T(8,128)(2,1)}, f32[1024,2048]{1,0:T(8,128)}, f32[1024,1]{0,1:T(1,128)S(1)}) conditional(s32[]{:T(128)} %convert_element_type.309, () %tuple.59, (bf16[128,2048]{1,0:T(8,128)(2,1)S(1)}, bf16[64,128]{1,0:T(8,128)(2,1)S(1)}, ...), branch_computations={%region_1.2_spmd, %region_2.4_spmd} | conditional | flops 105102336 | bytes 91427888 | solution.py:616
  51.5 5.5 collective-permute-done.2
  64.3 8.0 %collective-permute-done.3 = bf16[2,128,1024]{2,1,0:T(8,128)(2,1)S(1)} collective-permute-done((bf16[2,128,1024]{2,1,0:T(8,128)(2,1)S(1)}, bf16[2,128,1024]{2,1,0:T(8,128)(2,1)S(1)}, u32[]{:S(2)}, u32[]{:S(2)}) %collective-permute-start.3) | collective-permute-done | bytes 524320 | tf_op jit(solution)/shard_map/cond/branch_1_fun/ppermute | solution.py:466
  76.0 5.8 collective-permute-done.13
  85.2 5.3 collective-permute-done.8
  92.2 4.3 all-to-all-start
  102.0 3.7 pad_maximum_fusion
  105.7 6.2 %multiply_reduce_fusion = (f32[8,128]{1,0:T(8,128)S(1)}, f32[8,128,2048]{2,1,0:T(8,128)}) fusion(bf16[4,128,2048]{2,1,0:T(8,128)(2,1)} %collective-permute-done.14, bf16[1,128,1024]{2,1,0:T(8,128)(2,1)S(1)} %copy-done.30, bf16[1,128,1024]{2,1,0:T(8,128)(2,1)S(1)} %collective-permute-done.12, bf16[1,128,1024]{2,1,0:T(8,128)(2,1)S(1)} %copy-done.28, ...), kind=kLoop, calls=%fused_computation.5 | loop fusion | flops 37747712 | bytes 12587008 | tf_op jit(solution)/shard_map/reduce_sum | solution.py:688
  112.0 4.1 all-to-all-done
  123.8 4.2 multiply_convert_fusion.1
  133.3 10.4 %fusion.76 = f32[1024,1024]{1,0:T(8,128)} fusion(bf16[1024,2048]{1,0:T(8,128)(2,1)} %copy-done.10, bf16[2048,1024]{1,0:T(8,128)(2,1)} %all-gather.7.cloned.1.call-done.weight_ref), kind=kOutput, calls=%fused_computation.242 | convolution fusion | flops 4294967296 | bytes 12582912 | tf_op jit(solution)/shard_map/dot_general | solution.py:693
  144.6 3.6 fusion.74
  148.2 18.7 %inner_forward.1 = (f32[1024,256]{1,0:T(8,128)}, f32[1024,2]{1,0:T(8,128)}, f32[8,4,64,128]{3,2,1,0:T(8,128)}, f32[8,4,128]{2,1,0:T(4,128)}, f32[8,4,64,128]{3,2...) custom-call(s32[1]{0:T(128)} %bitcast.58.slot_ref, ...), custom_call_target="tpu_custom_call" | custom-call | tf_op jit(solution)/shard_map/inner_forward/pallas_call | solution.py:269
  168.9 13.2 %psum.14 = f32[2,8,128]{2,0,1:T(2,128)S(1)} all-reduce(f32[2,8,128]{2,0,1:T(2,128)S(1)} %select_bitcast_fusion.4), channel_id=1, replica_groups=mesh['rows'=4,'seq'=8] {'seq'}, use_global_device_ids=true, to_apply=%region_5.7 | all-reduce | flops 2048 | bytes 16384 | tf_op jit(solution)/shard_map/psum | solution.py:717
  182.9 2.9 fusion.73
  187.3 55.0 %conditional.5 = (f32[128,2048]{1,0:T(8,128)S(1)}, bf16[1024,2048]{1,0:T(8,128)(2,1)}) conditional(s32[]{:T(128)} %convert_element_type.309, () %tuple.58, (bf16[128,2048]{1,0:T(8,128)(2,1)S(1)}, f32[512,2048]{1,0:T(8,128)S(1)}, bf16[512,2048]{1,0:T(8,128)(2,1)S(1)}, f32[2048]{0:T(1024)S(1)}) %tuple.161), branch_computations={%region_6.8_spmd, %region_7.10_spmd} | conditional | flops 56098944 | bytes 79702488 | solution.py:616
  187.6 4.1 collective-permute-done.15
  194.7 12.4 %collective-permute-done.16 = bf16[2,128,1024]{2,1,0:T(8,128)(2,1)S(1)} collective-permute-done((bf16[2,128,1024]{2,1,0:T(8,128)(2,1)S(1)}, bf16[2,128,1024]{2,1,0:T(8,128)(2,1)S(1)}, u32[]{:S(2)}, u32[]{:S(2)}) %collective-permute-start.16) | collective-permute-done | bytes 524320 | tf_op jit(solution)/shard_map/cond/branch_1_fun/ppermute | solution.py:466
  210.5 4.4 collective-permute-done.17
  218.8 4.7 collective-permute-done.22
  226.5 8.6 %collective-permute-done.23 = bf16[2,128,1024]{2,1,0:T(8,128)(2,1)S(1)} collective-permute-done((bf16[2,128,1024]{2,1,0:T(8,128)(2,1)S(1)}, bf16[2,128,1024]{2,1,0:T(8,128)(2,1)S(1)}, u32[]{:S(2)}, u32[]{:S(2)}) %collective-permute-start.23) | collective-permute-done | bytes 524320 | tf_op jit(solution)/shard_map/cond/branch_1_fun/ppermute | solution.py:466
  236.0 4.1 collective-permute-done.24
  242.3 10.4 %fusion.77 = f32[1024,1408]{1,0:T(8,128)S(1)} fusion(bf16[1024,2048]{1,0:T(8,128)(2,1)} %get-tuple-element.205, bf16[2048,1408]{1,0:T(8,128)(2,1)} %all-gather.9.cloned.1.call-done), kind=kOutput, calls=%fused_computation.243 | convolution fusion | flops 5905580032 | bytes 15728640 | tf_op jit(solution)/shard_map/dot_general | solution.py:742
  252.8 2.5 copy-done.14
  256.1 6.9 %convolution_convert_fusion.2 = bf16[704,2048]{1,0:T(8,128)(2,1)} fusion(bf16[1024,704]{1,0:T(8,128)(2,1)S(1)} %multiply_convert_fusion.4, bf16[1024,2048]{1,0:T(8,128)(2,1)} %get-tuple-element.204), kind=kOutput, calls=%fused_computation.127 | convolution fusion | flops 2954231808 | bytes 8519680 | tf_op jit(solution)/shard_map/dot_general | solution.py:748
  263.1 26.1 %all-gather.11.cloned.1.call-done = bf16[704,2048]{1,0:T(8,128)(2,1)} async-done(((bf16[176,2048]{1,0:T(8,128)(2,1)}), bf16[704,2048]{1,0:T(8,128)(2,1)}) %all-gather.11.cloned.1.call-update) | async-done | bytes 2883600 | tf_op jit(solution)/shard_map/all_gather | solution.py:695
  289.6 9.1 %multiply_convert_fusion.3 = (bf16[1024,704]{1,0:T(8,128)(2,1)S(1)}, bf16[1024,704]{1,0:T(8,128)(2,1)S(1)}) fusion(f32[1024,1408]{1,0:T(8,128)} %copy-done.14, bf16[1024,2048]{1,0:T(8,128)(2,1)} %get-tuple-element.204, bf16[704,2048]{1,0:T(8,128)(2,1)} %all-gather.11.cloned.1.call-done), kind=kOutput, calls=%fused_computation.129 | convolution fusion | flops 2962161664 | bytes 15728640 | tf_op jit(solution)/shard_map/dot_general | solution.py:754
  301.2 10.9 %convolution_convert_fusion = bf16[2048,1408]{1,0:T(8,128)(2,1)} fusion(bf16[1024,2048]{1,0:T(8,128)(2,1)} %get-tuple-element.205, bf16[1024,1408]{1,0:T(8,128)(2,1)S(1)} %pad_maximum_fusion.20), kind=kOutput, calls=%fused_computation.125 | convolution fusion | flops 5908463616 | bytes 12845056 | tf_op jit(solution)/shard_map/dot_general | solution.py:748
  313.4 3.8 convolution_convert_fusion.4
  319.0 6.7 %convolution_convert_fusion.5 = bf16[512,2048]{1,0:T(8,128)(2,1)S(1)} fusion(bf16[2048,1408]{1,0:T(8,128)(2,1)} %all-gather.9.cloned.1.call-done, bf16[1024,1408]{1,0:T(8,128)(2,1)S(1)} %copy-done.20), kind=kOutput, calls=%fused_computation.134 | convolution fusion | flops 2953838592 | bytes 9306112 | tf_op jit(solution)/shard_map/dot_general | solution.py:729
  325.8 3.4 fusion.31
  329.2 72.2 %conditional.6 = (f32[128,2048]{1,0:T(8,128)}, bf16[1024,2048]{1,0:T(8,128)(2,1)}, bf16[2,64,2048]{2,1,0:T(8,128)(2,1)}) conditional(s32[]{:T(128)} %convert_element_type.309, () %tuple.56, (bf16[128,2048]{1,0:T(8,128)(2,1)S(1)}, f32[128,2048]{1,0:T(8,128)S(1)}, f32[512,2048]{1,0:T(8,128)S(1)}, bf16[512,2048]{1,0:T(8,128)(2,1)S(1)}, ...), branch_computations={%region_9.11_spmd, %region_10.14_spmd} | conditional | flops 63963520 | bytes 111695472 | solution.py:616
  329.8 3.6 collective-permute-done.25
  340.8 8.8 %collective-permute-done.26 = bf16[2,128,1024]{2,1,0:T(8,128)(2,1)S(1)} collective-permute-done((bf16[2,128,1024]{2,1,0:T(8,128)(2,1)S(1)}, bf16[2,128,1024]{2,1,0:T(8,128)(2,1)S(1)}, u32[]{:S(2)}, u32[]{:S(2)}) %collective-permute-start.26) | collective-permute-done | bytes 524320 | tf_op jit(solution)/shard_map/cond/branch_1_fun/ppermute | solution.py:466
  353.3 7.5 %collective-permute-done.36 = bf16[2,128,1024]{2,1,0:T(8,128)(2,1)S(1)} collective-permute-done((bf16[2,128,1024]{2,1,0:T(8,128)(2,1)S(1)}, bf16[2,128,1024]{2,1,0:T(8,128)(2,1)S(1)}, u32[]{:S(2)}, u32[]{:S(2)}) %collective-permute-start.36) | collective-permute-done | bytes 524320 | tf_op jit(solution)/shard_map/cond/branch_1_fun/ppermute | solution.py:466
  364.6 3.3 collective-permute-done.27
  368.5 4.0 collective-permute-done.37
  376.3 5.3 collective-permute-done.32
  383.9 10.1 %collective-permute-done.33 = bf16[2,128,1024]{2,1,0:T(8,128)(2,1)S(1)} collective-permute-done((bf16[2,128,1024]{2,1,0:T(8,128)(2,1)S(1)}, bf16[2,128,1024]{2,1,0:T(8,128)(2,1)S(1)}, u32[]{:S(2)}, u32[]{:S(2)}) %collective-permute-start.33) | collective-permute-done | bytes 524320 | tf_op jit(solution)/shard_map/cond/branch_1_fun/ppermute | solution.py:466
  395.8 3.3 collective-permute-done.34
  401.4 8.9 %branch_backward.1 = (bf16[1024,256]{1,0:T(8,128)(2,1)}, f32[1024,256]{1,0:T(8,128)}, f32[1024,2]{1,0:T(8,128)}, f32[1,256]{1,0:T(1,128)}, f32[1,256]{1,0:T(1,128)}) custom-call(bf16[1024,2048]{1,0:T(8,128)(2,1)} %get-tuple-element.211.delta_ref, bf16[256,2048]{1,0:T(8,128)(2,1)} %all-gather.5.cloned.1.call-done.matrix_ref, ...), custom_call_target="tpu_custom_call" | custom-call | tf_op jit(solution)/shard_map/branch_backward/pallas_call | solution.py:424
  410.3 4.7 convolution_convert_fusion.7
  415.9 14.1 %psum.15 = f32[2,8,128]{2,0,1:T(2,128)S(1)} all-reduce(f32[2,8,128]{2,0,1:T(2,128)S(1)} %select_bitcast_fusion.2), channel_id=1, replica_groups=mesh['rows'=4,'seq'=8] {'seq'}, use_global_device_ids=true, to_apply=%region_13.15 | all-reduce | flops 2048 | bytes 16384 | tf_op jit(solution)/shard_map/psum | solution.py:717
  430.7 4.4 convolution_convert_fusion.6
  437.5 13.0 %reduce-scatter.6.cloned.1.call-done = bf16[512,1408]{1,0:T(8,128)(2,1)} async-done(((bf16[2048,1408]{1,0:T(8,128)(2,1)}), bf16[512,1408]{1,0:T(8,128)(2,1)}) %reduce-scatter.6.cloned.1.call-update) | async-done | bytes 1441808 | tf_op jit(solution)/shard_map/reduce_scatter | solution.py:590
  450.5 4.3 all-to-all-start.3
  455.9 25.6 %inner_backward.1 = (bf16[1024,784]{1,0:T(8,128)(2,1)}, bf16[1024,1040]{1,0:T(8,128)(2,1)}, f32[64,512]{1,0:T(8,128)}, f32[64,128]{1,0:T(8,128)}, f32[64,128]{1,0:T(8,128)}, /*index=5*/f32[64,128]{1,0:T(8,128)}) custom-call(s32[1]{0:T(128)} %bitcast.58.slot_ref, f32[1024,256]{1,0:T(8,128)} %get-tuple-element.444.queries_ref, ...), custom_call_target="tpu_custom_call" | custom-call | tf_op jit(solution)/shard_map/inner_backward/pallas_call | solution.py:302
  481.5 8.1 %convolution_convert_fusion.1 = bf16[2048,784]{0,1:T(8,128)(2,1)} fusion(bf16[1024,2048]{1,0:T(8,128)(2,1)} %copy-done.10, bf16[1024,784]{1,0:T(8,128)(2,1)} %get-tuple-element.231), kind=kOutput, calls=%fused_computation.126 | convolution fusion | flops 3289939968 | bytes 9011200 | tf_op jit(solution)/shard_map/dot_general | solution.py:748
  505.7 4.3 spread_back.3
  510.0 4.6 spread_back.2
  514.6 48.0 %conditional.7 = (f32[2,64,2048]{2,1,0:T(8,128)S(1)}, f32[64,5504]{1,0:T(8,128)}, f32[64,5504]{1,0:T(8,128)}, f32[64,2048]{1,0:T(8,128)}, f32[64,128]{1,0:T(8,128)S(1)}, /*index=5*/f32[64]{0:T(128)S(1)}, f32[64]{0:T(128)S(1)}) conditional(s32[]{:T(128)} %convert_element_type.309, () %tuple.67, (bf16[128,2048]{1,0:T(8,128)(2,1)S(1)}, ...), branch_computations={%region_21.23_spmd, %region_22.26_spmd} | conditional | flops 9251207 | bytes 51459632 | solution.py:616
  514.9 4.1 collective-permute-done.40
  519.0 5.3 fusion.64
  529.4 2.9 collective-permute-start.45
  532.3 7.7 %collective-permute-done.45 = f32[128,128]{1,0:T(8,128)S(1)} collective-permute-done((f32[128,128]{1,0:T(8,128)S(1)}, f32[128,128]{1,0:T(8,128)S(1)}, u32[]{:S(2)}, u32[]{:S(2)}) %collective-permute-start.45) | collective-permute-done | bytes 65568 | tf_op jit(solution)/shard_map/cond/branch_1_fun/ppermute | solution.py:466
  547.6 3.4 all-to-all-start.1
  551.1 3.8 join_columns.3
  562.7 2.6 copy.247
  565.3 3.6 all-to-all-start.4
  570.3 13.3 %reduce-scatter.14.cloned.1.call-done = bf16[64,2048]{1,0:T(8,128)(2,1)} async-done(((bf16[256,2048]{1,0:T(8,128)(2,1)}), bf16[64,2048]{1,0:T(8,128)(2,1)}) %reduce-scatter.14.cloned.1.call-update) | async-done | bytes 262160 | tf_op jit(solution)/shard_map/reduce_scatter | solution.py:809
  (415 shorter events, 152.1 us)
Async XLA Ops:
  7.3 33.1 %all-gather.5.cloned.1.call-start = ((), (), s32[]{:S(2)}) async-start(), calls=%async_computation.10 | async-start | bytes 1310720 | tf_op jit(solution)/shard_map/all_gather | solution.py:625
  13.3 20.6 %all-to-all-start.2 = ((bf16[8,64,1024]{2,1,0:T(8,128)(2,1)}), bf16[8,64,1024]{2,1,0:T(8,128)(2,1)S(1)}, u32[]{:S(2)}, u32[]{:S(2)}) async-start(bf16[8,64,1024]{2,1,0:T(8,128)(2,1)} %cut_columns.2), calls=%async_computation.2 | async-start | bytes 2097152 | tf_op jit(solution)/shard_map/all_to_all | solution.py:587
  18.5 114.8 %all-gather.7.cloned.1.call-start = ((), (), s32[]{:S(2)}) async-start(), calls=%async_computation.11 | async-start | bytes 5242880 | tf_op jit(solution)/shard_map/all_gather | solution.py:635
  40.4 201.9 %all-gather.9.cloned.1.call-start = ((), (), s32[]{:S(2)}) async-start(), calls=%async_computation.12 | async-start | bytes 7208960 | tf_op jit(solution)/shard_map/all_gather | solution.py:648
  44.7 5.7 collective-permute-start.5
  46.1 11.5 %collective-permute-start = (bf16[1,128,1024]{2,1,0:T(8,128)(2,1)S(1)}, bf16[1,128,1024]{2,1,0:T(8,128)(2,1)S(1)}, u32[]{:S(2)}, u32[]{:S(2)}) collective-permute-start(bf16[1,128,1024]{2,1,0:T(8,128)(2,1)S(1)} %get-tuple-element.387), channel_id=1, source_target_pairs={{0,2},{1,3},{2,0},{3,1},{4,6},{5,7},{6,4},{7,5},{8,10},{9,11},{10,... | collective-permute-start | bytes 786440 | tf_op jit(solution)/shard_map/cond/branch_1_fun/ppermute | solution.py:466
  47.7 9.2 %collective-permute-start.2 = (bf16[1,128,1024]{2,1,0:T(8,128)(2,1)S(1)}, bf16[1,128,1024]{2,1,0:T(8,128)(2,1)S(1)}, u32[]{:S(2)}, u32[]{:S(2)}) collective-permute-start(bf16[1,128,1024]{2,1,0:T(8,128)(2,1)S(1)} %get-tuple-element.388), channel_id=1, source_target_pairs={{0,4},{1,5},{2,6},{3,7},{4,0},{5,1},{6,2},{7,3},{8,12},{9,13},{10,... | collective-permute-start | bytes 786440 | tf_op jit(solution)/shard_map/cond/branch_1_fun/ppermute | solution.py:466
  49.2 11.9 %collective-permute-start.10 = (bf16[1,128,1024]{2,1,0:T(8,128)(2,1)S(1)}, bf16[1,128,1024]{2,1,0:T(8,128)(2,1)S(1)}, u32[]{:S(2)}, u32[]{:S(2)}) collective-permute-start(bf16[1,128,1024]{2,1,0:T(8,128)(2,1)S(1)} %get-tuple-element.381), channel_id=1, source_target_pairs={{0,2},{1,3},{2,0},{3,1},{4,6},{5,7},{6,4},{7,5},{8,10},{9,11},{10,... | collective-permute-start | bytes 786440 | tf_op jit(solution)/shard_map/cond/branch_1_fun/ppermute | solution.py:466
  49.8 12.8 %collective-permute-start.12 = (bf16[1,128,1024]{2,1,0:T(8,128)(2,1)S(1)}, bf16[1,128,1024]{2,1,0:T(8,128)(2,1)S(1)}, u32[]{:S(2)}, u32[]{:S(2)}) collective-permute-start(bf16[1,128,1024]{2,1,0:T(8,128)(2,1)S(1)} %get-tuple-element.382), channel_id=1, source_target_pairs={{0,4},{1,5},{2,6},{3,7},{4,0},{5,1},{6,2},{7,3},{8,12},{9,13},{10,... | collective-permute-start | bytes 786440 | tf_op jit(solution)/shard_map/cond/branch_1_fun/ppermute | solution.py:466
  50.4 8.8 %collective-permute-start.6 = (bf16[128,128]{1,0:T(8,128)(2,1)S(1)}, bf16[128,128]{1,0:T(8,128)(2,1)S(1)}, u32[]{:S(2)}, u32[]{:S(2)}) collective-permute-start(bf16[128,128]{1,0:T(8,128)(2,1)S(1)} %pad_maximum_fusion.9), channel_id=1, source_target_pairs={{0,16},{8,24},{16,0},{24,8},{1,17},{9,25},{17,1},{25,9},{2,18},{10... | collective-permute-start | bytes 98312 | tf_op jit(solution)/shard_map/cond/branch_1_fun/ppermute | solution.py:466
  57.0 15.3 %collective-permute-start.3 = (bf16[2,128,1024]{2,1,0:T(8,128)(2,1)S(1)}, bf16[2,128,1024]{2,1,0:T(8,128)(2,1)S(1)}, u32[]{:S(2)}, u32[]{:S(2)}) collective-permute-start(bf16[2,128,1024]{2,1,0:T(8,128)(2,1)S(1)} %pad_maximum_fusion.2), channel_id=1, source_target_pairs={{0,2},{1,3},{2,0},{3,1},{4,6},{5,7},{6,4},{7,5},{8,10},{9,11},{10,... | collective-permute-start | bytes 1572872 | tf_op jit(solution)/shard_map/cond/branch_1_fun/ppermute | solution.py:466
  57.7 16.1 %collective-permute-start.1 = (bf16[2,128,1024]{2,1,0:T(8,128)(2,1)S(1)}, bf16[2,128,1024]{2,1,0:T(8,128)(2,1)S(1)}, u32[]{:S(2)}, u32[]{:S(2)}) collective-permute-start(bf16[2,128,1024]{2,1,0:T(8,128)(2,1)S(1)} %pad_maximum_fusion.1), channel_id=1, source_target_pairs={{0,4},{1,5},{2,6},{3,7},{4,0},{5,1},{6,2},{7,3},{8,12},{9,13},{10,... | collective-permute-start | bytes 1572872 | tf_op jit(solution)/shard_map/cond/branch_1_fun/ppermute | solution.py:466
  61.1 21.9 %collective-permute-start.11 = (bf16[2,128,1024]{2,1,0:T(8,128)(2,1)S(1)}, bf16[2,128,1024]{2,1,0:T(8,128)(2,1)S(1)}, u32[]{:S(2)}, u32[]{:S(2)}) collective-permute-start(bf16[2,128,1024]{2,1,0:T(8,128)(2,1)S(1)} %pad_maximum_fusion.4), channel_id=1, source_target_pairs={{0,4},{1,5},{2,6},{3,7},{4,0},{5,1},{6,2},{7,3},{8,12},{9,13},{10,... | collective-permute-start | bytes 1572872 | tf_op jit(solution)/shard_map/cond/branch_1_fun/ppermute | solution.py:466
  62.7 19.1 %collective-permute-start.13 = (bf16[2,128,1024]{2,1,0:T(8,128)(2,1)S(1)}, bf16[2,128,1024]{2,1,0:T(8,128)(2,1)S(1)}, u32[]{:S(2)}, u32[]{:S(2)}) collective-permute-start(bf16[2,128,1024]{2,1,0:T(8,128)(2,1)S(1)} %pad_maximum_fusion.5), channel_id=1, source_target_pairs={{0,2},{1,3},{2,0},{3,1},{4,6},{5,7},{6,4},{7,5},{8,10},{9,11},{10,... | collective-permute-start | bytes 1572872 | tf_op jit(solution)/shard_map/cond/branch_1_fun/ppermute | solution.py:466
  75.4 26.7 %collective-permute-start.4 = (bf16[4,128,2048]{2,1,0:T(8,128)(2,1)}, bf16[4,128,2048]{2,1,0:T(8,128)(2,1)}, u32[]{:S(2)}, u32[]{:S(2)}) collective-permute-start(bf16[4,128,2048]{2,1,0:T(8,128)(2,1)} %maximum_maximum_fusion), channel_id=1, source_target_pairs={{0,1},{1,0},{2,3},{3,2},{4,5},{5,4},{6,7},{7,6},{8,9},{9,8},{10,11... | collective-permute-start | bytes 6291464 | tf_op jit(solution)/shard_map/cond/branch_1_fun/ppermute | solution.py:466
  75.4 9.1 %collective-permute-start.7 = (bf16[64,512]{1,0:T(8,128)(2,1)S(1)}, bf16[64,512]{1,0:T(8,128)(2,1)S(1)}, u32[]{:S(2)}, u32[]{:S(2)}) collective-permute-start(bf16[64,512]{1,0:T(8,128)(2,1)S(1)} %bitcast.223), channel_id=1, source_target_pairs={{0,1},{1,0},{2,3},{3,2},{4,5},{5,4},{6,7},{7,6},{8,9},{9,8},{10,11... | collective-permute-start | bytes 196616 | tf_op jit(solution)/shard_map/cond/branch_1_fun/ppermute | solution.py:466
  84.5 21.2 %collective-permute-start.14 = (bf16[4,128,2048]{2,1,0:T(8,128)(2,1)}, bf16[4,128,2048]{2,1,0:T(8,128)(2,1)}, u32[]{:S(2)}, u32[]{:S(2)}) collective-permute-start(bf16[4,128,2048]{2,1,0:T(8,128)(2,1)} %maximum_maximum_fusion.1), channel_id=1, source_target_pairs={{0,1},{1,0},{2,3},{3,2},{4,5},{5,4},{6,7},{7,6},{8,9},{9,8},{10,11... | collective-permute-start | bytes 6291464 | tf_op jit(solution)/shard_map/cond/branch_1_fun/ppermute | solution.py:466
  84.6 6.0 %collective-permute-start.8 = (bf16[128,512]{1,0:T(8,128)(2,1)S(1)}, bf16[128,512]{1,0:T(8,128)(2,1)S(1)}, u32[]{:S(2)}, u32[]{:S(2)}) collective-permute-start(bf16[128,512]{1,0:T(8,128)(2,1)S(1)} %pad_maximum_fusion.7), channel_id=1, source_target_pairs={{0,2},{1,3},{2,0},{3,1},{4,6},{5,7},{6,4},{7,5},{8,10},{9,11},{10,... | collective-permute-start | bytes 393224 | tf_op jit(solution)/shard_map/cond/branch_1_fun/ppermute | solution.py:466
  90.6 8.2 %collective-permute-start.9 = (bf16[256,512]{1,0:T(8,128)(2,1)S(1)}, bf16[256,512]{1,0:T(8,128)(2,1)}, u32[]{:S(2)}, u32[]{:S(2)}) collective-permute-start(bf16[256,512]{1,0:T(8,128)(2,1)S(1)} %pad_maximum_fusion.6), channel_id=1, source_target_pairs={{0,4},{1,5},{2,6},{3,7},{4,0},{5,1},{6,2},{7,3},{8,12},{9,13},{10,... | collective-permute-start | bytes 786440 | tf_op jit(solution)/shard_map/cond/branch_1_fun/ppermute | solution.py:466
  92.2 23.9 %all-to-all-start = ((bf16[8,64,1408]{2,1,0:T(8,128)(2,1)}), bf16[8,64,1408]{2,1,0:T(8,128)(2,1)}, u32[]{:S(2)}, u32[]{:S(2)}) async-start(bf16[8,64,1408]{2,1,0:T(8,128)(2,1)} %get-tuple-element.72), calls=%async_computation | async-start | bytes 2883584 | tf_op jit(solution)/shard_map/cond/branch_1_fun/all_to_all | solution.py:587
  116.1 173.1 %all-gather.11.cloned.1.call-start = ((), (), s32[]{:S(2)}) async-start(), calls=%async_computation.13 | async-start | bytes 3604480 | tf_op jit(solution)/shard_map/all_gather | solution.py:695
  120.4 62.5 %copy-start.44 = (f32[256]{0:T(256)}, f32[256]{0:T(256)S(1)}, u32[]{:S(2)}) copy-start(f32[256]{0:T(256)S(1)} %get-tuple-element.357) | copy-start | bytes 3076
  120.4 62.5 %copy-start.45 = (f32[256]{0:T(256)}, f32[256]{0:T(256)S(1)}, u32[]{:S(2)}) copy-start(f32[256]{0:T(256)S(1)} %get-tuple-element.358) | copy-start | bytes 3076
  182.8 252.3 %reduce-scatter.8.cloned.1.call-start = ((), (), s32[]{:S(2)}) async-start(), calls=%async_computation.15 | async-start | bytes 3604480 | tf_op jit(solution)/shard_map/reduce_scatter | solution.py:752
  187.5 4.2 collective-permute-start.15
  193.0 14.0 %collective-permute-start.16 = (bf16[2,128,1024]{2,1,0:T(8,128)(2,1)S(1)}, bf16[2,128,1024]{2,1,0:T(8,128)(2,1)S(1)}, u32[]{:S(2)}, u32[]{:S(2)}) collective-permute-start(bf16[2,128,1024]{2,1,0:T(8,128)(2,1)S(1)} %pad_maximum_fusion.11), channel_id=1, source_target_pairs={{0,2},{1,3},{2,0},{3,1},{4,6},{5,7},{6,4},{7,5},{8,10},{9,11},{10,... | collective-permute-start | bytes 1572872 | tf_op jit(solution)/shard_map/cond/branch_1_fun/ppermute | solution.py:466
  193.1 14.0 %collective-permute-start.18 = (bf16[2,128,1024]{2,1,0:T(8,128)(2,1)S(1)}, bf16[2,128,1024]{2,1,0:T(8,128)(2,1)S(1)}, u32[]{:S(2)}, u32[]{:S(2)}) collective-permute-start(bf16[2,128,1024]{2,1,0:T(8,128)(2,1)S(1)} %slice.381), channel_id=1, source_target_pairs={{0,4},{1,5},{2,6},{3,7},{4,0},{5,1},{6,2},{7,3},{8,12},{9,13},{10,... | collective-permute-start | bytes 1572872 | tf_op jit(solution)/shard_map/cond/branch_1_fun/ppermute | solution.py:466
  207.3 7.7 %collective-permute-start.17 = (bf16[1,128,1024]{2,1,0:T(8,128)(2,1)S(1)}, bf16[1,128,1024]{2,1,0:T(8,128)(2,1)S(1)}, u32[]{:S(2)}, u32[]{:S(2)}) collective-permute-start(bf16[1,128,1024]{2,1,0:T(8,128)(2,1)S(1)} %get-tuple-element.401), channel_id=1, source_target_pairs={{0,4},{1,5},{2,6},{3,7},{4,0},{5,1},{6,2},{7,3},{8,12},{9,13},{10,... | collective-permute-start | bytes 786440 | tf_op jit(solution)/shard_map/cond/branch_1_fun/ppermute | solution.py:466
  208.9 7.3 %collective-permute-start.19 = (bf16[1,128,1024]{2,1,0:T(8,128)(2,1)S(1)}, bf16[1,128,1024]{2,1,0:T(8,128)(2,1)S(1)}, u32[]{:S(2)}, u32[]{:S(2)}) collective-permute-start(bf16[1,128,1024]{2,1,0:T(8,128)(2,1)S(1)} %get-tuple-element.402), channel_id=1, source_target_pairs={{0,2},{1,3},{2,0},{3,1},{4,6},{5,7},{6,4},{7,5},{8,10},{9,11},{10,... | collective-permute-start | bytes 786440 | tf_op jit(solution)/shard_map/cond/branch_1_fun/ppermute | solution.py:466
  216.9 6.6 %collective-permute-start.22 = (bf16[1,128,1024]{2,1,0:T(8,128)(2,1)S(1)}, bf16[1,128,1024]{2,1,0:T(8,128)(2,1)S(1)}, u32[]{:S(2)}, u32[]{:S(2)}) collective-permute-start(bf16[1,128,1024]{2,1,0:T(8,128)(2,1)S(1)} %get-tuple-element.406), channel_id=1, source_target_pairs={{0,4},{1,5},{2,6},{3,7},{4,0},{5,1},{6,2},{7,3},{8,12},{9,13},{10,... | collective-permute-start | bytes 786440 | tf_op jit(solution)/shard_map/cond/branch_1_fun/ppermute | solution.py:466
  217.5 7.3 %collective-permute-start.20 = (bf16[1,128,1024]{2,1,0:T(8,128)(2,1)S(1)}, bf16[1,128,1024]{2,1,0:T(8,128)(2,1)S(1)}, u32[]{:S(2)}, u32[]{:S(2)}) collective-permute-start(bf16[1,128,1024]{2,1,0:T(8,128)(2,1)S(1)} %get-tuple-element.405), channel_id=1, source_target_pairs={{0,2},{1,3},{2,0},{3,1},{4,6},{5,7},{6,4},{7,5},{8,10},{9,11},{10,... | collective-permute-start | bytes 786440 | tf_op jit(solution)/shard_map/cond/branch_1_fun/ppermute | solution.py:466
  223.6 11.5 %collective-permute-start.23 = (bf16[2,128,1024]{2,1,0:T(8,128)(2,1)S(1)}, bf16[2,128,1024]{2,1,0:T(8,128)(2,1)S(1)}, u32[]{:S(2)}, u32[]{:S(2)}) collective-permute-start(bf16[2,128,1024]{2,1,0:T(8,128)(2,1)S(1)} %pad_maximum_fusion.13), channel_id=1, source_target_pairs={{0,2},{1,3},{2,0},{3,1},{4,6},{5,7},{6,4},{7,5},{8,10},{9,11},{10,... | collective-permute-start | bytes 1572872 | tf_op jit(solution)/shard_map/cond/branch_1_fun/ppermute | solution.py:466
  224.9 10.9 %collective-permute-start.21 = (bf16[2,128,1024]{2,1,0:T(8,128)(2,1)S(1)}, bf16[2,128,1024]{2,1,0:T(8,128)(2,1)S(1)}, u32[]{:S(2)}, u32[]{:S(2)}) collective-permute-start(bf16[2,128,1024]{2,1,0:T(8,128)(2,1)S(1)} %pad_maximum_fusion.12), channel_id=1, source_target_pairs={{0,4},{1,5},{2,6},{3,7},{4,0},{5,1},{6,2},{7,3},{8,12},{9,13},{10,... | collective-permute-start | bytes 1572872 | tf_op jit(solution)/shard_map/cond/branch_1_fun/ppermute | solution.py:466
  236.0 4.2 collective-permute-start.24
  289.2 161.3 %reduce-scatter.6.cloned.1.call-start = ((), (), s32[]{:S(2)}) async-start(), calls=%async_computation.14 | async-start | bytes 7208960 | tf_op jit(solution)/shard_map/reduce_scatter | solution.py:590
  312.1 202.5 %reduce-scatter.10.cloned.1.call-start = ((), (), s32[]{:S(2)}) async-start(), calls=%async_computation.16 | async-start | bytes 1310720 | tf_op jit(solution)/shard_map/reduce_scatter | solution.py:590
  329.3 4.2 collective-permute-start.25
  329.3 8.4 %collective-permute-start.35 = (bf16[4,128,2048]{2,1,0:T(8,128)(2,1)S(1)}, bf16[4,128,2048]{2,1,0:T(8,128)(2,1)S(1)}, u32[]{:S(2)}, u32[]{:S(2)}) collective-permute-start(bf16[4,128,2048]{2,1,0:T(8,128)(2,1)S(1)} %bitcast.249), channel_id=1, source_target_pairs={{0,1},{1,0},{2,3},{3,2},{4,5},{5,4},{6,7},{7,6},{8,9},{9,8},{10,11... | collective-permute-start | bytes 6291464 | tf_op jit(solution)/shard_map/cond/branch_1_fun/ppermute | solution.py:466
  334.7 14.8 %collective-permute-start.26 = (bf16[2,128,1024]{2,1,0:T(8,128)(2,1)S(1)}, bf16[2,128,1024]{2,1,0:T(8,128)(2,1)S(1)}, u32[]{:S(2)}, u32[]{:S(2)}) collective-permute-start(bf16[2,128,1024]{2,1,0:T(8,128)(2,1)S(1)} %pad_maximum_fusion.15), channel_id=1, source_target_pairs={{0,2},{1,3},{2,0},{3,1},{4,6},{5,7},{6,4},{7,5},{8,10},{9,11},{10,... | collective-permute-start | bytes 1572872 | tf_op jit(solution)/shard_map/cond/branch_1_fun/ppermute | solution.py:466
  336.3 14.8 %collective-permute-start.28 = (bf16[2,128,1024]{2,1,0:T(8,128)(2,1)S(1)}, bf16[2,128,1024]{2,1,0:T(8,128)(2,1)S(1)}, u32[]{:S(2)}, u32[]{:S(2)}) collective-permute-start(bf16[2,128,1024]{2,1,0:T(8,128)(2,1)S(1)} %slice.396), channel_id=1, source_target_pairs={{0,4},{1,5},{2,6},{3,7},{4,0},{5,1},{6,2},{7,3},{8,12},{9,13},{10,... | collective-permute-start | bytes 1572872 | tf_op jit(solution)/shard_map/cond/branch_1_fun/ppermute | solution.py:466
  339.0 21.8 %collective-permute-start.36 = (bf16[2,128,1024]{2,1,0:T(8,128)(2,1)S(1)}, bf16[2,128,1024]{2,1,0:T(8,128)(2,1)S(1)}, u32[]{:S(2)}, u32[]{:S(2)}) collective-permute-start(bf16[2,128,1024]{2,1,0:T(8,128)(2,1)S(1)} %pad_maximum_fusion.18), channel_id=1, source_target_pairs={{0,2},{1,3},{2,0},{3,1},{4,6},{5,7},{6,4},{7,5},{8,10},{9,11},{10,... | collective-permute-start | bytes 1572872 | tf_op jit(solution)/shard_map/cond/branch_1_fun/ppermute | solution.py:466
  339.6 22.7 %collective-permute-start.38 = (bf16[2,128,1024]{2,1,0:T(8,128)(2,1)S(1)}, bf16[2,128,1024]{2,1,0:T(8,128)(2,1)S(1)}, u32[]{:S(2)}, u32[]{:S(2)}) collective-permute-start(bf16[2,128,1024]{2,1,0:T(8,128)(2,1)S(1)} %slice.411), channel_id=1, source_target_pairs={{0,4},{1,5},{2,6},{3,7},{4,0},{5,1},{6,2},{7,3},{8,12},{9,13},{10,... | collective-permute-start | bytes 1572872 | tf_op jit(solution)/shard_map/cond/branch_1_fun/ppermute | solution.py:466
  351.2 16.7 %collective-permute-start.27 = (bf16[1,128,1024]{2,1,0:T(8,128)(2,1)S(1)}, bf16[1,128,1024]{2,1,0:T(8,128)(2,1)S(1)}, u32[]{:S(2)}, u32[]{:S(2)}) collective-permute-start(bf16[1,128,1024]{2,1,0:T(8,128)(2,1)S(1)} %get-tuple-element.415), channel_id=1, source_target_pairs={{0,4},{1,5},{2,6},{3,7},{4,0},{5,1},{6,2},{7,3},{8,12},{9,13},{10,... | collective-permute-start | bytes 786440 | tf_op jit(solution)/shard_map/cond/branch_1_fun/ppermute | solution.py:466
  352.8 15.2 %collective-permute-start.29 = (bf16[1,128,1024]{2,1,0:T(8,128)(2,1)S(1)}, bf16[1,128,1024]{2,1,0:T(8,128)(2,1)S(1)}, u32[]{:S(2)}, u32[]{:S(2)}) collective-permute-start(bf16[1,128,1024]{2,1,0:T(8,128)(2,1)S(1)} %get-tuple-element.416), channel_id=1, source_target_pairs={{0,2},{1,3},{2,0},{3,1},{4,6},{5,7},{6,4},{7,5},{8,10},{9,11},{10,... | collective-permute-start | bytes 786440 | tf_op jit(solution)/shard_map/cond/branch_1_fun/ppermute | solution.py:466
  362.5 9.9 %collective-permute-start.37 = (bf16[1,128,1024]{2,1,0:T(8,128)(2,1)S(1)}, bf16[1,128,1024]{2,1,0:T(8,128)(2,1)S(1)}, u32[]{:S(2)}, u32[]{:S(2)}) collective-permute-start(bf16[1,128,1024]{2,1,0:T(8,128)(2,1)S(1)} %get-tuple-element.411), channel_id=1, source_target_pairs={{0,4},{1,5},{2,6},{3,7},{4,0},{5,1},{6,2},{7,3},{8,12},{9,13},{10,... | collective-permute-start | bytes 786440 | tf_op jit(solution)/shard_map/cond/branch_1_fun/ppermute | solution.py:466
  364.0 8.4 %collective-permute-start.39 = (bf16[1,128,1024]{2,1,0:T(8,128)(2,1)S(1)}, bf16[1,128,1024]{2,1,0:T(8,128)(2,1)S(1)}, u32[]{:S(2)}, u32[]{:S(2)}) collective-permute-start(bf16[1,128,1024]{2,1,0:T(8,128)(2,1)S(1)} %get-tuple-element.412), channel_id=1, source_target_pairs={{0,2},{1,3},{2,0},{3,1},{4,6},{5,7},{6,4},{7,5},{8,10},{9,11},{10,... | collective-permute-start | bytes 786440 | tf_op jit(solution)/shard_map/cond/branch_1_fun/ppermute | solution.py:466
  374.2 7.4 %collective-permute-start.32 = (bf16[1,128,1024]{2,1,0:T(8,128)(2,1)S(1)}, bf16[1,128,1024]{2,1,0:T(8,128)(2,1)S(1)}, u32[]{:S(2)}, u32[]{:S(2)}) collective-permute-start(bf16[1,128,1024]{2,1,0:T(8,128)(2,1)S(1)} %get-tuple-element.423), channel_id=1, source_target_pairs={{0,4},{1,5},{2,6},{3,7},{4,0},{5,1},{6,2},{7,3},{8,12},{9,13},{10,... | collective-permute-start | bytes 786440 | tf_op jit(solution)/shard_map/cond/branch_1_fun/ppermute | solution.py:466
  375.7 7.2 %collective-permute-start.30 = (bf16[1,128,1024]{2,1,0:T(8,128)(2,1)S(1)}, bf16[1,128,1024]{2,1,0:T(8,128)(2,1)S(1)}, u32[]{:S(2)}, u32[]{:S(2)}) collective-permute-start(bf16[1,128,1024]{2,1,0:T(8,128)(2,1)S(1)} %get-tuple-element.422), channel_id=1, source_target_pairs={{0,2},{1,3},{2,0},{3,1},{4,6},{5,7},{6,4},{7,5},{8,10},{9,11},{10,... | collective-permute-start | bytes 786440 | tf_op jit(solution)/shard_map/cond/branch_1_fun/ppermute | solution.py:466
  381.6 12.4 %collective-permute-start.33 = (bf16[2,128,1024]{2,1,0:T(8,128)(2,1)S(1)}, bf16[2,128,1024]{2,1,0:T(8,128)(2,1)S(1)}, u32[]{:S(2)}, u32[]{:S(2)}) collective-permute-start(bf16[2,128,1024]{2,1,0:T(8,128)(2,1)S(1)} %pad_maximum_fusion.17), channel_id=1, source_target_pairs={{0,2},{1,3},{2,0},{3,1},{4,6},{5,7},{6,4},{7,5},{8,10},{9,11},{10,... | collective-permute-start | bytes 1572872 | tf_op jit(solution)/shard_map/cond/branch_1_fun/ppermute | solution.py:466
  382.9 11.7 %collective-permute-start.31 = (bf16[2,128,1024]{2,1,0:T(8,128)(2,1)S(1)}, bf16[2,128,1024]{2,1,0:T(8,128)(2,1)S(1)}, u32[]{:S(2)}, u32[]{:S(2)}) collective-permute-start(bf16[2,128,1024]{2,1,0:T(8,128)(2,1)S(1)} %pad_maximum_fusion.16), channel_id=1, source_target_pairs={{0,4},{1,5},{2,6},{3,7},{4,0},{5,1},{6,2},{7,3},{8,12},{9,13},{10,... | collective-permute-start | bytes 1572872 | tf_op jit(solution)/shard_map/cond/branch_1_fun/ppermute | solution.py:466
  394.9 4.2 collective-permute-start.34
  450.5 30.9 %all-to-all-start.3 = ((bf16[8,64,1408]{2,1,0:T(8,128)(2,1)}), bf16[8,64,1408]{2,1,0:T(8,128)(2,1)}, u32[]{:S(2)}, u32[]{:S(2)}) async-start(bf16[8,64,1408]{2,1,0:T(8,128)(2,1)} %bitcast.202), calls=%async_computation.5 | async-start | bytes 2883584 | tf_op jit(solution)/shard_map/all_to_all | solution.py:594
  454.8 107.9 %reduce-scatter.12.cloned.1.call-start = ((), (), s32[]{:S(2)}) async-start(), calls=%async_computation.17 | async-start | bytes 4014080 | tf_op jit(solution)/shard_map/reduce_scatter | solution.py:590
  489.6 94.0 %reduce-scatter.14.cloned.1.call-start = ((), (), s32[]{:S(2)}) async-start(), calls=%async_computation.18 | async-start | bytes 1310720 | tf_op jit(solution)/shard_map/reduce_scatter | solution.py:809
  514.6 55.1 %copy-start.58 = (bf16[64]{0:T(256)(128)(2,1)S(1)}, bf16[64]{0:T(256)(128)(2,1)}, u32[]{:S(2)}) copy-start(bf16[64]{0:T(256)(128)(2,1)} %param.44) | copy-start | bytes 388
  514.6 4.4 collective-permute-start.40
  526.0 14.3 %collective-permute-start.41 = (bf16[2,128,1024]{2,1,0:T(8,128)(2,1)}, bf16[2,128,1024]{2,1,0:T(8,128)(2,1)S(1)}, u32[]{:S(2)}, u32[]{:S(2)}) collective-permute-start(bf16[2,128,1024]{2,1,0:T(8,128)(2,1)} %pad_maximum_fusion.19), channel_id=1, source_target_pairs={{0,2},{1,3},{2,0},{3,1},{4,6},{5,7},{6,4},{7,5},{8,10},{9,11},{10,... | collective-permute-start | bytes 1572872 | tf_op jit(solution)/shard_map/cond/branch_1_fun/ppermute | solution.py:466
  527.9 14.0 %collective-permute-start.43 = (bf16[2,128,1024]{2,1,0:T(8,128)(2,1)}, bf16[2,128,1024]{2,1,0:T(8,128)(2,1)}, u32[]{:S(2)}, u32[]{:S(2)}) collective-permute-start(bf16[2,128,1024]{2,1,0:T(8,128)(2,1)} %slice.422), channel_id=1, source_target_pairs={{0,4},{1,5},{2,6},{3,7},{4,0},{5,1},{6,2},{7,3},{8,12},{9,13},{10,... | collective-permute-start | bytes 1572872 | tf_op jit(solution)/shard_map/cond/branch_1_fun/ppermute | solution.py:466
  529.4 10.6 %collective-permute-start.45 = (f32[128,128]{1,0:T(8,128)S(1)}, f32[128,128]{1,0:T(8,128)S(1)}, u32[]{:S(2)}, u32[]{:S(2)}) collective-permute-start(f32[128,128]{1,0:T(8,128)S(1)} %fusion.29), channel_id=1, source_target_pairs={{0,16},{8,24},{16,0},{24,8},{1,17},{9,25},{17,1},{25,9},{2,18},{10... | collective-permute-start | bytes 196616 | tf_op jit(solution)/shard_map/cond/branch_1_fun/ppermute | solution.py:466
  544.1 14.9 %collective-permute-start.42 = (bf16[1,128,1024]{2,1,0:T(8,128)(2,1)}, bf16[1,128,1024]{2,1,0:T(8,128)(2,1)S(1)}, u32[]{:S(2)}, u32[]{:S(2)}) collective-permute-start(bf16[1,128,1024]{2,1,0:T(8,128)(2,1)} %get-tuple-element.431), channel_id=1, source_target_pairs={{0,4},{1,5},{2,6},{3,7},{4,0},{5,1},{6,2},{7,3},{8,12},{9,13},{10,... | collective-permute-start | bytes 786440 | tf_op jit(solution)/shard_map/cond/branch_1_fun/ppermute | solution.py:466
  545.5 13.5 %collective-permute-start.44 = (bf16[1,128,1024]{2,1,0:T(8,128)(2,1)}, bf16[1,128,1024]{2,1,0:T(8,128)(2,1)}, u32[]{:S(2)}, u32[]{:S(2)}) collective-permute-start(bf16[1,128,1024]{2,1,0:T(8,128)(2,1)} %get-tuple-element.432), channel_id=1, source_target_pairs={{0,2},{1,3},{2,0},{3,1},{4,6},{5,7},{6,4},{7,5},{8,10},{9,11},{10,... | collective-permute-start | bytes 786440 | tf_op jit(solution)/shard_map/cond/branch_1_fun/ppermute | solution.py:466
  546.1 9.4 %collective-permute-start.46 = (f32[64,128]{1,0:T(8,128)S(1)}, f32[64,128]{1,0:T(8,128)S(1)}, u32[]{:S(2)}, u32[]{:S(2)}) collective-permute-start(f32[64,128]{1,0:T(8,128)S(1)} %slice_select_fusion), channel_id=1, source_target_pairs={{0,8},{8,0},{16,24},{24,16},{1,9},{9,1},{17,25},{25,17},{2,10},{10... | collective-permute-start | bytes 98312 | tf_op jit(solution)/shard_map/cond/branch_1_fun/ppermute | solution.py:466
  547.6 10.3 %all-to-all-start.1 = ((bf16[8,64,256]{2,1,0:T(8,128)(2,1)}), bf16[8,64,256]{2,1,0:T(8,128)(2,1)S(1)}, u32[]{:S(2)}, u32[]{:S(2)}) async-start(bf16[8,64,256]{2,1,0:T(8,128)(2,1)} %bitcast.214), calls=%async_computation.1 | async-start | bytes 524288 | tf_op jit(solution)/shard_map/cond/branch_1_fun/all_to_all | solution.py:594
  565.3 20.1 %all-to-all-start.4 = ((bf16[8,64,784]{2,1,0:T(8,128)(2,1)}), bf16[8,64,784]{2,1,0:T(8,128)(2,1)S(1)}, u32[]{:S(2)}, u32[]{:S(2)}) async-start(bf16[8,64,784]{2,1,0:T(8,128)(2,1)} %bitcast.99), calls=%async_computation.8 | async-start | bytes 1835008 | tf_op jit(solution)/shard_map/all_to_all | solution.py:594
  (60 other events, 678.1 us)
Sparse Core Ops, SparseCore 0:
  9.7 30.6 all-gather.4
  42.5 80.9 all-gather.6
  125.1 105.0 all-gather.8
  231.7 57.4 all-gather.10
  291.3 54.8 reduce-scatter.7
  348.4 102.1 reduce-scatter.5
  452.8 27.6 reduce-scatter.9
  489.8 63.9 reduce-scatter.11
  556.0 27.5 reduce-scatter.13

commit v4 on v3

--- a/solution.py
+++ b/solution.py
@@ -20,6 +20,15 @@
 
 def mm(left, right, dims):
     return lax.dot_general(left, right, dims, preferred_element_type=F32)
+
+
+def in_two(values):
+    high = values.astype(BF16)
+    return high, (values - high.astype(F32)).astype(BF16)
+
+
+def mm_two(left, right, dims):
+    return mm(left[0], right[0], dims) + (mm(left[1], right[0], dims) + mm(left[0], right[1], dims))
 
 
 def packed(block, heads, head_dim, parts):
@@ -72,9 +81,9 @@
 
 def forward_kernel(
     heads, head_dim, parts,
-    slot_ref, queries_ref, keys_ref, values_ref, rate_ref, again_ref, again_wide_ref,
+    slot_ref, inputs_ref, rate_ref, again_ref, again_wide_ref,
     start_ref, start_bias_ref, gain_ref, shift_ref,
-    out_ref, sums_ref, normed_ref, spread_ref, grad_ref, rebuilt_ref, respread_ref, mix_ref, weight_ref,
+    out_ref, sums_ref, kept_ref, spreads_ref, mix_ref, weight_ref,
     state, bias,
 ):
     chains = rate_ref.shape[-1] // MINI
@@ -87,43 +96,49 @@
         state[...] = jnp.zeros_like(state)
         bias[...] = jnp.zeros_like(bias)
 
-    all_queries = packed(queries_ref[...], heads, head_dim, parts)
-    all_keys = packed(keys_ref[...], heads, head_dim, parts)
-    all_values = packed(values_ref[...], heads, head_dim, parts)
+    width = heads * head_dim
+    all_queries, all_keys, all_values = (
+        packed(inputs_ref[:, n * width : (n + 1) * width], heads, head_dim, parts) for n in range(3)
+    )
     weight = state[...]
     offset = bias[...]
     results = []
     for j in range(parts):
         query, key, value = all_queries[j], all_keys[j], all_values[j]
         rate = rate_ref[0, j : j + 1, :]
-        low_key, low_query = key.astype(BF16), query.astype(BF16)
-        wide_key = spread_out(low_key, spread, chains)
-        wide_query = spread_out(low_query, spread, chains)
-        mix = ((mm(low_key, low_query, TN) + 1.0) * scale).astype(BF16)
+        two_keys, two_queries = in_two(key), in_two(query)
+        wide_keys = [spread_out(k, spread, chains) for k in two_keys]
+        wide_both = [
+            jnp.concatenate([k, spread_out(q, spread, chains)], axis=1)
+            for k, q in zip(wide_keys, two_queries)
+        ]
+        mix = in_two((mm_two(two_keys, two_queries, TN) + 1.0) * scale)
         weight = jnp.where(again_wide_ref[0, j : j + 1, :] > 0.0, start_ref[...], weight)
         offset = jnp.where(again_ref[0, j : j + 1, :] > 0.0, start_bias_ref[...], offset)
-        low_weight = weight.astype(BF16)
-        first = mm(low_weight, wide_key, NN) + offset
+        two_weights = in_two(weight)
+        both = mm_two(two_weights, wide_both, NN)
+        lanes = offset.shape[1]
+        first = both[:, :lanes] + offset
         center = first - mean0(first)
         inverse = lax.rsqrt(mean0(center * center) + EPSILON)
         normed = center * inverse
         residue = (normed * gain + shift - (value - key)) * gain
         inner = (residue - mean0(residue) - normed * mean0(residue * normed)) * inverse
-        rated = (inner * rate).astype(BF16)
-        combined = mm(low_weight, wide_query, NN) + offset - mm(rated, mix, NN)
+        rated = in_two(inner * rate)
+        combined = both[:, lanes:] + offset - mm_two(rated, mix, NN)
         centered = combined - mean0(combined)
         inverse_out = lax.rsqrt(mean0(centered * centered) + EPSILON)
         rebuilt = centered * inverse_out
         results.append(query + rebuilt * gain + shift)
-        weight = weight - mm(rated, wide_key, NT) * (1.0 / MINI)
-        offset = offset - mm(rated, ones, NN)
-        normed_ref[0, j] = normed
-        grad_ref[0, j] = inner
-        rebuilt_ref[0, j] = rebuilt
-        spread_ref[0, j : j + 1, :] = inverse
-        respread_ref[0, j : j + 1, :] = inverse_out
-        mix_ref[0, j] = mix
-        weight_ref[0, j] = low_weight
+        weight = weight - mm_two(rated, wide_keys, NT) * (1.0 / MINI)
+        offset = offset - (mm(rated[0], ones, NN) + mm(rated[1], ones, NN))
+        kept_ref[0, 0, j] = normed
+        kept_ref[0, 1, j] = inner
+        kept_ref[0, 2, j] = rebuilt
+        spreads_ref[0, j : j + 1, :] = inverse
+        spreads_ref[0, parts + j : parts + j + 1, :] = inverse_out
+        mix_ref[0, j] = mix[0]
+        weight_ref[0, j] = two_weights[0]
     out = unpacked(results, heads)
     out_ref[...] = out
     sums_ref[:, 0:1] = jnp.sum(out, axis=1, keepdims=True)
@@ -141,10 +156,10 @@
 
 def backward_kernel(
     heads, head_dim, parts,
-    slot_ref, queries_ref, keys_ref, values_ref, pre_ref, post_ref, out_ref, token_ref,
+    slot_ref, inputs_ref, pre_ref, post_ref, out_ref, token_ref,
     rate_ref, again_ref, again_wide_ref, gain_ref, shift_ref,
-    normed_ref, spread_ref, grad_ref, rebuilt_ref, respread_ref, mix_ref, weight_ref,
-    inputs_ref, all_ref, dstart_ref, dstart_bias_ref, dgain_ref, dshift_ref,
+    kept_ref, spreads_ref, mix_ref, weight_ref,
+    all_ref, logits_ref, dstart_ref, dstart_bias_ref, dgain_ref, dshift_ref,
     state, bias,
 ):
     chains = rate_ref.shape[-1] // MINI
@@ -163,9 +178,10 @@
         dgain_ref[...] = jnp.zeros_like(dgain_ref)
         dshift_ref[...] = jnp.zeros_like(dshift_ref)
 
-    all_queries = packed(queries_ref[...], heads, head_dim, parts)
-    all_keys = packed(keys_ref[...], heads, head_dim, parts)
-    all_values = packed(values_ref[...], heads, head_dim, parts)
+    width = heads * head_dim
+    all_queries, all_keys, all_values = (
+        packed(inputs_ref[:, n * width : (n + 1) * width], heads, head_dim, parts) for n in range(3)
+    )
     center, inverse_all = token_ref[:, 0:1], token_ref[:, 1:2]
     along_post = (out_ref[...] - center) * inverse_all
     delta_post = (post_ref[...] - token_ref[:, 2:3] - along_post * token_ref[:, 3:4]) * inverse_all
@@ -178,8 +194,8 @@
     for j in reversed(range(parts)):
         query, key, value, delta = all_queries[j], all_keys[j], all_values[j], all_deltas[j]
         rate = rate_ref[0, j : j + 1, :]
-        normed, inner, rebuilt = normed_ref[0, j], grad_ref[0, j], rebuilt_ref[0, j]
-        inverse, inverse_out = spread_ref[0, j : j + 1, :], respread_ref[0, j : j + 1, :]
+        normed, inner, rebuilt = (kept_ref[0, n, j] for n in range(3))
+        inverse, inverse_out = (spreads_ref[0, n * parts + j : n * parts + j + 1, :] for n in range(2))
         mix, weight = mix_ref[0, j], weight_ref[0, j]
         low_key, low_query = key.astype(BF16), query.astype(BF16)
         wide_key = spread_out(low_key, spread, chains)
@@ -223,18 +239,15 @@
         dstart_bias = dstart_bias + jnp.where(again, doffset, 0.0)
         dweight = jnp.where(again_wide, 0.0, dweight)
         doffset = jnp.where(again, 0.0, doffset)
-    width = heads * head_dim
     for n, pieces in enumerate((dqueries, dkeys, dvalues)):
-        natural = unpacked(pieces, heads).astype(inputs_ref.dtype)
-        inputs_ref[:, n * width : (n + 1) * width] = natural
+        natural = unpacked(pieces, heads).astype(all_ref.dtype)
         all_ref[:, n * width : (n + 1) * width] = natural
     all_ref[:, 3 * width : 4 * width] = pre_ref[...]
     natural = unpacked(dlogits, heads)
-    spare = inputs_ref.shape[1] - 3 * width - heads
+    spare = logits_ref.shape[1] - heads
     if spare:
         natural = jnp.concatenate([natural, jnp.zeros((natural.shape[0], spare), F32)], axis=1)
-    inputs_ref[:, 3 * width :] = natural.astype(inputs_ref.dtype)
-    all_ref[:, 4 * width :] = natural.astype(all_ref.dtype)
+    logits_ref[...] = natural.astype(logits_ref.dtype)
     state[...] = dweight
     bias[...] = doffset
     dstart_ref[...] = dstart
@@ -252,9 +265,9 @@
     return jnp.bitwise_and(apart, 1) * (count // 2) + lax.shift_right_logical(apart, 1)
 
 
-def inner_forward(slot, queries, keys, values, rates, again, again_wide, start, start_bias, gain, shift, heads, head_dim, parts):
+def inner_forward(slot, projected, rates, again, again_wide, start, start_bias, gain, shift, heads, head_dim, parts):
     steps, _, lanes = rates.shape
-    tokens = queries.shape[0] // steps
+    tokens = projected.shape[0] // steps
     wide = start.shape[1]
     at_slot = pl.BlockSpec((tokens, heads * head_dim), lambda i, s: (place(i, s[0], steps), 0))
 
@@ -262,18 +275,17 @@
         return pl.BlockSpec((1,) + shape, lambda i, s: (i,) + (0,) * len(shape))
 
     saved = [
-        ((parts, head_dim, lanes), F32), ((parts, lanes), F32), ((parts, head_dim, lanes), F32),
-        ((parts, head_dim, lanes), F32), ((parts, lanes), F32),
+        ((3, parts, head_dim, lanes), F32), ((2 * parts, lanes), F32),
         ((parts, lanes, lanes), BF16), ((parts, head_dim, wide), BF16),
     ]
     return pl.pallas_call(
         functools.partial(forward_kernel, heads, head_dim, parts),
-        out_shape=[jax.ShapeDtypeStruct(queries.shape, F32), jax.ShapeDtypeStruct((steps * tokens, 2), F32)]
+        out_shape=[jax.ShapeDtypeStruct((steps * tokens, heads * head_dim), F32), jax.ShapeDtypeStruct((steps * tokens, 2), F32)]
         + [jax.ShapeDtypeStruct((steps,) + shape, kind) for shape, kind in saved],
         grid_spec=pltpu.PrefetchScalarGridSpec(
             num_scalar_prefetch=1,
             grid=(steps,),
-            in_specs=[at_slot] * 3
+            in_specs=[pl.BlockSpec((tokens, 3 * heads * head_dim), at_slot.index_map)]
             + [stepped(parts, lanes), stepped(parts, lanes), stepped(parts, wide)]
             + [whole(start.shape), whole(start_bias.shape), whole(gain.shape), whole(shift.shape)],
             out_specs=[at_slot, pl.BlockSpec((tokens, 2), at_slot.index_map)]
@@ -284,14 +296,14 @@
             dimension_semantics=("arbitrary",), vmem_limit_bytes=63 * 1024 * 1024
         ),
         name="inner_forward",
-    )(slot, queries, keys, values, rates, again, again_wide, start, start_bias, gain, shift)
-
-
-def inner_backward(slot, queries, keys, values, pre, deltas, outs, per_token, rates, again, again_wide, gain, shift, saved, heads, head_dim, parts):
+    )(slot, projected, rates, again, again_wide, start, start_bias, gain, shift)
+
+
+def inner_backward(slot, projected, pre, deltas, outs, per_token, rates, again, again_wide, gain, shift, saved, heads, head_dim, parts):
     steps, _, lanes = rates.shape
-    tokens = queries.shape[0] // steps
+    tokens = projected.shape[0] // steps
     wide = again_wide.shape[-1]
-    inputs = 3 * heads * head_dim + heads + -heads % 16
+    inputs, logits = 4 * heads * head_dim, heads + -heads % 16
     at_slot = pl.BlockSpec(
         (tokens, heads * head_dim), lambda i, s: (place(steps - 1 - i, s[0], steps), 0)
     )
@@ -303,7 +315,7 @@
         functools.partial(backward_kernel, heads, head_dim, parts),
         out_shape=[
             jax.ShapeDtypeStruct((steps * tokens, inputs), BF16),
-            jax.ShapeDtypeStruct((steps * tokens, inputs + heads * head_dim), BF16),
+            jax.ShapeDtypeStruct((steps * tokens, logits), BF16),
             jax.ShapeDtypeStruct((head_dim, wide), F32),
             jax.ShapeDtypeStruct((head_dim, lanes), F32),
             jax.ShapeDtypeStruct((head_dim, lanes), F32),
@@ -312,14 +324,15 @@
         grid_spec=pltpu.PrefetchScalarGridSpec(
             num_scalar_prefetch=1,
             grid=(steps,),
-            in_specs=[at_slot] * 6
+            in_specs=[pl.BlockSpec((tokens, 3 * heads * head_dim), at_slot.index_map)]
+            + [at_slot] * 3
             + [pl.BlockSpec((tokens, per_token.shape[1]), at_slot.index_map)]
             + [stepped(parts, lanes), stepped(parts, lanes), stepped(parts, wide)]
             + [whole(gain.shape), whole(shift.shape)]
             + [stepped(*array.shape[1:]) for array in saved],
             out_specs=[
                 pl.BlockSpec((tokens, inputs), at_slot.index_map),
-                pl.BlockSpec((tokens, inputs + heads * head_dim), at_slot.index_map),
+                pl.BlockSpec((tokens, logits), at_slot.index_map),
                 whole((head_dim, wide)),
             ]
             + [whole((head_dim, lanes))] * 3,
@@ -329,7 +342,7 @@
             dimension_semantics=("arbitrary",), vmem_limit_bytes=63 * 1024 * 1024
         ),
         name="inner_backward",
-    )(slot, queries, keys, values, pre, deltas, outs, per_token, rates, again, again_wide, gain, shift, *saved)
+    )(slot, projected, pre, deltas, outs, per_token, rates, again, again_wide, gain, shift, *saved)
 
 
 def cut_kernel(seq_count, kinds, *refs):
@@ -413,8 +426,9 @@
     sums_ref[:, 1:2] = jnp.sum(dnorm * norm, axis=1, keepdims=True)
 
 
-def branch_backward(delta, matrix, pre, out, per_token, scale, offset, block):
-    tokens, width = pre.shape
+def branch_backward(delta, matrix, projected, out, per_token, scale, offset, block):
+    tokens, width = out.shape
+    gate = pl.BlockSpec((block, width), lambda i: (i, 3))
 
     def by_block(array):
         return pl.BlockSpec((block, array.shape[1]), lambda i: (i, 0))
@@ -424,31 +438,30 @@
     return pl.pallas_call(
         branch_kernel,
         grid=(tokens // block,),
-        in_specs=[by_block(delta), whole(matrix.shape), by_block(pre), by_block(out), by_block(per_token)]
+        in_specs=[by_block(delta), whole(matrix.shape), gate, by_block(out), by_block(per_token)]
         + [whole((1, width))] * 2,
-        out_shape=[jax.ShapeDtypeStruct(pre.shape, BF16), jax.ShapeDtypeStruct(pre.shape, F32), sums, row, row],
-        out_specs=[by_block(pre), by_block(pre), by_block(sums), whole((1, width)), whole((1, width))],
+        out_shape=[jax.ShapeDtypeStruct(out.shape, BF16), jax.ShapeDtypeStruct(out.shape, F32), sums, row, row],
+        out_specs=[by_block(out), by_block(out), by_block(sums), whole((1, width)), whole((1, width))],
         compiler_params=pltpu.CompilerParams(
             dimension_semantics=("arbitrary",), vmem_limit_bytes=63 * 1024 * 1024
         ),
         name="branch_backward",
-    )(delta, matrix, pre, out, per_token, scale, offset)
-
-
-def spread_kernel(delta_ref, weight_ref, rate_ref, out_ref):
-    width = weight_ref.shape[1]
-    total = mm(delta_ref[:, :width], weight_ref[...], NT)
-    total = total + mm(delta_ref[:, width:], rate_ref[...], NT)
+    )(delta, matrix, projected, out, per_token, scale, offset)
+
+
+def spread_kernel(delta_ref, logits_ref, weight_ref, rate_ref, out_ref):
+    total = mm(delta_ref[...], weight_ref[...], NT) + mm(logits_ref[...], rate_ref[...], NT)
     out_ref[...] = total.astype(out_ref.dtype)
 
 
-def spread_back(delta, first, tokens, weight, rate, kind, block):
+def spread_back(delta, logits, first, tokens, weight, rate, kind, block):
     model = weight.shape[0]
     return pl.pallas_call(
         spread_kernel,
         grid=(model // block,),
         in_specs=[
             pl.BlockSpec((tokens, delta.shape[1]), lambda i: (first // tokens, 0)),
+            pl.BlockSpec((tokens, logits.shape[1]), lambda i: (first // tokens, 0)),
             pl.BlockSpec((block, weight.shape[1]), lambda i: (i, 0)),
             pl.BlockSpec((block, rate.shape[1]), lambda i: (i, 0)),
         ],
@@ -458,7 +471,7 @@
             dimension_semantics=("arbitrary",), vmem_limit_bytes=40 * 1024 * 1024
         ),
         name="spread_back",
-    )(delta, weight, rate)
+    )(delta, logits, weight, rate)
 
 
 def exchange(value, axis, bit):
@@ -695,7 +708,7 @@
     down_wide = lax.all_gather(
         jnp.pad(ffn_down_weight, ((0, spare), (0, 0))), "rows", axis=0, tiled=True
     )
-    queries, keys, values, gate_pre = (projected[:, n * width : (n + 1) * width] for n in range(4))
+    gate_pre = projected[:, 3 * width :]
     logits = jnp.dot(normed, rate_own, preferred_element_type=F32)
 
     def to_lanes(per_token):
@@ -707,7 +720,7 @@
     slot = me.astype(jnp.int32).reshape(1)
 
     inner_out, inner_sums, *saved = inner_forward(
-        slot, queries, keys, values, rates, again, again_wide, start, bias_lanes, gain_lanes,
+        slot, projected, rates, again, again_wide, start, bias_lanes, gain_lanes,
         shift_lanes, heads, head_dim, parts,
     )
 
@@ -750,7 +763,6 @@
     grad_down = token_grad(active, cot_all).astype(BF16)
     grad_down, down_wide = lax.optimization_barrier((grad_down, down_wide))
     grad_down = lax.psum_scatter(grad_down, "rows", scatter_dimension=0, tiled=True)
-    grad_down = grad_down[:unit_share].astype(F32)
     delta_active = lax.dot_general(cot_all, down_wide, NT, preferred_element_type=F32)
     delta_up = (delta_active * gate_value * sigmoid_gate).astype(BF16)
     delta_gate = (
@@ -758,7 +770,7 @@
     ).astype(BF16)
     delta_both = jnp.concatenate([delta_gate, delta_up], axis=1)
 
-    def out_of_ffn(own, away, own_down, away_down, residual, gain_ffn, cotangent):
+    def out_of_ffn(own, away, residual, gain_ffn, cotangent):
         delta_ffn = reduce_blocks(own, away, seq_bits)
         inverse_two = rms_inverse(residual)
         scaled_two = delta_ffn * gain_ffn
@@ -768,88 +780,86 @@
             - residual * inverse_two**3 * jnp.mean(scaled_two * residual, axis=-1, keepdims=True)
         )
         delta_branch = gather_blocks(delta_after.astype(BF16), seq_bits).reshape(-1, model)
-        block_out = restored(residual + reduce_blocks(own_down, away_down, seq_bits)).astype(BF16)
-        return delta_after, delta_branch, block_out
+        return delta_after, delta_branch
 
     grad_ffn = token_grad(ffn_in, delta_both).astype(BF16)
     delta_both, grad_ffn = lax.optimization_barrier((delta_both, grad_ffn))
     ffn_sums = row_sums(grad_ffn)
-    delta_after, delta_branch, block_out = apart(
-        out_of_ffn, *halves(delta_both, ffn_wide, NT), *halves(active, down_wide, NN), residual, gain_ffn,
-        cotangent,
+    delta_after, delta_branch = apart(
+        out_of_ffn, *halves(delta_both, ffn_wide, NT), residual, gain_ffn, cotangent
     )
 
     delta_pre, delta_norm, norm_sums, grad_post_scale, grad_post_shift = branch_backward(
-        delta_branch, out_own, gate_pre, inner_out, jnp.concatenate([post_mean, post_inverse], axis=1),
-        post_scale[None], post_offset[None], local,
-    )
-    grad_gate_weight = token_grad(normed, delta_pre).astype(BF16)
-    norm_sums, grad_gate_weight = lax.optimization_barrier((norm_sums, grad_gate_weight))
+        delta_branch, out_own, projected, inner_out, jnp.concatenate([post_mean, post_inverse], axis=1),
+        post_scale[None], post_offset[None], max(local, steps * local // 2),
+    )
     means = feature_mean(norm_sums)
-    grad_out = token_grad(gated, delta_branch).astype(BF16)
     per_token = jnp.concatenate([post_mean, post_inverse, means[0], means[1]], axis=1)
 
-    per_token, grad_out, grad_gate_weight, ffn_sums, grad_down = lax.optimization_barrier(
-        (per_token, grad_out, grad_gate_weight, ffn_sums, grad_down)
-    )
-    gate_sums = row_sums(grad_gate_weight)
     (
-        delta_inputs, delta_all,
+        delta_all, delta_logits,
         grad_start, grad_bias, grad_inner_gain, grad_inner_shift,
     ) = inner_backward(
-        slot, queries, keys, values, delta_pre, delta_norm, inner_out, per_token, rates, again, again_wide,
+        slot, projected, delta_pre, delta_norm, inner_out, per_token, rates, again, again_wide,
         gain_lanes, shift_lanes, saved, heads, head_dim, parts,
     )
-    ffn_parts = columns_out(ffn_sums)
-    delta_inputs, delta_all, ffn_parts = lax.optimization_barrier((delta_inputs, delta_all, ffn_parts))
-    grad_inputs = token_grad(normed, delta_inputs).astype(BF16)
-    delta_all, grad_inputs, grad_out = lax.optimization_barrier((delta_all, grad_inputs, grad_out))
-    input_sums = row_sums(grad_inputs)
-    if aligned:
-        grad_out = lax.psum_scatter(grad_out, "rows", scatter_dimension=0, tiled=True).astype(F32)
-
+    grad_inputs = token_grad(normed, delta_all).astype(BF16)
+    delta_all, grad_inputs = lax.optimization_barrier((delta_all, grad_inputs))
     half = delta_all.shape[0] // 2
     rate_wide = jnp.pad(rate_own, ((0, 0), (0, -heads % 16)))
-    away = spread_back(delta_all, half, half, mixer_weight, rate_wide, BF16, model // 4)
-    own = spread_back(delta_all, 0, half, mixer_weight, rate_wide, F32, model // 4)
+    away = spread_back(delta_all, delta_logits, half, half, mixer_weight, rate_wide, BF16, model // 4)
+    own = spread_back(delta_all, delta_logits, 0, half, mixer_weight, rate_wide, F32, model // 4)
     away, own = away.reshape(-1, local, model), own.reshape(-1, local, model)
-
-    def lane_sum(per_lane, repeat):
-        return per_lane.reshape(head_dim, heads, repeat).sum(axis=2).T.reshape(width, 1)
-
-    grad_start = grad_start.reshape(head_dim, heads, rows_here, head_dim).sum(axis=2)
-    grad_start = grad_start.transpose(1, 2, 0).reshape(width, head_dim)
-    grad_bias = grad_bias.reshape(head_dim, heads, rows_here, MINI)[..., 0]
-    own_grads = jnp.concatenate(
-        [
-            grad_start,
-            lane_sum(grad_bias, rows_here),
-            lane_sum(grad_inner_gain, rows_here * MINI),
-            lane_sum(grad_inner_shift, rows_here * MINI),
-            grad_post_scale.T,
-            grad_post_shift.T,
-        ],
-        axis=1,
-    )
+    away, own, grad_inputs, gated, active, ffn_sums, grad_down = lax.optimization_barrier(
+        (away, own, grad_inputs, gated, active, ffn_sums, grad_down)
+    )
+    input_sums = row_sums(grad_inputs)
+    grad_rate = token_grad(normed, delta_logits[:, :heads])
+    grad_out = token_grad(gated, delta_branch).astype(BF16)
     if aligned:
-        own_grads = jnp.pad(own_grads, ((0, 0), (0, -own_grads.shape[1] % 128)))
-    else:
-        own_grads = lax.psum_scatter(
-            placed(jnp.concatenate([own_grads.astype(BF16), grad_out], axis=1)),
-            everywhere, scatter_dimension=0, tiled=True,
-        ).astype(F32)
-
-    def out_of_mixer(own, away, hidden, delta_after, gain_attn, ffn_parts, gate_sums, own_grads):
+        grad_out = lax.psum_scatter(grad_out, "rows", scatter_dimension=0, tiled=True)
+
+    def out_of_mixer(
+        own, away, own_down, away_down, residual, hidden, delta_after, gain_attn, ffn_sums, grad_out, grad_start,
+        grad_bias, grad_inner_gain, grad_inner_shift, grad_post_scale, grad_post_shift, grad_rate,
+    ):
+        def lane_sum(per_lane, repeat):
+            return per_lane.reshape(head_dim, heads, repeat).sum(axis=2).T.reshape(width, 1)
+
+        grad_start = grad_start.reshape(head_dim, heads, rows_here, head_dim).sum(axis=2)
+        grad_start = grad_start.transpose(1, 2, 0).reshape(width, head_dim)
+        grad_bias = grad_bias.reshape(head_dim, heads, rows_here, MINI)[..., 0]
+        own_grads = jnp.concatenate(
+            [
+                grad_start,
+                lane_sum(grad_bias, rows_here),
+                lane_sum(grad_inner_gain, rows_here * MINI),
+                lane_sum(grad_inner_shift, rows_here * MINI),
+                grad_post_scale.T,
+                grad_post_shift.T,
+            ],
+            axis=1,
+        )
         grad_gate, grad_up, ffn_products = join_columns(
-            ffn_parts, (ffn_gate_weight, ffn_up_weight), (unit_kind,) * 2
-        )
-        grad_gate_weight, gate_products = join_columns(
-            columns_out(gate_sums), (gate_weight,), (head_kind,)
+            columns_out(ffn_sums), (ffn_gate_weight, ffn_up_weight), (unit_kind,) * 2
         )
         delta_normed = reduce_blocks(own, away, seq_bits)
+        block_out = restored(residual + reduce_blocks(own_down, away_down, seq_bits)).astype(BF16)
         if aligned:
+            rates = grad_rate.reshape(rows_count, seq_count, share, heads).transpose(0, 2, 1, 3)
+            own_grads = jnp.concatenate([own_grads, rates.reshape(width, -1)], axis=1)
+            own_grads = jnp.pad(own_grads, ((0, 0), (0, -own_grads.shape[1] % 128)))
             for axis, bit in reversed(row_bits):
                 own_grads = halved(own_grads, 0, axis, bit)
+            rates = own_grads[:, head_dim + 5 : head_dim + 5 + seq_count * heads]
+            rates = rates.reshape(share, seq_count, heads).transpose(1, 0, 2)
+        else:
+            rates = lax.psum_scatter(grad_rate, "rows", scatter_dimension=0, tiled=True)
+            rates = rates.reshape(seq_count, share, heads)
+            own_grads = lax.psum_scatter(
+                placed(jnp.concatenate([own_grads.astype(BF16), grad_out], axis=1)),
+                everywhere, scatter_dimension=0, tiled=True,
+            ).astype(F32)
         tokens = hidden.astype(F32)
         inverse_one = rms_inverse(tokens)
         scaled_one = delta_normed * gain_attn
@@ -858,24 +868,25 @@
             + inverse_one * scaled_one
             - tokens * inverse_one**3 * jnp.mean(scaled_one * tokens, axis=-1, keepdims=True)
         )
-        return (
-            restored(hidden_grad), grad_gate, grad_up, ffn_products, grad_gate_weight, gate_products,
-            own_grads,
-        )
-
-    (
-        hidden_grad, grad_gate, grad_up, ffn_products, grad_gate_weight, gate_products, own_grads
-    ) = apart(
-        out_of_mixer, own, away, hidden, delta_after, gain_attn, ffn_parts, gate_sums, own_grads
-    )
-    grad_query, grad_key, grad_value, grad_rate, input_products = join_columns(
-        columns_out(input_sums), (query_weight, key_weight, value_weight, rate_weight),
-        (head_kind,) * 3 + (rate_kind,),
-    )
-    grad_gain_attn = (input_products[:, 0] + gate_products[:, 0]) / attn_gain.astype(F32)
+        rates = jnp.pad(rates.astype(BF16), ((0, 0), (0, 0), (0, -heads % 16)))
+        return block_out, restored(hidden_grad), grad_gate, grad_up, ffn_products, own_grads, rates
+
+    block_out, hidden_grad, grad_gate, grad_up, ffn_products, own_grads, rates = apart(
+        out_of_mixer, own, away, *halves(active, down_wide, NN), residual, hidden, delta_after, gain_attn,
+        ffn_sums, grad_out, grad_start, grad_bias, grad_inner_gain, grad_inner_shift, grad_post_scale, grad_post_shift, grad_rate,
+    )
+    grad_query, grad_key, grad_value, grad_gate_weight, grad_rate, input_products = join_columns(
+        columns_out(jnp.concatenate([input_sums, rates], axis=2)), (query_weight, key_weight, value_weight, gate_weight, rate_weight),
+        (head_kind,) * 4 + (rate_kind,),
+    )
+    grad_gain_attn = input_products[:, 0] / attn_gain.astype(F32)
     grad_gain_ffn = ffn_products[:, 0] / ffn_gain.astype(F32)
     if not aligned:
         grad_out = own_grads[:, head_dim + 5 :]
+    grad_out, grad_rate, grad_down, own_grads, grad_gain_attn, grad_gain_ffn = lax.optimization_barrier(
+        (grad_out, grad_rate, grad_down, own_grads, grad_gain_attn, grad_gain_ffn)
+    )
+    grad_out = grad_out.astype(F32)
     own_vectors_grads = list(own_grads[:, head_dim : head_dim + 5].T)
     return (
         block_out,
@@ -892,7 +903,7 @@
         grad_gain_ffn,
         grad_gate,
         grad_up,
-        grad_down,
+        grad_down[:unit_share].astype(F32),
     )
 
 

time: 602 us -> 582 us (0.967)
  waiting for transfers between devices: 216 us -> 193 us
  local copies, waits for them, and re-layouts: 51.3 us -> 44.1 us
  matrix products: 83.4 us -> 90.3 us
  starting transfers between devices: 69.9 us -> 63.1 us
    all_to_all x3 -> x2, waiting for transfers between devices: 2.42 us -> 16.2 us  [columns_out(): return lax.all_to_all(values, 'seq', 0, 0, tiled=True)]
    reduce_scatter x3 -> x2, waiting for transfers between devices: 13 us -> 0.02 us  [row_sums(): summed = lax.psum_scatter(values, 'rows', scatter_dimension=0, tiled=True)]
    reduce_scatter x1, waiting for transfers between devices: 13.3 us -> 1.94 us  [shards(): lax.psum_scatter(grad_out, 'rows', scatter_dimension=0, tiled=True)]
    pallas_call x1, Pallas kernels: 18.7 us -> 29.2 us  [inner_forward(): pl.pallas_call(functools.partial(forward_kernel, heads, head_dim, parts),...]
    dot_general x3, matrix products: 5.99 us -> 13.2 us  [halves(): own = lax.dot_general(left[:half], matrix, dims, preferred_element_type=F32)]
    all_gather x1, waiting for transfers between devices: 26.1 us -> 19.7 us  [shards(): lax.all_gather(jnp.pad(ffn_down_weight, ((0, spare), (0, 0))), 'rows', ax...]
    unnamed x100 -> x102, local copies, waits for them, and re-layouts: 12.2 us -> 15.3 us
  transfers between devices with their start and end apart: 61 -> 59, of which waited for: 40 -> 39; matrix products, arithmetic and copies ran while one was open for 30% -> 31% of each run, Pallas kernels for 12% -> 14%
where the time goes in v4:
time: 582 us; the launch traced here: 576 us
  waiting for transfers between devices  193 us (33%)
  matrix products  90.3 us (16%)
  Pallas kernels  79.4 us (14%)
  starting transfers between devices  63.1 us (11%)
  other arithmetic  62 us (11%)
  local copies, waits for them, and re-layouts  44.1 us (8%)
  blocking collectives  26.5 us (5%)
  between operations  15.9 us (3%)
    ppermute x47, waiting for transfers between devices, exchange(): return lax.ppermute(value, axis, [(i, i ^ bit) for i in range(count)])  132 us
    ppermute x47, starting transfers between devices, exchange(): return lax.ppermute(value, axis, [(i, i ^ bit) for i in range(count)])  45.4 us
    dot_general x5, matrix products, token_grad(): return lax.dot_general(left, right, TN, preferred_element_type=F32)  35 us
    pallas_call x1, Pallas kernels, inner_forward(): pl.pallas_call(functools.partial(forward_kernel, heads, head_dim, parts),...  29.2 us
    psum x2, blocking collectives, feature_mean(): total = lax.psum(ordered, 'seq') / model  26.5 us
    pallas_call x1, Pallas kernels, inner_backward(): pl.pallas_call(functools.partial(backward_kernel, heads, head_dim, parts)...  25.2 us
    all_gather x1, waiting for transfers between devices, shards(): lax.all_gather(jnp.pad(ffn_down_weight, ((0, spare), (0, 0))), 'rows', ax...  19.7 us
    all_to_all x2, waiting for transfers between devices, columns_out(): return lax.all_to_all(values, 'seq', 0, 0, tiled=True)  16.2 us
  transfers between devices with their start and end apart: 59, of which 39 were waited for; matrix products, arithmetic and copies ran while one was open for 31% of the time, Pallas kernels for 14%

profile of v4, /device:TPU:0, one launch (start us, length us, event | category | flops | bytes accessed | tf_op | source)
XLA Modules:
  0.0 575.6 jit_solution(213566995285818277)
XLA Ops:
  13.2 5.2 all-to-all-start.2
  20.9 12.9 %all-to-all-done.2 = bf16[8,64,1024]{2,1,0:T(8,128)(2,1)S(1)} async-done(((bf16[8,64,1024]{2,1,0:T(8,128)(2,1)}), bf16[8,64,1024]{2,1,0:T(8,128)(2,1)S(1)}, u32[]{:S(2)}, u32[]{:S(2)}) %all-to-all-start.2) | async-done | bytes 1048608 | tf_op jit(solution)/shard_map/all_to_all | solution.py:600
  33.8 6.6 %all-gather.5.cloned.1.call-done.matrix_ref = bf16[256,2048]{1,0:T(8,128)(2,1)} async-done(((bf16[64,2048]{1,0:T(8,128)(2,1)}), bf16[256,2048]{1,0:T(8,128)(2,1)}) %all-gather.5.cloned.1.call-update) | async-done | bytes 1048592 | tf_op jit(solution)/shard_map/all_gather | solution.py:638
  41.8 3.1 cut_columns.3
  44.9 69.5 %conditional.4 = (bf16[1024,2048]{1,0:T(8,128)(2,1)}, bf16[2048,128]{1,0:T(8,128)(2,1)S(1)}, bf16[512,1408]{1,0:T(8,128)(2,1)}, f32[1024,2048]{1,0:T(8,128)}, f32[1024,1]{0,1:T(1,128)S(1)}) conditional(s32[]{:T(128)} %convert_element_type.315, () %tuple.54, (bf16[128,2048]{1,0:T(8,128)(2,1)S(1)}, bf16[64,128]{1,0:T(8,128)(2,1)S(1)}, ...), branch_computations={%region_1.2_spmd, %region_2.4_spmd} | conditional | flops 105102336 | bytes 92476480 | solution.py:629
  63.0 9.6 %collective-permute-done.3 = bf16[2,128,1024]{2,1,0:T(8,128)(2,1)S(1)} collective-permute-done((bf16[2,128,1024]{2,1,0:T(8,128)(2,1)S(1)}, bf16[2,128,1024]{2,1,0:T(8,128)(2,1)S(1)}, u32[]{:S(2)}, u32[]{:S(2)}) %collective-permute-start.3) | collective-permute-done | bytes 524320 | tf_op jit(solution)/shard_map/cond/branch_1_fun/ppermute | solution.py:479
  74.8 7.3 %collective-permute-done.13 = bf16[2,128,1024]{2,1,0:T(8,128)(2,1)S(1)} collective-permute-done((bf16[2,128,1024]{2,1,0:T(8,128)(2,1)S(1)}, bf16[2,128,1024]{2,1,0:T(8,128)(2,1)S(1)}, u32[]{:S(2)}, u32[]{:S(2)}) %collective-permute-start.13) | collective-permute-done | bytes 524320 | tf_op jit(solution)/shard_map/cond/branch_1_fun/ppermute | solution.py:479
  85.4 4.4 collective-permute-done.8
  90.5 4.3 all-to-all-start
  94.7 3.4 collective-permute-done.9
  101.4 3.7 pad_maximum_fusion
  105.1 6.2 %multiply_reduce_fusion = (f32[8,128]{1,0:T(8,128)S(1)}, f32[8,128,2048]{2,1,0:T(8,128)}) fusion(bf16[4,128,2048]{2,1,0:T(8,128)(2,1)} %collective-permute-done.14, bf16[1,128,1024]{2,1,0:T(8,128)(2,1)S(1)} %copy-done.37, bf16[1,128,1024]{2,1,0:T(8,128)(2,1)S(1)} %collective-permute-done.12, bf16[1,128,1024]{2,1,0:T(8,128)(2,1)S(1)} %copy-done.35, ...), kind=kLoop, calls=%fused_computation.5 | loop fusion | flops 37747712 | bytes 12587008 | tf_op jit(solution)/shard_map/reduce_sum | solution.py:701
  111.4 3.0 all-to-all-done
  117.7 4.3 multiply_convert_fusion.1
  131.3 10.7 %fusion.76.inputs_ref.pre_ref = f32[1024,1024]{1,0:T(8,128)} fusion(bf16[1024,2048]{1,0:T(8,128)(2,1)} %copy-done.13, bf16[2048,1024]{1,0:T(8,128)(2,1)} %all-gather.7.cloned.1.call-done.weight_ref), kind=kOutput, calls=%fused_computation.244 | convolution fusion | flops 4294967296 | bytes 12582912 | tf_op jit(solution)/shard_map/dot_general | solution.py:706
  142.0 29.2 %inner_forward.1 = (f32[1024,256]{1,0:T(8,128)}, f32[1024,2]{1,0:T(8,128)}, f32[8,3,4,64,128]{4,3,2,1,0:T(8,128)}, f32[8,8,128]{2,1,0:T(8,128)}, bf16[8,4,128,12...) custom-call(s32[1]{0:T(128)} %bitcast.51.slot_ref, f32[1024,1024]{1,0:T(8,128)} %fusion.76.inputs_ref.pre_ref, ...), custom_call_target="tpu_custom_call" | custom-call | tf_op jit(solution)/shard_map/inner_forward/pallas_call | solution.py:281
  175.3 13.2 %psum.14 = f32[2,8,128]{2,0,1:T(2,128)S(1)} all-reduce(f32[2,8,128]{2,0,1:T(2,128)S(1)} %select_bitcast_fusion.4), channel_id=1, replica_groups=mesh['rows'=4,'seq'=8] {'seq'}, use_global_device_ids=true, to_apply=%region_5.7 | all-reduce | flops 2048 | bytes 16384 | tf_op jit(solution)/shard_map/psum | solution.py:730
  192.8 54.9 %conditional.5 = (f32[128,2048]{1,0:T(8,128)S(1)}, bf16[1024,2048]{1,0:T(8,128)(2,1)}) conditional(s32[]{:T(128)} %convert_element_type.315, () %tuple.60, (bf16[128,2048]{1,0:T(8,128)(2,1)S(1)}, f32[512,2048]{1,0:T(8,128)S(1)}, bf16[512,2048]{1,0:T(8,128)(2,1)S(1)}, f32[2048]{0:T(1024)S(1)}) %tuple.159), branch_computations={%region_6.8_spmd, %region_7.10_spmd} | conditional | flops 56098944 | bytes 79702488 | solution.py:629
  193.1 4.1 collective-permute-done.15
  200.1 12.5 %collective-permute-done.16 = bf16[2,128,1024]{2,1,0:T(8,128)(2,1)S(1)} collective-permute-done((bf16[2,128,1024]{2,1,0:T(8,128)(2,1)S(1)}, bf16[2,128,1024]{2,1,0:T(8,128)(2,1)S(1)}, u32[]{:S(2)}, u32[]{:S(2)}) %collective-permute-start.16) | collective-permute-done | bytes 524320 | tf_op jit(solution)/shard_map/cond/branch_1_fun/ppermute | solution.py:479
  215.9 4.5 collective-permute-done.17
  224.3 4.6 collective-permute-done.22
  231.9 8.7 %collective-permute-done.23 = bf16[2,128,1024]{2,1,0:T(8,128)(2,1)S(1)} collective-permute-done((bf16[2,128,1024]{2,1,0:T(8,128)(2,1)S(1)}, bf16[2,128,1024]{2,1,0:T(8,128)(2,1)S(1)}, u32[]{:S(2)}, u32[]{:S(2)}) %collective-permute-start.23) | collective-permute-done | bytes 524320 | tf_op jit(solution)/shard_map/cond/branch_1_fun/ppermute | solution.py:479
  241.4 4.1 collective-permute-done.24
  247.7 10.8 %fusion.77 = f32[1024,1408]{1,0:T(8,128)S(1)} fusion(bf16[1024,2048]{1,0:T(8,128)(2,1)} %get-tuple-element.211, bf16[2048,1408]{1,0:T(8,128)(2,1)} %all-gather.9.cloned.1.call-done), kind=kOutput, calls=%fused_computation.245 | convolution fusion | flops 5905580032 | bytes 15728640 | tf_op jit(solution)/shard_map/dot_general | solution.py:755
  258.5 2.5 copy-done.22
  263.0 7.0 %convolution_convert_fusion.2 = bf16[704,2048]{1,0:T(8,128)(2,1)} fusion(bf16[1024,704]{1,0:T(8,128)(2,1)S(1)} %multiply_convert_fusion.4, bf16[1024,2048]{1,0:T(8,128)(2,1)} %get-tuple-element.210), kind=kOutput, calls=%fused_computation.132 | convolution fusion | flops 2954231808 | bytes 8519680 | tf_op jit(solution)/shard_map/dot_general | solution.py:761
  270.0 19.7 %all-gather.11.cloned.1.call-done = bf16[704,2048]{1,0:T(8,128)(2,1)} async-done(((bf16[176,2048]{1,0:T(8,128)(2,1)}), bf16[704,2048]{1,0:T(8,128)(2,1)}) %all-gather.11.cloned.1.call-update) | async-done | bytes 2883600 | tf_op jit(solution)/shard_map/all_gather | solution.py:708
  290.0 9.1 %multiply_convert_fusion.3 = (bf16[1024,704]{1,0:T(8,128)(2,1)S(1)}, bf16[1024,704]{1,0:T(8,128)(2,1)S(1)}) fusion(f32[1024,1408]{1,0:T(8,128)} %copy-done.22, bf16[1024,2048]{1,0:T(8,128)(2,1)} %get-tuple-element.210, bf16[704,2048]{1,0:T(8,128)(2,1)} %all-gather.11.cloned.1.call-done), kind=kOutput, calls=%fused_computation.134 | convolution fusion | flops 2962161664 | bytes 15728640 | tf_op jit(solution)/shard_map/dot_general | solution.py:766
  301.6 10.9 %convolution_convert_fusion = bf16[2048,1408]{1,0:T(8,128)(2,1)} fusion(bf16[1024,2048]{1,0:T(8,128)(2,1)} %get-tuple-element.211, bf16[1024,1408]{1,0:T(8,128)(2,1)S(1)} %pad_maximum_fusion.20), kind=kOutput, calls=%fused_computation.130 | convolution fusion | flops 5908463616 | bytes 12845056 | tf_op jit(solution)/shard_map/dot_general | solution.py:761
  314.8 6.7 %fusion.31 = f32[512,2048]{1,0:T(8,128)S(1)} fusion(bf16[2048,1408]{1,0:T(8,128)(2,1)} %all-gather.9.cloned.1.call-done, bf16[1024,1408]{1,0:T(8,128)(2,1)} %copy-done.28), kind=kOutput, calls=%fused_computation.144 | convolution fusion | flops 2952790016 | bytes 11403264 | tf_op jit(solution)/shard_map/dot_general | solution.py:743
  321.5 6.5 %convolution_convert_fusion.5 = bf16[512,2048]{1,0:T(8,128)(2,1)S(1)} fusion(bf16[2048,1408]{1,0:T(8,128)(2,1)} %all-gather.9.cloned.1.call-done, bf16[1024,1408]{1,0:T(8,128)(2,1)S(1)} %copy-done.29), kind=kOutput, calls=%fused_computation.139 | convolution fusion | flops 2953838592 | bytes 9306112 | tf_op jit(solution)/shard_map/dot_general | solution.py:742
  328.0 56.6 %conditional.6 = (f32[128,2048]{1,0:T(8,128)}, bf16[1024,2048]{1,0:T(8,128)(2,1)}) conditional(s32[]{:T(128)} %convert_element_type.315, () %tuple.59, (bf16[128,2048]{1,0:T(8,128)(2,1)S(1)}, f32[128,2048]{1,0:T(8,128)S(1)}, f32[512,2048]{1,0:T(8,128)S(1)}, bf16[512,2048]{1,0:T(8,128)(2,1)S(1)}, f32[2048]{0:T(1024)S(1)}) %tuple.162), branch_computations={%region_9.11_spmd, %region_10.14_spmd} | conditional | flops 57934208 | bytes 73422240 | solution.py:629
  328.5 4.1 collective-permute-done.25
  336.9 11.0 %collective-permute-done.26 = bf16[2,128,1024]{2,1,0:T(8,128)(2,1)S(1)} collective-permute-done((bf16[2,128,1024]{2,1,0:T(8,128)(2,1)S(1)}, bf16[2,128,1024]{2,1,0:T(8,128)(2,1)S(1)}, u32[]{:S(2)}, u32[]{:S(2)}) %collective-permute-start.26) | collective-permute-done | bytes 524320 | tf_op jit(solution)/shard_map/cond/branch_1_fun/ppermute | solution.py:479
  351.4 5.1 collective-permute-done.27
  360.9 5.2 collective-permute-done.32
  367.5 2.5 collective-permute-start.31
  370.0 7.9 %collective-permute-done.33 = bf16[2,128,1024]{2,1,0:T(8,128)(2,1)S(1)} collective-permute-done((bf16[2,128,1024]{2,1,0:T(8,128)(2,1)S(1)}, bf16[2,128,1024]{2,1,0:T(8,128)(2,1)S(1)}, u32[]{:S(2)}, u32[]{:S(2)}) %collective-permute-start.33) | collective-permute-done | bytes 524320 | tf_op jit(solution)/shard_map/cond/branch_1_fun/ppermute | solution.py:479
  378.3 4.1 collective-permute-done.34
  384.6 5.8 %branch_backward.1 = (bf16[1024,256]{1,0:T(8,128)(2,1)}, f32[1024,256]{1,0:T(8,128)}, f32[1024,2]{1,0:T(8,128)}, f32[1,256]{1,0:T(1,128)}, f32[1,256]{1,0:T(1,128)}) custom-call(bf16[1024,2048]{1,0:T(8,128)(2,1)} %get-tuple-element.216.delta_ref, bf16[256,2048]{1,0:T(8,128)(2,1)} %all-gather.5.cloned.1.call-done.matrix_ref, ...), custom_call_target="tpu_custom_call" | custom-call | tf_op jit(solution)/shard_map/branch_backward/pallas_call | solution.py:438
  392.2 13.3 %psum.15 = f32[2,8,128]{2,0,1:T(2,128)S(1)} all-reduce(f32[2,8,128]{2,0,1:T(2,128)S(1)} %select_bitcast_fusion.2), channel_id=1, replica_groups=mesh['rows'=4,'seq'=8] {'seq'}, use_global_device_ids=true, to_apply=%region_13.15 | all-reduce | flops 2048 | bytes 16384 | tf_op jit(solution)/shard_map/psum | solution.py:730
  407.3 25.2 %inner_backward.1 = (bf16[1024,1024]{1,0:T(8,128)(2,1)}, bf16[1024,16]{1,0:T(8,128)(2,1)}, f32[64,512]{1,0:T(8,128)S(1)}, f32[64,128]{1,0:T(8,128)S(1)}, f32[64,128]{1,0:T(8,128)S(1)}, /*index=5*/f32[64,128]{1,0:T(8,128)}) custom-call(s32[1]{0:T(128)} %bitcast.51.slot_ref, f32[1024,1024]{1,0:T(8,128)} %fusion.76.inputs_ref.pre_ref, ...), custom_call_target="tpu_custom_call" | custom-call | tf_op jit(solution)/shard_map/inner_backward/pallas_call | solution.py:314
  432.5 9.6 %convolution_convert_fusion.1 = bf16[2048,1024]{1,0:T(8,128)(2,1)} fusion(bf16[1024,2048]{1,0:T(8,128)(2,1)} %copy-done.13, bf16[1024,1024]{1,0:T(8,128)(2,1)} %get-tuple-element.225.delta_ref), kind=kOutput, calls=%fused_computation.131 | convolution fusion | flops 4297064448 | bytes 10485760 | tf_op jit(solution)/shard_map/dot_general | solution.py:761
  442.1 2.3 copy-done
  444.4 4.3 spread_back.2
  448.7 4.6 spread_back.3
  453.6 2.9 fusion.53
  456.5 4.6 convolution_convert_fusion.6
  461.1 5.8 %fusion.48 = f32[512,2048]{1,0:T(8,128)} fusion(bf16[704,2048]{1,0:T(8,128)(2,1)} %all-gather.11.cloned.1.call-done, bf16[1024,704]{1,0:T(8,128)(2,1)S(1)} %copy-done.42), kind=kOutput, calls=%fused_computation.164 | convolution fusion | flops 1476395008 | bytes 7864320 | tf_op jit(solution)/shard_map/dot_general | solution.py:743
  466.9 3.1 convolution_convert_fusion.4
  470.1 66.0 %conditional.7 = (bf16[2,64,2048]{2,1,0:T(8,128)(2,1)}, f32[2,64,2048]{2,1,0:T(8,128)}, f32[64,5504]{1,0:T(8,128)}, f32[64,5504]{1,0:T(8,128)}, f32[64,128]{0,1:...) conditional(s32[]{:T(128)} %convert_element_type.315, () %tuple.53, (f32[512,2048]{1,0:T(8,128)}, ...), branch_computations={%region_16.18_spmd, %region_17.25_spmd} | conditional | flops 15313031 | bytes 106042600 | solution.py:629
  474.7 3.6 all-to-all-start.1
  478.3 4.1 collective-permute-done.45
  482.7 6.0 %fusion.66 = (bf16[4,128,2048]{2,1,0:T(8,128)(2,1)S(1)}, f32[4,128,2048]{2,1,0:T(8,128)}) fusion(f32[4,128,2048]{2,1,0:T(8,128)} %bitcast.213, bf16[4,128,2048]{2,1,0:T(8,128)(2,1)} %collective-permute-done.35), kind=kLoop, calls=%fused_computation.234 | loop fusion | flops 3145728 | bytes 12582912 | tf_op jit(solution)/shard_map/convert.17
  493.3 4.5 fusion.65
  501.1 3.7 join_columns.2
  504.9 3.8 collective-permute-done.36
  512.4 7.6 %collective-permute-done.41 = bf16[2,128,1024]{2,1,0:T(8,128)(2,1)} collective-permute-done((bf16[2,128,1024]{2,1,0:T(8,128)(2,1)}, bf16[2,128,1024]{2,1,0:T(8,128)(2,1)}, u32[]{:S(2)}, u32[]{:S(2)}) %collective-permute-start.41) | collective-permute-done | bytes 524320 | tf_op jit(solution)/shard_map/cond/branch_1_fun/ppermute | solution.py:479
  523.6 2.4 collective-permute-done.37
  528.6 3.0 collective-permute-done.42
  536.2 2.5 pad_maximum_fusion.21
  538.6 3.6 all-to-all-start.3
  542.7 16.2 %all-to-all-done.3.refs_0_ = bf16[8,64,1040]{2,1,0:T(8,128)(2,1)S(1)} async-done(((bf16[8,64,1040]{2,1,0:T(8,128)(2,1)}), bf16[8,64,1040]{2,1,0:T(8,128)(2,1)S(1)}, u32[]{:S(2)}, u32[]{:S(2)}) %all-to-all-start.3) | async-done | bytes 1064992 | tf_op jit(solution)/shard_map/all_to_all | solution.py:607
  (414 shorter events, 136.8 us)
Async XLA Ops:
  7.3 33.2 %copy-start.53 = (s32[2,6]{1,0:T(2,128)S(1)}, s32[2,6]{1,0:T(2,128)}, u32[]{:S(2)}) copy-start(s32[2,6]{1,0:T(2,128)} %param.48) | copy-start | bytes 148
  7.3 33.1 %all-gather.5.cloned.1.call-start = ((), (), s32[]{:S(2)}) async-start(), calls=%async_computation.8 | async-start | bytes 1310720 | tf_op jit(solution)/shard_map/all_gather | solution.py:638
  13.2 20.6 %all-to-all-start.2 = ((bf16[8,64,1024]{2,1,0:T(8,128)(2,1)}), bf16[8,64,1024]{2,1,0:T(8,128)(2,1)S(1)}, u32[]{:S(2)}, u32[]{:S(2)}) async-start(bf16[8,64,1024]{2,1,0:T(8,128)(2,1)} %cut_columns.2), calls=%async_computation.2 | async-start | bytes 2097152 | tf_op jit(solution)/shard_map/all_to_all | solution.py:600
  18.4 112.8 %all-gather.7.cloned.1.call-start = ((), (), s32[]{:S(2)}) async-start(), calls=%async_computation.9 | async-start | bytes 5242880 | tf_op jit(solution)/shard_map/all_gather | solution.py:648
  18.5 174.3 %copy-start.19 = (bf16[2,4,16,2048]{3,2,0,1:T(8,128)(2,1)}, bf16[2,4,16,2048]{3,2,0,1:T(8,128)(2,1)S(1)}, u32[]{:S(2)}) copy-start(bf16[2,4,16,2048]{3,2,0,1:T(8,128)(2,1)S(1)} %copy.200) | copy-start | bytes 1572868
  40.5 207.2 %all-gather.9.cloned.1.call-start = ((), (), s32[]{:S(2)}) async-start(), calls=%async_computation.10 | async-start | bytes 7208960 | tf_op jit(solution)/shard_map/all_gather | solution.py:661
  45.0 9.3 %collective-permute-start.2 = (bf16[1,128,1024]{2,1,0:T(8,128)(2,1)S(1)}, bf16[1,128,1024]{2,1,0:T(8,128)(2,1)S(1)}, u32[]{:S(2)}, u32[]{:S(2)}) collective-permute-start(bf16[1,128,1024]{2,1,0:T(8,128)(2,1)S(1)} %get-tuple-element.461), channel_id=1, source_target_pairs={{0,4},{1,5},{2,6},{3,7},{4,0},{5,1},{6,2},{7,3},{8,12},{9,13},{10,... | collective-permute-start | bytes 786440 | tf_op jit(solution)/shard_map/cond/branch_1_fun/ppermute | solution.py:479
  46.4 9.3 %collective-permute-start = (bf16[1,128,1024]{2,1,0:T(8,128)(2,1)S(1)}, bf16[1,128,1024]{2,1,0:T(8,128)(2,1)S(1)}, u32[]{:S(2)}, u32[]{:S(2)}) collective-permute-start(bf16[1,128,1024]{2,1,0:T(8,128)(2,1)S(1)} %get-tuple-element.460), channel_id=1, source_target_pairs={{0,2},{1,3},{2,0},{3,1},{4,6},{5,7},{6,4},{7,5},{8,10},{9,11},{10,... | collective-permute-start | bytes 786440 | tf_op jit(solution)/shard_map/cond/branch_1_fun/ppermute | solution.py:479
  47.9 3.7 collective-permute-start.5
  49.4 10.5 %collective-permute-start.12 = (bf16[1,128,1024]{2,1,0:T(8,128)(2,1)S(1)}, bf16[1,128,1024]{2,1,0:T(8,128)(2,1)S(1)}, u32[]{:S(2)}, u32[]{:S(2)}) collective-permute-start(bf16[1,128,1024]{2,1,0:T(8,128)(2,1)S(1)} %get-tuple-element.455), channel_id=1, source_target_pairs={{0,4},{1,5},{2,6},{3,7},{4,0},{5,1},{6,2},{7,3},{8,12},{9,13},{10,... | collective-permute-start | bytes 786440 | tf_op jit(solution)/shard_map/cond/branch_1_fun/ppermute | solution.py:479
  50.0 11.4 %collective-permute-start.10 = (bf16[1,128,1024]{2,1,0:T(8,128)(2,1)S(1)}, bf16[1,128,1024]{2,1,0:T(8,128)(2,1)S(1)}, u32[]{:S(2)}, u32[]{:S(2)}) collective-permute-start(bf16[1,128,1024]{2,1,0:T(8,128)(2,1)S(1)} %get-tuple-element.454), channel_id=1, source_target_pairs={{0,2},{1,3},{2,0},{3,1},{4,6},{5,7},{6,4},{7,5},{8,10},{9,11},{10,... | collective-permute-start | bytes 786440 | tf_op jit(solution)/shard_map/cond/branch_1_fun/ppermute | solution.py:479
  51.7 7.3 %collective-permute-start.6 = (bf16[128,128]{1,0:T(8,128)(2,1)S(1)}, bf16[128,128]{1,0:T(8,128)(2,1)S(1)}, u32[]{:S(2)}, u32[]{:S(2)}) collective-permute-start(bf16[128,128]{1,0:T(8,128)(2,1)S(1)} %pad_maximum_fusion.9), channel_id=1, source_target_pairs={{0,16},{8,24},{16,0},{24,8},{1,17},{9,25},{17,1},{25,9},{2,18},{10... | collective-permute-start | bytes 98312 | tf_op jit(solution)/shard_map/cond/branch_1_fun/ppermute | solution.py:479
  54.3 18.2 %collective-permute-start.3 = (bf16[2,128,1024]{2,1,0:T(8,128)(2,1)S(1)}, bf16[2,128,1024]{2,1,0:T(8,128)(2,1)S(1)}, u32[]{:S(2)}, u32[]{:S(2)}) collective-permute-start(bf16[2,128,1024]{2,1,0:T(8,128)(2,1)S(1)} %pad_maximum_fusion.2), channel_id=1, source_target_pairs={{0,2},{1,3},{2,0},{3,1},{4,6},{5,7},{6,4},{7,5},{8,10},{9,11},{10,... | collective-permute-start | bytes 1572872 | tf_op jit(solution)/shard_map/cond/branch_1_fun/ppermute | solution.py:479
  55.8 16.8 %collective-permute-start.1 = (bf16[2,128,1024]{2,1,0:T(8,128)(2,1)S(1)}, bf16[2,128,1024]{2,1,0:T(8,128)(2,1)S(1)}, u32[]{:S(2)}, u32[]{:S(2)}) collective-permute-start(bf16[2,128,1024]{2,1,0:T(8,128)(2,1)S(1)} %pad_maximum_fusion.1), channel_id=1, source_target_pairs={{0,4},{1,5},{2,6},{3,7},{4,0},{5,1},{6,2},{7,3},{8,12},{9,13},{10,... | collective-permute-start | bytes 1572872 | tf_op jit(solution)/shard_map/cond/branch_1_fun/ppermute | solution.py:479
  59.9 22.2 %collective-permute-start.13 = (bf16[2,128,1024]{2,1,0:T(8,128)(2,1)S(1)}, bf16[2,128,1024]{2,1,0:T(8,128)(2,1)S(1)}, u32[]{:S(2)}, u32[]{:S(2)}) collective-permute-start(bf16[2,128,1024]{2,1,0:T(8,128)(2,1)S(1)} %pad_maximum_fusion.5), channel_id=1, source_target_pairs={{0,2},{1,3},{2,0},{3,1},{4,6},{5,7},{6,4},{7,5},{8,10},{9,11},{10,... | collective-permute-start | bytes 1572872 | tf_op jit(solution)/shard_map/cond/branch_1_fun/ppermute | solution.py:479
  61.4 20.8 %collective-permute-start.11 = (bf16[2,128,1024]{2,1,0:T(8,128)(2,1)S(1)}, bf16[2,128,1024]{2,1,0:T(8,128)(2,1)S(1)}, u32[]{:S(2)}, u32[]{:S(2)}) collective-permute-start(bf16[2,128,1024]{2,1,0:T(8,128)(2,1)S(1)} %pad_maximum_fusion.4), channel_id=1, source_target_pairs={{0,4},{1,5},{2,6},{3,7},{4,0},{5,1},{6,2},{7,3},{8,12},{9,13},{10,... | collective-permute-start | bytes 1572872 | tf_op jit(solution)/shard_map/cond/branch_1_fun/ppermute | solution.py:479
  74.2 27.2 %collective-permute-start.4 = (bf16[4,128,2048]{2,1,0:T(8,128)(2,1)}, bf16[4,128,2048]{2,1,0:T(8,128)(2,1)}, u32[]{:S(2)}, u32[]{:S(2)}) collective-permute-start(bf16[4,128,2048]{2,1,0:T(8,128)(2,1)} %maximum_maximum_fusion), channel_id=1, source_target_pairs={{0,1},{1,0},{2,3},{3,2},{4,5},{5,4},{6,7},{7,6},{8,9},{9,8},{10,11... | collective-permute-start | bytes 6291464 | tf_op jit(solution)/shard_map/cond/branch_1_fun/ppermute | solution.py:479
  74.3 9.6 %collective-permute-start.7 = (bf16[64,512]{1,0:T(8,128)(2,1)S(1)}, bf16[64,512]{1,0:T(8,128)(2,1)S(1)}, u32[]{:S(2)}, u32[]{:S(2)}) collective-permute-start(bf16[64,512]{1,0:T(8,128)(2,1)S(1)} %bitcast.239), channel_id=1, source_target_pairs={{0,1},{1,0},{2,3},{3,2},{4,5},{5,4},{6,7},{7,6},{8,9},{9,8},{10,11... | collective-permute-start | bytes 196616 | tf_op jit(solution)/shard_map/cond/branch_1_fun/ppermute | solution.py:479
  83.8 21.3 %collective-permute-start.14 = (bf16[4,128,2048]{2,1,0:T(8,128)(2,1)}, bf16[4,128,2048]{2,1,0:T(8,128)(2,1)}, u32[]{:S(2)}, u32[]{:S(2)}) collective-permute-start(bf16[4,128,2048]{2,1,0:T(8,128)(2,1)} %maximum_maximum_fusion.1), channel_id=1, source_target_pairs={{0,1},{1,0},{2,3},{3,2},{4,5},{5,4},{6,7},{7,6},{8,9},{9,8},{10,11... | collective-permute-start | bytes 6291464 | tf_op jit(solution)/shard_map/cond/branch_1_fun/ppermute | solution.py:479
  83.9 6.0 %collective-permute-start.8 = (bf16[128,512]{1,0:T(8,128)(2,1)S(1)}, bf16[128,512]{1,0:T(8,128)(2,1)S(1)}, u32[]{:S(2)}, u32[]{:S(2)}) collective-permute-start(bf16[128,512]{1,0:T(8,128)(2,1)S(1)} %pad_maximum_fusion.7), channel_id=1, source_target_pairs={{0,2},{1,3},{2,0},{3,1},{4,6},{5,7},{6,4},{7,5},{8,10},{9,11},{10,... | collective-permute-start | bytes 393224 | tf_op jit(solution)/shard_map/cond/branch_1_fun/ppermute | solution.py:479
  89.9 8.3 %collective-permute-start.9 = (bf16[256,512]{1,0:T(8,128)(2,1)S(1)}, bf16[256,512]{1,0:T(8,128)(2,1)}, u32[]{:S(2)}, u32[]{:S(2)}) collective-permute-start(bf16[256,512]{1,0:T(8,128)(2,1)S(1)} %pad_maximum_fusion.6), channel_id=1, source_target_pairs={{0,4},{1,5},{2,6},{3,7},{4,0},{5,1},{6,2},{7,3},{8,12},{9,13},{10,... | collective-permute-start | bytes 786440 | tf_op jit(solution)/shard_map/cond/branch_1_fun/ppermute | solution.py:479
  90.5 23.9 %all-to-all-start = ((bf16[8,64,1408]{2,1,0:T(8,128)(2,1)}), bf16[8,64,1408]{2,1,0:T(8,128)(2,1)}, u32[]{:S(2)}, u32[]{:S(2)}) async-start(bf16[8,64,1408]{2,1,0:T(8,128)(2,1)} %get-tuple-element.76), calls=%async_computation | async-start | bytes 2883584 | tf_op jit(solution)/shard_map/cond/branch_1_fun/all_to_all | solution.py:600
  114.4 175.3 %all-gather.11.cloned.1.call-start = ((), (), s32[]{:S(2)}) async-start(), calls=%async_computation.11 | async-start | bytes 3604480 | tf_op jit(solution)/shard_map/all_gather | solution.py:708
  128.5 60.8 %copy-start.50 = (f32[256]{0:T(256)}, f32[256]{0:T(256)S(1)}, u32[]{:S(2)}) copy-start(f32[256]{0:T(256)S(1)} %get-tuple-element.435) | copy-start | bytes 3076
  128.5 60.8 %copy-start.51 = (f32[256]{0:T(256)}, f32[256]{0:T(256)S(1)}, u32[]{:S(2)}) copy-start(f32[256]{0:T(256)S(1)} %get-tuple-element.436) | copy-start | bytes 3076
  189.2 264.1 %reduce-scatter.7.cloned.1.call-start = ((), (), s32[]{:S(2)}) async-start(), calls=%async_computation.13 | async-start | bytes 3604480 | tf_op jit(solution)/shard_map/reduce_scatter | solution.py:765
  193.0 4.2 collective-permute-start.15
  198.5 14.0 %collective-permute-start.16 = (bf16[2,128,1024]{2,1,0:T(8,128)(2,1)S(1)}, bf16[2,128,1024]{2,1,0:T(8,128)(2,1)S(1)}, u32[]{:S(2)}, u32[]{:S(2)}) collective-permute-start(bf16[2,128,1024]{2,1,0:T(8,128)(2,1)S(1)} %pad_maximum_fusion.11), channel_id=1, source_target_pairs={{0,2},{1,3},{2,0},{3,1},{4,6},{5,7},{6,4},{7,5},{8,10},{9,11},{10,... | collective-permute-start | bytes 1572872 | tf_op jit(solution)/shard_map/cond/branch_1_fun/ppermute | solution.py:479
  198.6 14.0 %collective-permute-start.18 = (bf16[2,128,1024]{2,1,0:T(8,128)(2,1)S(1)}, bf16[2,128,1024]{2,1,0:T(8,128)(2,1)S(1)}, u32[]{:S(2)}, u32[]{:S(2)}) collective-permute-start(bf16[2,128,1024]{2,1,0:T(8,128)(2,1)S(1)} %slice.376), channel_id=1, source_target_pairs={{0,4},{1,5},{2,6},{3,7},{4,0},{5,1},{6,2},{7,3},{8,12},{9,13},{10,... | collective-permute-start | bytes 1572872 | tf_op jit(solution)/shard_map/cond/branch_1_fun/ppermute | solution.py:479
  212.8 7.7 %collective-permute-start.17 = (bf16[1,128,1024]{2,1,0:T(8,128)(2,1)S(1)}, bf16[1,128,1024]{2,1,0:T(8,128)(2,1)S(1)}, u32[]{:S(2)}, u32[]{:S(2)}) collective-permute-start(bf16[1,128,1024]{2,1,0:T(8,128)(2,1)S(1)} %get-tuple-element.474), channel_id=1, source_target_pairs={{0,4},{1,5},{2,6},{3,7},{4,0},{5,1},{6,2},{7,3},{8,12},{9,13},{10,... | collective-permute-start | bytes 786440 | tf_op jit(solution)/shard_map/cond/branch_1_fun/ppermute | solution.py:479
  214.2 7.3 %collective-permute-start.19 = (bf16[1,128,1024]{2,1,0:T(8,128)(2,1)S(1)}, bf16[1,128,1024]{2,1,0:T(8,128)(2,1)S(1)}, u32[]{:S(2)}, u32[]{:S(2)}) collective-permute-start(bf16[1,128,1024]{2,1,0:T(8,128)(2,1)S(1)} %get-tuple-element.475), channel_id=1, source_target_pairs={{0,2},{1,3},{2,0},{3,1},{4,6},{5,7},{6,4},{7,5},{8,10},{9,11},{10,... | collective-permute-start | bytes 786440 | tf_op jit(solution)/shard_map/cond/branch_1_fun/ppermute | solution.py:479
  222.3 6.6 %collective-permute-start.22 = (bf16[1,128,1024]{2,1,0:T(8,128)(2,1)S(1)}, bf16[1,128,1024]{2,1,0:T(8,128)(2,1)S(1)}, u32[]{:S(2)}, u32[]{:S(2)}) collective-permute-start(bf16[1,128,1024]{2,1,0:T(8,128)(2,1)S(1)} %get-tuple-element.479), channel_id=1, source_target_pairs={{0,4},{1,5},{2,6},{3,7},{4,0},{5,1},{6,2},{7,3},{8,12},{9,13},{10,... | collective-permute-start | bytes 786440 | tf_op jit(solution)/shard_map/cond/branch_1_fun/ppermute | solution.py:479
  222.9 7.2 %collective-permute-start.20 = (bf16[1,128,1024]{2,1,0:T(8,128)(2,1)S(1)}, bf16[1,128,1024]{2,1,0:T(8,128)(2,1)S(1)}, u32[]{:S(2)}, u32[]{:S(2)}) collective-permute-start(bf16[1,128,1024]{2,1,0:T(8,128)(2,1)S(1)} %get-tuple-element.478), channel_id=1, source_target_pairs={{0,2},{1,3},{2,0},{3,1},{4,6},{5,7},{6,4},{7,5},{8,10},{9,11},{10,... | collective-permute-start | bytes 786440 | tf_op jit(solution)/shard_map/cond/branch_1_fun/ppermute | solution.py:479
  228.9 11.6 %collective-permute-start.23 = (bf16[2,128,1024]{2,1,0:T(8,128)(2,1)S(1)}, bf16[2,128,1024]{2,1,0:T(8,128)(2,1)S(1)}, u32[]{:S(2)}, u32[]{:S(2)}) collective-permute-start(bf16[2,128,1024]{2,1,0:T(8,128)(2,1)S(1)} %pad_maximum_fusion.13), channel_id=1, source_target_pairs={{0,2},{1,3},{2,0},{3,1},{4,6},{5,7},{6,4},{7,5},{8,10},{9,11},{10,... | collective-permute-start | bytes 1572872 | tf_op jit(solution)/shard_map/cond/branch_1_fun/ppermute | solution.py:479
  230.2 10.9 %collective-permute-start.21 = (bf16[2,128,1024]{2,1,0:T(8,128)(2,1)S(1)}, bf16[2,128,1024]{2,1,0:T(8,128)(2,1)S(1)}, u32[]{:S(2)}, u32[]{:S(2)}) collective-permute-start(bf16[2,128,1024]{2,1,0:T(8,128)(2,1)S(1)} %pad_maximum_fusion.12), channel_id=1, source_target_pairs={{0,4},{1,5},{2,6},{3,7},{4,0},{5,1},{6,2},{7,3},{8,12},{9,13},{10,... | collective-permute-start | bytes 1572872 | tf_op jit(solution)/shard_map/cond/branch_1_fun/ppermute | solution.py:479
  241.3 4.2 collective-permute-start.24
  247.7 80.3 %copy-start.16 = (f32[128,2048]{1,0:T(8,128)}, f32[128,2048]{1,0:T(8,128)S(1)}, u32[]{:S(2)}) copy-start(f32[128,2048]{1,0:T(8,128)S(1)} %get-tuple-element.209) | copy-start | bytes 3145732
  289.8 163.6 %reduce-scatter.5.cloned.1.call-start = ((), (), s32[]{:S(2)}) async-start(), calls=%async_computation.12 | async-start | bytes 7208960 | tf_op jit(solution)/shard_map/reduce_scatter | solution.py:603
  312.6 223.6 %reduce-scatter.11.cloned.1.call-start = ((), (), s32[]{:S(2)}) async-start(), calls=%async_computation.15 | async-start | bytes 5242880 | tf_op jit(solution)/shard_map/reduce_scatter | solution.py:603
  328.5 4.2 collective-permute-start.25
  333.9 14.0 %collective-permute-start.26 = (bf16[2,128,1024]{2,1,0:T(8,128)(2,1)S(1)}, bf16[2,128,1024]{2,1,0:T(8,128)(2,1)S(1)}, u32[]{:S(2)}, u32[]{:S(2)}) collective-permute-start(bf16[2,128,1024]{2,1,0:T(8,128)(2,1)S(1)} %pad_maximum_fusion.15), channel_id=1, source_target_pairs={{0,2},{1,3},{2,0},{3,1},{4,6},{5,7},{6,4},{7,5},{8,10},{9,11},{10,... | collective-permute-start | bytes 1572872 | tf_op jit(solution)/shard_map/cond/branch_1_fun/ppermute | solution.py:479
  335.4 13.7 %collective-permute-start.28 = (bf16[2,128,1024]{2,1,0:T(8,128)(2,1)S(1)}, bf16[2,128,1024]{2,1,0:T(8,128)(2,1)S(1)}, u32[]{:S(2)}, u32[]{:S(2)}) collective-permute-start(bf16[2,128,1024]{2,1,0:T(8,128)(2,1)S(1)} %slice.391), channel_id=1, source_target_pairs={{0,4},{1,5},{2,6},{3,7},{4,0},{5,1},{6,2},{7,3},{8,12},{9,13},{10,... | collective-permute-start | bytes 1572872 | tf_op jit(solution)/shard_map/cond/branch_1_fun/ppermute | solution.py:479
  349.3 7.3 %collective-permute-start.27 = (bf16[1,128,1024]{2,1,0:T(8,128)(2,1)S(1)}, bf16[1,128,1024]{2,1,0:T(8,128)(2,1)S(1)}, u32[]{:S(2)}, u32[]{:S(2)}) collective-permute-start(bf16[1,128,1024]{2,1,0:T(8,128)(2,1)S(1)} %get-tuple-element.484), channel_id=1, source_target_pairs={{0,4},{1,5},{2,6},{3,7},{4,0},{5,1},{6,2},{7,3},{8,12},{9,13},{10,... | collective-permute-start | bytes 786440 | tf_op jit(solution)/shard_map/cond/branch_1_fun/ppermute | solution.py:479
  350.9 6.9 %collective-permute-start.29 = (bf16[1,128,1024]{2,1,0:T(8,128)(2,1)S(1)}, bf16[1,128,1024]{2,1,0:T(8,128)(2,1)S(1)}, u32[]{:S(2)}, u32[]{:S(2)}) collective-permute-start(bf16[1,128,1024]{2,1,0:T(8,128)(2,1)S(1)} %get-tuple-element.485), channel_id=1, source_target_pairs={{0,2},{1,3},{2,0},{3,1},{4,6},{5,7},{6,4},{7,5},{8,10},{9,11},{10,... | collective-permute-start | bytes 786440 | tf_op jit(solution)/shard_map/cond/branch_1_fun/ppermute | solution.py:479
  359.7 6.4 %collective-permute-start.32 = (bf16[1,128,1024]{2,1,0:T(8,128)(2,1)S(1)}, bf16[1,128,1024]{2,1,0:T(8,128)(2,1)S(1)}, u32[]{:S(2)}, u32[]{:S(2)}) collective-permute-start(bf16[1,128,1024]{2,1,0:T(8,128)(2,1)S(1)} %get-tuple-element.489), channel_id=1, source_target_pairs={{0,4},{1,5},{2,6},{3,7},{4,0},{5,1},{6,2},{7,3},{8,12},{9,13},{10,... | collective-permute-start | bytes 786440 | tf_op jit(solution)/shard_map/cond/branch_1_fun/ppermute | solution.py:479
  360.3 7.1 %collective-permute-start.30 = (bf16[1,128,1024]{2,1,0:T(8,128)(2,1)S(1)}, bf16[1,128,1024]{2,1,0:T(8,128)(2,1)S(1)}, u32[]{:S(2)}, u32[]{:S(2)}) collective-permute-start(bf16[1,128,1024]{2,1,0:T(8,128)(2,1)S(1)} %get-tuple-element.488), channel_id=1, source_target_pairs={{0,2},{1,3},{2,0},{3,1},{4,6},{5,7},{6,4},{7,5},{8,10},{9,11},{10,... | collective-permute-start | bytes 786440 | tf_op jit(solution)/shard_map/cond/branch_1_fun/ppermute | solution.py:479
  366.2 11.7 %collective-permute-start.33 = (bf16[2,128,1024]{2,1,0:T(8,128)(2,1)S(1)}, bf16[2,128,1024]{2,1,0:T(8,128)(2,1)S(1)}, u32[]{:S(2)}, u32[]{:S(2)}) collective-permute-start(bf16[2,128,1024]{2,1,0:T(8,128)(2,1)S(1)} %pad_maximum_fusion.17), channel_id=1, source_target_pairs={{0,2},{1,3},{2,0},{3,1},{4,6},{5,7},{6,4},{7,5},{8,10},{9,11},{10,... | collective-permute-start | bytes 1572872 | tf_op jit(solution)/shard_map/cond/branch_1_fun/ppermute | solution.py:479
  367.5 10.5 %collective-permute-start.31 = (bf16[2,128,1024]{2,1,0:T(8,128)(2,1)S(1)}, bf16[2,128,1024]{2,1,0:T(8,128)(2,1)S(1)}, u32[]{:S(2)}, u32[]{:S(2)}) collective-permute-start(bf16[2,128,1024]{2,1,0:T(8,128)(2,1)S(1)} %pad_maximum_fusion.16), channel_id=1, source_target_pairs={{0,4},{1,5},{2,6},{3,7},{4,0},{5,1},{6,2},{7,3},{8,12},{9,13},{10,... | collective-permute-start | bytes 1572872 | tf_op jit(solution)/shard_map/cond/branch_1_fun/ppermute | solution.py:479
  378.2 4.2 collective-permute-start.34
  453.4 110.3 %reduce-scatter.9.cloned.1.call-start = ((), (), s32[]{:S(2)}) async-start(), calls=%async_computation.14 | async-start | bytes 1310720 | tf_op jit(solution)/shard_map/reduce_scatter | solution.py:820
  470.1 12.7 %collective-permute-start.35 = (bf16[4,128,2048]{2,1,0:T(8,128)(2,1)}, bf16[4,128,2048]{2,1,0:T(8,128)(2,1)}, u32[]{:S(2)}, u32[]{:S(2)}) collective-permute-start(bf16[4,128,2048]{2,1,0:T(8,128)(2,1)} %bitcast.27), channel_id=1, source_target_pairs={{0,1},{1,0},{2,3},{3,2},{4,5},{5,4},{6,7},{7,6},{8,9},{9,8},{10,11... | collective-permute-start | bytes 6291464 | tf_op jit(solution)/shard_map/cond/branch_1_fun/ppermute | solution.py:479
  470.2 23.2 %collective-permute-start.40 = (bf16[4,128,2048]{2,1,0:T(8,128)(2,1)}, bf16[4,128,2048]{2,1,0:T(8,128)(2,1)}, u32[]{:S(2)}, u32[]{:S(2)}) collective-permute-start(bf16[4,128,2048]{2,1,0:T(8,128)(2,1)} %get-tuple-element.93), channel_id=1, source_target_pairs={{0,1},{1,0},{2,3},{3,2},{4,5},{5,4},{6,7},{7,6},{8,9},{9,8},{10,11... | collective-permute-start | bytes 6291464 | tf_op jit(solution)/shard_map/cond/branch_1_fun/ppermute | solution.py:479
  473.1 9.3 %collective-permute-start.45 = (f32[128,128]{0,1:T(8,128)S(1)}, f32[128,128]{0,1:T(8,128)S(1)}, u32[]{:S(2)}, u32[]{:S(2)}) collective-permute-start(f32[128,128]{0,1:T(8,128)S(1)} %fusion.29), channel_id=1, source_target_pairs={{0,16},{8,24},{16,0},{24,8},{1,17},{9,25},{17,1},{25,9},{2,18},{10... | collective-permute-start | bytes 196616 | tf_op jit(solution)/shard_map/cond/branch_1_fun/ppermute | solution.py:479
  474.7 26.4 %all-to-all-start.1 = ((bf16[8,64,1408]{2,1,0:T(8,128)(2,1)}), bf16[8,64,1408]{2,1,0:T(8,128)(2,1)S(1)}, u32[]{:S(2)}, u32[]{:S(2)}) async-start(bf16[8,64,1408]{2,1,0:T(8,128)(2,1)} %get-tuple-element.95), calls=%async_computation.1 | async-start | bytes 2883584 | tf_op jit(solution)/shard_map/cond/branch_1_fun/all_to_all | solution.py:607
  482.5 18.3 %collective-permute-start.46 = (f32[64,128]{0,1:T(8,128)S(1)}, f32[64,128]{0,1:T(8,128)S(1)}, u32[]{:S(2)}, u32[]{:S(2)}) collective-permute-start(f32[64,128]{0,1:T(8,128)S(1)} %slice_select_fusion), channel_id=1, source_target_pairs={{0,8},{8,0},{16,24},{24,16},{1,9},{9,1},{17,25},{25,17},{2,10},{10... | collective-permute-start | bytes 98312 | tf_op jit(solution)/shard_map/cond/branch_1_fun/ppermute | solution.py:479
  490.5 18.3 %collective-permute-start.36 = (bf16[2,128,1024]{2,1,0:T(8,128)(2,1)}, bf16[2,128,1024]{2,1,0:T(8,128)(2,1)}, u32[]{:S(2)}, u32[]{:S(2)}) collective-permute-start(bf16[2,128,1024]{2,1,0:T(8,128)(2,1)} %pad_maximum_fusion.18), channel_id=1, source_target_pairs={{0,2},{1,3},{2,0},{3,1},{4,6},{5,7},{6,4},{7,5},{8,10},{9,11},{10,... | collective-permute-start | bytes 1572872 | tf_op jit(solution)/shard_map/cond/branch_1_fun/ppermute | solution.py:479
  491.8 17.4 %collective-permute-start.38 = (bf16[2,128,1024]{2,1,0:T(8,128)(2,1)}, bf16[2,128,1024]{2,1,0:T(8,128)(2,1)}, u32[]{:S(2)}, u32[]{:S(2)}) collective-permute-start(bf16[2,128,1024]{2,1,0:T(8,128)(2,1)} %slice.406), channel_id=1, source_target_pairs={{0,4},{1,5},{2,6},{3,7},{4,0},{5,1},{6,2},{7,3},{8,12},{9,13},{10,... | collective-permute-start | bytes 1572872 | tf_op jit(solution)/shard_map/cond/branch_1_fun/ppermute | solution.py:479
  499.5 20.5 %collective-permute-start.41 = (bf16[2,128,1024]{2,1,0:T(8,128)(2,1)}, bf16[2,128,1024]{2,1,0:T(8,128)(2,1)}, u32[]{:S(2)}, u32[]{:S(2)}) collective-permute-start(bf16[2,128,1024]{2,1,0:T(8,128)(2,1)} %pad_maximum_fusion.19), channel_id=1, source_target_pairs={{0,2},{1,3},{2,0},{3,1},{4,6},{5,7},{6,4},{7,5},{8,10},{9,11},{10,... | collective-permute-start | bytes 1572872 | tf_op jit(solution)/shard_map/cond/branch_1_fun/ppermute | solution.py:479
  500.2 20.2 %collective-permute-start.43 = (bf16[2,128,1024]{2,1,0:T(8,128)(2,1)}, bf16[2,128,1024]{2,1,0:T(8,128)(2,1)}, u32[]{:S(2)}, u32[]{:S(2)}) collective-permute-start(bf16[2,128,1024]{2,1,0:T(8,128)(2,1)} %slice.417), channel_id=1, source_target_pairs={{0,4},{1,5},{2,6},{3,7},{4,0},{5,1},{6,2},{7,3},{8,12},{9,13},{10,... | collective-permute-start | bytes 1572872 | tf_op jit(solution)/shard_map/cond/branch_1_fun/ppermute | solution.py:479
  510.7 15.3 %collective-permute-start.37 = (bf16[1,128,1024]{2,1,0:T(8,128)(2,1)S(1)}, bf16[1,128,1024]{2,1,0:T(8,128)(2,1)S(1)}, u32[]{:S(2)}, u32[]{:S(2)}) collective-permute-start(bf16[1,128,1024]{2,1,0:T(8,128)(2,1)S(1)} %get-tuple-element.501), channel_id=1, source_target_pairs={{0,4},{1,5},{2,6},{3,7},{4,0},{5,1},{6,2},{7,3},{8,12},{9,13},{10,... | collective-permute-start | bytes 786440 | tf_op jit(solution)/shard_map/cond/branch_1_fun/ppermute | solution.py:479
  511.8 14.2 %collective-permute-start.39 = (bf16[1,128,1024]{2,1,0:T(8,128)(2,1)S(1)}, bf16[1,128,1024]{2,1,0:T(8,128)(2,1)S(1)}, u32[]{:S(2)}, u32[]{:S(2)}) collective-permute-start(bf16[1,128,1024]{2,1,0:T(8,128)(2,1)S(1)} %get-tuple-element.502), channel_id=1, source_target_pairs={{0,2},{1,3},{2,0},{3,1},{4,6},{5,7},{6,4},{7,5},{8,10},{9,11},{10,... | collective-permute-start | bytes 786440 | tf_op jit(solution)/shard_map/cond/branch_1_fun/ppermute | solution.py:479
  522.0 9.5 %collective-permute-start.42 = (bf16[1,128,1024]{2,1,0:T(8,128)(2,1)S(1)}, bf16[1,128,1024]{2,1,0:T(8,128)(2,1)S(1)}, u32[]{:S(2)}, u32[]{:S(2)}) collective-permute-start(bf16[1,128,1024]{2,1,0:T(8,128)(2,1)S(1)} %get-tuple-element.497), channel_id=1, source_target_pairs={{0,4},{1,5},{2,6},{3,7},{4,0},{5,1},{6,2},{7,3},{8,12},{9,13},{10,... | collective-permute-start | bytes 786440 | tf_op jit(solution)/shard_map/cond/branch_1_fun/ppermute | solution.py:479
  523.0 8.5 %collective-permute-start.44 = (bf16[1,128,1024]{2,1,0:T(8,128)(2,1)S(1)}, bf16[1,128,1024]{2,1,0:T(8,128)(2,1)S(1)}, u32[]{:S(2)}, u32[]{:S(2)}) collective-permute-start(bf16[1,128,1024]{2,1,0:T(8,128)(2,1)S(1)} %get-tuple-element.498), channel_id=1, source_target_pairs={{0,2},{1,3},{2,0},{3,1},{4,6},{5,7},{6,4},{7,5},{8,10},{9,11},{10,... | collective-permute-start | bytes 786440 | tf_op jit(solution)/shard_map/cond/branch_1_fun/ppermute | solution.py:479
  538.6 20.3 %all-to-all-start.3 = ((bf16[8,64,1040]{2,1,0:T(8,128)(2,1)}), bf16[8,64,1040]{2,1,0:T(8,128)(2,1)S(1)}, u32[]{:S(2)}, u32[]{:S(2)}) async-start(bf16[8,64,1040]{2,1,0:T(8,128)(2,1)} %pad_maximum_fusion.21), calls=%async_computation.7 | async-start | bytes 2359296 | tf_op jit(solution)/shard_map/all_to_all | solution.py:607
  (59 other events, 565.6 us)
Sparse Core Ops, SparseCore 0:
  9.7 30.6 all-gather.4
  42.6 81.0 all-gather.6
  125.2 104.9 all-gather.8
  232.2 57.4 all-gather.10
  291.9 54.8 reduce-scatter.6
  348.9 102.1 reduce-scatter.4
  453.5 80.0 reduce-scatter.10
  535.9 27.6 reduce-scatter.8

commit v5 on v4

--- a/solution.py
+++ b/solution.py
@@ -507,11 +507,11 @@
     return whole if tied is None else (whole, tied)
 
 
-def reduce_blocks(own, away, bits, kind=BF16):
+def reduce_blocks(own, away, bits, near_kind=BF16, last_kind=BF16):
     near, far = bits[0], bits[1:]
     ways = max(1, len(far))
     cuts = cuts_of(own.shape[-1], ways)
-    half = own.astype(F32) + exchange(away.astype(kind), *near).astype(F32)
+    half = own.astype(F32) + exchange(away.astype(near_kind), *near).astype(F32)
     held = [
         {k: half[k, :, cuts[way] : cuts[way + 1]] for k in range(half.shape[0])} for way in range(ways)
     ]
@@ -519,6 +519,7 @@
         for way in range(ways):
             bit = (way + step) % len(far)
             gone = sorted(k for k in held[way] if k >> bit & 1)
+            kind = last_kind if step == len(far) - 1 else BF16
             moved = exchange(jnp.stack([held[way][k].astype(kind) for k in gone]), *far[bit])
             for n, k in enumerate(gone):
                 held[way][k ^ 1 << bit] = held[way][k ^ 1 << bit] + moved[n].astype(F32)
@@ -737,9 +738,9 @@
     post_out = post_norm * post_scale + post_offset
     gated = (gelu_tanh(gate_pre) * post_out).astype(BF16)
 
-    def halves(left, matrix, dims):
+    def halves(left, matrix, dims, kind=BF16):
         half = left.shape[0] // 2
-        away = lax.dot_general(left[half:], matrix, dims, preferred_element_type=F32).astype(BF16)
+        away = lax.dot_general(left[half:], matrix, dims, preferred_element_type=F32).astype(kind)
         own = lax.dot_general(left[:half], matrix, dims, preferred_element_type=F32)
         return own.reshape(-1, local, model), away.reshape(-1, local, model)
 
@@ -747,11 +748,11 @@
         return lax.rsqrt(jnp.mean(values * values, axis=-1, keepdims=True) + EPSILON)
 
     def into_ffn(own, away, hidden, gain_ffn):
-        residual = hidden.astype(F32) + reduce_blocks(own, away, seq_bits)
+        residual = hidden.astype(F32) + reduce_blocks(own, away, seq_bits, F32, F32)
         scaled = (residual * rms_inverse(residual) * gain_ffn).astype(BF16)
         return residual, gather_blocks(scaled, seq_bits).reshape(-1, model)
 
-    residual, ffn_in = apart(into_ffn, *halves(gated, out_own, NN), hidden, gain_ffn)
+    residual, ffn_in = apart(into_ffn, *halves(gated, out_own, NN, F32), hidden, gain_ffn)
     gate_up = jnp.dot(ffn_in, ffn_wide, preferred_element_type=F32)
     gate_value, up_value = gate_up[:, :units], gate_up[:, units:]
     sigmoid_gate = jax.nn.sigmoid(gate_value)
@@ -883,12 +884,7 @@
     grad_gain_ffn = ffn_products[:, 0] / ffn_gain.astype(F32)
     if not aligned:
         grad_out = own_grads[:, head_dim + 5 :]
-    grad_out, grad_rate, grad_down, own_grads, grad_gain_attn, grad_gain_ffn = lax.optimization_barrier(
-        (grad_out, grad_rate, grad_down, own_grads, grad_gain_attn, grad_gain_ffn)
-    )
-    grad_out = grad_out.astype(F32)
-    own_vectors_grads = list(own_grads[:, head_dim : head_dim + 5].T)
-    return (
+    results = (
         block_out,
         hidden_grad,
         grad_gain_attn,
@@ -898,13 +894,16 @@
         grad_rate,
         grad_gate_weight,
         own_grads[:, :head_dim],
-        *own_vectors_grads,
+        *list(own_grads[:, head_dim : head_dim + 5].T),
         grad_out,
         grad_gain_ffn,
         grad_gate,
         grad_up,
         grad_down[:unit_share].astype(F32),
     )
+    results = list(lax.optimization_barrier(results))
+    results[14] = results[14].astype(F32)
+    return tuple(results)
 
 
 def solution(mesh):

time: 582 us -> 580 us (level)
    all_gather x1, waiting for transfers between devices: 19.7 us -> 11.1 us  [shards(): lax.all_gather(jnp.pad(ffn_down_weight, ((0, spare), (0, 0))), 'rows', ax...]
    ppermute x47, waiting for transfers between devices: 132 us -> 140 us  [exchange(): return lax.ppermute(value, axis, [(i, i ^ bit) for i in range(count)])]
    unnamed x102 -> x98, local copies, waits for them, and re-layouts: 15.3 us -> 15.3 us
  transfers between devices with their start and end apart: 59 -> 59, of which waited for: 39 -> 38; matrix products, arithmetic and copies ran while one was open for 31% -> 32% of each run, Pallas kernels for 14% -> 14%
where the time goes in v5:
time: 580 us; the launch traced here: 574 us
  waiting for transfers between devices  189 us (33%)
  matrix products  92.2 us (16%)
  Pallas kernels  79.3 us (14%)
  starting transfers between devices  63.2 us (11%)
  other arithmetic  62.4 us (11%)
  local copies, waits for them, and re-layouts  44.1 us (8%)
  blocking collectives  26.5 us (5%)
  between operations  15.8 us (3%)
    ppermute x47, waiting for transfers between devices, exchange(): return lax.ppermute(value, axis, [(i, i ^ bit) for i in range(count)])  140 us
    ppermute x47, starting transfers between devices, exchange(): return lax.ppermute(value, axis, [(i, i ^ bit) for i in range(count)])  45.4 us
    dot_general x5, matrix products, token_grad(): return lax.dot_general(left, right, TN, preferred_element_type=F32)  34.9 us
    pallas_call x1, Pallas kernels, inner_forward(): pl.pallas_call(functools.partial(forward_kernel, heads, head_dim, parts),...  29.2 us
    psum x2, blocking collectives, feature_mean(): total = lax.psum(ordered, 'seq') / model  26.5 us
    pallas_call x1, Pallas kernels, inner_backward(): pl.pallas_call(functools.partial(backward_kernel, heads, head_dim, parts)...  25.2 us
    all_to_all x2, waiting for transfers between devices, shuffled(): lax.all_to_all(values, 'seq', 0, 0, tiled=True)  15.9 us
    unnamed x98, local copies, waits for them, and re-layouts  15.3 us
  transfers between devices with their start and end apart: 59, of which 38 were waited for; matrix products, arithmetic and copies ran while one was open for 32% of the time, Pallas kernels for 14%

profile of v5, /device:TPU:0, one launch (start us, length us, event | category | flops | bytes accessed | tf_op | source)
XLA Modules:
  0.0 573.7 jit_solution(8150903798335340126)
XLA Ops:
  13.2 5.2 all-to-all-start.2
  20.9 12.9 %all-to-all-done.2 = bf16[8,64,1024]{2,1,0:T(8,128)(2,1)S(1)} async-done(((bf16[8,64,1024]{2,1,0:T(8,128)(2,1)}), bf16[8,64,1024]{2,1,0:T(8,128)(2,1)S(1)}, u32[]{:S(2)}, u32[]{:S(2)}) %all-to-all-start.2) | async-done | bytes 1048608 | tf_op jit(solution)/shard_map/all_to_all | solution.py:601
  33.8 6.6 %all-gather.5.cloned.1.call-done.matrix_ref = bf16[256,2048]{1,0:T(8,128)(2,1)} async-done(((bf16[64,2048]{1,0:T(8,128)(2,1)}), bf16[256,2048]{1,0:T(8,128)(2,1)}) %all-gather.5.cloned.1.call-update) | async-done | bytes 1048592 | tf_op jit(solution)/shard_map/all_gather | solution.py:639
  41.8 3.1 cut_columns.3
  44.9 69.5 %conditional.4 = (bf16[1024,2048]{1,0:T(8,128)(2,1)}, bf16[2048,128]{1,0:T(8,128)(2,1)S(1)}, bf16[512,1408]{1,0:T(8,128)(2,1)}, f32[1024,2048]{1,0:T(8,128)}, f32[1024,1]{0,1:T(1,128)S(1)}) conditional(s32[]{:T(128)} %convert_element_type.293, () %tuple.54, (bf16[128,2048]{1,0:T(8,128)(2,1)S(1)}, bf16[64,128]{1,0:T(8,128)(2,1)S(1)}, ...), branch_computations={%region_1.2_spmd, %region_2.4_spmd} | conditional | flops 105102336 | bytes 92476480 | solution.py:630
  63.0 9.6 %collective-permute-done.3 = bf16[2,128,1024]{2,1,0:T(8,128)(2,1)S(1)} collective-permute-done((bf16[2,128,1024]{2,1,0:T(8,128)(2,1)S(1)}, bf16[2,128,1024]{2,1,0:T(8,128)(2,1)S(1)}, u32[]{:S(2)}, u32[]{:S(2)}) %collective-permute-start.3) | collective-permute-done | bytes 524320 | tf_op jit(solution)/shard_map/cond/branch_1_fun/ppermute | solution.py:479
  74.8 7.3 %collective-permute-done.13 = bf16[2,128,1024]{2,1,0:T(8,128)(2,1)S(1)} collective-permute-done((bf16[2,128,1024]{2,1,0:T(8,128)(2,1)S(1)}, bf16[2,128,1024]{2,1,0:T(8,128)(2,1)S(1)}, u32[]{:S(2)}, u32[]{:S(2)}) %collective-permute-start.13) | collective-permute-done | bytes 524320 | tf_op jit(solution)/shard_map/cond/branch_1_fun/ppermute | solution.py:479
  85.4 4.4 collective-permute-done.8
  90.5 4.3 all-to-all-start
  94.8 3.4 collective-permute-done.9
  101.4 3.7 pad_maximum_fusion
  105.1 6.3 %multiply_reduce_fusion = (f32[8,128]{1,0:T(8,128)S(1)}, f32[8,128,2048]{2,1,0:T(8,128)}) fusion(bf16[4,128,2048]{2,1,0:T(8,128)(2,1)} %collective-permute-done.14, bf16[1,128,1024]{2,1,0:T(8,128)(2,1)S(1)} %copy-done.37, bf16[1,128,1024]{2,1,0:T(8,128)(2,1)S(1)} %collective-permute-done.12, bf16[1,128,1024]{2,1,0:T(8,128)(2,1)S(1)} %copy-done.35, ...), kind=kLoop, calls=%fused_computation.5 | loop fusion | flops 37747712 | bytes 12587008 | tf_op jit(solution)/shard_map/reduce_sum | solution.py:702
  111.4 3.0 all-to-all-done
  117.7 4.3 multiply_convert_fusion.1
  131.3 10.7 %fusion.75.inputs_ref.pre_ref = f32[1024,1024]{1,0:T(8,128)} fusion(bf16[1024,2048]{1,0:T(8,128)(2,1)} %copy-done.13, bf16[2048,1024]{1,0:T(8,128)(2,1)} %all-gather.7.cloned.1.call-done.weight_ref), kind=kOutput, calls=%fused_computation.241 | convolution fusion | flops 4294967296 | bytes 12582912 | tf_op jit(solution)/shard_map/dot_general | solution.py:707
  142.0 29.2 %inner_forward.1 = (f32[1024,256]{1,0:T(8,128)}, f32[1024,2]{1,0:T(8,128)}, f32[8,3,4,64,128]{4,3,2,1,0:T(8,128)}, f32[8,8,128]{2,1,0:T(8,128)}, bf16[8,4,128,12...) custom-call(s32[1]{0:T(128)} %bitcast.51.slot_ref, f32[1024,1024]{1,0:T(8,128)} %fusion.75.inputs_ref.pre_ref, ...), custom_call_target="tpu_custom_call" | custom-call | tf_op jit(solution)/shard_map/inner_forward/pallas_call | solution.py:281
  175.3 13.2 %psum.14 = f32[2,8,128]{2,0,1:T(2,128)S(1)} all-reduce(f32[2,8,128]{2,0,1:T(2,128)S(1)} %select_bitcast_fusion.4), channel_id=1, replica_groups=mesh['rows'=4,'seq'=8] {'seq'}, use_global_device_ids=true, to_apply=%region_5.7 | all-reduce | flops 2048 | bytes 16384 | tf_op jit(solution)/shard_map/psum | solution.py:731
  192.8 63.5 %conditional.5 = (f32[128,2048]{1,0:T(8,128)S(1)}, bf16[1024,2048]{1,0:T(8,128)(2,1)}) conditional(s32[]{:T(128)} %convert_element_type.293, () %tuple.60, (bf16[128,2048]{1,0:T(8,128)(2,1)S(1)}, f32[512,2048]{1,0:T(8,128)S(1)}, f32[512,2048]{1,0:T(8,128)S(1)}, f32[2048]{0:T(1024)S(1)}) %tuple.159), branch_computations={%region_6.8_spmd, %region_7.10_spmd} | conditional | flops 54526080 | bytes 93333976 | solution.py:630
  193.1 7.1 %collective-permute-done.15 = f32[4,128,2048]{2,1,0:T(8,128)S(1)} collective-permute-done((f32[4,128,2048]{2,1,0:T(8,128)S(1)}, f32[4,128,2048]{2,1,0:T(8,128)S(1)}, u32[]{:S(2)}, u32[]{:S(2)}) %collective-permute-start.15) | collective-permute-done | bytes 4194336 | tf_op jit(solution)/shard_map/cond/branch_1_fun/ppermute | solution.py:479
  203.4 12.4 %collective-permute-done.16 = bf16[2,128,1024]{2,1,0:T(8,128)(2,1)S(1)} collective-permute-done((bf16[2,128,1024]{2,1,0:T(8,128)(2,1)S(1)}, bf16[2,128,1024]{2,1,0:T(8,128)(2,1)S(1)}, u32[]{:S(2)}, u32[]{:S(2)}) %collective-permute-start.16) | collective-permute-done | bytes 524320 | tf_op jit(solution)/shard_map/cond/branch_1_fun/ppermute | solution.py:479
  219.3 10.1 %collective-permute-done.17 = f32[1,128,1024]{2,1,0:T(8,128)S(1)} collective-permute-done((f32[1,128,1024]{2,1,0:T(8,128)S(1)}, f32[1,128,1024]{2,1,0:T(8,128)S(1)}, u32[]{:S(2)}, u32[]{:S(2)}) %collective-permute-start.17) | collective-permute-done | bytes 524320 | tf_op jit(solution)/shard_map/cond/branch_1_fun/ppermute | solution.py:479
  233.2 4.6 collective-permute-done.22
  241.0 8.5 %collective-permute-done.23 = bf16[2,128,1024]{2,1,0:T(8,128)(2,1)S(1)} collective-permute-done((bf16[2,128,1024]{2,1,0:T(8,128)(2,1)S(1)}, bf16[2,128,1024]{2,1,0:T(8,128)(2,1)S(1)}, u32[]{:S(2)}, u32[]{:S(2)}) %collective-permute-start.23) | collective-permute-done | bytes 524320 | tf_op jit(solution)/shard_map/cond/branch_1_fun/ppermute | solution.py:479
  250.0 4.1 collective-permute-done.24
  256.3 10.8 %fusion.76 = f32[1024,1408]{1,0:T(8,128)S(1)} fusion(bf16[1024,2048]{1,0:T(8,128)(2,1)} %get-tuple-element.224, bf16[2048,1408]{1,0:T(8,128)(2,1)} %all-gather.9.cloned.1.call-done), kind=kOutput, calls=%fused_computation.242 | convolution fusion | flops 5905580032 | bytes 15728640 | tf_op jit(solution)/shard_map/dot_general | solution.py:756
  267.1 2.5 copy-done.22
  271.7 7.0 %convolution_convert_fusion.2 = bf16[704,2048]{1,0:T(8,128)(2,1)} fusion(bf16[1024,704]{1,0:T(8,128)(2,1)S(1)} %multiply_convert_fusion.4, bf16[1024,2048]{1,0:T(8,128)(2,1)} %get-tuple-element.223), kind=kOutput, calls=%fused_computation.129 | convolution fusion | flops 2954231808 | bytes 8519680 | tf_op jit(solution)/shard_map/dot_general | solution.py:762
  278.6 11.1 %all-gather.11.cloned.1.call-done = bf16[704,2048]{1,0:T(8,128)(2,1)} async-done(((bf16[176,2048]{1,0:T(8,128)(2,1)}), bf16[704,2048]{1,0:T(8,128)(2,1)}) %all-gather.11.cloned.1.call-update) | async-done | bytes 2883600 | tf_op jit(solution)/shard_map/all_gather | solution.py:709
  290.0 9.1 %multiply_convert_fusion.3 = (bf16[1024,704]{1,0:T(8,128)(2,1)S(1)}, bf16[1024,704]{1,0:T(8,128)(2,1)S(1)}) fusion(f32[1024,1408]{1,0:T(8,128)} %copy-done.22, bf16[1024,2048]{1,0:T(8,128)(2,1)} %get-tuple-element.223, bf16[704,2048]{1,0:T(8,128)(2,1)} %all-gather.11.cloned.1.call-done), kind=kOutput, calls=%fused_computation.131 | convolution fusion | flops 2962161664 | bytes 15728640 | tf_op jit(solution)/shard_map/dot_general | solution.py:767
  301.6 10.9 %convolution_convert_fusion = bf16[2048,1408]{1,0:T(8,128)(2,1)} fusion(bf16[1024,2048]{1,0:T(8,128)(2,1)} %get-tuple-element.224, bf16[1024,1408]{1,0:T(8,128)(2,1)S(1)} %pad_maximum_fusion.20), kind=kOutput, calls=%fused_computation.127 | convolution fusion | flops 5908463616 | bytes 12845056 | tf_op jit(solution)/shard_map/dot_general | solution.py:762
  314.8 6.7 %fusion.29 = f32[512,2048]{1,0:T(8,128)S(1)} fusion(bf16[2048,1408]{1,0:T(8,128)(2,1)} %all-gather.9.cloned.1.call-done, bf16[1024,1408]{1,0:T(8,128)(2,1)} %copy-done.30), kind=kOutput, calls=%fused_computation.140 | convolution fusion | flops 2952790016 | bytes 11403264 | tf_op jit(solution)/shard_map/dot_general | solution.py:744
  321.5 6.5 %convolution_convert_fusion.4 = bf16[512,2048]{1,0:T(8,128)(2,1)S(1)} fusion(bf16[2048,1408]{1,0:T(8,128)(2,1)} %all-gather.9.cloned.1.call-done, bf16[1024,1408]{1,0:T(8,128)(2,1)S(1)} %copy-done.31), kind=kOutput, calls=%fused_computation.135 | convolution fusion | flops 2953838592 | bytes 9306112 | tf_op jit(solution)/shard_map/dot_general | solution.py:743
  328.0 56.6 %conditional.6 = (f32[128,2048]{1,0:T(8,128)}, bf16[1024,2048]{1,0:T(8,128)(2,1)}) conditional(s32[]{:T(128)} %convert_element_type.293, () %tuple.59, (bf16[128,2048]{1,0:T(8,128)(2,1)S(1)}, f32[128,2048]{1,0:T(8,128)S(1)}, f32[512,2048]{1,0:T(8,128)S(1)}, bf16[512,2048]{1,0:T(8,128)(2,1)S(1)}, f32[2048]{0:T(1024)S(1)}) %tuple.162), branch_computations={%region_9.11_spmd, %region_10.14_spmd} | conditional | flops 57934208 | bytes 73422240 | solution.py:630
  328.6 4.1 collective-permute-done.25
  336.9 11.0 %collective-permute-done.26 = bf16[2,128,1024]{2,1,0:T(8,128)(2,1)S(1)} collective-permute-done((bf16[2,128,1024]{2,1,0:T(8,128)(2,1)S(1)}, bf16[2,128,1024]{2,1,0:T(8,128)(2,1)S(1)}, u32[]{:S(2)}, u32[]{:S(2)}) %collective-permute-start.26) | collective-permute-done | bytes 524320 | tf_op jit(solution)/shard_map/cond/branch_1_fun/ppermute | solution.py:479
  351.4 5.2 collective-permute-done.27
  360.9 5.2 collective-permute-done.32
  367.5 2.5 collective-permute-start.31
  370.0 7.9 %collective-permute-done.33 = bf16[2,128,1024]{2,1,0:T(8,128)(2,1)S(1)} collective-permute-done((bf16[2,128,1024]{2,1,0:T(8,128)(2,1)S(1)}, bf16[2,128,1024]{2,1,0:T(8,128)(2,1)S(1)}, u32[]{:S(2)}, u32[]{:S(2)}) %collective-permute-start.33) | collective-permute-done | bytes 524320 | tf_op jit(solution)/shard_map/cond/branch_1_fun/ppermute | solution.py:479
  378.3 4.1 collective-permute-done.34
  384.6 5.8 %branch_backward.1 = (bf16[1024,256]{1,0:T(8,128)(2,1)}, f32[1024,256]{1,0:T(8,128)}, f32[1024,2]{1,0:T(8,128)}, f32[1,256]{1,0:T(1,128)}, f32[1,256]{1,0:T(1,128)}) custom-call(bf16[1024,2048]{1,0:T(8,128)(2,1)} %get-tuple-element.229.delta_ref, bf16[256,2048]{1,0:T(8,128)(2,1)} %all-gather.5.cloned.1.call-done.matrix_ref, ...), custom_call_target="tpu_custom_call" | custom-call | tf_op jit(solution)/shard_map/branch_backward/pallas_call | solution.py:438
  392.3 13.3 %psum.15 = f32[2,8,128]{2,0,1:T(2,128)S(1)} all-reduce(f32[2,8,128]{2,0,1:T(2,128)S(1)} %select_bitcast_fusion.2), channel_id=1, replica_groups=mesh['rows'=4,'seq'=8] {'seq'}, use_global_device_ids=true, to_apply=%region_13.15 | all-reduce | flops 2048 | bytes 16384 | tf_op jit(solution)/shard_map/psum | solution.py:731
  407.3 25.2 %inner_backward.1 = (bf16[1024,1024]{1,0:T(8,128)(2,1)}, bf16[1024,16]{1,0:T(8,128)(2,1)}, f32[64,512]{1,0:T(8,128)S(1)}, f32[64,128]{1,0:T(8,128)S(1)}, f32[64,128]{1,0:T(8,128)S(1)}, /*index=5*/f32[64,128]{1,0:T(8,128)}) custom-call(s32[1]{0:T(128)} %bitcast.51.slot_ref, f32[1024,1024]{1,0:T(8,128)} %fusion.75.inputs_ref.pre_ref, ...), custom_call_target="tpu_custom_call" | custom-call | tf_op jit(solution)/shard_map/inner_backward/pallas_call | solution.py:314
  432.5 9.6 %convolution_convert_fusion.1 = bf16[2048,1024]{1,0:T(8,128)(2,1)} fusion(bf16[1024,2048]{1,0:T(8,128)(2,1)} %copy-done.13, bf16[1024,1024]{1,0:T(8,128)(2,1)} %get-tuple-element.238.delta_ref), kind=kOutput, calls=%fused_computation.128 | convolution fusion | flops 4297064448 | bytes 10485760 | tf_op jit(solution)/shard_map/dot_general | solution.py:762
  442.1 2.3 copy-done
  444.4 4.3 spread_back.2
  448.7 4.6 spread_back.3
  453.5 2.9 fusion.52
  456.4 4.6 convolution_convert_fusion.5
  461.0 5.6 fusion.46
  466.7 5.3 convolution_convert_fusion.3
  471.9 66.1 %conditional.7 = (bf16[2,64,2048]{2,1,0:T(8,128)(2,1)}, f32[2,64,2048]{2,1,0:T(8,128)}, f32[64,5504]{1,0:T(8,128)}, f32[64,5504]{1,0:T(8,128)}, f32[64,128]{0,1:...) conditional(s32[]{:T(128)} %convert_element_type.293, () %tuple.53, (f32[512,2048]{1,0:T(8,128)}, ...), branch_computations={%region_16.18_spmd, %region_17.25_spmd} | conditional | flops 15313031 | bytes 106042600 | solution.py:630
  476.7 3.6 all-to-all-start.1
  480.3 5.6 collective-permute-done.45
  486.1 6.0 %fusion.65 = (bf16[4,128,2048]{2,1,0:T(8,128)(2,1)S(1)}, f32[4,128,2048]{2,1,0:T(8,128)}) fusion(f32[4,128,2048]{2,1,0:T(8,128)} %bitcast.214, bf16[4,128,2048]{2,1,0:T(8,128)(2,1)} %collective-permute-done.35), kind=kLoop, calls=%fused_computation.231 | loop fusion | flops 3145728 | bytes 12582912 | tf_op jit(solution)/shard_map/convert.17
  494.9 4.5 fusion.64
  504.5 3.7 join_columns.2
  508.3 2.5 collective-permute-done.36
  514.4 7.6 %collective-permute-done.41 = bf16[2,128,1024]{2,1,0:T(8,128)(2,1)} collective-permute-done((bf16[2,128,1024]{2,1,0:T(8,128)(2,1)}, bf16[2,128,1024]{2,1,0:T(8,128)(2,1)}, u32[]{:S(2)}, u32[]{:S(2)}) %collective-permute-start.41) | collective-permute-done | bytes 524320 | tf_op jit(solution)/shard_map/cond/branch_1_fun/ppermute | solution.py:479
  525.6 2.4 collective-permute-done.37
  530.6 2.9 collective-permute-done.42
  538.8 2.4 pad_maximum_fusion.21
  541.1 3.6 all-to-all-start.3
  547.0 14.4 %all-to-all-done.3.refs_0_ = bf16[8,64,1040]{2,1,0:T(8,128)(2,1)S(1)} async-done(((bf16[8,64,1040]{2,1,0:T(8,128)(2,1)}), bf16[8,64,1040]{2,1,0:T(8,128)(2,1)S(1)}, u32[]{:S(2)}, u32[]{:S(2)}) %all-to-all-start.3) | async-done | bytes 1064992 | tf_op jit(solution)/shard_map/all_to_all | solution.py:608
  (410 shorter events, 135.1 us)
Async XLA Ops:
  7.3 33.2 %copy-start.52 = (s32[2,6]{1,0:T(2,128)S(1)}, s32[2,6]{1,0:T(2,128)}, u32[]{:S(2)}) copy-start(s32[2,6]{1,0:T(2,128)} %param.48) | copy-start | bytes 148
  7.3 33.1 %all-gather.5.cloned.1.call-start = ((), (), s32[]{:S(2)}) async-start(), calls=%async_computation.8 | async-start | bytes 1310720 | tf_op jit(solution)/shard_map/all_gather | solution.py:639
  13.2 20.6 %all-to-all-start.2 = ((bf16[8,64,1024]{2,1,0:T(8,128)(2,1)}), bf16[8,64,1024]{2,1,0:T(8,128)(2,1)S(1)}, u32[]{:S(2)}, u32[]{:S(2)}) async-start(bf16[8,64,1024]{2,1,0:T(8,128)(2,1)} %cut_columns.2), calls=%async_computation.2 | async-start | bytes 2097152 | tf_op jit(solution)/shard_map/all_to_all | solution.py:601
  18.4 112.9 %all-gather.7.cloned.1.call-start = ((), (), s32[]{:S(2)}) async-start(), calls=%async_computation.9 | async-start | bytes 5242880 | tf_op jit(solution)/shard_map/all_gather | solution.py:649
  18.5 174.3 %copy-start.19 = (bf16[2,4,16,2048]{3,2,0,1:T(8,128)(2,1)}, bf16[2,4,16,2048]{3,2,0,1:T(8,128)(2,1)S(1)}, u32[]{:S(2)}) copy-start(bf16[2,4,16,2048]{3,2,0,1:T(8,128)(2,1)S(1)} %copy.200) | copy-start | bytes 1572868
  40.5 215.9 %all-gather.9.cloned.1.call-start = ((), (), s32[]{:S(2)}) async-start(), calls=%async_computation.10 | async-start | bytes 7208960 | tf_op jit(solution)/shard_map/all_gather | solution.py:662
  45.0 9.3 %collective-permute-start.2 = (bf16[1,128,1024]{2,1,0:T(8,128)(2,1)S(1)}, bf16[1,128,1024]{2,1,0:T(8,128)(2,1)S(1)}, u32[]{:S(2)}, u32[]{:S(2)}) collective-permute-start(bf16[1,128,1024]{2,1,0:T(8,128)(2,1)S(1)} %get-tuple-element.487), channel_id=1, source_target_pairs={{0,4},{1,5},{2,6},{3,7},{4,0},{5,1},{6,2},{7,3},{8,12},{9,13},{10,... | collective-permute-start | bytes 786440 | tf_op jit(solution)/shard_map/cond/branch_1_fun/ppermute | solution.py:479
  46.4 9.3 %collective-permute-start = (bf16[1,128,1024]{2,1,0:T(8,128)(2,1)S(1)}, bf16[1,128,1024]{2,1,0:T(8,128)(2,1)S(1)}, u32[]{:S(2)}, u32[]{:S(2)}) collective-permute-start(bf16[1,128,1024]{2,1,0:T(8,128)(2,1)S(1)} %get-tuple-element.486), channel_id=1, source_target_pairs={{0,2},{1,3},{2,0},{3,1},{4,6},{5,7},{6,4},{7,5},{8,10},{9,11},{10,... | collective-permute-start | bytes 786440 | tf_op jit(solution)/shard_map/cond/branch_1_fun/ppermute | solution.py:479
  47.9 3.7 collective-permute-start.5
  49.4 10.5 %collective-permute-start.12 = (bf16[1,128,1024]{2,1,0:T(8,128)(2,1)S(1)}, bf16[1,128,1024]{2,1,0:T(8,128)(2,1)S(1)}, u32[]{:S(2)}, u32[]{:S(2)}) collective-permute-start(bf16[1,128,1024]{2,1,0:T(8,128)(2,1)S(1)} %get-tuple-element.481), channel_id=1, source_target_pairs={{0,4},{1,5},{2,6},{3,7},{4,0},{5,1},{6,2},{7,3},{8,12},{9,13},{10,... | collective-permute-start | bytes 786440 | tf_op jit(solution)/shard_map/cond/branch_1_fun/ppermute | solution.py:479
  50.0 11.4 %collective-permute-start.10 = (bf16[1,128,1024]{2,1,0:T(8,128)(2,1)S(1)}, bf16[1,128,1024]{2,1,0:T(8,128)(2,1)S(1)}, u32[]{:S(2)}, u32[]{:S(2)}) collective-permute-start(bf16[1,128,1024]{2,1,0:T(8,128)(2,1)S(1)} %get-tuple-element.480), channel_id=1, source_target_pairs={{0,2},{1,3},{2,0},{3,1},{4,6},{5,7},{6,4},{7,5},{8,10},{9,11},{10,... | collective-permute-start | bytes 786440 | tf_op jit(solution)/shard_map/cond/branch_1_fun/ppermute | solution.py:479
  51.7 7.3 %collective-permute-start.6 = (bf16[128,128]{1,0:T(8,128)(2,1)S(1)}, bf16[128,128]{1,0:T(8,128)(2,1)S(1)}, u32[]{:S(2)}, u32[]{:S(2)}) collective-permute-start(bf16[128,128]{1,0:T(8,128)(2,1)S(1)} %pad_maximum_fusion.9), channel_id=1, source_target_pairs={{0,16},{8,24},{16,0},{24,8},{1,17},{9,25},{17,1},{25,9},{2,18},{10... | collective-permute-start | bytes 98312 | tf_op jit(solution)/shard_map/cond/branch_1_fun/ppermute | solution.py:479
  54.3 18.2 %collective-permute-start.3 = (bf16[2,128,1024]{2,1,0:T(8,128)(2,1)S(1)}, bf16[2,128,1024]{2,1,0:T(8,128)(2,1)S(1)}, u32[]{:S(2)}, u32[]{:S(2)}) collective-permute-start(bf16[2,128,1024]{2,1,0:T(8,128)(2,1)S(1)} %pad_maximum_fusion.2), channel_id=1, source_target_pairs={{0,2},{1,3},{2,0},{3,1},{4,6},{5,7},{6,4},{7,5},{8,10},{9,11},{10,... | collective-permute-start | bytes 1572872 | tf_op jit(solution)/shard_map/cond/branch_1_fun/ppermute | solution.py:479
  55.8 16.8 %collective-permute-start.1 = (bf16[2,128,1024]{2,1,0:T(8,128)(2,1)S(1)}, bf16[2,128,1024]{2,1,0:T(8,128)(2,1)S(1)}, u32[]{:S(2)}, u32[]{:S(2)}) collective-permute-start(bf16[2,128,1024]{2,1,0:T(8,128)(2,1)S(1)} %pad_maximum_fusion.1), channel_id=1, source_target_pairs={{0,4},{1,5},{2,6},{3,7},{4,0},{5,1},{6,2},{7,3},{8,12},{9,13},{10,... | collective-permute-start | bytes 1572872 | tf_op jit(solution)/shard_map/cond/branch_1_fun/ppermute | solution.py:479
  59.9 22.2 %collective-permute-start.13 = (bf16[2,128,1024]{2,1,0:T(8,128)(2,1)S(1)}, bf16[2,128,1024]{2,1,0:T(8,128)(2,1)S(1)}, u32[]{:S(2)}, u32[]{:S(2)}) collective-permute-start(bf16[2,128,1024]{2,1,0:T(8,128)(2,1)S(1)} %pad_maximum_fusion.5), channel_id=1, source_target_pairs={{0,2},{1,3},{2,0},{3,1},{4,6},{5,7},{6,4},{7,5},{8,10},{9,11},{10,... | collective-permute-start | bytes 1572872 | tf_op jit(solution)/shard_map/cond/branch_1_fun/ppermute | solution.py:479
  61.4 20.8 %collective-permute-start.11 = (bf16[2,128,1024]{2,1,0:T(8,128)(2,1)S(1)}, bf16[2,128,1024]{2,1,0:T(8,128)(2,1)S(1)}, u32[]{:S(2)}, u32[]{:S(2)}) collective-permute-start(bf16[2,128,1024]{2,1,0:T(8,128)(2,1)S(1)} %pad_maximum_fusion.4), channel_id=1, source_target_pairs={{0,4},{1,5},{2,6},{3,7},{4,0},{5,1},{6,2},{7,3},{8,12},{9,13},{10,... | collective-permute-start | bytes 1572872 | tf_op jit(solution)/shard_map/cond/branch_1_fun/ppermute | solution.py:479
  74.2 27.2 %collective-permute-start.4 = (bf16[4,128,2048]{2,1,0:T(8,128)(2,1)}, bf16[4,128,2048]{2,1,0:T(8,128)(2,1)}, u32[]{:S(2)}, u32[]{:S(2)}) collective-permute-start(bf16[4,128,2048]{2,1,0:T(8,128)(2,1)} %maximum_maximum_fusion), channel_id=1, source_target_pairs={{0,1},{1,0},{2,3},{3,2},{4,5},{5,4},{6,7},{7,6},{8,9},{9,8},{10,11... | collective-permute-start | bytes 6291464 | tf_op jit(solution)/shard_map/cond/branch_1_fun/ppermute | solution.py:479
  74.3 9.6 %collective-permute-start.7 = (bf16[64,512]{1,0:T(8,128)(2,1)S(1)}, bf16[64,512]{1,0:T(8,128)(2,1)S(1)}, u32[]{:S(2)}, u32[]{:S(2)}) collective-permute-start(bf16[64,512]{1,0:T(8,128)(2,1)S(1)} %bitcast.239), channel_id=1, source_target_pairs={{0,1},{1,0},{2,3},{3,2},{4,5},{5,4},{6,7},{7,6},{8,9},{9,8},{10,11... | collective-permute-start | bytes 196616 | tf_op jit(solution)/shard_map/cond/branch_1_fun/ppermute | solution.py:479
  83.8 21.3 %collective-permute-start.14 = (bf16[4,128,2048]{2,1,0:T(8,128)(2,1)}, bf16[4,128,2048]{2,1,0:T(8,128)(2,1)}, u32[]{:S(2)}, u32[]{:S(2)}) collective-permute-start(bf16[4,128,2048]{2,1,0:T(8,128)(2,1)} %maximum_maximum_fusion.1), channel_id=1, source_target_pairs={{0,1},{1,0},{2,3},{3,2},{4,5},{5,4},{6,7},{7,6},{8,9},{9,8},{10,11... | collective-permute-start | bytes 6291464 | tf_op jit(solution)/shard_map/cond/branch_1_fun/ppermute | solution.py:479
  83.9 6.0 %collective-permute-start.8 = (bf16[128,512]{1,0:T(8,128)(2,1)S(1)}, bf16[128,512]{1,0:T(8,128)(2,1)S(1)}, u32[]{:S(2)}, u32[]{:S(2)}) collective-permute-start(bf16[128,512]{1,0:T(8,128)(2,1)S(1)} %pad_maximum_fusion.7), channel_id=1, source_target_pairs={{0,2},{1,3},{2,0},{3,1},{4,6},{5,7},{6,4},{7,5},{8,10},{9,11},{10,... | collective-permute-start | bytes 393224 | tf_op jit(solution)/shard_map/cond/branch_1_fun/ppermute | solution.py:479
  89.9 8.3 %collective-permute-start.9 = (bf16[256,512]{1,0:T(8,128)(2,1)S(1)}, bf16[256,512]{1,0:T(8,128)(2,1)}, u32[]{:S(2)}, u32[]{:S(2)}) collective-permute-start(bf16[256,512]{1,0:T(8,128)(2,1)S(1)} %pad_maximum_fusion.6), channel_id=1, source_target_pairs={{0,4},{1,5},{2,6},{3,7},{4,0},{5,1},{6,2},{7,3},{8,12},{9,13},{10,... | collective-permute-start | bytes 786440 | tf_op jit(solution)/shard_map/cond/branch_1_fun/ppermute | solution.py:479
  90.5 23.9 %all-to-all-start = ((bf16[8,64,1408]{2,1,0:T(8,128)(2,1)}), bf16[8,64,1408]{2,1,0:T(8,128)(2,1)}, u32[]{:S(2)}, u32[]{:S(2)}) async-start(bf16[8,64,1408]{2,1,0:T(8,128)(2,1)} %get-tuple-element.76), calls=%async_computation | async-start | bytes 2883584 | tf_op jit(solution)/shard_map/cond/branch_1_fun/all_to_all | solution.py:601
  114.4 175.3 %all-gather.11.cloned.1.call-start = ((), (), s32[]{:S(2)}) async-start(), calls=%async_computation.11 | async-start | bytes 3604480 | tf_op jit(solution)/shard_map/all_gather | solution.py:709
  128.5 60.8 %copy-start.49 = (f32[256]{0:T(256)}, f32[256]{0:T(256)S(1)}, u32[]{:S(2)}) copy-start(f32[256]{0:T(256)S(1)} %get-tuple-element.461) | copy-start | bytes 3076
  128.5 60.8 %copy-start.50 = (f32[256]{0:T(256)}, f32[256]{0:T(256)S(1)}, u32[]{:S(2)}) copy-start(f32[256]{0:T(256)S(1)} %get-tuple-element.462) | copy-start | bytes 3076
  189.2 264.1 %reduce-scatter.7.cloned.1.call-start = ((), (), s32[]{:S(2)}) async-start(), calls=%async_computation.13 | async-start | bytes 3604480 | tf_op jit(solution)/shard_map/reduce_scatter | solution.py:766
  193.0 7.2 %collective-permute-start.15 = (f32[4,128,2048]{2,1,0:T(8,128)S(1)}, f32[4,128,2048]{2,1,0:T(8,128)S(1)}, u32[]{:S(2)}, u32[]{:S(2)}) collective-permute-start(f32[4,128,2048]{2,1,0:T(8,128)S(1)} %bitcast.208), channel_id=1, source_target_pairs={{0,1},{1,0},{2,3},{3,2},{4,5},{5,4},{6,7},{7,6},{8,9},{9,8},{10,11... | collective-permute-start | bytes 12582920 | tf_op jit(solution)/shard_map/cond/branch_1_fun/ppermute | solution.py:479
  201.8 14.0 %collective-permute-start.16 = (bf16[2,128,1024]{2,1,0:T(8,128)(2,1)S(1)}, bf16[2,128,1024]{2,1,0:T(8,128)(2,1)S(1)}, u32[]{:S(2)}, u32[]{:S(2)}) collective-permute-start(bf16[2,128,1024]{2,1,0:T(8,128)(2,1)S(1)} %pad_maximum_fusion.11), channel_id=1, source_target_pairs={{0,2},{1,3},{2,0},{3,1},{4,6},{5,7},{6,4},{7,5},{8,10},{9,11},{10,... | collective-permute-start | bytes 1572872 | tf_op jit(solution)/shard_map/cond/branch_1_fun/ppermute | solution.py:479
  201.9 14.0 %collective-permute-start.18 = (bf16[2,128,1024]{2,1,0:T(8,128)(2,1)S(1)}, bf16[2,128,1024]{2,1,0:T(8,128)(2,1)S(1)}, u32[]{:S(2)}, u32[]{:S(2)}) collective-permute-start(bf16[2,128,1024]{2,1,0:T(8,128)(2,1)S(1)} %slice.376), channel_id=1, source_target_pairs={{0,4},{1,5},{2,6},{3,7},{4,0},{5,1},{6,2},{7,3},{8,12},{9,13},{10,... | collective-permute-start | bytes 1572872 | tf_op jit(solution)/shard_map/cond/branch_1_fun/ppermute | solution.py:479
  216.1 13.3 %collective-permute-start.17 = (f32[1,128,1024]{2,1,0:T(8,128)S(1)}, f32[1,128,1024]{2,1,0:T(8,128)S(1)}, u32[]{:S(2)}, u32[]{:S(2)}) collective-permute-start(f32[1,128,1024]{2,1,0:T(8,128)S(1)} %get-tuple-element.500), channel_id=1, source_target_pairs={{0,4},{1,5},{2,6},{3,7},{4,0},{5,1},{6,2},{7,3},{8,12},{9,13},{10,... | collective-permute-start | bytes 1572872 | tf_op jit(solution)/shard_map/cond/branch_1_fun/ppermute | solution.py:479
  217.6 13.0 %collective-permute-start.19 = (f32[1,128,1024]{2,1,0:T(8,128)S(1)}, f32[1,128,1024]{2,1,0:T(8,128)S(1)}, u32[]{:S(2)}, u32[]{:S(2)}) collective-permute-start(f32[1,128,1024]{2,1,0:T(8,128)S(1)} %get-tuple-element.501), channel_id=1, source_target_pairs={{0,2},{1,3},{2,0},{3,1},{4,6},{5,7},{6,4},{7,5},{8,10},{9,11},{10,... | collective-permute-start | bytes 1572872 | tf_op jit(solution)/shard_map/cond/branch_1_fun/ppermute | solution.py:479
  231.3 6.6 %collective-permute-start.22 = (bf16[1,128,1024]{2,1,0:T(8,128)(2,1)S(1)}, bf16[1,128,1024]{2,1,0:T(8,128)(2,1)S(1)}, u32[]{:S(2)}, u32[]{:S(2)}) collective-permute-start(bf16[1,128,1024]{2,1,0:T(8,128)(2,1)S(1)} %get-tuple-element.505), channel_id=1, source_target_pairs={{0,4},{1,5},{2,6},{3,7},{4,0},{5,1},{6,2},{7,3},{8,12},{9,13},{10,... | collective-permute-start | bytes 786440 | tf_op jit(solution)/shard_map/cond/branch_1_fun/ppermute | solution.py:479
  231.9 7.3 %collective-permute-start.20 = (bf16[1,128,1024]{2,1,0:T(8,128)(2,1)S(1)}, bf16[1,128,1024]{2,1,0:T(8,128)(2,1)S(1)}, u32[]{:S(2)}, u32[]{:S(2)}) collective-permute-start(bf16[1,128,1024]{2,1,0:T(8,128)(2,1)S(1)} %get-tuple-element.504), channel_id=1, source_target_pairs={{0,2},{1,3},{2,0},{3,1},{4,6},{5,7},{6,4},{7,5},{8,10},{9,11},{10,... | collective-permute-start | bytes 786440 | tf_op jit(solution)/shard_map/cond/branch_1_fun/ppermute | solution.py:479
  237.9 11.6 %collective-permute-start.23 = (bf16[2,128,1024]{2,1,0:T(8,128)(2,1)S(1)}, bf16[2,128,1024]{2,1,0:T(8,128)(2,1)S(1)}, u32[]{:S(2)}, u32[]{:S(2)}) collective-permute-start(bf16[2,128,1024]{2,1,0:T(8,128)(2,1)S(1)} %pad_maximum_fusion.13), channel_id=1, source_target_pairs={{0,2},{1,3},{2,0},{3,1},{4,6},{5,7},{6,4},{7,5},{8,10},{9,11},{10,... | collective-permute-start | bytes 1572872 | tf_op jit(solution)/shard_map/cond/branch_1_fun/ppermute | solution.py:479
  239.2 10.5 %collective-permute-start.21 = (bf16[2,128,1024]{2,1,0:T(8,128)(2,1)S(1)}, bf16[2,128,1024]{2,1,0:T(8,128)(2,1)S(1)}, u32[]{:S(2)}, u32[]{:S(2)}) collective-permute-start(bf16[2,128,1024]{2,1,0:T(8,128)(2,1)S(1)} %pad_maximum_fusion.12), channel_id=1, source_target_pairs={{0,4},{1,5},{2,6},{3,7},{4,0},{5,1},{6,2},{7,3},{8,12},{9,13},{10,... | collective-permute-start | bytes 1572872 | tf_op jit(solution)/shard_map/cond/branch_1_fun/ppermute | solution.py:479
  249.9 4.2 collective-permute-start.24
  256.3 71.7 %copy-start.16 = (f32[128,2048]{1,0:T(8,128)}, f32[128,2048]{1,0:T(8,128)S(1)}, u32[]{:S(2)}) copy-start(f32[128,2048]{1,0:T(8,128)S(1)} %get-tuple-element.222) | copy-start | bytes 3145732
  289.8 163.5 %reduce-scatter.5.cloned.1.call-start = ((), (), s32[]{:S(2)}) async-start(), calls=%async_computation.12 | async-start | bytes 7208960 | tf_op jit(solution)/shard_map/reduce_scatter | solution.py:604
  312.6 226.2 %reduce-scatter.9.cloned.1.call-start = ((), (), s32[]{:S(2)}) async-start(), calls=%async_computation.14 | async-start | bytes 5242880 | tf_op jit(solution)/shard_map/reduce_scatter | solution.py:604
  328.5 4.2 collective-permute-start.25
  334.0 14.0 %collective-permute-start.26 = (bf16[2,128,1024]{2,1,0:T(8,128)(2,1)S(1)}, bf16[2,128,1024]{2,1,0:T(8,128)(2,1)S(1)}, u32[]{:S(2)}, u32[]{:S(2)}) collective-permute-start(bf16[2,128,1024]{2,1,0:T(8,128)(2,1)S(1)} %pad_maximum_fusion.15), channel_id=1, source_target_pairs={{0,2},{1,3},{2,0},{3,1},{4,6},{5,7},{6,4},{7,5},{8,10},{9,11},{10,... | collective-permute-start | bytes 1572872 | tf_op jit(solution)/shard_map/cond/branch_1_fun/ppermute | solution.py:479
  335.5 13.7 %collective-permute-start.28 = (bf16[2,128,1024]{2,1,0:T(8,128)(2,1)S(1)}, bf16[2,128,1024]{2,1,0:T(8,128)(2,1)S(1)}, u32[]{:S(2)}, u32[]{:S(2)}) collective-permute-start(bf16[2,128,1024]{2,1,0:T(8,128)(2,1)S(1)} %slice.391), channel_id=1, source_target_pairs={{0,4},{1,5},{2,6},{3,7},{4,0},{5,1},{6,2},{7,3},{8,12},{9,13},{10,... | collective-permute-start | bytes 1572872 | tf_op jit(solution)/shard_map/cond/branch_1_fun/ppermute | solution.py:479
  349.3 7.3 %collective-permute-start.27 = (bf16[1,128,1024]{2,1,0:T(8,128)(2,1)S(1)}, bf16[1,128,1024]{2,1,0:T(8,128)(2,1)S(1)}, u32[]{:S(2)}, u32[]{:S(2)}) collective-permute-start(bf16[1,128,1024]{2,1,0:T(8,128)(2,1)S(1)} %get-tuple-element.510), channel_id=1, source_target_pairs={{0,4},{1,5},{2,6},{3,7},{4,0},{5,1},{6,2},{7,3},{8,12},{9,13},{10,... | collective-permute-start | bytes 786440 | tf_op jit(solution)/shard_map/cond/branch_1_fun/ppermute | solution.py:479
  350.9 6.9 %collective-permute-start.29 = (bf16[1,128,1024]{2,1,0:T(8,128)(2,1)S(1)}, bf16[1,128,1024]{2,1,0:T(8,128)(2,1)S(1)}, u32[]{:S(2)}, u32[]{:S(2)}) collective-permute-start(bf16[1,128,1024]{2,1,0:T(8,128)(2,1)S(1)} %get-tuple-element.511), channel_id=1, source_target_pairs={{0,2},{1,3},{2,0},{3,1},{4,6},{5,7},{6,4},{7,5},{8,10},{9,11},{10,... | collective-permute-start | bytes 786440 | tf_op jit(solution)/shard_map/cond/branch_1_fun/ppermute | solution.py:479
  359.7 6.4 %collective-permute-start.32 = (bf16[1,128,1024]{2,1,0:T(8,128)(2,1)S(1)}, bf16[1,128,1024]{2,1,0:T(8,128)(2,1)S(1)}, u32[]{:S(2)}, u32[]{:S(2)}) collective-permute-start(bf16[1,128,1024]{2,1,0:T(8,128)(2,1)S(1)} %get-tuple-element.515), channel_id=1, source_target_pairs={{0,4},{1,5},{2,6},{3,7},{4,0},{5,1},{6,2},{7,3},{8,12},{9,13},{10,... | collective-permute-start | bytes 786440 | tf_op jit(solution)/shard_map/cond/branch_1_fun/ppermute | solution.py:479
  360.3 7.1 %collective-permute-start.30 = (bf16[1,128,1024]{2,1,0:T(8,128)(2,1)S(1)}, bf16[1,128,1024]{2,1,0:T(8,128)(2,1)S(1)}, u32[]{:S(2)}, u32[]{:S(2)}) collective-permute-start(bf16[1,128,1024]{2,1,0:T(8,128)(2,1)S(1)} %get-tuple-element.514), channel_id=1, source_target_pairs={{0,2},{1,3},{2,0},{3,1},{4,6},{5,7},{6,4},{7,5},{8,10},{9,11},{10,... | collective-permute-start | bytes 786440 | tf_op jit(solution)/shard_map/cond/branch_1_fun/ppermute | solution.py:479
  366.2 11.7 %collective-permute-start.33 = (bf16[2,128,1024]{2,1,0:T(8,128)(2,1)S(1)}, bf16[2,128,1024]{2,1,0:T(8,128)(2,1)S(1)}, u32[]{:S(2)}, u32[]{:S(2)}) collective-permute-start(bf16[2,128,1024]{2,1,0:T(8,128)(2,1)S(1)} %pad_maximum_fusion.17), channel_id=1, source_target_pairs={{0,2},{1,3},{2,0},{3,1},{4,6},{5,7},{6,4},{7,5},{8,10},{9,11},{10,... | collective-permute-start | bytes 1572872 | tf_op jit(solution)/shard_map/cond/branch_1_fun/ppermute | solution.py:479
  367.5 10.5 %collective-permute-start.31 = (bf16[2,128,1024]{2,1,0:T(8,128)(2,1)S(1)}, bf16[2,128,1024]{2,1,0:T(8,128)(2,1)S(1)}, u32[]{:S(2)}, u32[]{:S(2)}) collective-permute-start(bf16[2,128,1024]{2,1,0:T(8,128)(2,1)S(1)} %pad_maximum_fusion.16), channel_id=1, source_target_pairs={{0,4},{1,5},{2,6},{3,7},{4,0},{5,1},{6,2},{7,3},{8,12},{9,13},{10,... | collective-permute-start | bytes 1572872 | tf_op jit(solution)/shard_map/cond/branch_1_fun/ppermute | solution.py:479
  378.2 4.2 collective-permute-start.34
  453.3 110.9 %reduce-scatter.11.cloned.1.call-start = ((), (), s32[]{:S(2)}) async-start(), calls=%async_computation.15 | async-start | bytes 1310720 | tf_op jit(solution)/shard_map/reduce_scatter | solution.py:821
  472.0 14.1 %collective-permute-start.35 = (bf16[4,128,2048]{2,1,0:T(8,128)(2,1)}, bf16[4,128,2048]{2,1,0:T(8,128)(2,1)}, u32[]{:S(2)}, u32[]{:S(2)}) collective-permute-start(bf16[4,128,2048]{2,1,0:T(8,128)(2,1)} %bitcast.27), channel_id=1, source_target_pairs={{0,1},{1,0},{2,3},{3,2},{4,5},{5,4},{6,7},{7,6},{8,9},{9,8},{10,11... | collective-permute-start | bytes 6291464 | tf_op jit(solution)/shard_map/cond/branch_1_fun/ppermute | solution.py:479
  472.0 22.8 %collective-permute-start.40 = (bf16[4,128,2048]{2,1,0:T(8,128)(2,1)}, bf16[4,128,2048]{2,1,0:T(8,128)(2,1)}, u32[]{:S(2)}, u32[]{:S(2)}) collective-permute-start(bf16[4,128,2048]{2,1,0:T(8,128)(2,1)} %get-tuple-element.93), channel_id=1, source_target_pairs={{0,1},{1,0},{2,3},{3,2},{4,5},{5,4},{6,7},{7,6},{8,9},{9,8},{10,11... | collective-permute-start | bytes 6291464 | tf_op jit(solution)/shard_map/cond/branch_1_fun/ppermute | solution.py:479
  475.0 10.9 %collective-permute-start.45 = (f32[128,128]{0,1:T(8,128)S(1)}, f32[128,128]{0,1:T(8,128)S(1)}, u32[]{:S(2)}, u32[]{:S(2)}) collective-permute-start(f32[128,128]{0,1:T(8,128)S(1)} %fusion.27), channel_id=1, source_target_pairs={{0,16},{8,24},{16,0},{24,8},{1,17},{9,25},{17,1},{25,9},{2,18},{10... | collective-permute-start | bytes 196616 | tf_op jit(solution)/shard_map/cond/branch_1_fun/ppermute | solution.py:479
  476.7 27.7 %all-to-all-start.1 = ((bf16[8,64,1408]{2,1,0:T(8,128)(2,1)}), bf16[8,64,1408]{2,1,0:T(8,128)(2,1)S(1)}, u32[]{:S(2)}, u32[]{:S(2)}) async-start(bf16[8,64,1408]{2,1,0:T(8,128)(2,1)} %get-tuple-element.95), calls=%async_computation.1 | async-start | bytes 2883584 | tf_op jit(solution)/shard_map/cond/branch_1_fun/all_to_all | solution.py:608
  486.0 18.1 %collective-permute-start.46 = (f32[64,128]{0,1:T(8,128)S(1)}, f32[64,128]{0,1:T(8,128)S(1)}, u32[]{:S(2)}, u32[]{:S(2)}) collective-permute-start(f32[64,128]{0,1:T(8,128)S(1)} %slice_select_fusion), channel_id=1, source_target_pairs={{0,8},{8,0},{16,24},{24,16},{1,9},{9,1},{17,25},{25,17},{2,10},{10... | collective-permute-start | bytes 98312 | tf_op jit(solution)/shard_map/cond/branch_1_fun/ppermute | solution.py:479
  493.9 16.9 %collective-permute-start.36 = (bf16[2,128,1024]{2,1,0:T(8,128)(2,1)}, bf16[2,128,1024]{2,1,0:T(8,128)(2,1)}, u32[]{:S(2)}, u32[]{:S(2)}) collective-permute-start(bf16[2,128,1024]{2,1,0:T(8,128)(2,1)} %pad_maximum_fusion.18), channel_id=1, source_target_pairs={{0,2},{1,3},{2,0},{3,1},{4,6},{5,7},{6,4},{7,5},{8,10},{9,11},{10,... | collective-permute-start | bytes 1572872 | tf_op jit(solution)/shard_map/cond/branch_1_fun/ppermute | solution.py:479
  493.9 17.4 %collective-permute-start.38 = (bf16[2,128,1024]{2,1,0:T(8,128)(2,1)}, bf16[2,128,1024]{2,1,0:T(8,128)(2,1)}, u32[]{:S(2)}, u32[]{:S(2)}) collective-permute-start(bf16[2,128,1024]{2,1,0:T(8,128)(2,1)} %slice.406), channel_id=1, source_target_pairs={{0,4},{1,5},{2,6},{3,7},{4,0},{5,1},{6,2},{7,3},{8,12},{9,13},{10,... | collective-permute-start | bytes 1572872 | tf_op jit(solution)/shard_map/cond/branch_1_fun/ppermute | solution.py:479
  501.1 21.0 %collective-permute-start.41 = (bf16[2,128,1024]{2,1,0:T(8,128)(2,1)}, bf16[2,128,1024]{2,1,0:T(8,128)(2,1)}, u32[]{:S(2)}, u32[]{:S(2)}) collective-permute-start(bf16[2,128,1024]{2,1,0:T(8,128)(2,1)} %pad_maximum_fusion.19), channel_id=1, source_target_pairs={{0,2},{1,3},{2,0},{3,1},{4,6},{5,7},{6,4},{7,5},{8,10},{9,11},{10,... | collective-permute-start | bytes 1572872 | tf_op jit(solution)/shard_map/cond/branch_1_fun/ppermute | solution.py:479
  503.1 19.4 %collective-permute-start.43 = (bf16[2,128,1024]{2,1,0:T(8,128)(2,1)}, bf16[2,128,1024]{2,1,0:T(8,128)(2,1)}, u32[]{:S(2)}, u32[]{:S(2)}) collective-permute-start(bf16[2,128,1024]{2,1,0:T(8,128)(2,1)} %slice.417), channel_id=1, source_target_pairs={{0,4},{1,5},{2,6},{3,7},{4,0},{5,1},{6,2},{7,3},{8,12},{9,13},{10,... | collective-permute-start | bytes 1572872 | tf_op jit(solution)/shard_map/cond/branch_1_fun/ppermute | solution.py:479
  512.8 15.3 %collective-permute-start.37 = (bf16[1,128,1024]{2,1,0:T(8,128)(2,1)S(1)}, bf16[1,128,1024]{2,1,0:T(8,128)(2,1)S(1)}, u32[]{:S(2)}, u32[]{:S(2)}) collective-permute-start(bf16[1,128,1024]{2,1,0:T(8,128)(2,1)S(1)} %get-tuple-element.527), channel_id=1, source_target_pairs={{0,4},{1,5},{2,6},{3,7},{4,0},{5,1},{6,2},{7,3},{8,12},{9,13},{10,... | collective-permute-start | bytes 786440 | tf_op jit(solution)/shard_map/cond/branch_1_fun/ppermute | solution.py:479
  513.8 14.2 %collective-permute-start.39 = (bf16[1,128,1024]{2,1,0:T(8,128)(2,1)S(1)}, bf16[1,128,1024]{2,1,0:T(8,128)(2,1)S(1)}, u32[]{:S(2)}, u32[]{:S(2)}) collective-permute-start(bf16[1,128,1024]{2,1,0:T(8,128)(2,1)S(1)} %get-tuple-element.528), channel_id=1, source_target_pairs={{0,2},{1,3},{2,0},{3,1},{4,6},{5,7},{6,4},{7,5},{8,10},{9,11},{10,... | collective-permute-start | bytes 786440 | tf_op jit(solution)/shard_map/cond/branch_1_fun/ppermute | solution.py:479
  524.0 9.4 %collective-permute-start.42 = (bf16[1,128,1024]{2,1,0:T(8,128)(2,1)S(1)}, bf16[1,128,1024]{2,1,0:T(8,128)(2,1)S(1)}, u32[]{:S(2)}, u32[]{:S(2)}) collective-permute-start(bf16[1,128,1024]{2,1,0:T(8,128)(2,1)S(1)} %get-tuple-element.523), channel_id=1, source_target_pairs={{0,4},{1,5},{2,6},{3,7},{4,0},{5,1},{6,2},{7,3},{8,12},{9,13},{10,... | collective-permute-start | bytes 786440 | tf_op jit(solution)/shard_map/cond/branch_1_fun/ppermute | solution.py:479
  525.1 8.4 %collective-permute-start.44 = (bf16[1,128,1024]{2,1,0:T(8,128)(2,1)S(1)}, bf16[1,128,1024]{2,1,0:T(8,128)(2,1)S(1)}, u32[]{:S(2)}, u32[]{:S(2)}) collective-permute-start(bf16[1,128,1024]{2,1,0:T(8,128)(2,1)S(1)} %get-tuple-element.524), channel_id=1, source_target_pairs={{0,2},{1,3},{2,0},{3,1},{4,6},{5,7},{6,4},{7,5},{8,10},{9,11},{10,... | collective-permute-start | bytes 786440 | tf_op jit(solution)/shard_map/cond/branch_1_fun/ppermute | solution.py:479
  541.1 20.3 %all-to-all-start.3 = ((bf16[8,64,1040]{2,1,0:T(8,128)(2,1)}), bf16[8,64,1040]{2,1,0:T(8,128)(2,1)S(1)}, u32[]{:S(2)}, u32[]{:S(2)}) async-start(bf16[8,64,1040]{2,1,0:T(8,128)(2,1)} %pad_maximum_fusion.21), calls=%async_computation.6 | async-start | bytes 2359296 | tf_op jit(solution)/shard_map/all_to_all | solution.py:608
  (57 other events, 536.9 us)
Sparse Core Ops, SparseCore 0:
  9.7 30.6 all-gather.4
  42.6 81.0 all-gather.6
  125.2 104.9 all-gather.8
  232.2 57.4 all-gather.10
  291.9 54.8 reduce-scatter.6
  348.9 102.1 reduce-scatter.4
  453.4 80.0 reduce-scatter.8
  535.9 27.6 reduce-scatter.10

commit v6 on v5

--- a/solution.py
+++ b/solution.py
@@ -811,10 +811,10 @@
     away = spread_back(delta_all, delta_logits, half, half, mixer_weight, rate_wide, BF16, model // 4)
     own = spread_back(delta_all, delta_logits, 0, half, mixer_weight, rate_wide, F32, model // 4)
     away, own = away.reshape(-1, local, model), own.reshape(-1, local, model)
-    away, own, grad_inputs, gated, active, ffn_sums, grad_down = lax.optimization_barrier(
-        (away, own, grad_inputs, gated, active, ffn_sums, grad_down)
-    )
     input_sums = row_sums(grad_inputs)
+    away, own, gated, active, ffn_sums, grad_down = lax.optimization_barrier(
+        (away, own, gated, active, ffn_sums, grad_down)
+    )
     grad_rate = token_grad(normed, delta_logits[:, :heads])
     grad_out = token_grad(gated, delta_branch).astype(BF16)
     if aligned:

time: 580 us -> 580 us (level)
    unnamed x98 -> x92, local copies, waits for them, and re-layouts: 15.3 us -> 14.8 us
  transfers between devices with their start and end apart: 59 -> 59, of which waited for: 38 -> 38; matrix products, arithmetic and copies ran while one was open for 32% -> 31% of each run, Pallas kernels for 14% -> 14%
where the time goes in v6:
time: 580 us; the launch traced here: 573 us
  waiting for transfers between devices  191 us (33%)
  matrix products  90.3 us (16%)
  Pallas kernels  79.3 us (14%)
  other arithmetic  62.6 us (11%)
  starting transfers between devices  61.9 us (11%)
  local copies, waits for them, and re-layouts  43.9 us (8%)
  blocking collectives  26.9 us (5%)
  between operations  15.8 us (3%)
    ppermute x47, waiting for transfers between devices, exchange(): return lax.ppermute(value, axis, [(i, i ^ bit) for i in range(count)])  140 us
    ppermute x47, starting transfers between devices, exchange(): return lax.ppermute(value, axis, [(i, i ^ bit) for i in range(count)])  44.1 us
    dot_general x5, matrix products, token_grad(): return lax.dot_general(left, right, TN, preferred_element_type=F32)  32.6 us
    pallas_call x1, Pallas kernels, inner_forward(): pl.pallas_call(functools.partial(forward_kernel, heads, head_dim, parts),...  29.2 us
    psum x2, blocking collectives, feature_mean(): total = lax.psum(ordered, 'seq') / model  26.9 us
    pallas_call x1, Pallas kernels, inner_backward(): pl.pallas_call(functools.partial(backward_kernel, heads, head_dim, parts)...  25.2 us
    all_to_all x2, waiting for transfers between devices, shuffled(): lax.all_to_all(values, 'seq', 0, 0, tiled=True)  16.3 us
    unnamed x92, local copies, waits for them, and re-layouts  14.8 us
  transfers between devices with their start and end apart: 59, of which 38 were waited for; matrix products, arithmetic and copies ran while one was open for 31% of the time, Pallas kernels for 14%

profile of v6, /device:TPU:0, one launch (start us, length us, event | category | flops | bytes accessed | tf_op | source)
XLA Modules:
  0.0 573.0 jit_solution(10606468515362256273)
XLA Ops:
  13.2 5.2 all-to-all-start.2
  20.7 13.1 %all-to-all-done.2 = bf16[8,64,1024]{2,1,0:T(8,128)(2,1)S(1)} async-done(((bf16[8,64,1024]{2,1,0:T(8,128)(2,1)}), bf16[8,64,1024]{2,1,0:T(8,128)(2,1)S(1)}, u32[]{:S(2)}, u32[]{:S(2)}) %all-to-all-start.2) | async-done | bytes 1048608 | tf_op jit(solution)/shard_map/all_to_all | solution.py:601
  33.8 6.6 %all-gather.5.cloned.1.call-done.matrix_ref = bf16[256,2048]{1,0:T(8,128)(2,1)} async-done(((bf16[64,2048]{1,0:T(8,128)(2,1)}), bf16[256,2048]{1,0:T(8,128)(2,1)}) %all-gather.5.cloned.1.call-update) | async-done | bytes 1048592 | tf_op jit(solution)/shard_map/all_gather | solution.py:639
  41.8 3.1 cut_columns.3
  44.9 69.6 %conditional.4 = (bf16[1024,2048]{1,0:T(8,128)(2,1)}, bf16[2048,128]{1,0:T(8,128)(2,1)S(1)}, bf16[512,1408]{1,0:T(8,128)(2,1)}, f32[1024,2048]{1,0:T(8,128)}, f32[1024,1]{0,1:T(1,128)S(1)}) conditional(s32[]{:T(128)} %convert_element_type.293, () %tuple.54, (bf16[128,2048]{1,0:T(8,128)(2,1)S(1)}, bf16[64,128]{1,0:T(8,128)(2,1)S(1)}, ...), branch_computations={%region_1.2_spmd, %region_2.4_spmd} | conditional | flops 105102336 | bytes 92476480 | solution.py:630
  63.0 9.6 %collective-permute-done.3 = bf16[2,128,1024]{2,1,0:T(8,128)(2,1)S(1)} collective-permute-done((bf16[2,128,1024]{2,1,0:T(8,128)(2,1)S(1)}, bf16[2,128,1024]{2,1,0:T(8,128)(2,1)S(1)}, u32[]{:S(2)}, u32[]{:S(2)}) %collective-permute-start.3) | collective-permute-done | bytes 524320 | tf_op jit(solution)/shard_map/cond/branch_1_fun/ppermute | solution.py:479
  74.9 7.3 %collective-permute-done.13 = bf16[2,128,1024]{2,1,0:T(8,128)(2,1)S(1)} collective-permute-done((bf16[2,128,1024]{2,1,0:T(8,128)(2,1)S(1)}, bf16[2,128,1024]{2,1,0:T(8,128)(2,1)S(1)}, u32[]{:S(2)}, u32[]{:S(2)}) %collective-permute-start.13) | collective-permute-done | bytes 524320 | tf_op jit(solution)/shard_map/cond/branch_1_fun/ppermute | solution.py:479
  85.4 4.4 collective-permute-done.8
  90.5 4.3 all-to-all-start
  94.8 3.2 collective-permute-done.9
  101.3 3.7 pad_maximum_fusion
  105.0 6.3 %multiply_reduce_fusion = (f32[8,128]{1,0:T(8,128)S(1)}, f32[8,128,2048]{2,1,0:T(8,128)}) fusion(bf16[4,128,2048]{2,1,0:T(8,128)(2,1)} %collective-permute-done.14, bf16[1,128,1024]{2,1,0:T(8,128)(2,1)S(1)} %copy-done.35, bf16[1,128,1024]{2,1,0:T(8,128)(2,1)S(1)} %collective-permute-done.12, bf16[1,128,1024]{2,1,0:T(8,128)(2,1)S(1)} %copy-done.33, ...), kind=kLoop, calls=%fused_computation.5 | loop fusion | flops 37747712 | bytes 12587008 | tf_op jit(solution)/shard_map/reduce_sum | solution.py:702
  111.3 3.2 all-to-all-done
  117.8 4.3 multiply_convert_fusion.1
  131.3 10.7 %fusion.75.inputs_ref.pre_ref = f32[1024,1024]{1,0:T(8,128)} fusion(bf16[1024,2048]{1,0:T(8,128)(2,1)} %copy-done.13, bf16[2048,1024]{1,0:T(8,128)(2,1)} %all-gather.7.cloned.1.call-done.weight_ref), kind=kOutput, calls=%fused_computation.241 | convolution fusion | flops 4294967296 | bytes 12582912 | tf_op jit(solution)/shard_map/dot_general | solution.py:707
  142.1 29.2 %inner_forward.1 = (f32[1024,256]{1,0:T(8,128)}, f32[1024,2]{1,0:T(8,128)}, f32[8,3,4,64,128]{4,3,2,1,0:T(8,128)}, f32[8,8,128]{2,1,0:T(8,128)}, bf16[8,4,128,12...) custom-call(s32[1]{0:T(128)} %bitcast.51.slot_ref, f32[1024,1024]{1,0:T(8,128)} %fusion.75.inputs_ref.pre_ref, ...), custom_call_target="tpu_custom_call" | custom-call | tf_op jit(solution)/shard_map/inner_forward/pallas_call | solution.py:281
  175.3 13.2 %psum.14 = f32[2,8,128]{2,0,1:T(2,128)S(1)} all-reduce(f32[2,8,128]{2,0,1:T(2,128)S(1)} %select_bitcast_fusion.4), channel_id=1, replica_groups=mesh['rows'=4,'seq'=8] {'seq'}, use_global_device_ids=true, to_apply=%region_5.7 | all-reduce | flops 2048 | bytes 16384 | tf_op jit(solution)/shard_map/psum | solution.py:731
  192.9 63.3 %conditional.5 = (f32[128,2048]{1,0:T(8,128)S(1)}, bf16[1024,2048]{1,0:T(8,128)(2,1)}) conditional(s32[]{:T(128)} %convert_element_type.293, () %tuple.60, (bf16[128,2048]{1,0:T(8,128)(2,1)S(1)}, f32[512,2048]{1,0:T(8,128)S(1)}, f32[512,2048]{1,0:T(8,128)S(1)}, f32[2048]{0:T(1024)S(1)}) %tuple.159), branch_computations={%region_6.8_spmd, %region_7.10_spmd} | conditional | flops 54526080 | bytes 93333976 | solution.py:630
  193.1 7.1 %collective-permute-done.15 = f32[4,128,2048]{2,1,0:T(8,128)S(1)} collective-permute-done((f32[4,128,2048]{2,1,0:T(8,128)S(1)}, f32[4,128,2048]{2,1,0:T(8,128)S(1)}, u32[]{:S(2)}, u32[]{:S(2)}) %collective-permute-start.15) | collective-permute-done | bytes 4194336 | tf_op jit(solution)/shard_map/cond/branch_1_fun/ppermute | solution.py:479
  203.3 12.5 %collective-permute-done.16 = bf16[2,128,1024]{2,1,0:T(8,128)(2,1)S(1)} collective-permute-done((bf16[2,128,1024]{2,1,0:T(8,128)(2,1)S(1)}, bf16[2,128,1024]{2,1,0:T(8,128)(2,1)S(1)}, u32[]{:S(2)}, u32[]{:S(2)}) %collective-permute-start.16) | collective-permute-done | bytes 524320 | tf_op jit(solution)/shard_map/cond/branch_1_fun/ppermute | solution.py:479
  219.2 10.2 %collective-permute-done.17 = f32[1,128,1024]{2,1,0:T(8,128)S(1)} collective-permute-done((f32[1,128,1024]{2,1,0:T(8,128)S(1)}, f32[1,128,1024]{2,1,0:T(8,128)S(1)}, u32[]{:S(2)}, u32[]{:S(2)}) %collective-permute-start.17) | collective-permute-done | bytes 524320 | tf_op jit(solution)/shard_map/cond/branch_1_fun/ppermute | solution.py:479
  233.3 4.5 collective-permute-done.22
  240.8 8.8 %collective-permute-done.23 = bf16[2,128,1024]{2,1,0:T(8,128)(2,1)S(1)} collective-permute-done((bf16[2,128,1024]{2,1,0:T(8,128)(2,1)S(1)}, bf16[2,128,1024]{2,1,0:T(8,128)(2,1)S(1)}, u32[]{:S(2)}, u32[]{:S(2)}) %collective-permute-start.23) | collective-permute-done | bytes 524320 | tf_op jit(solution)/shard_map/cond/branch_1_fun/ppermute | solution.py:479
  249.9 4.1 collective-permute-done.24
  256.2 10.8 %fusion.76 = f32[1024,1408]{1,0:T(8,128)S(1)} fusion(bf16[1024,2048]{1,0:T(8,128)(2,1)} %get-tuple-element.223, bf16[2048,1408]{1,0:T(8,128)(2,1)} %all-gather.9.cloned.1.call-done), kind=kOutput, calls=%fused_computation.242 | convolution fusion | flops 5905580032 | bytes 15728640 | tf_op jit(solution)/shard_map/dot_general | solution.py:756
  267.0 2.5 copy-done.21
  271.6 7.0 %convolution_convert_fusion.2 = bf16[704,2048]{1,0:T(8,128)(2,1)} fusion(bf16[1024,704]{1,0:T(8,128)(2,1)S(1)} %multiply_convert_fusion.4, bf16[1024,2048]{1,0:T(8,128)(2,1)} %get-tuple-element.222), kind=kOutput, calls=%fused_computation.129 | convolution fusion | flops 2954231808 | bytes 8519680 | tf_op jit(solution)/shard_map/dot_general | solution.py:762
  278.5 11.2 %all-gather.11.cloned.1.call-done = bf16[704,2048]{1,0:T(8,128)(2,1)} async-done(((bf16[176,2048]{1,0:T(8,128)(2,1)}), bf16[704,2048]{1,0:T(8,128)(2,1)}) %all-gather.11.cloned.1.call-update) | async-done | bytes 2883600 | tf_op jit(solution)/shard_map/all_gather | solution.py:709
  290.0 9.1 %multiply_convert_fusion.3 = (bf16[1024,704]{1,0:T(8,128)(2,1)S(1)}, bf16[1024,704]{1,0:T(8,128)(2,1)S(1)}) fusion(f32[1024,1408]{1,0:T(8,128)} %copy-done.21, bf16[1024,2048]{1,0:T(8,128)(2,1)} %get-tuple-element.222, bf16[704,2048]{1,0:T(8,128)(2,1)} %all-gather.11.cloned.1.call-done), kind=kOutput, calls=%fused_computation.131 | convolution fusion | flops 2962161664 | bytes 15728640 | tf_op jit(solution)/shard_map/dot_general | solution.py:767
  301.7 10.9 %convolution_convert_fusion = bf16[2048,1408]{1,0:T(8,128)(2,1)} fusion(bf16[1024,2048]{1,0:T(8,128)(2,1)} %get-tuple-element.223, bf16[1024,1408]{1,0:T(8,128)(2,1)S(1)} %pad_maximum_fusion.20), kind=kOutput, calls=%fused_computation.127 | convolution fusion | flops 5908463616 | bytes 12845056 | tf_op jit(solution)/shard_map/dot_general | solution.py:762
  313.7 6.7 %fusion.29 = f32[512,2048]{1,0:T(8,128)S(1)} fusion(bf16[2048,1408]{1,0:T(8,128)(2,1)} %all-gather.9.cloned.1.call-done, bf16[1024,1408]{1,0:T(8,128)(2,1)} %copy-done.28), kind=kOutput, calls=%fused_computation.140 | convolution fusion | flops 2952790016 | bytes 11403264 | tf_op jit(solution)/shard_map/dot_general | solution.py:744
  320.4 6.5 %convolution_convert_fusion.4 = bf16[512,2048]{1,0:T(8,128)(2,1)S(1)} fusion(bf16[2048,1408]{1,0:T(8,128)(2,1)} %all-gather.9.cloned.1.call-done, bf16[1024,1408]{1,0:T(8,128)(2,1)S(1)} %copy-done.29), kind=kOutput, calls=%fused_computation.135 | convolution fusion | flops 2953838592 | bytes 9306112 | tf_op jit(solution)/shard_map/dot_general | solution.py:743
  326.9 56.7 %conditional.6 = (f32[128,2048]{1,0:T(8,128)}, bf16[1024,2048]{1,0:T(8,128)(2,1)}) conditional(s32[]{:T(128)} %convert_element_type.293, () %tuple.59, (bf16[128,2048]{1,0:T(8,128)(2,1)S(1)}, f32[128,2048]{1,0:T(8,128)S(1)}, f32[512,2048]{1,0:T(8,128)S(1)}, bf16[512,2048]{1,0:T(8,128)(2,1)S(1)}, f32[2048]{0:T(1024)S(1)}) %tuple.162), branch_computations={%region_9.11_spmd, %region_10.14_spmd} | conditional | flops 57934208 | bytes 73422240 | solution.py:630
  327.5 4.1 collective-permute-done.25
  335.9 11.0 %collective-permute-done.26 = bf16[2,128,1024]{2,1,0:T(8,128)(2,1)S(1)} collective-permute-done((bf16[2,128,1024]{2,1,0:T(8,128)(2,1)S(1)}, bf16[2,128,1024]{2,1,0:T(8,128)(2,1)S(1)}, u32[]{:S(2)}, u32[]{:S(2)}) %collective-permute-start.26) | collective-permute-done | bytes 524320 | tf_op jit(solution)/shard_map/cond/branch_1_fun/ppermute | solution.py:479
  350.4 5.2 collective-permute-done.27
  359.9 5.2 collective-permute-done.32
  366.5 2.5 collective-permute-start.31
  369.0 7.9 %collective-permute-done.33 = bf16[2,128,1024]{2,1,0:T(8,128)(2,1)S(1)} collective-permute-done((bf16[2,128,1024]{2,1,0:T(8,128)(2,1)S(1)}, bf16[2,128,1024]{2,1,0:T(8,128)(2,1)S(1)}, u32[]{:S(2)}, u32[]{:S(2)}) %collective-permute-start.33) | collective-permute-done | bytes 524320 | tf_op jit(solution)/shard_map/cond/branch_1_fun/ppermute | solution.py:479
  377.3 4.1 collective-permute-done.34
  383.6 5.8 %branch_backward.1 = (bf16[1024,256]{1,0:T(8,128)(2,1)}, f32[1024,256]{1,0:T(8,128)}, f32[1024,2]{1,0:T(8,128)}, f32[1,256]{1,0:T(1,128)S(1)}, f32[1,256]{1,0:T(1,128)S(1)}) custom-call(bf16[1024,2048]{1,0:T(8,128)(2,1)} %get-tuple-element.228.delta_ref, bf16[256,2048]{1,0:T(8,128)(2,1)} %all-gather.5.cloned.1.call-done.matrix_ref, ...), custom_call_target="tpu_custom_call" | custom-call | tf_op jit(solution)/shard_map/branch_backward/pallas_call | solution.py:438
  391.3 13.7 %psum.15 = f32[2,8,128]{2,0,1:T(2,128)S(1)} all-reduce(f32[2,8,128]{2,0,1:T(2,128)S(1)} %select_bitcast_fusion.2), channel_id=1, replica_groups=mesh['rows'=4,'seq'=8] {'seq'}, use_global_device_ids=true, to_apply=%region_13.15 | all-reduce | flops 2048 | bytes 16384 | tf_op jit(solution)/shard_map/psum | solution.py:731
  406.7 25.2 %inner_backward.1 = (bf16[1024,1024]{1,0:T(8,128)(2,1)}, bf16[1024,16]{1,0:T(8,128)(2,1)}, f32[64,512]{1,0:T(8,128)S(1)}, f32[64,128]{1,0:T(8,128)S(1)}, f32[64,128]{1,0:T(8,128)S(1)}, /*index=5*/f32[64,128]{1,0:T(8,128)S(1)}) custom-call(s32[1]{0:T(128)} %bitcast.51.slot_ref, f32[1024,1024]{1,0:T(8,128)} %fusion.75.inputs_ref.pre_ref, ...), custom_call_target="tpu_custom_call" | custom-call | tf_op jit(solution)/shard_map/inner_backward/pallas_call | solution.py:314
  431.9 9.5 %convolution_convert_fusion.1 = bf16[2048,1024]{1,0:T(8,128)(2,1)} fusion(bf16[1024,2048]{1,0:T(8,128)(2,1)} %copy-done.13, bf16[1024,1024]{1,0:T(8,128)(2,1)} %get-tuple-element.237.delta_ref), kind=kOutput, calls=%fused_computation.128 | convolution fusion | flops 4297064448 | bytes 10485760 | tf_op jit(solution)/shard_map/dot_general | solution.py:762
  443.2 2.2 copy-done
  445.4 4.3 spread_back.2
  449.7 4.6 spread_back.3
  455.3 4.6 convolution_convert_fusion.5
  459.9 6.0 %fusion.46 = f32[512,2048]{1,0:T(8,128)} fusion(bf16[704,2048]{1,0:T(8,128)(2,1)} %all-gather.11.cloned.1.call-done, bf16[1024,704]{1,0:T(8,128)(2,1)S(1)} %copy-done.40), kind=kOutput, calls=%fused_computation.160 | convolution fusion | flops 1476395008 | bytes 7864320 | tf_op jit(solution)/shard_map/dot_general | solution.py:744
  465.8 5.2 convolution_convert_fusion.3
  471.1 64.0 %conditional.7 = (bf16[2,64,2048]{2,1,0:T(8,128)(2,1)}, f32[2,64,2048]{2,1,0:T(8,128)}, f32[64,5504]{1,0:T(8,128)}, f32[64,5504]{1,0:T(8,128)}, f32[64,128]{0,1:...) conditional(s32[]{:T(128)} %convert_element_type.293, () %tuple.53, (f32[512,2048]{1,0:T(8,128)}, ...), branch_computations={%region_16.18_spmd, %region_17.25_spmd} | conditional | flops 15313031 | bytes 106042600 | solution.py:630
  473.9 3.6 all-to-all-start.1
  477.5 4.9 collective-permute-done.45
  482.6 6.0 %fusion.65 = (bf16[4,128,2048]{2,1,0:T(8,128)(2,1)S(1)}, f32[4,128,2048]{2,1,0:T(8,128)}) fusion(f32[4,128,2048]{2,1,0:T(8,128)} %bitcast.214, bf16[4,128,2048]{2,1,0:T(8,128)(2,1)} %collective-permute-done.35), kind=kLoop, calls=%fused_computation.231 | loop fusion | flops 3145728 | bytes 12582912 | tf_op jit(solution)/shard_map/convert.17
  492.2 4.5 fusion.64
  501.0 3.7 join_columns.2
  504.8 3.2 collective-permute-done.36
  511.6 7.6 %collective-permute-done.41 = bf16[2,128,1024]{2,1,0:T(8,128)(2,1)} collective-permute-done((bf16[2,128,1024]{2,1,0:T(8,128)(2,1)}, bf16[2,128,1024]{2,1,0:T(8,128)(2,1)}, u32[]{:S(2)}, u32[]{:S(2)}) %collective-permute-start.41) | collective-permute-done | bytes 524320 | tf_op jit(solution)/shard_map/cond/branch_1_fun/ppermute | solution.py:479
  522.8 2.4 collective-permute-done.37
  527.8 2.7 collective-permute-done.42
  535.2 2.5 pad_maximum_fusion.21
  537.7 3.6 all-to-all-start.3
  544.3 13.7 %all-to-all-done.3.refs_0_ = bf16[8,64,1040]{2,1,0:T(8,128)(2,1)S(1)} async-done(((bf16[8,64,1040]{2,1,0:T(8,128)(2,1)}), bf16[8,64,1040]{2,1,0:T(8,128)(2,1)S(1)}, u32[]{:S(2)}, u32[]{:S(2)}) %all-to-all-start.3) | async-done | bytes 1064992 | tf_op jit(solution)/shard_map/all_to_all | solution.py:608
  560.8 2.7 reduce-scatter.11.cloned.1.call-done
  (404 shorter events, 134.2 us)
Async XLA Ops:
  7.3 33.2 %copy-start.49 = (s32[2,6]{1,0:T(2,128)S(1)}, s32[2,6]{1,0:T(2,128)}, u32[]{:S(2)}) copy-start(s32[2,6]{1,0:T(2,128)} %param.48) | copy-start | bytes 148
  7.3 33.1 %all-gather.5.cloned.1.call-start = ((), (), s32[]{:S(2)}) async-start(), calls=%async_computation.8 | async-start | bytes 1310720 | tf_op jit(solution)/shard_map/all_gather | solution.py:639
  13.2 20.6 %all-to-all-start.2 = ((bf16[8,64,1024]{2,1,0:T(8,128)(2,1)}), bf16[8,64,1024]{2,1,0:T(8,128)(2,1)S(1)}, u32[]{:S(2)}, u32[]{:S(2)}) async-start(bf16[8,64,1024]{2,1,0:T(8,128)(2,1)} %cut_columns.2), calls=%async_computation.2 | async-start | bytes 2097152 | tf_op jit(solution)/shard_map/all_to_all | solution.py:601
  18.4 112.9 %all-gather.7.cloned.1.call-start = ((), (), s32[]{:S(2)}) async-start(), calls=%async_computation.9 | async-start | bytes 5242880 | tf_op jit(solution)/shard_map/all_gather | solution.py:649
  40.4 215.8 %all-gather.9.cloned.1.call-start = ((), (), s32[]{:S(2)}) async-start(), calls=%async_computation.10 | async-start | bytes 7208960 | tf_op jit(solution)/shard_map/all_gather | solution.py:662
  44.9 9.3 %collective-permute-start.2 = (bf16[1,128,1024]{2,1,0:T(8,128)(2,1)S(1)}, bf16[1,128,1024]{2,1,0:T(8,128)(2,1)S(1)}, u32[]{:S(2)}, u32[]{:S(2)}) collective-permute-start(bf16[1,128,1024]{2,1,0:T(8,128)(2,1)S(1)} %get-tuple-element.485), channel_id=1, source_target_pairs={{0,4},{1,5},{2,6},{3,7},{4,0},{5,1},{6,2},{7,3},{8,12},{9,13},{10,... | collective-permute-start | bytes 786440 | tf_op jit(solution)/shard_map/cond/branch_1_fun/ppermute | solution.py:479
  46.4 9.3 %collective-permute-start = (bf16[1,128,1024]{2,1,0:T(8,128)(2,1)S(1)}, bf16[1,128,1024]{2,1,0:T(8,128)(2,1)S(1)}, u32[]{:S(2)}, u32[]{:S(2)}) collective-permute-start(bf16[1,128,1024]{2,1,0:T(8,128)(2,1)S(1)} %get-tuple-element.484), channel_id=1, source_target_pairs={{0,2},{1,3},{2,0},{3,1},{4,6},{5,7},{6,4},{7,5},{8,10},{9,11},{10,... | collective-permute-start | bytes 786440 | tf_op jit(solution)/shard_map/cond/branch_1_fun/ppermute | solution.py:479
  47.9 3.7 collective-permute-start.5
  49.4 10.4 %collective-permute-start.12 = (bf16[1,128,1024]{2,1,0:T(8,128)(2,1)S(1)}, bf16[1,128,1024]{2,1,0:T(8,128)(2,1)S(1)}, u32[]{:S(2)}, u32[]{:S(2)}) collective-permute-start(bf16[1,128,1024]{2,1,0:T(8,128)(2,1)S(1)} %get-tuple-element.479), channel_id=1, source_target_pairs={{0,4},{1,5},{2,6},{3,7},{4,0},{5,1},{6,2},{7,3},{8,12},{9,13},{10,... | collective-permute-start | bytes 786440 | tf_op jit(solution)/shard_map/cond/branch_1_fun/ppermute | solution.py:479
  50.0 11.4 %collective-permute-start.10 = (bf16[1,128,1024]{2,1,0:T(8,128)(2,1)S(1)}, bf16[1,128,1024]{2,1,0:T(8,128)(2,1)S(1)}, u32[]{:S(2)}, u32[]{:S(2)}) collective-permute-start(bf16[1,128,1024]{2,1,0:T(8,128)(2,1)S(1)} %get-tuple-element.478), channel_id=1, source_target_pairs={{0,2},{1,3},{2,0},{3,1},{4,6},{5,7},{6,4},{7,5},{8,10},{9,11},{10,... | collective-permute-start | bytes 786440 | tf_op jit(solution)/shard_map/cond/branch_1_fun/ppermute | solution.py:479
  51.7 7.3 %collective-permute-start.6 = (bf16[128,128]{1,0:T(8,128)(2,1)S(1)}, bf16[128,128]{1,0:T(8,128)(2,1)S(1)}, u32[]{:S(2)}, u32[]{:S(2)}) collective-permute-start(bf16[128,128]{1,0:T(8,128)(2,1)S(1)} %pad_maximum_fusion.9), channel_id=1, source_target_pairs={{0,16},{8,24},{16,0},{24,8},{1,17},{9,25},{17,1},{25,9},{2,18},{10... | collective-permute-start | bytes 98312 | tf_op jit(solution)/shard_map/cond/branch_1_fun/ppermute | solution.py:479
  54.3 18.3 %collective-permute-start.3 = (bf16[2,128,1024]{2,1,0:T(8,128)(2,1)S(1)}, bf16[2,128,1024]{2,1,0:T(8,128)(2,1)S(1)}, u32[]{:S(2)}, u32[]{:S(2)}) collective-permute-start(bf16[2,128,1024]{2,1,0:T(8,128)(2,1)S(1)} %pad_maximum_fusion.2), channel_id=1, source_target_pairs={{0,2},{1,3},{2,0},{3,1},{4,6},{5,7},{6,4},{7,5},{8,10},{9,11},{10,... | collective-permute-start | bytes 1572872 | tf_op jit(solution)/shard_map/cond/branch_1_fun/ppermute | solution.py:479
  55.8 16.8 %collective-permute-start.1 = (bf16[2,128,1024]{2,1,0:T(8,128)(2,1)S(1)}, bf16[2,128,1024]{2,1,0:T(8,128)(2,1)S(1)}, u32[]{:S(2)}, u32[]{:S(2)}) collective-permute-start(bf16[2,128,1024]{2,1,0:T(8,128)(2,1)S(1)} %pad_maximum_fusion.1), channel_id=1, source_target_pairs={{0,4},{1,5},{2,6},{3,7},{4,0},{5,1},{6,2},{7,3},{8,12},{9,13},{10,... | collective-permute-start | bytes 1572872 | tf_op jit(solution)/shard_map/cond/branch_1_fun/ppermute | solution.py:479
  59.9 22.3 %collective-permute-start.13 = (bf16[2,128,1024]{2,1,0:T(8,128)(2,1)S(1)}, bf16[2,128,1024]{2,1,0:T(8,128)(2,1)S(1)}, u32[]{:S(2)}, u32[]{:S(2)}) collective-permute-start(bf16[2,128,1024]{2,1,0:T(8,128)(2,1)S(1)} %pad_maximum_fusion.5), channel_id=1, source_target_pairs={{0,2},{1,3},{2,0},{3,1},{4,6},{5,7},{6,4},{7,5},{8,10},{9,11},{10,... | collective-permute-start | bytes 1572872 | tf_op jit(solution)/shard_map/cond/branch_1_fun/ppermute | solution.py:479
  61.4 20.8 %collective-permute-start.11 = (bf16[2,128,1024]{2,1,0:T(8,128)(2,1)S(1)}, bf16[2,128,1024]{2,1,0:T(8,128)(2,1)S(1)}, u32[]{:S(2)}, u32[]{:S(2)}) collective-permute-start(bf16[2,128,1024]{2,1,0:T(8,128)(2,1)S(1)} %pad_maximum_fusion.4), channel_id=1, source_target_pairs={{0,4},{1,5},{2,6},{3,7},{4,0},{5,1},{6,2},{7,3},{8,12},{9,13},{10,... | collective-permute-start | bytes 1572872 | tf_op jit(solution)/shard_map/cond/branch_1_fun/ppermute | solution.py:479
  74.2 27.1 %collective-permute-start.4 = (bf16[4,128,2048]{2,1,0:T(8,128)(2,1)}, bf16[4,128,2048]{2,1,0:T(8,128)(2,1)}, u32[]{:S(2)}, u32[]{:S(2)}) collective-permute-start(bf16[4,128,2048]{2,1,0:T(8,128)(2,1)} %maximum_maximum_fusion), channel_id=1, source_target_pairs={{0,1},{1,0},{2,3},{3,2},{4,5},{5,4},{6,7},{7,6},{8,9},{9,8},{10,11... | collective-permute-start | bytes 6291464 | tf_op jit(solution)/shard_map/cond/branch_1_fun/ppermute | solution.py:479
  74.3 9.5 %collective-permute-start.7 = (bf16[64,512]{1,0:T(8,128)(2,1)S(1)}, bf16[64,512]{1,0:T(8,128)(2,1)S(1)}, u32[]{:S(2)}, u32[]{:S(2)}) collective-permute-start(bf16[64,512]{1,0:T(8,128)(2,1)S(1)} %bitcast.239), channel_id=1, source_target_pairs={{0,1},{1,0},{2,3},{3,2},{4,5},{5,4},{6,7},{7,6},{8,9},{9,8},{10,11... | collective-permute-start | bytes 196616 | tf_op jit(solution)/shard_map/cond/branch_1_fun/ppermute | solution.py:479
  83.8 21.2 %collective-permute-start.14 = (bf16[4,128,2048]{2,1,0:T(8,128)(2,1)}, bf16[4,128,2048]{2,1,0:T(8,128)(2,1)}, u32[]{:S(2)}, u32[]{:S(2)}) collective-permute-start(bf16[4,128,2048]{2,1,0:T(8,128)(2,1)} %maximum_maximum_fusion.1), channel_id=1, source_target_pairs={{0,1},{1,0},{2,3},{3,2},{4,5},{5,4},{6,7},{7,6},{8,9},{9,8},{10,11... | collective-permute-start | bytes 6291464 | tf_op jit(solution)/shard_map/cond/branch_1_fun/ppermute | solution.py:479
  83.9 5.9 %collective-permute-start.8 = (bf16[128,512]{1,0:T(8,128)(2,1)S(1)}, bf16[128,512]{1,0:T(8,128)(2,1)S(1)}, u32[]{:S(2)}, u32[]{:S(2)}) collective-permute-start(bf16[128,512]{1,0:T(8,128)(2,1)S(1)} %pad_maximum_fusion.7), channel_id=1, source_target_pairs={{0,2},{1,3},{2,0},{3,1},{4,6},{5,7},{6,4},{7,5},{8,10},{9,11},{10,... | collective-permute-start | bytes 393224 | tf_op jit(solution)/shard_map/cond/branch_1_fun/ppermute | solution.py:479
  89.9 8.2 %collective-permute-start.9 = (bf16[256,512]{1,0:T(8,128)(2,1)S(1)}, bf16[256,512]{1,0:T(8,128)(2,1)}, u32[]{:S(2)}, u32[]{:S(2)}) collective-permute-start(bf16[256,512]{1,0:T(8,128)(2,1)S(1)} %pad_maximum_fusion.6), channel_id=1, source_target_pairs={{0,4},{1,5},{2,6},{3,7},{4,0},{5,1},{6,2},{7,3},{8,12},{9,13},{10,... | collective-permute-start | bytes 786440 | tf_op jit(solution)/shard_map/cond/branch_1_fun/ppermute | solution.py:479
  90.5 23.9 %all-to-all-start = ((bf16[8,64,1408]{2,1,0:T(8,128)(2,1)}), bf16[8,64,1408]{2,1,0:T(8,128)(2,1)}, u32[]{:S(2)}, u32[]{:S(2)}) async-start(bf16[8,64,1408]{2,1,0:T(8,128)(2,1)} %get-tuple-element.76), calls=%async_computation | async-start | bytes 2883584 | tf_op jit(solution)/shard_map/cond/branch_1_fun/all_to_all | solution.py:601
  114.5 175.3 %all-gather.11.cloned.1.call-start = ((), (), s32[]{:S(2)}) async-start(), calls=%async_computation.11 | async-start | bytes 3604480 | tf_op jit(solution)/shard_map/all_gather | solution.py:709
  128.6 60.8 %copy-start.46 = (f32[256]{0:T(256)}, f32[256]{0:T(256)S(1)}, u32[]{:S(2)}) copy-start(f32[256]{0:T(256)S(1)} %get-tuple-element.459) | copy-start | bytes 3076
  128.6 60.8 %copy-start.47 = (f32[256]{0:T(256)}, f32[256]{0:T(256)S(1)}, u32[]{:S(2)}) copy-start(f32[256]{0:T(256)S(1)} %get-tuple-element.460) | copy-start | bytes 3076
  189.3 265.7 %reduce-scatter.7.cloned.1.call-start = ((), (), s32[]{:S(2)}) async-start(), calls=%async_computation.13 | async-start | bytes 3604480 | tf_op jit(solution)/shard_map/reduce_scatter | solution.py:766
  193.1 7.2 %collective-permute-start.15 = (f32[4,128,2048]{2,1,0:T(8,128)S(1)}, f32[4,128,2048]{2,1,0:T(8,128)S(1)}, u32[]{:S(2)}, u32[]{:S(2)}) collective-permute-start(f32[4,128,2048]{2,1,0:T(8,128)S(1)} %bitcast.208), channel_id=1, source_target_pairs={{0,1},{1,0},{2,3},{3,2},{4,5},{5,4},{6,7},{7,6},{8,9},{9,8},{10,11... | collective-permute-start | bytes 12582920 | tf_op jit(solution)/shard_map/cond/branch_1_fun/ppermute | solution.py:479
  201.9 14.0 %collective-permute-start.16 = (bf16[2,128,1024]{2,1,0:T(8,128)(2,1)S(1)}, bf16[2,128,1024]{2,1,0:T(8,128)(2,1)S(1)}, u32[]{:S(2)}, u32[]{:S(2)}) collective-permute-start(bf16[2,128,1024]{2,1,0:T(8,128)(2,1)S(1)} %pad_maximum_fusion.11), channel_id=1, source_target_pairs={{0,2},{1,3},{2,0},{3,1},{4,6},{5,7},{6,4},{7,5},{8,10},{9,11},{10,... | collective-permute-start | bytes 1572872 | tf_op jit(solution)/shard_map/cond/branch_1_fun/ppermute | solution.py:479
  201.9 14.0 %collective-permute-start.18 = (bf16[2,128,1024]{2,1,0:T(8,128)(2,1)S(1)}, bf16[2,128,1024]{2,1,0:T(8,128)(2,1)S(1)}, u32[]{:S(2)}, u32[]{:S(2)}) collective-permute-start(bf16[2,128,1024]{2,1,0:T(8,128)(2,1)S(1)} %slice.376), channel_id=1, source_target_pairs={{0,4},{1,5},{2,6},{3,7},{4,0},{5,1},{6,2},{7,3},{8,12},{9,13},{10,... | collective-permute-start | bytes 1572872 | tf_op jit(solution)/shard_map/cond/branch_1_fun/ppermute | solution.py:479
  216.2 13.3 %collective-permute-start.17 = (f32[1,128,1024]{2,1,0:T(8,128)S(1)}, f32[1,128,1024]{2,1,0:T(8,128)S(1)}, u32[]{:S(2)}, u32[]{:S(2)}) collective-permute-start(f32[1,128,1024]{2,1,0:T(8,128)S(1)} %get-tuple-element.498), channel_id=1, source_target_pairs={{0,4},{1,5},{2,6},{3,7},{4,0},{5,1},{6,2},{7,3},{8,12},{9,13},{10,... | collective-permute-start | bytes 1572872 | tf_op jit(solution)/shard_map/cond/branch_1_fun/ppermute | solution.py:479
  217.6 13.0 %collective-permute-start.19 = (f32[1,128,1024]{2,1,0:T(8,128)S(1)}, f32[1,128,1024]{2,1,0:T(8,128)S(1)}, u32[]{:S(2)}, u32[]{:S(2)}) collective-permute-start(f32[1,128,1024]{2,1,0:T(8,128)S(1)} %get-tuple-element.499), channel_id=1, source_target_pairs={{0,2},{1,3},{2,0},{3,1},{4,6},{5,7},{6,4},{7,5},{8,10},{9,11},{10,... | collective-permute-start | bytes 1572872 | tf_op jit(solution)/shard_map/cond/branch_1_fun/ppermute | solution.py:479
  231.2 6.6 %collective-permute-start.22 = (bf16[1,128,1024]{2,1,0:T(8,128)(2,1)S(1)}, bf16[1,128,1024]{2,1,0:T(8,128)(2,1)S(1)}, u32[]{:S(2)}, u32[]{:S(2)}) collective-permute-start(bf16[1,128,1024]{2,1,0:T(8,128)(2,1)S(1)} %get-tuple-element.503), channel_id=1, source_target_pairs={{0,4},{1,5},{2,6},{3,7},{4,0},{5,1},{6,2},{7,3},{8,12},{9,13},{10,... | collective-permute-start | bytes 786440 | tf_op jit(solution)/shard_map/cond/branch_1_fun/ppermute | solution.py:479
  232.0 7.2 %collective-permute-start.20 = (bf16[1,128,1024]{2,1,0:T(8,128)(2,1)S(1)}, bf16[1,128,1024]{2,1,0:T(8,128)(2,1)S(1)}, u32[]{:S(2)}, u32[]{:S(2)}) collective-permute-start(bf16[1,128,1024]{2,1,0:T(8,128)(2,1)S(1)} %get-tuple-element.502), channel_id=1, source_target_pairs={{0,2},{1,3},{2,0},{3,1},{4,6},{5,7},{6,4},{7,5},{8,10},{9,11},{10,... | collective-permute-start | bytes 786440 | tf_op jit(solution)/shard_map/cond/branch_1_fun/ppermute | solution.py:479
  237.9 11.7 %collective-permute-start.23 = (bf16[2,128,1024]{2,1,0:T(8,128)(2,1)S(1)}, bf16[2,128,1024]{2,1,0:T(8,128)(2,1)S(1)}, u32[]{:S(2)}, u32[]{:S(2)}) collective-permute-start(bf16[2,128,1024]{2,1,0:T(8,128)(2,1)S(1)} %pad_maximum_fusion.13), channel_id=1, source_target_pairs={{0,2},{1,3},{2,0},{3,1},{4,6},{5,7},{6,4},{7,5},{8,10},{9,11},{10,... | collective-permute-start | bytes 1572872 | tf_op jit(solution)/shard_map/cond/branch_1_fun/ppermute | solution.py:479
  239.2 10.5 %collective-permute-start.21 = (bf16[2,128,1024]{2,1,0:T(8,128)(2,1)S(1)}, bf16[2,128,1024]{2,1,0:T(8,128)(2,1)S(1)}, u32[]{:S(2)}, u32[]{:S(2)}) collective-permute-start(bf16[2,128,1024]{2,1,0:T(8,128)(2,1)S(1)} %pad_maximum_fusion.12), channel_id=1, source_target_pairs={{0,4},{1,5},{2,6},{3,7},{4,0},{5,1},{6,2},{7,3},{8,12},{9,13},{10,... | collective-permute-start | bytes 1572872 | tf_op jit(solution)/shard_map/cond/branch_1_fun/ppermute | solution.py:479
  249.8 4.2 collective-permute-start.24
  256.2 70.7 %copy-start.17 = (f32[128,2048]{1,0:T(8,128)}, f32[128,2048]{1,0:T(8,128)S(1)}, u32[]{:S(2)}) copy-start(f32[128,2048]{1,0:T(8,128)S(1)} %get-tuple-element.221) | copy-start | bytes 3145732
  289.8 165.2 %reduce-scatter.5.cloned.1.call-start = ((), (), s32[]{:S(2)}) async-start(), calls=%async_computation.12 | async-start | bytes 7208960 | tf_op jit(solution)/shard_map/reduce_scatter | solution.py:604
  312.6 222.6 %reduce-scatter.9.cloned.1.call-start = ((), (), s32[]{:S(2)}) async-start(), calls=%async_computation.14 | async-start | bytes 5242880 | tf_op jit(solution)/shard_map/reduce_scatter | solution.py:604
  327.4 4.2 collective-permute-start.25
  332.9 14.0 %collective-permute-start.26 = (bf16[2,128,1024]{2,1,0:T(8,128)(2,1)S(1)}, bf16[2,128,1024]{2,1,0:T(8,128)(2,1)S(1)}, u32[]{:S(2)}, u32[]{:S(2)}) collective-permute-start(bf16[2,128,1024]{2,1,0:T(8,128)(2,1)S(1)} %pad_maximum_fusion.15), channel_id=1, source_target_pairs={{0,2},{1,3},{2,0},{3,1},{4,6},{5,7},{6,4},{7,5},{8,10},{9,11},{10,... | collective-permute-start | bytes 1572872 | tf_op jit(solution)/shard_map/cond/branch_1_fun/ppermute | solution.py:479
  334.5 13.7 %collective-permute-start.28 = (bf16[2,128,1024]{2,1,0:T(8,128)(2,1)S(1)}, bf16[2,128,1024]{2,1,0:T(8,128)(2,1)S(1)}, u32[]{:S(2)}, u32[]{:S(2)}) collective-permute-start(bf16[2,128,1024]{2,1,0:T(8,128)(2,1)S(1)} %slice.391), channel_id=1, source_target_pairs={{0,4},{1,5},{2,6},{3,7},{4,0},{5,1},{6,2},{7,3},{8,12},{9,13},{10,... | collective-permute-start | bytes 1572872 | tf_op jit(solution)/shard_map/cond/branch_1_fun/ppermute | solution.py:479
  348.3 7.3 %collective-permute-start.27 = (bf16[1,128,1024]{2,1,0:T(8,128)(2,1)S(1)}, bf16[1,128,1024]{2,1,0:T(8,128)(2,1)S(1)}, u32[]{:S(2)}, u32[]{:S(2)}) collective-permute-start(bf16[1,128,1024]{2,1,0:T(8,128)(2,1)S(1)} %get-tuple-element.508), channel_id=1, source_target_pairs={{0,4},{1,5},{2,6},{3,7},{4,0},{5,1},{6,2},{7,3},{8,12},{9,13},{10,... | collective-permute-start | bytes 786440 | tf_op jit(solution)/shard_map/cond/branch_1_fun/ppermute | solution.py:479
  349.9 6.9 %collective-permute-start.29 = (bf16[1,128,1024]{2,1,0:T(8,128)(2,1)S(1)}, bf16[1,128,1024]{2,1,0:T(8,128)(2,1)S(1)}, u32[]{:S(2)}, u32[]{:S(2)}) collective-permute-start(bf16[1,128,1024]{2,1,0:T(8,128)(2,1)S(1)} %get-tuple-element.509), channel_id=1, source_target_pairs={{0,2},{1,3},{2,0},{3,1},{4,6},{5,7},{6,4},{7,5},{8,10},{9,11},{10,... | collective-permute-start | bytes 786440 | tf_op jit(solution)/shard_map/cond/branch_1_fun/ppermute | solution.py:479
  358.7 6.4 %collective-permute-start.32 = (bf16[1,128,1024]{2,1,0:T(8,128)(2,1)S(1)}, bf16[1,128,1024]{2,1,0:T(8,128)(2,1)S(1)}, u32[]{:S(2)}, u32[]{:S(2)}) collective-permute-start(bf16[1,128,1024]{2,1,0:T(8,128)(2,1)S(1)} %get-tuple-element.513), channel_id=1, source_target_pairs={{0,4},{1,5},{2,6},{3,7},{4,0},{5,1},{6,2},{7,3},{8,12},{9,13},{10,... | collective-permute-start | bytes 786440 | tf_op jit(solution)/shard_map/cond/branch_1_fun/ppermute | solution.py:479
  359.3 7.1 %collective-permute-start.30 = (bf16[1,128,1024]{2,1,0:T(8,128)(2,1)S(1)}, bf16[1,128,1024]{2,1,0:T(8,128)(2,1)S(1)}, u32[]{:S(2)}, u32[]{:S(2)}) collective-permute-start(bf16[1,128,1024]{2,1,0:T(8,128)(2,1)S(1)} %get-tuple-element.512), channel_id=1, source_target_pairs={{0,2},{1,3},{2,0},{3,1},{4,6},{5,7},{6,4},{7,5},{8,10},{9,11},{10,... | collective-permute-start | bytes 786440 | tf_op jit(solution)/shard_map/cond/branch_1_fun/ppermute | solution.py:479
  365.2 11.7 %collective-permute-start.33 = (bf16[2,128,1024]{2,1,0:T(8,128)(2,1)S(1)}, bf16[2,128,1024]{2,1,0:T(8,128)(2,1)S(1)}, u32[]{:S(2)}, u32[]{:S(2)}) collective-permute-start(bf16[2,128,1024]{2,1,0:T(8,128)(2,1)S(1)} %pad_maximum_fusion.17), channel_id=1, source_target_pairs={{0,2},{1,3},{2,0},{3,1},{4,6},{5,7},{6,4},{7,5},{8,10},{9,11},{10,... | collective-permute-start | bytes 1572872 | tf_op jit(solution)/shard_map/cond/branch_1_fun/ppermute | solution.py:479
  366.5 10.5 %collective-permute-start.31 = (bf16[2,128,1024]{2,1,0:T(8,128)(2,1)S(1)}, bf16[2,128,1024]{2,1,0:T(8,128)(2,1)S(1)}, u32[]{:S(2)}, u32[]{:S(2)}) collective-permute-start(bf16[2,128,1024]{2,1,0:T(8,128)(2,1)S(1)} %pad_maximum_fusion.16), channel_id=1, source_target_pairs={{0,4},{1,5},{2,6},{3,7},{4,0},{5,1},{6,2},{7,3},{8,12},{9,13},{10,... | collective-permute-start | bytes 1572872 | tf_op jit(solution)/shard_map/cond/branch_1_fun/ppermute | solution.py:479
  377.2 4.2 collective-permute-start.34
  441.4 122.0 %reduce-scatter.11.cloned.1.call-start = ((), (), s32[]{:S(2)}) async-start(), calls=%async_computation.15 | async-start | bytes 1310720 | tf_op jit(solution)/shard_map/reduce_scatter | solution.py:821
  471.1 11.5 %collective-permute-start.35 = (bf16[4,128,2048]{2,1,0:T(8,128)(2,1)}, bf16[4,128,2048]{2,1,0:T(8,128)(2,1)}, u32[]{:S(2)}, u32[]{:S(2)}) collective-permute-start(bf16[4,128,2048]{2,1,0:T(8,128)(2,1)} %bitcast.27), channel_id=1, source_target_pairs={{0,1},{1,0},{2,3},{3,2},{4,5},{5,4},{6,7},{7,6},{8,9},{9,8},{10,11... | collective-permute-start | bytes 6291464 | tf_op jit(solution)/shard_map/cond/branch_1_fun/ppermute | solution.py:479
  471.1 21.1 %collective-permute-start.40 = (bf16[4,128,2048]{2,1,0:T(8,128)(2,1)}, bf16[4,128,2048]{2,1,0:T(8,128)(2,1)}, u32[]{:S(2)}, u32[]{:S(2)}) collective-permute-start(bf16[4,128,2048]{2,1,0:T(8,128)(2,1)} %get-tuple-element.93), channel_id=1, source_target_pairs={{0,1},{1,0},{2,3},{3,2},{4,5},{5,4},{6,7},{7,6},{8,9},{9,8},{10,11... | collective-permute-start | bytes 6291464 | tf_op jit(solution)/shard_map/cond/branch_1_fun/ppermute | solution.py:479
  473.4 9.0 %collective-permute-start.45 = (f32[128,128]{0,1:T(8,128)S(1)}, f32[128,128]{0,1:T(8,128)S(1)}, u32[]{:S(2)}, u32[]{:S(2)}) collective-permute-start(f32[128,128]{0,1:T(8,128)S(1)} %fusion.27), channel_id=1, source_target_pairs={{0,16},{8,24},{16,0},{24,8},{1,17},{9,25},{17,1},{25,9},{2,18},{10... | collective-permute-start | bytes 196616 | tf_op jit(solution)/shard_map/cond/branch_1_fun/ppermute | solution.py:479
  473.9 27.1 %all-to-all-start.1 = ((bf16[8,64,1408]{2,1,0:T(8,128)(2,1)}), bf16[8,64,1408]{2,1,0:T(8,128)(2,1)S(1)}, u32[]{:S(2)}, u32[]{:S(2)}) async-start(bf16[8,64,1408]{2,1,0:T(8,128)(2,1)} %get-tuple-element.95), calls=%async_computation.1 | async-start | bytes 2883584 | tf_op jit(solution)/shard_map/cond/branch_1_fun/all_to_all | solution.py:608
  482.5 18.2 %collective-permute-start.46 = (f32[64,128]{0,1:T(8,128)S(1)}, f32[64,128]{0,1:T(8,128)S(1)}, u32[]{:S(2)}, u32[]{:S(2)}) collective-permute-start(f32[64,128]{0,1:T(8,128)S(1)} %slice_select_fusion), channel_id=1, source_target_pairs={{0,8},{8,0},{16,24},{24,16},{1,9},{9,1},{17,25},{25,17},{2,10},{10... | collective-permute-start | bytes 98312 | tf_op jit(solution)/shard_map/cond/branch_1_fun/ppermute | solution.py:479
  490.4 17.6 %collective-permute-start.36 = (bf16[2,128,1024]{2,1,0:T(8,128)(2,1)}, bf16[2,128,1024]{2,1,0:T(8,128)(2,1)}, u32[]{:S(2)}, u32[]{:S(2)}) collective-permute-start(bf16[2,128,1024]{2,1,0:T(8,128)(2,1)} %pad_maximum_fusion.18), channel_id=1, source_target_pairs={{0,2},{1,3},{2,0},{3,1},{4,6},{5,7},{6,4},{7,5},{8,10},{9,11},{10,... | collective-permute-start | bytes 1572872 | tf_op jit(solution)/shard_map/cond/branch_1_fun/ppermute | solution.py:479
  490.7 17.8 %collective-permute-start.38 = (bf16[2,128,1024]{2,1,0:T(8,128)(2,1)}, bf16[2,128,1024]{2,1,0:T(8,128)(2,1)}, u32[]{:S(2)}, u32[]{:S(2)}) collective-permute-start(bf16[2,128,1024]{2,1,0:T(8,128)(2,1)} %slice.406), channel_id=1, source_target_pairs={{0,4},{1,5},{2,6},{3,7},{4,0},{5,1},{6,2},{7,3},{8,12},{9,13},{10,... | collective-permute-start | bytes 1572872 | tf_op jit(solution)/shard_map/cond/branch_1_fun/ppermute | solution.py:479
  498.4 20.8 %collective-permute-start.41 = (bf16[2,128,1024]{2,1,0:T(8,128)(2,1)}, bf16[2,128,1024]{2,1,0:T(8,128)(2,1)}, u32[]{:S(2)}, u32[]{:S(2)}) collective-permute-start(bf16[2,128,1024]{2,1,0:T(8,128)(2,1)} %pad_maximum_fusion.19), channel_id=1, source_target_pairs={{0,2},{1,3},{2,0},{3,1},{4,6},{5,7},{6,4},{7,5},{8,10},{9,11},{10,... | collective-permute-start | bytes 1572872 | tf_op jit(solution)/shard_map/cond/branch_1_fun/ppermute | solution.py:479
  500.0 19.7 %collective-permute-start.43 = (bf16[2,128,1024]{2,1,0:T(8,128)(2,1)}, bf16[2,128,1024]{2,1,0:T(8,128)(2,1)}, u32[]{:S(2)}, u32[]{:S(2)}) collective-permute-start(bf16[2,128,1024]{2,1,0:T(8,128)(2,1)} %slice.417), channel_id=1, source_target_pairs={{0,4},{1,5},{2,6},{3,7},{4,0},{5,1},{6,2},{7,3},{8,12},{9,13},{10,... | collective-permute-start | bytes 1572872 | tf_op jit(solution)/shard_map/cond/branch_1_fun/ppermute | solution.py:479
  500.8 26.1 %copy-start.43 = (f32[64,128]{0,1:T(8,128)}, f32[64,128]{0,1:T(8,128)S(1)}, u32[]{:S(2)}) copy-start(f32[64,128]{0,1:T(8,128)S(1)} %select_add_fusion) | copy-start | bytes 98308 | tf_op jit(solution)/shard_map/cond
  510.0 15.2 %collective-permute-start.37 = (bf16[1,128,1024]{2,1,0:T(8,128)(2,1)S(1)}, bf16[1,128,1024]{2,1,0:T(8,128)(2,1)S(1)}, u32[]{:S(2)}, u32[]{:S(2)}) collective-permute-start(bf16[1,128,1024]{2,1,0:T(8,128)(2,1)S(1)} %get-tuple-element.525), channel_id=1, source_target_pairs={{0,4},{1,5},{2,6},{3,7},{4,0},{5,1},{6,2},{7,3},{8,12},{9,13},{10,... | collective-permute-start | bytes 786440 | tf_op jit(solution)/shard_map/cond/branch_1_fun/ppermute | solution.py:479
  511.1 14.2 %collective-permute-start.39 = (bf16[1,128,1024]{2,1,0:T(8,128)(2,1)S(1)}, bf16[1,128,1024]{2,1,0:T(8,128)(2,1)S(1)}, u32[]{:S(2)}, u32[]{:S(2)}) collective-permute-start(bf16[1,128,1024]{2,1,0:T(8,128)(2,1)S(1)} %get-tuple-element.526), channel_id=1, source_target_pairs={{0,2},{1,3},{2,0},{3,1},{4,6},{5,7},{6,4},{7,5},{8,10},{9,11},{10,... | collective-permute-start | bytes 786440 | tf_op jit(solution)/shard_map/cond/branch_1_fun/ppermute | solution.py:479
  521.2 9.3 %collective-permute-start.42 = (bf16[1,128,1024]{2,1,0:T(8,128)(2,1)S(1)}, bf16[1,128,1024]{2,1,0:T(8,128)(2,1)S(1)}, u32[]{:S(2)}, u32[]{:S(2)}) collective-permute-start(bf16[1,128,1024]{2,1,0:T(8,128)(2,1)S(1)} %get-tuple-element.521), channel_id=1, source_target_pairs={{0,4},{1,5},{2,6},{3,7},{4,0},{5,1},{6,2},{7,3},{8,12},{9,13},{10,... | collective-permute-start | bytes 786440 | tf_op jit(solution)/shard_map/cond/branch_1_fun/ppermute | solution.py:479
  522.3 8.3 %collective-permute-start.44 = (bf16[1,128,1024]{2,1,0:T(8,128)(2,1)S(1)}, bf16[1,128,1024]{2,1,0:T(8,128)(2,1)S(1)}, u32[]{:S(2)}, u32[]{:S(2)}) collective-permute-start(bf16[1,128,1024]{2,1,0:T(8,128)(2,1)S(1)} %get-tuple-element.522), channel_id=1, source_target_pairs={{0,2},{1,3},{2,0},{3,1},{4,6},{5,7},{6,4},{7,5},{8,10},{9,11},{10,... | collective-permute-start | bytes 786440 | tf_op jit(solution)/shard_map/cond/branch_1_fun/ppermute | solution.py:479
  537.7 20.3 %all-to-all-start.3 = ((bf16[8,64,1040]{2,1,0:T(8,128)(2,1)}), bf16[8,64,1040]{2,1,0:T(8,128)(2,1)S(1)}, u32[]{:S(2)}, u32[]{:S(2)}) async-start(bf16[8,64,1040]{2,1,0:T(8,128)(2,1)} %pad_maximum_fusion.21), calls=%async_computation.6 | async-start | bytes 2359296 | tf_op jit(solution)/shard_map/all_to_all | solution.py:608
  (54 other events, 483.6 us)
Sparse Core Ops, SparseCore 0:
  9.7 30.6 all-gather.4
  42.5 81.0 all-gather.6
  125.2 104.9 all-gather.8
  232.2 57.4 all-gather.10
  291.9 54.8 reduce-scatter.6
  348.9 102.1 reduce-scatter.4
  453.4 80.0 reduce-scatter.8
  535.9 27.5 reduce-scatter.10
